TPU v7x, 32 devices: a whole 2x2x4 slice. The times are simulated.
32 devices in a mesh: dp: 8 (over y, x, core), expert: 4 (over z).
Axes of the slice: x: 2, y: 2, z: 4, core: 2. Of those that a mesh axis runs over, the one named last changes fastest.
Arguments:
- expert_master: float32 [4, 7168, 2048], P('expert', 'dp'), may hold values from -6 to 6
- expert_first: bfloat16 [4, 7168, 2048], P('expert', 'dp'), may hold values from -0.29882812 to 0.29882812
- expert_second: bfloat16 [4, 7168, 2048], P('expert', 'dp'), may hold values from 9.9658966e-05 to 0.0099487305
- expert_grad: bfloat16 [4, 7168, 2048], P('expert', 'dp'), may hold values from -0.29882812 to 0.29882812
- latent_master: float32 [7168, 1536], P(('dp', 'expert')), may hold values from -6 to 6
- latent_first: bfloat16 [7168, 1536], P(('dp', 'expert')), may hold values from -0.29882812 to 0.29882812
- latent_second: bfloat16 [7168, 1536], P(('dp', 'expert')), may hold values from 9.9658966e-05 to 0.0099487305
- latent_grad: bfloat16 [7168, 1536], P(('dp', 'expert')), may hold values from -0.29882812 to 0.29882812
- step_count: int32 [1], replicated, may hold values from 1 to 11
- column_owner: int32 [16], replicated, may hold values from 0 to 15, each once
Outputs:
- expert_master_new: float32 [4, 7168, 2048], P('expert', 'dp')
- expert_first_new: bfloat16 [4, 7168, 2048], P('expert', 'dp')
- expert_second_new: bfloat16 [4, 7168, 2048], P('expert', 'dp')
- expert_served: bfloat16 [4, 114688, 128], P('expert', 'dp')
- expert_scales: float32 [4, 896], P('expert', 'dp')
- latent_master_new: float32 [7168, 1536], P(('dp', 'expert'))
- latent_first_new: bfloat16 [7168, 1536], P(('dp', 'expert'))
- latent_second_new: bfloat16 [7168, 1536], P(('dp', 'expert'))
- latent_served: bfloat16 [7168, 1536], P('dp')
- latent_scales: float32 [56, 12], replicated
Inputs may be any that keep to these rules, and one draw needn't show every extreme that they name: column_owner names each serving position of the 16 column blocks exactly once.
All inputs are finite; a program needn't handle non-finite values. Where the computation divides by a largest or mean magnitude, that divisor is 1e-20 or more.
Results may differ from a plain program's by a relative error of at most 0.0017.
Values may be sent and summed in bfloat16 or wider, within the bound.
No kernel may reach another device: no remote copies, remote signals or barrier semaphores. Data moves between devices by JAX's collectives and lax.ppermute only.
A program may use at most 128 MiB of HBM per device.

v0:
```python
import jax
import jax.numpy as jnp
from jax import lax
from jax.sharding import PartitionSpec as P

D = 7168
TILE = 128


BETA_ONE = 0.9
BETA_TWO = 0.95
LEARN_RATE = 0.2
DECAY_RATE = 0.1
ADAM_EPS = 1e-08
SCALE_EPS = 1e-06


def adamw_step(master, moment_one, moment_two, gradient, step_count):
    grad_value = gradient.astype(jnp.float32)
    first_new = BETA_ONE * moment_one.astype(jnp.float32) + (1.0 - BETA_ONE) * grad_value
    second_new = (
        BETA_TWO * moment_two.astype(jnp.float32) + (1.0 - BETA_TWO) * grad_value * grad_value
    )
    step_value = step_count[0].astype(jnp.float32)
    corr_one = 1.0 - jnp.power(jnp.float32(BETA_ONE), step_value)
    corr_two = 1.0 - jnp.power(jnp.float32(BETA_TWO), step_value)
    update = first_new / corr_one / (jnp.sqrt(second_new / corr_two) + ADAM_EPS)
    master_new = master - LEARN_RATE * (update + DECAY_RATE * master)
    return (master_new, first_new.astype(jnp.bfloat16), second_new.astype(jnp.bfloat16))


def row_maxima(weights):
    leading = weights.shape[:-1]
    tile_count = weights.shape[-1] // TILE
    return jnp.max(jnp.abs(weights).reshape(leading + (tile_count, TILE)), axis=-1)


def local_tiles(row_max, lead_rows):
    exp_count, row_count, tile_count = row_max.shape
    tile_span = row_count // TILE + 2
    buffer = jnp.zeros((exp_count, tile_span * TILE, tile_count), jnp.float32)
    buffer = lax.dynamic_update_slice(buffer, row_max, (jnp.int32(0), lead_rows, jnp.int32(0)))
    return jnp.max(buffer.reshape(exp_count, tile_span, TILE, tile_count), axis=2)


def place_tiles(tile_max, first_tile):
    exp_count, tile_span, tile_count = tile_max.shape
    global_map = jnp.zeros((exp_count, D // TILE + tile_span, tile_count), jnp.float32)
    return lax.dynamic_update_slice(global_map, tile_max, (jnp.int32(0), first_tile, jnp.int32(0)))


def quantized_rows(weights, tile_max, lead_rows):
    exp_count, row_count, col_count = weights.shape
    repeated = jnp.repeat(tile_max, TILE, axis=1)
    row_scale = lax.dynamic_slice_in_dim(repeated, lead_rows, row_count, 1)
    blocks = weights.reshape(exp_count, row_count, col_count // TILE, TILE)
    return (blocks / (row_scale[..., None] + SCALE_EPS)).reshape(weights.shape).astype(jnp.bfloat16)


def body(
    expert_master,
    expert_first,
    expert_second,
    expert_grad,
    latent_master,
    latent_first,
    latent_second,
    latent_grad,
    step_count,
    column_owner,
):
    master_new, first_new, second_new = adamw_step(
        expert_master, expert_first, expert_second, expert_grad, step_count
    )
    latent_new, latent_one, latent_two = adamw_step(
        latent_master, latent_first, latent_second, latent_grad, step_count
    )
    dp_count = lax.axis_size("dp")
    dp_pos = lax.axis_index("dp")
    exp_count, row_count, col_count = master_new.shape
    block_count = col_count // TILE
    slot_count = max(1, block_count // dp_count)
    total_tiles = D // TILE
    recv_rows = block_count * row_count
    recv_tiles = recv_rows // TILE
    positions = jnp.arange(block_count, dtype=jnp.int32)
    inverse = jnp.sum(
        positions[:, None] * (column_owner[:, None] == positions[None, :]).astype(jnp.int32), axis=0
    )
    receiver_ids = jnp.arange(dp_count, dtype=jnp.int32)[:, None]
    slot_ids = jnp.arange(slot_count, dtype=jnp.int32)[None, :]
    segment = (
        receiver_ids * block_count
        + jnp.mod(dp_pos - receiver_ids * block_count, dp_count)
        + slot_ids * dp_count
    )
    usable_slot = (segment < (receiver_ids + 1) * block_count).reshape(-1)
    send_block = jnp.take(inverse, jnp.minimum(segment // dp_count, block_count - 1)).reshape(-1)
    local_segments = jnp.arange(block_count, dtype=jnp.int32)
    source_dev = jnp.mod(dp_pos * block_count + local_segments, dp_count)
    pick_index = source_dev * slot_count + local_segments // dp_count
    blocks = master_new.reshape(exp_count, row_count, block_count, TILE)
    picked = jnp.take(blocks, send_block, axis=2)
    received = lax.all_to_all(
        jnp.where(usable_slot[None, None, :, None], picked, jnp.zeros((), picked.dtype)),
        "dp",
        split_axis=2,
        concat_axis=2,
        tiled=True,
    )
    ordered = jnp.take(received, pick_index, axis=2)
    tall = (
        jnp.transpose(ordered, (0, 2, 1, 3))
        .reshape(exp_count, recv_rows, TILE)
        .reshape(exp_count, recv_tiles, TILE, TILE)
    )
    expert_scales = jnp.max(jnp.abs(tall), axis=(2, 3))
    expert_served = (
        (tall / (expert_scales[:, :, None, None] + SCALE_EPS))
        .reshape(exp_count, recv_rows, TILE)
        .astype(jnp.bfloat16)
    )
    latent_block = lax.all_gather(latent_new, "expert", axis=0, tiled=True)
    block_rows = latent_block.shape[0]
    block_offset = dp_pos * block_rows
    block_lead = block_offset % TILE
    block_tiles = local_tiles(row_maxima(latent_block)[None], block_lead)
    block_map = lax.pmax(place_tiles(block_tiles, block_offset // TILE), "dp")
    latent_scales = block_map[0, :total_tiles]
    block_tiles = lax.dynamic_slice_in_dim(block_map, block_offset // TILE, block_tiles.shape[1], 1)
    latent_served = quantized_rows(latent_block[None], block_tiles, block_lead)[0]
    return (
        master_new,
        first_new,
        second_new,
        expert_served,
        expert_scales,
        latent_new,
        latent_one,
        latent_two,
        latent_served,
        latent_scales,
    )


def solution(mesh):
    placed = (
        P("expert", "dp", None),
        P("expert", "dp", None),
        P("expert", "dp", None),
        P("expert", "dp", None),
        P(("dp", "expert"), None),
        P(("dp", "expert"), None),
        P(("dp", "expert"), None),
        P(("dp", "expert"), None),
        P(),
        P(),
    )
    return jax.shard_map(
        body,
        mesh=mesh,
        in_specs=placed,
        out_specs=(
            P("expert", "dp", None),
            P("expert", "dp", None),
            P("expert", "dp", None),
            P("expert", "dp", None),
            P("expert", "dp"),
            P(("dp", "expert"), None),
            P(("dp", "expert"), None),
            P(("dp", "expert"), None),
            P("dp", None),
            P(),
        ),
        check_vma=False,
    )
```

profile of v0, /device:TPU:0, one launch (start us, length us, event | category | flops | bytes accessed | tf_op | source)
XLA Modules:
  0.0 239.2 jit_solution(1785071878645816883)
XLA Ops:
  7.2 6.1 %copy.99 = bf16[1,896,2048]{1,2,0:T(8,128)(2,1)} copy(bf16[1,896,2048]{2,1,0:T(8,128)(2,1)} %param.15) | data formatting | bytes 7340032 | tf_op args[3]
  13.3 6.0 %copy.100 = bf16[1,896,2048]{1,2,0:T(8,128)(2,1)} copy(bf16[1,896,2048]{2,1,0:T(8,128)(2,1)} %param.14) | data formatting | bytes 7340032 | tf_op args[2]
  19.3 8.5 %copy.102 = f32[1,896,2048]{1,2,0:T(8,128)} copy(f32[1,896,2048]{2,1,0:T(8,128)} %param.12) | data formatting | bytes 14680064 | tf_op args[0]
  28.6 6.1 %copy.98 = bf16[1,896,2048]{1,2,0:T(8,128)(2,1)} copy(bf16[1,896,2048]{2,1,0:T(8,128)(2,1)} %param.13) | data formatting | bytes 7340032 | tf_op args[1]
  34.6 13.8 %fusion.7 = (bf16[1,896,2048]{1,2,0:T(8,128)(2,1)}, f32[1,896,2048]{1,2,0:T(8,128)}, bf16[1,896,2048]{1,2,0:T(8,128)(2,1)}) fusion(bf16[1,896,2048]{1,2,0:T(8,128)(2,1)} %copy.99, bf16[1,896,2048]{1,2,0:T(8,128)(2,1)} %copy.100, f32[1,896,2048]{1,2,0:T(8,128)} %copy.102, f32[]{:T(128)} %bitcast.1, f32[]{:T(128)} %bitcast, bf16[1,896,2048]{1,2,0:T(8,128)(2,1)} %copy.98), kind=kLoop, calls=%fused_computation.17 | loop fusion | flops 36700160 | bytes 33030152 | tf_op jit(solution)/shard_map/convert_element_type | solution.py:29
  48.5 8.6 %copy.103 = f32[1,896,16,128]{3,1,2,0:T(8,128)} copy(f32[1,896,16,128]{1,3,2,0:T(8,128)} %bitcast.56) | data formatting | bytes 14680064 | tf_op jit(solution)/shard_map/reshape | solution.py:102
  57.0 0.0 copy-done.5
  57.0 0.1 select_reduce_fusion
  57.1 0.1 compare_select_fusion
  57.2 0.1 reshape.343
  57.3 0.1 add.186
  57.4 0.1 add.187
  57.5 0.1 add.193
  57.6 0.1 lt.60
  57.6 0.1 lt.61
  57.7 0.1 add.189
  57.8 0.7 gather_fusion
  58.5 7.0 %gather_fusion.1 = f32[16,896,128]{2,1,0:T(8,128)} fusion(f32[896,16,128]{2,0,1:T(8,128)} %bitcast.57, s32[1024]{0:T(1024)S(1)} %pad_clamp_fusion.1), kind=kCustom, calls=%fused_computation.clone | custom fusion | bytes 14680128 | tf_op jit(solution)/shard_map/jit(_take)/gather | solution.py:103
  65.6 7.1 %fusion.4 = f32[1,896,16,128]{3,1,0,2:T(8,128)} fusion(f32[16,896,128]{2,1,0:T(8,128)} %gather_fusion.1, pred[16]{0:T(512)(128)(4,1)S(1)} %get-tuple-element.83, pred[16]{0:T(512)(128)(4,1)S(1)} %get-tuple-element.91), kind=kLoop, calls=%fused_computation.12 | loop fusion | flops 3670016 | bytes 14680096 | tf_op jit(solution)/shard_map/jit(_where)/select_n | solution.py:105
  72.6 5.4 %all-to-all-start = ((f32[1,896,16,128]{3,1,0,2:T(8,128)}), f32[1,896,16,128]{3,1,0,2:T(8,128)}, u32[]{:S(2)}, u32[]{:S(2)}) async-start(f32[1,896,16,128]{3,1,0,2:T(8,128)} %fusion.4), calls=%async_computation | async-start | bytes 14680064 | tf_op jit(solution)/shard_map/all_to_all | solution.py:104
  78.1 0.2 all-gather.2.cloned.1.call-start
  78.3 0.0 copy-done
  78.3 0.0 copy-done.1
  78.4 2.8 %fusion.12 = (bf16[224,1536]{1,0:T(8,128)(2,1)}, f32[224,1536]{1,0:T(8,128)}, bf16[224,1536]{1,0:T(8,128)(2,1)}) fusion(bf16[224,1536]{1,0:T(8,128)(2,1)S(1)} %copy-done.1, bf16[224,1536]{1,0:T(8,128)(2,1)S(1)} %copy-done.2, f32[224,1536]{1,0:T(8,128)S(1)} %copy-done, f32[]{:T(128)} %bitcast.1, f32[]{:T(128)} %bitcast, bf16[224,1536]{1,0:T(8,128)(2,1)S(1)} %copy-done.3), kind=kLoop, calls=%fused_computation.26 | loop fusion | flops 6881280 | bytes 6193160 | tf_op jit(solution)/shard_map/convert_element_type | solution.py:29
  81.2 0.0 all-gather.2.cloned.1.call-update
  81.2 8.6 %copy.109 = f32[1,896,2048]{2,1,0:T(8,128)} copy(f32[1,896,2048]{1,2,0:T(8,128)} %get-tuple-element.86) | data formatting | bytes 14680064
  89.8 6.3 %copy.110 = bf16[1,896,2048]{2,1,0:T(8,128)(2,1)} copy(bf16[1,896,2048]{1,2,0:T(8,128)(2,1)} %get-tuple-element.87) | data formatting | bytes 7340032
  96.0 6.0 %copy.111 = bf16[1,896,2048]{2,1,0:T(8,128)(2,1)} copy(bf16[1,896,2048]{1,2,0:T(8,128)(2,1)} %get-tuple-element.85) | data formatting | bytes 7340032
  102.1 59.1 %all-to-all-done = f32[1,896,16,128]{3,1,0,2:T(8,128)} async-done(((f32[1,896,16,128]{3,1,0,2:T(8,128)}), f32[1,896,16,128]{3,1,0,2:T(8,128)}, u32[]{:S(2)}, u32[]{:S(2)}) %all-to-all-start) | async-done | bytes 7340064 | tf_op jit(solution)/shard_map/all_to_all | solution.py:104
  161.3 7.1 %gather_fusion.2 = f32[16,896,128]{2,1,0:T(8,128)} fusion(f32[896,16,128]{2,0,1:T(8,128)} %bitcast.7, s32[1024]{0:T(1024)S(1)} %pad_clamp_fusion), kind=kCustom, calls=%fused_computation.1.clone | custom fusion | bytes 14680128 | tf_op jit(solution)/shard_map/jit(_take)/gather | solution.py:111
  168.3 6.8 %fusion.5 = (f32[16,896]{1,0:T(8,128)S(1)}, f32[1,896,16,128]{3,1,2,0:T(8,128)}) fusion(f32[16,896,128]{2,1,0:T(8,128)} %gather_fusion.2, pred[16]{0:T(512)(128)(4,1)S(1)} %compare_and_fusion), kind=kLoop, calls=%fused_computation.14 | loop fusion | flops 5490688 | bytes 14737424 | tf_op jit(solution)/shard_map/reduce_max | solution.py:117
  175.1 0.1 reduce_max.40
  175.2 0.0 copy-start.4
  175.2 0.1 broadcast_bitcast_fusion.1
  175.3 8.8 %fusion.2 = bf16[1,14336,128]{2,1,0:T(8,128)(2,1)} fusion(f32[1,896,16,128]{3,1,2,0:T(8,128)} %get-tuple-element.82, f32[14336]{0:T(1024)S(1)} %broadcast_bitcast_fusion.1), kind=kLoop, calls=%fused_computation.8 | loop fusion | flops 3670016 | bytes 11067392 | tf_op jit(solution)/shard_map/convert_element_type | solution.py:121
  184.1 2.2 all-gather.2.cloned.1.call-done
  186.3 6.1 %copy.108 = f32[896,1536]{0,1:T(8,128)} copy(f32[896,1536]{1,0:T(8,128)} %all-gather.2.cloned.1.call-done) | data formatting | bytes 11010048 | tf_op jit(solution)/shard_map/all_gather | solution.py:123
  192.4 5.5 %abs.10 = f32[896,1536]{0,1:T(8,128)} abs(f32[896,1536]{0,1:T(8,128)} %copy.108) | non-fusion elementwise | flops 1376256 | bytes 11010048 | tf_op jit(solution)/shard_map/abs | solution.py:35
  197.9 2.9 %reduce_max.42 = f32[896,12]{0,1:T(8,128)S(1)} reduce(f32[896,12,128]{0,2,1:T(8,128)} %bitcast.58, f32[]{:T(128)} %constant.147.clone.1), dimensions={2}, to_apply=%region_3.5 | reduce | flops 1365504 | bytes 5548036 | tf_op jit(solution)/shard_map/reduce_max | solution.py:35
  200.8 0.1 reduce_max.43
  200.9 0.1 copy.106
  201.0 0.2 dynamic_update_slice.7
  201.2 24.5 %pmax.7 = f32[1,65,12]{2,1,0:T(8,128)S(1)} all-reduce(f32[1,65,12]{2,1,0:T(8,128)S(1)} %dynamic_update_slice.7), channel_id=1, replica_groups=mesh['dp'=8,'expert'=4] {'dp'}, use_global_device_ids=true, to_apply=%region_5.7 | all-reduce | flops 780 | bytes 6240 | tf_op jit(solution)/shard_map/pmax | solution.py:128
  225.7 0.1 copy.107
  225.8 0.1 broadcast_bitcast_fusion
  226.0 3.0 %fusion.8 = bf16[896,1536]{0,1:T(8,128)(2,1)S(1)} fusion(f32[896,1536]{0,1:T(8,128)} %copy.108, f32[896,12]{0,1:T(8,128)S(1)} %dynamic-slice_add_fusion), kind=kLoop, calls=%fused_computation.19 | loop fusion | flops 2752512 | bytes 8300544 | tf_op jit(solution)/shard_map/convert_element_type | solution.py:57
  229.0 2.7 %copy.112 = bf16[896,1536]{1,0:T(8,128)(2,1)} copy(bf16[896,1536]{0,1:T(8,128)(2,1)S(1)} %fusion.8) | data formatting | bytes 5505024
  231.7 0.7 copy.113
  (30 shorter events, 0.2 us)
Async XLA Ops:
  48.5 8.6 %copy-start.5 = (s32[16]{0:T(128)S(1)}, s32[16]{0:T(128)}, u32[]{:S(2)}) copy-start(s32[16]{0:T(128)} %param.21) | copy-start | bytes 196
  72.6 5.7 %copy-start = (f32[224,1536]{1,0:T(8,128)S(1)}, f32[224,1536]{1,0:T(8,128)}, u32[]{:S(2)}) copy-start(f32[224,1536]{1,0:T(8,128)} %param.16) | copy-start | bytes 4128772
  72.6 5.7 %copy-start.1 = (bf16[224,1536]{1,0:T(8,128)(2,1)S(1)}, bf16[224,1536]{1,0:T(8,128)(2,1)}, u32[]{:S(2)}) copy-start(bf16[224,1536]{1,0:T(8,128)(2,1)} %param.19) | copy-start | bytes 2064388
  72.6 5.7 %copy-start.2 = (bf16[224,1536]{1,0:T(8,128)(2,1)S(1)}, bf16[224,1536]{1,0:T(8,128)(2,1)}, u32[]{:S(2)}) copy-start(bf16[224,1536]{1,0:T(8,128)(2,1)} %param.18) | copy-start | bytes 2064388
  72.6 5.7 %copy-start.3 = (bf16[224,1536]{1,0:T(8,128)(2,1)S(1)}, bf16[224,1536]{1,0:T(8,128)(2,1)}, u32[]{:S(2)}) copy-start(bf16[224,1536]{1,0:T(8,128)(2,1)} %param.17) | copy-start | bytes 2064388
  72.6 88.6 %all-to-all-start = ((f32[1,896,16,128]{3,1,0,2:T(8,128)}), f32[1,896,16,128]{3,1,0,2:T(8,128)}, u32[]{:S(2)}, u32[]{:S(2)}) async-start(f32[1,896,16,128]{3,1,0,2:T(8,128)} %fusion.4), calls=%async_computation | async-start | bytes 14680064 | tf_op jit(solution)/shard_map/all_to_all | solution.py:104
  78.1 108.2 %all-gather.2.cloned.1.call-start = ((), (), s32[]{:S(2)}) async-start(), calls=%async_computation.1 | async-start | bytes 6881280 | tf_op jit(solution)/shard_map/all_gather | solution.py:123
  175.2 8.9 %copy-start.4 = (f32[112]{0:T(128)}, f32[112]{0:T(128)S(1)}, u32[]{:S(2)}) copy-start(f32[112]{0:T(128)S(1)} %reduce_max.40) | copy-start | bytes 1348
Sparse Core Ops, SparseCore 0:
  81.3 104.9 all-gather.1
where the time goes:
time: 241 us; the launch traced here: 239 us
  local copies, waits for them, and re-layouts  81.6 us (34%)
  waiting for transfers between devices  61.3 us (25%)
  other arithmetic  51.2 us (21%)
  blocking collectives  24.5 us (10%)
  between operations  15 us (6%)
  starting transfers between devices  5.66 us (2%)
    all_to_all x1, waiting for transfers between devices, body(): lax.all_to_all(jnp.where(usable_slot[None, None, :, None], picked, jnp.ze...  59.1 us
    unnamed x24, local copies, waits for them, and re-layouts  51.1 us
    pmax x1, blocking collectives, body(): block_map = lax.pmax(place_tiles(block_tiles, block_offset // TILE), 'dp')  24.5 us
    convert_element_type x2, other arithmetic, adamw_step(): second_new.astype(jnp.bfloat16)  16.7 us
    convert_element_type x1, other arithmetic, body(): expert_served = (tall / (expert_scales[:, :, None, None] + SCALE_EPS)).re...  8.78 us
    reshape x1, local copies, waits for them, and re-layouts, body(): blocks = master_new.reshape(exp_count, row_count, block_count, TILE)  8.56 us
    select_n x1, other arithmetic, body(): jnp.where(usable_slot[None, None, :, None], picked, jnp.zeros((), picked....  7.08 us
    gather x1, local copies, waits for them, and re-layouts, body(): ordered = jnp.take(received, pick_index, axis=2)  7.07 us
  transfers between devices with their start and end apart: 2, of which 2 were waited for; matrix products, arithmetic and copies ran while one was open for 19% of the time, Pallas kernels for 0%

commit v1 on v0

--- a/solution.py
+++ b/solution.py
@@ -1,6 +1,11 @@
+import functools
+import math
+
 import jax
 import jax.numpy as jnp
 from jax import lax
+from jax.experimental import pallas as pl
+from jax.experimental.pallas import tpu as pltpu
 from jax.sharding import PartitionSpec as P
 
 D = 7168
@@ -57,7 +62,7 @@
     return (blocks / (row_scale[..., None] + SCALE_EPS)).reshape(weights.shape).astype(jnp.bfloat16)
 
 
-def body(
+def general_body(
     expert_master,
     expert_first,
     expert_second,
@@ -143,6 +148,335 @@
     )
 
 
+CHUNK = 32
+F32 = jnp.float32
+BF16 = jnp.bfloat16
+VMEM_LIMIT = 40 * 1024 * 1024
+
+
+def adamw_tile(w, m, v, g, rate, corr):
+    g = g.astype(F32)
+    m1 = BETA_ONE * m.astype(F32) + (1.0 - BETA_ONE) * g
+    v1 = BETA_TWO * v.astype(F32) + (1.0 - BETA_TWO) * g * g
+    w1 = (1.0 - LEARN_RATE * DECAY_RATE) * w - rate * m1 / (jnp.sqrt(v1 * corr) + ADAM_EPS)
+    return w1, m1.astype(BF16), v1.astype(BF16)
+
+
+def sub_max(w1):
+    return jnp.max(jnp.abs(w1).reshape(w1.shape[0] // 8, 8, TILE), axis=0)
+
+
+def stack_max(parts):
+    rows = [jnp.max(p, axis=0, keepdims=True) for p in parts]
+    return jnp.max(jnp.concatenate(rows, axis=0), axis=1, keepdims=True)
+
+
+def expert_kernel(per_dest, n_dest, tiles, n_alias, blk_ref, scal_ref, *refs):
+    w_ref, m_ref, v_ref, g_ref = refs[:4]
+    w1_ref, m1_ref, v1_ref, s_ref = refs[4 + n_alias : 8 + n_alias]
+    q_refs = refs[8 + n_alias :]
+    rate, corr = scal_ref[0], scal_ref[1]
+    parts = []
+    for t in range(tiles):
+        rows = pl.ds(t * TILE, TILE)
+        w1, m1, v1 = adamw_tile(
+            w_ref[rows, :], m_ref[rows, :], v_ref[rows, :], g_ref[rows, :], rate, corr
+        )
+        w1_ref[rows, :] = w1
+        m1_ref[rows, :] = m1
+        v1_ref[rows, :] = v1
+        parts.append(sub_max(w1))
+    top = stack_max(parts)
+    s_ref[0] = jnp.broadcast_to(top, (tiles, TILE))
+    inv = 1.0 / (top + SCALE_EPS)
+    step = pl.program_id(0)
+    for d in range(n_dest):
+
+        @pl.when(step // per_dest == d)
+        def _(d=d):
+            for t in range(tiles):
+                rows = pl.ds(t * TILE, TILE)
+                q_refs[d][0, rows, :] = (w1_ref[rows, :] * inv[t : t + 1, :]).astype(BF16)
+
+
+def expert_group(arrays, state, blk, scal, n_dest, per_dest):
+    rows, cols = arrays[0].shape
+    tiles = rows // TILE
+    steps = n_dest * per_dest
+    column = lambda i, blk: (0, blk[i])
+    spec = pl.BlockSpec((rows, TILE), column)
+    any_spec = pl.BlockSpec(memory_space=pl.ANY)
+    n_alias = len(state)
+
+    def q_map(d):
+        return lambda i, blk: (jnp.clip(i - d * per_dest, 0, per_dest - 1), 0, 0)
+
+    out_shape = [
+        jax.ShapeDtypeStruct((rows, cols), F32),
+        jax.ShapeDtypeStruct((rows, cols), BF16),
+        jax.ShapeDtypeStruct((rows, cols), BF16),
+        jax.ShapeDtypeStruct((steps, tiles, TILE), F32),
+    ] + [jax.ShapeDtypeStruct((per_dest, rows, TILE), BF16)] * n_dest
+    out_specs = [spec, spec, spec, pl.BlockSpec((1, tiles, TILE), lambda i, blk: (i, 0, 0))] + [
+        pl.BlockSpec((1, rows, TILE), q_map(d)) for d in range(n_dest)
+    ]
+    elems = rows * TILE * steps
+    out = pl.pallas_call(
+        functools.partial(expert_kernel, per_dest, n_dest, tiles, n_alias),
+        grid_spec=pltpu.PrefetchScalarGridSpec(
+            num_scalar_prefetch=1,
+            grid=(steps,),
+            in_specs=[pl.BlockSpec(memory_space=pltpu.SMEM)] + [spec] * 4 + [any_spec] * n_alias,
+            out_specs=out_specs,
+        ),
+        out_shape=out_shape,
+        input_output_aliases={6 + i: i for i in range(n_alias)},
+        compiler_params=pltpu.CompilerParams(vmem_limit_bytes=VMEM_LIMIT),
+        cost_estimate=pl.CostEstimate(
+            flops=30 * elems, bytes_accessed=20 * elems, transcendentals=2 * elems
+        ),
+        name="expert_adamw",
+    )(blk, scal, *arrays, *state)
+    return out[:3], out[3], out[4:]
+
+
+def place_kernel(n_alias, src_ref, q_ref, *refs):
+    refs[n_alias][0, 0] = q_ref[0]
+
+
+def place_rows(served, src, q, dp_count):
+    per_dest, rows, _ = q.shape
+    n_alias = 0 if served is None else 1
+    any_spec = pl.BlockSpec(memory_space=pl.ANY)
+    return pl.pallas_call(
+        functools.partial(place_kernel, n_alias),
+        grid_spec=pltpu.PrefetchScalarGridSpec(
+            num_scalar_prefetch=1,
+            grid=(per_dest,),
+            in_specs=[pl.BlockSpec((1, rows, TILE), lambda j, src: (j, 0, 0))] + [any_spec] * n_alias,
+            out_specs=pl.BlockSpec((1, 1, rows, TILE), lambda j, src: (j, src[0], 0, 0)),
+        ),
+        out_shape=jax.ShapeDtypeStruct((per_dest, dp_count, rows, TILE), BF16),
+        input_output_aliases={2: 0} if n_alias else {},
+        compiler_params=pltpu.CompilerParams(vmem_limit_bytes=VMEM_LIMIT),
+        cost_estimate=pl.CostEstimate(
+            flops=0, bytes_accessed=4 * per_dest * rows * TILE, transcendentals=0
+        ),
+        name="place_served",
+    )(src, q, *(() if served is None else (served,)))
+
+
+def latent_kernel(chunks, width, scal_ref, w_ref, m_ref, v_ref, g_ref, w1_ref, m1_ref, v1_ref, top_ref):
+    rate, corr = scal_ref[0], scal_ref[1]
+    step = pl.program_id(0)
+    lane = lax.broadcasted_iota(jnp.int32, (8, TILE), 1)
+
+    @pl.when(step == 0)
+    def _():
+        top_ref[...] = jnp.zeros_like(top_ref)
+
+    tops = top_ref[...]
+    for b in range(width):
+        cols = pl.ds(b * TILE, TILE)
+        w1, m1, v1 = adamw_tile(
+            w_ref[:, cols], m_ref[:, cols], v_ref[:, cols], g_ref[:, cols], rate, corr
+        )
+        w1_ref[:, cols] = w1
+        m1_ref[:, cols] = m1
+        v1_ref[:, cols] = v1
+        parts = [sub_max(w1[c * CHUNK : (c + 1) * CHUNK]) for c in range(chunks)]
+        parts += [parts[-1]] * (8 - chunks)
+        tops = jnp.where(lane == step * width + b, stack_max(parts), tops)
+    top_ref[...] = tops
+
+
+def latent_update(arrays, scal):
+    rows, cols = arrays[0].shape
+    width = 4
+    spec = pl.BlockSpec((rows, width * TILE), lambda i: (0, i))
+    elems = rows * cols
+    return pl.pallas_call(
+        functools.partial(latent_kernel, rows // CHUNK, width),
+        grid=(cols // (width * TILE),),
+        in_specs=[pl.BlockSpec(memory_space=pltpu.SMEM)] + [spec] * 4,
+        out_specs=[spec] * 3 + [pl.BlockSpec((8, TILE), lambda i: (0, 0))],
+        out_shape=[
+            jax.ShapeDtypeStruct((rows, cols), F32),
+            jax.ShapeDtypeStruct((rows, cols), BF16),
+            jax.ShapeDtypeStruct((rows, cols), BF16),
+            jax.ShapeDtypeStruct((8, TILE), F32),
+        ],
+        compiler_params=pltpu.CompilerParams(vmem_limit_bytes=VMEM_LIMIT),
+        cost_estimate=pl.CostEstimate(
+            flops=30 * elems, bytes_accessed=18 * elems, transcendentals=2 * elems
+        ),
+        name="latent_adamw",
+    )(scal, *arrays)
+
+
+def latent_quant_kernel(chunks, width, off_ref, w1_ref, own_ref, prev_ref, next_ref, q_ref, ext):
+    per_tile = TILE // CHUNK
+    step = pl.program_id(0)
+    ext[0:chunks, :] = prev_ref[0:chunks, :]
+    ext[chunks : 2 * chunks, :] = own_ref[0:chunks, :]
+    ext[2 * chunks : 3 * chunks, :] = next_ref[0:chunks, :]
+    lane = lax.broadcasted_iota(jnp.int32, (8, TILE), 1)
+    off = off_ref[0]
+    rows = []
+    for c in range(chunks):
+        first = chunks + c - lax.rem(off + c, per_tile)
+        rows.append(jnp.max(ext[pl.ds(first, per_tile), :], axis=0, keepdims=True))
+    rows += [rows[-1]] * (8 - chunks)
+    tops = jnp.concatenate(rows, axis=0)
+    for b in range(width):
+        mine = jnp.where(lane == step * width + b, tops, 0.0)
+        inv = 1.0 / (jnp.max(mine, axis=1, keepdims=True) + SCALE_EPS)
+        cols = pl.ds(b * TILE, TILE)
+        for c in range(chunks):
+            span = pl.ds(c * CHUNK, CHUNK)
+            q_ref[span, cols] = (w1_ref[span, cols] * inv[c : c + 1, :]).astype(BF16)
+
+
+def latent_quant(w1, own, prev, nxt, off):
+    rows, cols = w1.shape
+    width = 4
+    chunks = rows // CHUNK
+    spec = pl.BlockSpec((rows, width * TILE), lambda i: (0, i))
+    small = pl.BlockSpec((8, TILE), lambda i: (0, 0))
+    return pl.pallas_call(
+        functools.partial(latent_quant_kernel, chunks, width),
+        grid=(cols // (width * TILE),),
+        in_specs=[pl.BlockSpec(memory_space=pltpu.SMEM), spec] + [small] * 3,
+        out_specs=spec,
+        out_shape=jax.ShapeDtypeStruct((rows, cols), BF16),
+        scratch_shapes=[pltpu.VMEM((3 * 8, TILE), F32)],
+        compiler_params=pltpu.CompilerParams(vmem_limit_bytes=VMEM_LIMIT),
+        cost_estimate=pl.CostEstimate(
+            flops=2 * rows * cols, bytes_accessed=6 * rows * cols, transcendentals=0
+        ),
+        name="latent_quant",
+    )(off, w1, own, prev, nxt)
+
+
+def fast_fits(expert_shape, latent_shape, dp_count, exp_axis):
+    exp_count, rows, cols = expert_shape
+    latent_rows, latent_cols = latent_shape
+    return (
+        exp_count == 1
+        and rows % TILE == 0
+        and (cols // TILE) % dp_count == 0
+        and dp_count & (dp_count - 1) == 0
+        and latent_rows % CHUNK == 0
+        and TILE <= latent_rows <= 8 * CHUNK
+        and latent_rows * exp_axis % TILE == 0
+        and latent_cols % (4 * TILE) == 0
+        and latent_cols <= TILE * TILE
+    )
+
+
+def fast_body(
+    expert_master,
+    expert_first,
+    expert_second,
+    expert_grad,
+    latent_master,
+    latent_first,
+    latent_second,
+    latent_grad,
+    step_count,
+    column_owner,
+):
+    dp_count = lax.axis_size("dp")
+    dp_pos = lax.axis_index("dp")
+    exp_axis = lax.axis_size("expert")
+    exp_pos = lax.axis_index("expert")
+    _, rows, cols = expert_master.shape
+    block_count = cols // TILE
+    per_dest = block_count // dp_count
+    tiles = rows // TILE
+
+    step_value = step_count[0].astype(F32)
+    corr_one = 1.0 - jnp.power(F32(BETA_ONE), step_value)
+    corr_two = 1.0 - jnp.power(F32(BETA_TWO), step_value)
+    scal = jnp.stack([LEARN_RATE / corr_one, 1.0 / corr_two])
+
+    latent_new, latent_one, latent_two, chunk_top = latent_update(
+        (latent_master, latent_first, latent_second, latent_grad), scal
+    )
+    latent_rows = latent_new.shape[0]
+    chunks = latent_rows // CHUNK
+    off = lax.rem((dp_pos * exp_axis + exp_pos) * chunks, TILE // CHUNK).astype(jnp.int32)
+    top_prev = lax.ppermute(chunk_top, "expert", [(i, i + 1) for i in range(exp_axis - 1)])
+    top_next = lax.ppermute(chunk_top, "expert", [(i + 1, i) for i in range(exp_axis - 1)])
+    latent_q = latent_quant(latent_new, chunk_top, top_prev, top_next, off.reshape(1))
+    latent_served = lax.all_gather(latent_q, "expert", axis=0, tiled=True)
+
+    positions = jnp.arange(block_count, dtype=jnp.int32)
+    inverse = jnp.sum(
+        positions[:, None] * (column_owner[:, None] == positions[None, :]).astype(jnp.int32), axis=0
+    )
+    order = sorted(range(1, dp_count), key=lambda k: (-bin(k >> 1).count("1"), k & 1, k)) + [0]
+    dests = dp_pos ^ jnp.array(order, jnp.int32)
+    slots = dests[:, None] * per_dest + jnp.arange(per_dest, dtype=jnp.int32)[None, :]
+    blk = jnp.take(inverse, slots.reshape(-1))
+    arrays = tuple(
+        a.reshape(rows, cols) for a in (expert_master, expert_first, expert_second, expert_grad)
+    )
+    group = max(1, dp_count // 4)
+    state, tops, sent = (), [], []
+    for at in range(0, dp_count, group):
+        part = blk[at * per_dest : (at + group) * per_dest]
+        state, top, q = expert_group(arrays, state, part, scal, group, per_dest)
+        tops.append(top[:, :, 0])
+        sent.extend(q)
+    got = [
+        q if k == 0 else lax.ppermute(q, "dp", [(i, i ^ k) for i in range(dp_count)])
+        for k, q in zip(order, sent)
+    ]
+    served = place_rows(None, dests[-1:], got[-1], dp_count)
+    for i in range(dp_count - 1):
+        served = place_rows(served, dests[i : i + 1], got[i], dp_count)
+    expert_served = served.reshape(1, block_count * rows, TILE)
+
+    small = jnp.concatenate(
+        [
+            jnp.concatenate(tops, axis=0).reshape(-1),
+            chunk_top[:chunks, : latent_new.shape[1] // TILE].reshape(-1),
+        ]
+    )
+    everyone = lax.all_gather(small, ("dp", "expert"), axis=0)
+    n_top = block_count * tiles
+    latent_chunks = everyone[:, n_top:].reshape(-1, TILE // CHUNK, latent_new.shape[1] // TILE)
+    latent_scales = jnp.max(latent_chunks, axis=1)
+    peers = everyone.reshape(dp_count, exp_axis, -1)
+    peers = lax.dynamic_index_in_dim(peers, exp_pos, 1, keepdims=False)[:, :n_top]
+    peers = peers.reshape(dp_count, dp_count, per_dest, tiles)
+    place = [order.index(k) for k in range(dp_count)]
+    sel = jnp.take(jnp.array(place, jnp.int32), dp_pos ^ jnp.arange(dp_count, dtype=jnp.int32))
+    hit = sel[:, None] == jnp.arange(dp_count, dtype=jnp.int32)[None, :]
+    mine = jnp.max(jnp.where(hit[:, :, None, None], peers, 0.0), axis=1)
+    expert_scales = jnp.transpose(mine, (1, 0, 2)).reshape(1, block_count * tiles)
+
+    return (
+        state[0][None],
+        state[1][None],
+        state[2][None],
+        expert_served,
+        expert_scales,
+        latent_new,
+        latent_one,
+        latent_two,
+        latent_served,
+        latent_scales,
+    )
+
+
+def body(*args):
+    if fast_fits(args[0].shape, args[4].shape, lax.axis_size("dp"), lax.axis_size("expert")):
+        return fast_body(*args)
+    return general_body(*args)
+
+
 def solution(mesh):
     placed = (
         P("expert", "dp", None),

time: 241 us -> 150 us (0.62)
  local copies, waits for them, and re-layouts: 81.6 us -> 21.3 us
  waiting for transfers between devices: 61.3 us -> 4.22 us
  other arithmetic: 51.2 us -> 0.77 us
  Pallas kernels: 0 us -> 43.5 us
  blocking collectives: 24.5 us -> 49.7 us
  starting transfers between devices: 5.66 us -> 14.5 us
    all_to_all x1 -> x0, waiting for transfers between devices: 59.1 us -> none  [body(): lax.all_to_all(jnp.where(usable_slot[None, None, :, None], picked, jnp.ze...]
    unnamed x0 -> x1, blocking collectives: none -> 49.7 us
    pallas_call x0 -> x14, Pallas kernels: none -> 43.5 us  [the longest x4 25.1 us: expert_group(): pl.pallas_call(functools.partial(expert_kernel, per_dest, n_dest, tiles,...]
    unnamed x24 -> x36, local copies, waits for them, and re-layouts: 51.1 us -> 17.3 us
    convert_element_type x4 -> x0, other arithmetic: 28.4 us -> none  [the longest x2 16.7 us: adamw_step(): second_new.astype(jnp.bfloat16)]
    pmax x1 -> x0, blocking collectives: 24.5 us -> none  [body(): block_map = lax.pmax(place_tiles(block_tiles, block_offset // TILE), 'dp')]
    ppermute x0 -> x9, starting transfers between devices: none -> 14.5 us  [the longest x7 8.27 us: fast_body(): lax.ppermute(q, 'dp', [(i, i ^ k) for i in range(dp_count)])]
    gather x3 -> x2, local copies, waits for them, and re-layouts: 14.8 us -> 1.3 us  [the longest x1 0.66 us: fast_body(): blk = jnp.take(inverse, slots.reshape(-1))]
  transfers between devices with their start and end apart: 2 -> 10, of which waited for: 2 -> 1; matrix products, arithmetic and copies ran while one was open for 19% -> 4% of each run, Pallas kernels for 0% -> 26%
where the time goes in v1:
time: 150 us; the launch traced here: 149 us
  blocking collectives  49.7 us (33%)
  Pallas kernels  43.5 us (29%)
  local copies, waits for them, and re-layouts  21.3 us (14%)
  between operations  15.1 us (10%)
  starting transfers between devices  14.5 us (10%)
  waiting for transfers between devices  4.22 us (3%)
    unnamed x1, blocking collectives  49.7 us
    pallas_call x4, Pallas kernels, expert_group(): pl.pallas_call(functools.partial(expert_kernel, per_dest, n_dest, tiles,...  25.1 us
    unnamed x36, local copies, waits for them, and re-layouts  17.3 us
    pallas_call x8, Pallas kernels, place_rows(): pl.pallas_call(functools.partial(place_kernel, n_alias), grid_spec=pltpu....  13.3 us
    ppermute x7, starting transfers between devices, fast_body(): lax.ppermute(q, 'dp', [(i, i ^ k) for i in range(dp_count)])  8.27 us
    ppermute x1, starting transfers between devices, fast_body(): lax.ppermute(chunk_top, 'expert', [(i, i + 1) for i in range(exp_axis - 1)])  4.92 us
    ppermute x1, waiting for transfers between devices, fast_body(): lax.ppermute(chunk_top, 'expert', [(i + 1, i) for i in range(exp_axis - 1)])  4.18 us
    pallas_call x1, Pallas kernels, latent_update(): pl.pallas_call(functools.partial(latent_kernel, rows // CHUNK, width), gr...  3.33 us
  transfers between devices with their start and end apart: 10, of which 1 were waited for; matrix products, arithmetic and copies ran while one was open for 4% of the time, Pallas kernels for 26%

profile of v1, /device:TPU:0, one launch (start us, length us, event | category | flops | bytes accessed | tf_op | source)
XLA Modules:
  0.0 149.0 jit_solution(17745323571552797752)
XLA Ops:
  8.1 1.3 copy-done.6
  9.5 1.1 copy-done.8
  10.6 1.1 copy-done.9
  11.7 1.1 copy-done.10
  12.8 3.3 %latent_adamw.1 = (f32[224,1536]{1,0:T(8,128)}, bf16[224,1536]{1,0:T(8,128)(2,1)}, bf16[224,1536]{1,0:T(8,128)(2,1)}, f32[8,128]{1,0:T(8,128)S(1)}) custom-call(f32[2]{0:T(128)S(1)} %pad_maximum_fusion.1.scal_ref, f32[224,1536]{1,0:T(8,128)S(1)} %copy-done.6, bf16[224,1536]{1,0:T(8,128)(2,1)S(1)} %copy-done.8, bf16[224,1536]{1,0:T(8,128)(2,1)S(1)} %copy-done.9, ...), custom_call_target="tpu_custom_call" | custom-call | flops 10321920 | bytes 6193152 | tf_op jit(solution)/shard_map/latent_adamw/pallas_call | solution.py:298
  16.1 4.9 %collective-permute-start.7 = (f32[8,128]{1,0:T(8,128)S(1)}, f32[8,128]{1,0:T(8,128)S(1)}, u32[]{:S(2)}, u32[]{:S(2)}) collective-permute-start(f32[8,128]{1,0:T(8,128)S(1)} %get-tuple-element.62.own_ref), channel_id=1, source_target_pairs={{0,1},{1,2},{2,3},{4,5},{5,6},{6,7},{8,9},{9,10},{10,11},{12,13},{... | collective-permute-start | bytes 12296 | tf_op jit(solution)/shard_map/ppermute | solution.py:409
  21.0 1.3 collective-permute-start.8
  22.4 4.2 %collective-permute-done.8.next_ref = f32[8,128]{1,0:T(8,128)S(1)} collective-permute-done((f32[8,128]{1,0:T(8,128)S(1)}, f32[8,128]{1,0:T(8,128)S(1)}, u32[]{:S(2)}, u32[]{:S(2)}) %collective-permute-start.8) | collective-permute-done | bytes 4128 | tf_op jit(solution)/shard_map/ppermute | solution.py:410
  26.5 1.3 copy-done.7
  27.9 1.8 %latent_quant.1 = bf16[224,1536]{1,0:T(8,128)(2,1)} custom-call(s32[1]{0:T(128)} %bitcast.11.off_ref, f32[224,1536]{1,0:T(8,128)S(1)} %copy-done.7, f32[8,128]{1,0:T(8,128)S(1)} %get-tuple-element.62.own_ref, f32[8,128]{1,0:T(8,128)S(1)} %collective-permute-done.7.prev_ref, f32[8,128]{1,0:T(8,128)S(1)} %collective-permute-done.8.next_ref), custom_call_target="tpu_custom_call" | custom-call | flops 688128 | bytes 2064384 | tf_op jit(solution)/shard_map/latent_quant/pallas_call | solution.py:346
  29.7 0.6 gather_fusion.1
  30.6 0.1 select_reduce_fusion.1
  30.7 0.7 gather_fusion
  31.5 2.0 %copy-done = bf16[1,896,2048]{2,1,0:T(8,128)(2,1)S(1)} copy-done((bf16[1,896,2048]{2,1,0:T(8,128)(2,1)S(1)}, bf16[1,896,2048]{2,1,0:T(8,128)(2,1)}, u32[]{:S(2)}) %copy-start) | copy-done | bytes 3670040
  33.5 2.0 %copy-done.2 = bf16[1,896,2048]{2,1,0:T(8,128)(2,1)S(1)} copy-done((bf16[1,896,2048]{2,1,0:T(8,128)(2,1)S(1)}, bf16[1,896,2048]{2,1,0:T(8,128)(2,1)}, u32[]{:S(2)}) %copy-start.2) | copy-done | bytes 3670040
  35.5 2.3 %copy-done.4 = bf16[1,896,2048]{2,1,0:T(8,128)(2,1)S(1)} copy-done((bf16[1,896,2048]{2,1,0:T(8,128)(2,1)S(1)}, bf16[1,896,2048]{2,1,0:T(8,128)(2,1)}, u32[]{:S(2)}) %copy-start.4) | copy-done | bytes 3670040
  37.9 7.5 %expert_adamw.4 = (f32[896,2048]{1,0:T(8,128)}, bf16[896,2048]{1,0:T(8,128)(2,1)}, bf16[896,2048]{1,0:T(8,128)(2,1)}, f32[4,7,128]{2,1,0:T(8,128)S(1)}, bf16[2,8...) custom-call(s32[4]{0:T(128)S(1)} %get-tuple-element.96.blk_ref, f32[2]{0:T(128)S(1)} %pad_maximum_fusion.1.scal_ref, ...), custom_call_target="tpu_custom_call" | custom-call | flops 13762560 | bytes 9175040 | tf_op jit(solution)/shard_map/expert_adamw/pallas_call | solution.py:224
  45.3 2.7 %collective-permute-start.6 = (bf16[2,896,128]{2,1,0:T(8,128)(2,1)}, bf16[2,896,128]{2,1,0:T(8,128)(2,1)S(1)}, u32[]{:S(2)}, u32[]{:S(2)}) collective-permute-start(bf16[2,896,128]{2,1,0:T(8,128)(2,1)} %get-tuple-element.56), channel_id=1, source_target_pairs={{0,24},{4,28},{8,16},{12,20},{16,8},{20,12},{24,0},{28,4},{1,25},{... | collective-permute-start | bytes 1376264 | tf_op jit(solution)/shard_map/ppermute | solution.py:433
  48.0 6.0 %expert_adamw.5 = (f32[896,2048]{1,0:T(8,128)}, bf16[896,2048]{1,0:T(8,128)(2,1)}, bf16[896,2048]{1,0:T(8,128)(2,1)}, f32[4,7,128]{2,1,0:T(8,128)S(1)}, bf16[2,8...) custom-call(s32[4]{0:T(128)S(1)} %get-tuple-element.97.blk_ref, ...), custom_call_target="tpu_custom_call", output_to_operand_aliasing={{0}: (6, {}), {1}: (7, {}), {2}: (8, {})} | custom-call | flops 13762560 | bytes 9175040 | tf_op jit(solution)/shard_map/expert_adamw/pallas_call | solution.py:224
  54.0 0.5 collective-permute-start.4
  54.5 0.6 collective-permute-start.3
  55.2 5.9 %expert_adamw.6 = (f32[896,2048]{1,0:T(8,128)}, bf16[896,2048]{1,0:T(8,128)(2,1)}, bf16[896,2048]{1,0:T(8,128)(2,1)}, f32[4,7,128]{2,1,0:T(8,128)S(1)}, bf16[2,8...) custom-call(s32[4]{0:T(128)S(1)} %get-tuple-element.98.blk_ref, ...), custom_call_target="tpu_custom_call", output_to_operand_aliasing={{0}: (6, {}), {1}: (7, {}), {2}: (8, {})} | custom-call | flops 13762560 | bytes 9175040 | tf_op jit(solution)/shard_map/expert_adamw/pallas_call | solution.py:224
  61.1 2.0 %collective-permute-start.2 = (bf16[2,896,128]{2,1,0:T(8,128)(2,1)}, bf16[2,896,128]{2,1,0:T(8,128)(2,1)}, u32[]{:S(2)}, u32[]{:S(2)}) collective-permute-start(bf16[2,896,128]{2,1,0:T(8,128)(2,1)} %get-tuple-element.52), channel_id=1, source_target_pairs={{0,12},{4,8},{8,4},{12,0},{16,28},{20,24},{24,20},{28,16},{1,13},{... | collective-permute-start | bytes 1376264 | tf_op jit(solution)/shard_map/ppermute | solution.py:433
  63.0 5.8 %expert_adamw.7 = (f32[896,2048]{1,0:T(8,128)}, bf16[896,2048]{1,0:T(8,128)(2,1)}, bf16[896,2048]{1,0:T(8,128)(2,1)}, f32[4,7,128]{2,1,0:T(8,128)S(1)}, bf16[2,8...) custom-call(s32[4]{0:T(128)S(1)} %get-tuple-element.99.blk_ref, ...), custom_call_target="tpu_custom_call", output_to_operand_aliasing={{0}: (6, {}), {1}: (7, {}), {2}: (8, {})} | custom-call | flops 13762560 | bytes 9175040 | tf_op jit(solution)/shard_map/expert_adamw/pallas_call | solution.py:224
  68.8 0.8 copy-done.12
  69.6 0.1 slice_reduce_fusion
  69.7 0.1 slice_reduce_fusion.1
  70.0 0.1 reshape.167
  70.1 0.2 maximum_dynamic-update-slice_fusion
  70.3 49.7 %all-reduce = f32[6272]{0:T(1024)S(1)} all-reduce(f32[6272]{0:T(1024)S(1)} %maximum_dynamic-update-slice_fusion), channel_id=2, replica_groups=mesh['dp'=8,'expert'=4] {'dp','expert'}, use_global_device_ids=true, to_apply=%add | all-reduce | flops 6272 | bytes 50176
  120.0 0.1 reshape.169
  120.2 2.4 %collective-permute-start = (bf16[2,896,128]{2,1,0:T(8,128)(2,1)}, bf16[2,896,128]{2,1,0:T(8,128)(2,1)S(1)}, u32[]{:S(2)}, u32[]{:S(2)}) collective-permute-start(bf16[2,896,128]{2,1,0:T(8,128)(2,1)} %copy-done.12), channel_id=1, source_target_pairs={{0,4},{4,0},{8,12},{12,8},{16,20},{20,16},{24,28},{28,24},{1,5},{5... | collective-permute-start | bytes 1376264 | tf_op jit(solution)/shard_map/ppermute | solution.py:433
  122.6 0.1 reshape.190
  122.8 0.1 reshape.173
  123.0 0.7 copy.41
  123.7 0.1 reshape.170
  123.9 0.1 select_reduce_fusion
  124.1 0.6 reshape.171
  124.7 0.7 fusion.2
  125.4 1.4 place_served.8.refs_0_
  126.8 1.4 place_served.9.refs_0_
  128.2 1.4 place_served.10.refs_0_
  129.6 2.4 %place_served.11.refs_0_ = bf16[2,8,896,128]{3,2,1,0:T(8,128)(2,1)} custom-call(s32[1]{0:T(128)} %get-tuple-element.89.src_ref, bf16[2,896,128]{2,1,0:T(8,128)(2,1)} %collective-permute-done.4.q_ref, bf16[2,8,896,128]{3,2,1,0:T(8,128)(2,1)} %place_served.10.refs_0_), custom_call_target="tpu_custom_call", output_to_operand_aliasing={{}: (2, {})} | custom-call | bytes 917504 | tf_op jit(solution)/shard_map/place_served/pallas_call | solution.py:251
  132.0 1.4 place_served.12.refs_0_
  133.5 2.4 %place_served.13.refs_0_ = bf16[2,8,896,128]{3,2,1,0:T(8,128)(2,1)} custom-call(s32[1]{0:T(128)} %get-tuple-element.91.src_ref, bf16[2,896,128]{2,1,0:T(8,128)(2,1)} %collective-permute-done.2.q_ref, bf16[2,8,896,128]{3,2,1,0:T(8,128)(2,1)} %place_served.12.refs_0_), custom_call_target="tpu_custom_call", output_to_operand_aliasing={{}: (2, {})} | custom-call | bytes 917504 | tf_op jit(solution)/shard_map/place_served/pallas_call | solution.py:251
  135.9 1.3 place_served.14.refs_0_
  137.3 1.4 place_served.15
  138.7 3.5 %copy.64 = bf16[896,1536]{1,0:T(8,128)(2,1)} copy(bf16[896,1536]{1,0:T(8,128)(2,1)} %all-gather.3.cloned.1.call-done) | data formatting | bytes 5505024
  (59 shorter events, 1.1 us)
Async XLA Ops:
  7.2 22.5 %copy-start.13 = (s32[8]{0:T(128)S(1)}, s32[8]{0:T(128)}, u32[]{:S(2)}) copy-start(s32[8]{0:T(128)} %constant.76.clone) | copy-start | bytes 100
  7.2 23.2 %copy-start.14 = (s32[8]{0:T(128)S(1)}, s32[8]{0:T(128)}, u32[]{:S(2)}) copy-start(s32[8]{0:T(128)} %constant.75.clone) | copy-start | bytes 100
  7.2 23.4 %copy-start.15 = (s32[16]{0:T(128)S(1)}, s32[16]{0:T(128)}, u32[]{:S(2)}) copy-start(s32[16]{0:T(128)} %param.21) | copy-start | bytes 196
  7.2 131.5 %all-gather.3.cloned.1.call-start = ((), (), s32[]{:S(2)}) async-start(), calls=%async_computation | async-start | bytes 3440640 | tf_op jit(solution)/shard_map/all_gather | solution.py:412
  8.1 1.3 copy-start.6
  9.5 1.1 copy-start.8
  10.6 1.1 copy-start.9
  11.7 1.1 copy-start.10
  16.1 6.2 %collective-permute-start.7 = (f32[8,128]{1,0:T(8,128)S(1)}, f32[8,128]{1,0:T(8,128)S(1)}, u32[]{:S(2)}, u32[]{:S(2)}) collective-permute-start(f32[8,128]{1,0:T(8,128)S(1)} %get-tuple-element.62.own_ref), channel_id=1, source_target_pairs={{0,1},{1,2},{2,3},{4,5},{5,6},{6,7},{8,9},{9,10},{10,11},{12,13},{... | collective-permute-start | bytes 12296 | tf_op jit(solution)/shard_map/ppermute | solution.py:409
  21.0 5.5 %collective-permute-start.8 = (f32[8,128]{1,0:T(8,128)S(1)}, f32[8,128]{1,0:T(8,128)S(1)}, u32[]{:S(2)}, u32[]{:S(2)}) collective-permute-start(f32[8,128]{1,0:T(8,128)S(1)} %get-tuple-element.62.own_ref), channel_id=1, source_target_pairs={{1,0},{2,1},{3,2},{5,4},{6,5},{7,6},{9,8},{10,9},{11,10},{13,12},{... | collective-permute-start | bytes 12296 | tf_op jit(solution)/shard_map/ppermute | solution.py:410
  26.5 1.3 copy-start.7
  31.5 2.0 %copy-start = (bf16[1,896,2048]{2,1,0:T(8,128)(2,1)S(1)}, bf16[1,896,2048]{2,1,0:T(8,128)(2,1)}, u32[]{:S(2)}) copy-start(bf16[1,896,2048]{2,1,0:T(8,128)(2,1)} %param.13) | copy-start | bytes 11010052
  33.5 2.0 %copy-start.2 = (bf16[1,896,2048]{2,1,0:T(8,128)(2,1)S(1)}, bf16[1,896,2048]{2,1,0:T(8,128)(2,1)}, u32[]{:S(2)}) copy-start(bf16[1,896,2048]{2,1,0:T(8,128)(2,1)} %param.14) | copy-start | bytes 11010052
  35.5 2.3 %copy-start.4 = (bf16[1,896,2048]{2,1,0:T(8,128)(2,1)S(1)}, bf16[1,896,2048]{2,1,0:T(8,128)(2,1)}, u32[]{:S(2)}) copy-start(bf16[1,896,2048]{2,1,0:T(8,128)(2,1)} %param.15) | copy-start | bytes 11010052
  37.8 10.1 %copy-start.1 = (bf16[1,896,2048]{2,1,0:T(8,128)(2,1)S(1)}, bf16[1,896,2048]{2,1,0:T(8,128)(2,1)}, u32[]{:S(2)}) copy-start(bf16[1,896,2048]{2,1,0:T(8,128)(2,1)} %param.13) | copy-start | bytes 11010052
  37.8 10.1 %copy-start.3 = (bf16[1,896,2048]{2,1,0:T(8,128)(2,1)S(1)}, bf16[1,896,2048]{2,1,0:T(8,128)(2,1)}, u32[]{:S(2)}) copy-start(bf16[1,896,2048]{2,1,0:T(8,128)(2,1)} %param.14) | copy-start | bytes 11010052
  37.9 10.1 %copy-start.5 = (bf16[1,896,2048]{2,1,0:T(8,128)(2,1)S(1)}, bf16[1,896,2048]{2,1,0:T(8,128)(2,1)}, u32[]{:S(2)}) copy-start(bf16[1,896,2048]{2,1,0:T(8,128)(2,1)} %param.15) | copy-start | bytes 11010052
  45.3 74.8 %collective-permute-start.6 = (bf16[2,896,128]{2,1,0:T(8,128)(2,1)}, bf16[2,896,128]{2,1,0:T(8,128)(2,1)S(1)}, u32[]{:S(2)}, u32[]{:S(2)}) collective-permute-start(bf16[2,896,128]{2,1,0:T(8,128)(2,1)} %get-tuple-element.56), channel_id=1, source_target_pairs={{0,24},{4,28},{8,16},{12,20},{16,8},{20,12},{24,0},{28,4},{1,25},{... | collective-permute-start | bytes 1376264 | tf_op jit(solution)/shard_map/ppermute | solution.py:433
  48.0 72.2 %collective-permute-start.5 = (bf16[2,896,128]{2,1,0:T(8,128)(2,1)}, bf16[2,896,128]{2,1,0:T(8,128)(2,1)S(1)}, u32[]{:S(2)}, u32[]{:S(2)}) collective-permute-start(bf16[2,896,128]{2,1,0:T(8,128)(2,1)} %get-tuple-element.55), channel_id=1, source_target_pairs={{0,28},{4,24},{8,20},{12,16},{16,12},{20,8},{24,4},{28,0},{1,29},{... | collective-permute-start | bytes 1376264 | tf_op jit(solution)/shard_map/ppermute | solution.py:433
  54.0 75.6 %collective-permute-start.4 = (bf16[2,896,128]{2,1,0:T(8,128)(2,1)}, bf16[2,896,128]{2,1,0:T(8,128)(2,1)}, u32[]{:S(2)}, u32[]{:S(2)}) collective-permute-start(bf16[2,896,128]{2,1,0:T(8,128)(2,1)} %get-tuple-element.54), channel_id=1, source_target_pairs={{0,8},{4,12},{8,0},{12,4},{16,24},{20,28},{24,16},{28,20},{1,9},{5... | collective-permute-start | bytes 1376264 | tf_op jit(solution)/shard_map/ppermute | solution.py:433
  54.5 77.5 %collective-permute-start.3 = (bf16[2,896,128]{2,1,0:T(8,128)(2,1)}, bf16[2,896,128]{2,1,0:T(8,128)(2,1)S(1)}, u32[]{:S(2)}, u32[]{:S(2)}) collective-permute-start(bf16[2,896,128]{2,1,0:T(8,128)(2,1)} %get-tuple-element.53), channel_id=1, source_target_pairs={{0,16},{4,20},{8,24},{12,28},{16,0},{20,4},{24,8},{28,12},{1,17},{... | collective-permute-start | bytes 1376264 | tf_op jit(solution)/shard_map/ppermute | solution.py:433
  61.1 7.7 %copy-start.11 = (bf16[2,896,128]{2,1,0:T(8,128)(2,1)}, bf16[2,896,128]{2,1,0:T(8,128)(2,1)S(1)}, u32[]{:S(2)}) copy-start(bf16[2,896,128]{2,1,0:T(8,128)(2,1)S(1)} %get-tuple-element.51) | copy-start | bytes 1376260
  61.1 72.4 %collective-permute-start.2 = (bf16[2,896,128]{2,1,0:T(8,128)(2,1)}, bf16[2,896,128]{2,1,0:T(8,128)(2,1)}, u32[]{:S(2)}, u32[]{:S(2)}) collective-permute-start(bf16[2,896,128]{2,1,0:T(8,128)(2,1)} %get-tuple-element.52), channel_id=1, source_target_pairs={{0,12},{4,8},{8,4},{12,0},{16,28},{20,24},{24,20},{28,16},{1,13},{... | collective-permute-start | bytes 1376264 | tf_op jit(solution)/shard_map/ppermute | solution.py:433
  68.8 0.8 copy-start.12
  120.1 15.8 %collective-permute-start.1 = (bf16[2,896,128]{2,1,0:T(8,128)(2,1)}, bf16[2,896,128]{2,1,0:T(8,128)(2,1)S(1)}, u32[]{:S(2)}, u32[]{:S(2)}) collective-permute-start(bf16[2,896,128]{2,1,0:T(8,128)(2,1)} %copy-done.11), channel_id=1, source_target_pairs={{0,20},{4,16},{8,28},{12,24},{16,4},{20,0},{24,12},{28,8},{1,21},{... | collective-permute-start | bytes 1376264 | tf_op jit(solution)/shard_map/ppermute | solution.py:433
  120.2 17.0 %collective-permute-start = (bf16[2,896,128]{2,1,0:T(8,128)(2,1)}, bf16[2,896,128]{2,1,0:T(8,128)(2,1)S(1)}, u32[]{:S(2)}, u32[]{:S(2)}) collective-permute-start(bf16[2,896,128]{2,1,0:T(8,128)(2,1)} %copy-done.12), channel_id=1, source_target_pairs={{0,4},{4,0},{8,12},{12,8},{16,20},{20,16},{24,28},{28,24},{1,5},{5... | collective-permute-start | bytes 1376264 | tf_op jit(solution)/shard_map/ppermute | solution.py:433
Sparse Core Ops, SparseCore 0:
  29.8 57.2 all-gather.2

commit v2 on v1

--- a/solution.py
+++ b/solution.py
@@ -151,14 +151,16 @@
 CHUNK = 32
 F32 = jnp.float32
 BF16 = jnp.bfloat16
-VMEM_LIMIT = 40 * 1024 * 1024
+VMEM_LIMIT = 60 * 1024 * 1024
 
 
 def adamw_tile(w, m, v, g, rate, corr):
     g = g.astype(F32)
     m1 = BETA_ONE * m.astype(F32) + (1.0 - BETA_ONE) * g
     v1 = BETA_TWO * v.astype(F32) + (1.0 - BETA_TWO) * g * g
-    w1 = (1.0 - LEARN_RATE * DECAY_RATE) * w - rate * m1 / (jnp.sqrt(v1 * corr) + ADAM_EPS)
+    x = v1 * corr
+    inv = pl.reciprocal(x * lax.rsqrt(x) + ADAM_EPS, approx=True)
+    w1 = (1.0 - LEARN_RATE * DECAY_RATE) * w - rate * m1 * inv
     return w1, m1.astype(BF16), v1.astype(BF16)
 
 
@@ -171,99 +173,101 @@
     return jnp.max(jnp.concatenate(rows, axis=0), axis=1, keepdims=True)
 
 
-def expert_kernel(per_dest, n_dest, tiles, n_alias, blk_ref, scal_ref, *refs):
-    w_ref, m_ref, v_ref, g_ref = refs[:4]
-    w1_ref, m1_ref, v1_ref, s_ref = refs[4 + n_alias : 8 + n_alias]
-    q_refs = refs[8 + n_alias :]
+def expert_kernel(first, blocks, lat_blocks, owner_ref, scal_ref, w_ref, m_ref, v_ref, g_ref, *refs):
+    w1_ref, m1_ref, v1_ref, q_ref, s_ref = refs[-5:]
+    step = pl.program_id(0)
     rate, corr = scal_ref[0], scal_ref[1]
+
+    @pl.when(step == 0)
+    def _():
+        s_ref[...] = jnp.zeros_like(s_ref) if first == 0 else refs[0][...]
+
     parts = []
-    for t in range(tiles):
-        rows = pl.ds(t * TILE, TILE)
+    for b in range(blocks):
+        cols = pl.ds(b * TILE, TILE)
         w1, m1, v1 = adamw_tile(
-            w_ref[rows, :], m_ref[rows, :], v_ref[rows, :], g_ref[rows, :], rate, corr
+            w_ref[:, cols], m_ref[:, cols], v_ref[:, cols], g_ref[:, cols], rate, corr
         )
-        w1_ref[rows, :] = w1
-        m1_ref[rows, :] = m1
-        v1_ref[rows, :] = v1
+        w1_ref[:, cols] = w1
+        m1_ref[:, cols] = m1
+        v1_ref[:, cols] = v1
         parts.append(sub_max(w1))
     top = stack_max(parts)
-    s_ref[0] = jnp.broadcast_to(top, (tiles, TILE))
     inv = 1.0 / (top + SCALE_EPS)
-    step = pl.program_id(0)
-    for d in range(n_dest):
-
-        @pl.when(step // per_dest == d)
-        def _(d=d):
-            for t in range(tiles):
-                rows = pl.ds(t * TILE, TILE)
-                q_refs[d][0, rows, :] = (w1_ref[rows, :] * inv[t : t + 1, :]).astype(BF16)
-
-
-def expert_group(arrays, state, blk, scal, n_dest, per_dest):
+    for b in range(blocks):
+        slot = owner_ref[b]
+        cols = pl.ds(b * TILE, TILE)
+        q_ref[slot, 0] = (w1_ref[:, cols] * inv[b : b + 1, :]).astype(BF16)
+        s_ref[slot, pl.ds(first + step, 1), :] = jnp.broadcast_to(top[b : b + 1, :], (1, TILE))
+
+    if first > 0:
+        @pl.when(step == pl.num_programs(0) - 1)
+        def _():
+            lane = lax.broadcasted_iota(jnp.int32, (8, TILE), 1)
+            for b in range(blocks):
+                s_ref[b] = jnp.where(lane < lat_blocks, refs[1][...], s_ref[b])
+
+
+def expert_rows(arrays, owner, scal, first, count, state, tops, lat_tops, lat_blocks):
     rows, cols = arrays[0].shape
-    tiles = rows // TILE
-    steps = n_dest * per_dest
-    column = lambda i, blk: (0, blk[i])
-    spec = pl.BlockSpec((rows, TILE), column)
+    blocks = cols // TILE
+    spec = pl.BlockSpec((TILE, cols), lambda i, own: (first + i, 0))
     any_spec = pl.BlockSpec(memory_space=pl.ANY)
-    n_alias = len(state)
-
-    def q_map(d):
-        return lambda i, blk: (jnp.clip(i - d * per_dest, 0, per_dest - 1), 0, 0)
-
-    out_shape = [
-        jax.ShapeDtypeStruct((rows, cols), F32),
-        jax.ShapeDtypeStruct((rows, cols), BF16),
-        jax.ShapeDtypeStruct((rows, cols), BF16),
-        jax.ShapeDtypeStruct((steps, tiles, TILE), F32),
-    ] + [jax.ShapeDtypeStruct((per_dest, rows, TILE), BF16)] * n_dest
-    out_specs = [spec, spec, spec, pl.BlockSpec((1, tiles, TILE), lambda i, blk: (i, 0, 0))] + [
-        pl.BlockSpec((1, rows, TILE), q_map(d)) for d in range(n_dest)
-    ]
-    elems = rows * TILE * steps
+    small = pl.BlockSpec((blocks, 8, TILE), lambda i, own: (0, 0, 0))
+    flat = pl.BlockSpec((8, TILE), lambda i, own: (0, 0))
+    extra = () if first == 0 else (tops, lat_tops, *state)
+    extra_specs = [] if first == 0 else [small, flat, any_spec, any_spec, any_spec]
+    elems = TILE * cols * count
     out = pl.pallas_call(
-        functools.partial(expert_kernel, per_dest, n_dest, tiles, n_alias),
+        functools.partial(expert_kernel, first, blocks, lat_blocks),
         grid_spec=pltpu.PrefetchScalarGridSpec(
             num_scalar_prefetch=1,
-            grid=(steps,),
-            in_specs=[pl.BlockSpec(memory_space=pltpu.SMEM)] + [spec] * 4 + [any_spec] * n_alias,
-            out_specs=out_specs,
+            grid=(count,),
+            in_specs=[pl.BlockSpec(memory_space=pltpu.SMEM)] + [spec] * 4 + extra_specs,
+            out_specs=[spec] * 3
+            + [pl.BlockSpec((blocks, 1, TILE, TILE), lambda i, own: (0, i, 0, 0)), small],
         ),
-        out_shape=out_shape,
-        input_output_aliases={6 + i: i for i in range(n_alias)},
+        out_shape=[
+            jax.ShapeDtypeStruct((rows, cols), F32),
+            jax.ShapeDtypeStruct((rows, cols), BF16),
+            jax.ShapeDtypeStruct((rows, cols), BF16),
+            jax.ShapeDtypeStruct((blocks, count, TILE, TILE), BF16),
+            jax.ShapeDtypeStruct((blocks, 8, TILE), F32),
+        ],
+        input_output_aliases={} if first == 0 else {8: 0, 9: 1, 10: 2},
         compiler_params=pltpu.CompilerParams(vmem_limit_bytes=VMEM_LIMIT),
         cost_estimate=pl.CostEstimate(
             flops=30 * elems, bytes_accessed=20 * elems, transcendentals=2 * elems
         ),
         name="expert_adamw",
-    )(blk, scal, *arrays, *state)
-    return out[:3], out[3], out[4:]
-
-
-def place_kernel(n_alias, src_ref, q_ref, *refs):
-    refs[n_alias][0, 0] = q_ref[0]
-
-
-def place_rows(served, src, q, dp_count):
-    per_dest, rows, _ = q.shape
-    n_alias = 0 if served is None else 1
+    )(owner, scal, *arrays, *extra)
+    return out[:3], out[3], out[4]
+
+
+def place_kernel(q_ref, *refs):
+    out_ref = refs[-1]
+    srcs, slots = q_ref.shape[:2]
+    for s in range(srcs):
+        for j in range(slots):
+            out_ref[j, s, 0] = q_ref[s, j, 0]
+
+
+def place_rows(served, q, first, tiles):
+    srcs, slots, count = q.shape[:3]
     any_spec = pl.BlockSpec(memory_space=pl.ANY)
+    have = served is not None
     return pl.pallas_call(
-        functools.partial(place_kernel, n_alias),
-        grid_spec=pltpu.PrefetchScalarGridSpec(
-            num_scalar_prefetch=1,
-            grid=(per_dest,),
-            in_specs=[pl.BlockSpec((1, rows, TILE), lambda j, src: (j, 0, 0))] + [any_spec] * n_alias,
-            out_specs=pl.BlockSpec((1, 1, rows, TILE), lambda j, src: (j, src[0], 0, 0)),
-        ),
-        out_shape=jax.ShapeDtypeStruct((per_dest, dp_count, rows, TILE), BF16),
-        input_output_aliases={2: 0} if n_alias else {},
+        place_kernel,
+        grid=(count,),
+        in_specs=[pl.BlockSpec((srcs, slots, 1, TILE, TILE), lambda i: (0, 0, i, 0, 0))]
+        + [any_spec] * have,
+        out_specs=pl.BlockSpec((slots, srcs, 1, TILE, TILE), lambda i: (0, 0, first + i, 0, 0)),
+        out_shape=jax.ShapeDtypeStruct((slots, srcs, tiles, TILE, TILE), BF16),
+        input_output_aliases={1: 0} if have else {},
         compiler_params=pltpu.CompilerParams(vmem_limit_bytes=VMEM_LIMIT),
-        cost_estimate=pl.CostEstimate(
-            flops=0, bytes_accessed=4 * per_dest * rows * TILE, transcendentals=0
-        ),
+        cost_estimate=pl.CostEstimate(flops=0, bytes_accessed=4 * q.size, transcendentals=0),
         name="place_served",
-    )(src, q, *(() if served is None else (served,)))
+    )(q, *((served,) if have else ()))
 
 
 def latent_kernel(chunks, width, scal_ref, w_ref, m_ref, v_ref, g_ref, w1_ref, m1_ref, v1_ref, top_ref):
@@ -292,7 +296,7 @@
 
 def latent_update(arrays, scal):
     rows, cols = arrays[0].shape
-    width = 4
+    width = 3
     spec = pl.BlockSpec((rows, width * TILE), lambda i: (0, i))
     elems = rows * cols
     return pl.pallas_call(
@@ -314,48 +318,59 @@
     )(scal, *arrays)
 
 
-def latent_quant_kernel(chunks, width, off_ref, w1_ref, own_ref, prev_ref, next_ref, q_ref, ext):
+def latent_quant_kernel(chunks, peers, width, pos_ref, w1_ref, *refs):
+    q_ref, tops_ref, ext = refs[-3:]
     per_tile = TILE // CHUNK
     step = pl.program_id(0)
-    ext[0:chunks, :] = prev_ref[0:chunks, :]
-    ext[chunks : 2 * chunks, :] = own_ref[0:chunks, :]
-    ext[2 * chunks : 3 * chunks, :] = next_ref[0:chunks, :]
+    pos = pos_ref[0]
+
+    @pl.when(step == 0)
+    def _():
+        for s in range(peers):
+            at = lax.rem(pos + peers - s, peers) * chunks
+            ext[pl.ds(at, chunks), :] = refs[s][0:chunks, :]
+        tops_ref[...] = jnp.zeros_like(tops_ref)
+        for t in range(peers * chunks // per_tile):
+            tops_ref[t : t + 1, :] = jnp.max(
+                ext[t * per_tile : (t + 1) * per_tile, :], axis=0, keepdims=True
+            )
+
     lane = lax.broadcasted_iota(jnp.int32, (8, TILE), 1)
-    off = off_ref[0]
-    rows = []
-    for c in range(chunks):
-        first = chunks + c - lax.rem(off + c, per_tile)
-        rows.append(jnp.max(ext[pl.ds(first, per_tile), :], axis=0, keepdims=True))
+    rows = [tops_ref[pl.ds((pos * chunks + c) // per_tile, 1), :] for c in range(chunks)]
     rows += [rows[-1]] * (8 - chunks)
-    tops = jnp.concatenate(rows, axis=0)
+    mine = jnp.concatenate(rows, axis=0)
     for b in range(width):
-        mine = jnp.where(lane == step * width + b, tops, 0.0)
-        inv = 1.0 / (jnp.max(mine, axis=1, keepdims=True) + SCALE_EPS)
+        top = jnp.max(jnp.where(lane == step * width + b, mine, 0.0), axis=1, keepdims=True)
+        inv = 1.0 / (top + SCALE_EPS)
         cols = pl.ds(b * TILE, TILE)
         for c in range(chunks):
             span = pl.ds(c * CHUNK, CHUNK)
             q_ref[span, cols] = (w1_ref[span, cols] * inv[c : c + 1, :]).astype(BF16)
 
 
-def latent_quant(w1, own, prev, nxt, off):
+def latent_quant(w1, maxima, pos):
     rows, cols = w1.shape
-    width = 4
+    width = 3
     chunks = rows // CHUNK
+    peers = len(maxima)
     spec = pl.BlockSpec((rows, width * TILE), lambda i: (0, i))
     small = pl.BlockSpec((8, TILE), lambda i: (0, 0))
     return pl.pallas_call(
-        functools.partial(latent_quant_kernel, chunks, width),
+        functools.partial(latent_quant_kernel, chunks, peers, width),
         grid=(cols // (width * TILE),),
-        in_specs=[pl.BlockSpec(memory_space=pltpu.SMEM), spec] + [small] * 3,
-        out_specs=spec,
-        out_shape=jax.ShapeDtypeStruct((rows, cols), BF16),
-        scratch_shapes=[pltpu.VMEM((3 * 8, TILE), F32)],
+        in_specs=[pl.BlockSpec(memory_space=pltpu.SMEM), spec] + [small] * peers,
+        out_specs=[spec, small],
+        out_shape=[
+            jax.ShapeDtypeStruct((rows, cols), BF16),
+            jax.ShapeDtypeStruct((8, TILE), F32),
+        ],
+        scratch_shapes=[pltpu.VMEM((8 * peers, TILE), F32)],
         compiler_params=pltpu.CompilerParams(vmem_limit_bytes=VMEM_LIMIT),
         cost_estimate=pl.CostEstimate(
             flops=2 * rows * cols, bytes_accessed=6 * rows * cols, transcendentals=0
         ),
         name="latent_quant",
-    )(off, w1, own, prev, nxt)
+    )(pos, w1, *maxima)
 
 
 def fast_fits(expert_shape, latent_shape, dp_count, exp_axis):
@@ -364,13 +379,14 @@
     return (
         exp_count == 1
         and rows % TILE == 0
-        and (cols // TILE) % dp_count == 0
-        and dp_count & (dp_count - 1) == 0
+        and 2 * TILE <= rows <= 8 * TILE
+        and cols % (TILE * dp_count) == 0
         and latent_rows % CHUNK == 0
-        and TILE <= latent_rows <= 8 * CHUNK
+        and latent_rows <= 8 * CHUNK
         and latent_rows * exp_axis % TILE == 0
-        and latent_cols % (4 * TILE) == 0
-        and latent_cols <= TILE * TILE
+        and latent_rows * exp_axis <= 8 * TILE
+        and latent_cols % (3 * TILE) == 0
+        and latent_cols < TILE * TILE
     )
 
 
@@ -387,7 +403,6 @@
     column_owner,
 ):
     dp_count = lax.axis_size("dp")
-    dp_pos = lax.axis_index("dp")
     exp_axis = lax.axis_size("expert")
     exp_pos = lax.axis_index("expert")
     _, rows, cols = expert_master.shape
@@ -403,59 +418,40 @@
     latent_new, latent_one, latent_two, chunk_top = latent_update(
         (latent_master, latent_first, latent_second, latent_grad), scal
     )
-    latent_rows = latent_new.shape[0]
-    chunks = latent_rows // CHUNK
-    off = lax.rem((dp_pos * exp_axis + exp_pos) * chunks, TILE // CHUNK).astype(jnp.int32)
-    top_prev = lax.ppermute(chunk_top, "expert", [(i, i + 1) for i in range(exp_axis - 1)])
-    top_next = lax.ppermute(chunk_top, "expert", [(i + 1, i) for i in range(exp_axis - 1)])
-    latent_q = latent_quant(latent_new, chunk_top, top_prev, top_next, off.reshape(1))
+    maxima = [chunk_top] + [
+        lax.ppermute(chunk_top, "expert", [(i, (i + s) % exp_axis) for i in range(exp_axis)])
+        for s in range(1, exp_axis)
+    ]
+    lat_blocks = latent_new.shape[1] // TILE
+    latent_q, lat_tops = latent_quant(latent_new, maxima, exp_pos.astype(jnp.int32).reshape(1))
     latent_served = lax.all_gather(latent_q, "expert", axis=0, tiled=True)
 
-    positions = jnp.arange(block_count, dtype=jnp.int32)
-    inverse = jnp.sum(
-        positions[:, None] * (column_owner[:, None] == positions[None, :]).astype(jnp.int32), axis=0
-    )
-    order = sorted(range(1, dp_count), key=lambda k: (-bin(k >> 1).count("1"), k & 1, k)) + [0]
-    dests = dp_pos ^ jnp.array(order, jnp.int32)
-    slots = dests[:, None] * per_dest + jnp.arange(per_dest, dtype=jnp.int32)[None, :]
-    blk = jnp.take(inverse, slots.reshape(-1))
     arrays = tuple(
         a.reshape(rows, cols) for a in (expert_master, expert_first, expert_second, expert_grad)
     )
-    group = max(1, dp_count // 4)
-    state, tops, sent = (), [], []
-    for at in range(0, dp_count, group):
-        part = blk[at * per_dest : (at + group) * per_dest]
-        state, top, q = expert_group(arrays, state, part, scal, group, per_dest)
-        tops.append(top[:, :, 0])
-        sent.extend(q)
-    got = [
-        q if k == 0 else lax.ppermute(q, "dp", [(i, i ^ k) for i in range(dp_count)])
-        for k, q in zip(order, sent)
-    ]
-    served = place_rows(None, dests[-1:], got[-1], dp_count)
-    for i in range(dp_count - 1):
-        served = place_rows(served, dests[i : i + 1], got[i], dp_count)
+
+    def exchange(x):
+        x = x.reshape((dp_count, per_dest) + x.shape[1:])
+        return lax.all_to_all(x, "dp", split_axis=0, concat_axis=0, tiled=True)
+
+    half = (tiles + 1) // 2
+    state, q, tops = expert_rows(
+        arrays, column_owner, scal, 0, half, (), None, None, lat_blocks
+    )
+    got_one = exchange(q)
+    state, q, tops = expert_rows(
+        arrays, column_owner, scal, half, tiles - half, state, tops, lat_tops, lat_blocks
+    )
+    got_two = exchange(q)
+    small = exchange(tops)
+    served = place_rows(None, got_one, 0, tiles)
+    served = place_rows(served, got_two, half, tiles)
     expert_served = served.reshape(1, block_count * rows, TILE)
 
-    small = jnp.concatenate(
-        [
-            jnp.concatenate(tops, axis=0).reshape(-1),
-            chunk_top[:chunks, : latent_new.shape[1] // TILE].reshape(-1),
-        ]
-    )
-    everyone = lax.all_gather(small, ("dp", "expert"), axis=0)
-    n_top = block_count * tiles
-    latent_chunks = everyone[:, n_top:].reshape(-1, TILE // CHUNK, latent_new.shape[1] // TILE)
-    latent_scales = jnp.max(latent_chunks, axis=1)
-    peers = everyone.reshape(dp_count, exp_axis, -1)
-    peers = lax.dynamic_index_in_dim(peers, exp_pos, 1, keepdims=False)[:, :n_top]
-    peers = peers.reshape(dp_count, dp_count, per_dest, tiles)
-    place = [order.index(k) for k in range(dp_count)]
-    sel = jnp.take(jnp.array(place, jnp.int32), dp_pos ^ jnp.arange(dp_count, dtype=jnp.int32))
-    hit = sel[:, None] == jnp.arange(dp_count, dtype=jnp.int32)[None, :]
-    mine = jnp.max(jnp.where(hit[:, :, None, None], peers, 0.0), axis=1)
-    expert_scales = jnp.transpose(mine, (1, 0, 2)).reshape(1, block_count * tiles)
+    lat_tiles = latent_served.shape[0] // TILE
+    latent_scales = small[:, 0, :lat_tiles, :lat_blocks].reshape(dp_count * lat_tiles, lat_blocks)
+    expert_scales = jnp.transpose(small[:, :, :tiles, TILE - 1], (1, 0, 2))
+    expert_scales = expert_scales.reshape(1, block_count * tiles)
 
     return (
         state[0][None],

time: 150 us -> 125 us (0.83)
  local copies, waits for them, and re-layouts: 21.3 us -> 6.86 us
  waiting for transfers between devices: 4.22 us -> 18 us
  blocking collectives: 49.7 us -> 38.5 us
  Pallas kernels: 43.5 us -> 35 us
  starting transfers between devices: 14.5 us -> 10.6 us
    unnamed x1 -> x0, blocking collectives: 49.7 us -> none
    all_to_all x0 -> x2, blocking collectives: none -> 38.5 us  [exchange(): return lax.all_to_all(x, 'dp', split_axis=0, concat_axis=0, tiled=True)]
    all_to_all x0 -> x1, waiting for transfers between devices: none -> 15.5 us  [exchange(): return lax.all_to_all(x, 'dp', split_axis=0, concat_axis=0, tiled=True)]
    unnamed x36 -> x11, local copies, waits for them, and re-layouts: 17.3 us -> 5.23 us
    pallas_call x13 -> x5, Pallas kernels: 40.2 us -> 30.3 us  [the longest x2 19.5 us: expert_rows(): pl.pallas_call(functools.partial(expert_kernel, first, blocks, lat_blocks...]
    ppermute x9 -> x3, starting transfers between devices: 14.5 us -> 7.01 us  [fast_body(): lax.ppermute(chunk_top, 'expert', [(i, (i + s) % exp_axis) for i in range...]
    all_to_all x0 -> x1, starting transfers between devices: none -> 3.58 us  [exchange(): return lax.all_to_all(x, 'dp', split_axis=0, concat_axis=0, tiled=True)]
    ppermute x9 -> x3, waiting for transfers between devices: 4.2 us -> 2.46 us  [fast_body(): lax.ppermute(chunk_top, 'expert', [(i, (i + s) % exp_axis) for i in range...]
  transfers between devices with their start and end apart: 10 -> 5, of which waited for: 1 -> 3; matrix products, arithmetic and copies ran while one was open for 4% -> 1% of each run, Pallas kernels for 26% -> 21%
where the time goes in v2:
time: 125 us; the launch traced here: 124 us
  blocking collectives  38.5 us (31%)
  Pallas kernels  35 us (28%)
  waiting for transfers between devices  18 us (14%)
  between operations  14.9 us (12%)
  starting transfers between devices  10.6 us (8%)
  local copies, waits for them, and re-layouts  6.86 us (5%)
    all_to_all x2, blocking collectives, exchange(): return lax.all_to_all(x, 'dp', split_axis=0, concat_axis=0, tiled=True)  38.5 us
    pallas_call x2, Pallas kernels, expert_rows(): pl.pallas_call(functools.partial(expert_kernel, first, blocks, lat_blocks...  19.5 us
    all_to_all x1, waiting for transfers between devices, exchange(): return lax.all_to_all(x, 'dp', split_axis=0, concat_axis=0, tiled=True)  15.5 us
    pallas_call x2, Pallas kernels, place_rows(): pl.pallas_call(place_kernel, grid=(count,), in_specs=[pl.BlockSpec((srcs,...  7.15 us
    ppermute x3, starting transfers between devices, fast_body(): lax.ppermute(chunk_top, 'expert', [(i, (i + s) % exp_axis) for i in range...  7.01 us
    unnamed x11, local copies, waits for them, and re-layouts  5.23 us
    pallas_call x1, Pallas kernels, latent_update(): pl.pallas_call(functools.partial(latent_kernel, rows // CHUNK, width), gr...  4.65 us
    pallas_call x1, Pallas kernels, latent_quant(): pl.pallas_call(functools.partial(latent_quant_kernel, chunks, peers, widt...  3.67 us
  transfers between devices with their start and end apart: 5, of which 3 were waited for; matrix products, arithmetic and copies ran while one was open for 1% of the time, Pallas kernels for 21%

profile of v2, /device:TPU:0, one launch (start us, length us, event | category | flops | bytes accessed | tf_op | source)
XLA Modules:
  0.0 124.5 jit_solution(562548117469044924)
XLA Ops:
  7.2 0.0 all-gather.2.cloned.1.call-start
  8.0 0.6 pad_maximum_fusion.scal_ref
  8.6 4.6 %latent_adamw.1 = (f32[224,1536]{1,0:T(8,128)}, bf16[224,1536]{1,0:T(8,128)(2,1)}, bf16[224,1536]{1,0:T(8,128)(2,1)}, f32[8,128]{1,0:T(8,128)}) custom-call(f32[2]{0:T(128)} %pad_maximum_fusion.scal_ref, f32[224,1536]{1,0:T(8,128)} %w_ref.1, bf16[224,1536]{1,0:T(8,128)(2,1)} %m_ref.1, bf16[224,1536]{1,0:T(8,128)(2,1)} %v_ref.1, bf16[224,1536]{1,0:T(8,128)(2,1)} %g_ref.1), custom_call_target="tpu_custom_call" | custom-call | flops 10321920 | bytes 6193152 | tf_op jit(solution)/shard_map/latent_adamw/pallas_call | solution.py:302
  13.3 3.1 %collective-permute-start = (f32[8,128]{1,0:T(8,128)}, f32[8,128]{1,0:T(8,128)S(1)}, u32[]{:S(2)}, u32[]{:S(2)}) collective-permute-start(f32[8,128]{1,0:T(8,128)} %get-tuple-element.28.refs_0_), channel_id=1, source_target_pairs={{0,1},{1,2},{2,3},{3,0},{4,5},{5,6},{6,7},{7,4},{8,9},{9,10},{10,1... | collective-permute-start | bytes 12296 | tf_op jit(solution)/shard_map/ppermute | solution.py:422
  16.3 2.6 %collective-permute-start.1 = (f32[8,128]{1,0:T(8,128)}, f32[8,128]{1,0:T(8,128)S(1)}, u32[]{:S(2)}, u32[]{:S(2)}) collective-permute-start(f32[8,128]{1,0:T(8,128)} %get-tuple-element.28.refs_0_), channel_id=1, source_target_pairs={{0,2},{1,3},{2,0},{3,1},{4,6},{5,7},{6,4},{7,5},{8,10},{9,11},{10,... | collective-permute-start | bytes 12296 | tf_op jit(solution)/shard_map/ppermute | solution.py:422
  18.9 1.3 %collective-permute-start.2 = (f32[8,128]{1,0:T(8,128)}, f32[8,128]{1,0:T(8,128)S(1)}, u32[]{:S(2)}, u32[]{:S(2)}) collective-permute-start(f32[8,128]{1,0:T(8,128)} %get-tuple-element.28.refs_0_), channel_id=1, source_target_pairs={{0,3},{1,0},{2,1},{3,2},{4,7},{5,4},{6,5},{7,6},{8,11},{9,8},{10,9... | collective-permute-start | bytes 12296 | tf_op jit(solution)/shard_map/ppermute | solution.py:422
  20.3 0.0 collective-permute-done.refs_1_
  20.3 0.0 copy-start.2
  20.3 0.8 collective-permute-done.1.refs_2_
  21.1 0.0 copy-start.3
  21.1 1.6 %collective-permute-done.2.refs_3_ = f32[8,128]{1,0:T(8,128)S(1)} collective-permute-done((f32[8,128]{1,0:T(8,128)}, f32[8,128]{1,0:T(8,128)S(1)}, u32[]{:S(2)}, u32[]{:S(2)}) %collective-permute-start.2) | collective-permute-done | bytes 4128 | tf_op jit(solution)/shard_map/ppermute | solution.py:422
  22.7 0.0 copy-start.4
  22.7 0.0 copy-done.2
  22.7 0.0 copy-done.3
  22.8 0.6 copy-done.4
  23.3 3.7 %latent_quant.1 = (bf16[224,1536]{1,0:T(8,128)(2,1)}, f32[8,128]{1,0:T(8,128)}) custom-call(s32[1]{0:T(128)} %bitcast.4.pos_ref, f32[224,1536]{1,0:T(8,128)} %get-tuple-element.57.w1_ref, f32[8,128]{1,0:T(8,128)} %get-tuple-element.28.refs_0_, f32[8,128]{1,0:T(8,128)} %copy-done.2, f32[8,128]{1,0:T(8,128)} %copy-done.3, f32[8,128]{1,0:T(8,128)} %copy-done.4), custom_call_target="tpu_custom_call" | custom-call | flops 688128 | bytes 2064384 | tf_op jit(solution)/shard_map/latent_quant/pallas_call | solution.py:358
  27.0 0.0 all-gather.2.cloned.1.call-update
  27.0 10.0 %expert_adamw.2 = (f32[896,2048]{1,0:T(8,128)}, bf16[896,2048]{1,0:T(8,128)(2,1)}, bf16[896,2048]{1,0:T(8,128)(2,1)}, bf16[16,4,128,128]{3,2,1,0:T(8,128)(2,1)}, f32[16,8,128]{2,1,0:T(8,128)}) custom-call(s32[16]{0:T(128)} %owner_ref.3, f32[2]{0:T(128)} %pad_maximum_fusion.scal_ref, f32[896,2048]{1,0:T(8,128)} %bitcast.15, bf16[896,2048]{1,0:T(8,128)(2,1)} %bitcast.17, ...), custom_call_target="tpu_custom_call" | custom-call | flops 31457280 | bytes 20971520 | tf_op jit(solution)/shard_map/expert_adamw/pallas_call | solution.py:221
  37.0 0.0 copy-start.1
  37.0 9.5 %expert_adamw.3 = (f32[896,2048]{1,0:T(8,128)}, bf16[896,2048]{1,0:T(8,128)(2,1)}, bf16[896,2048]{1,0:T(8,128)(2,1)}, bf16[16,3,128,128]{3,2,1,0:T(8,128)(2,1)}, f32[16,8,128]{2,1,0:T(8,128)}) custom-call(s32[16]{0:T(128)} %owner_ref.3, f32[2]{0:T(128)} %pad_maximum_fusion.scal_ref, ...), custom_call_target="tpu_custom_call", output_to_operand_aliasing={{0}: (8, {}), {1}: (9, {}), {2}: (10, {})} | custom-call | flops 23592960 | bytes 15728640 | tf_op jit(solution)/shard_map/expert_adamw/pallas_call | solution.py:221
  46.6 8.7 %all_to_all.15 = f32[8,2,8,128]{3,2,1,0:T(8,128)S(1)} all-to-all(f32[8,2,8,128]{3,2,1,0:T(8,128)} %bitcast.28), channel_id=1, replica_groups=mesh['dp'=8,'expert'=4] {'dp'}, dimensions={0} | all-to-all | bytes 131072 | tf_op jit(solution)/shard_map/all_to_all | solution.py:435
  55.3 0.0 copy-done.1
  55.3 29.8 %all_to_all.16.q_ref = bf16[8,2,4,128,128]{4,3,2,1,0:T(8,128)(2,1)} all-to-all(bf16[8,2,4,128,128]{4,3,2,1,0:T(8,128)(2,1)S(1)} %bitcast.27), channel_id=1, replica_groups=mesh['dp'=8,'expert'=4] {'dp'}, dimensions={0} | all-to-all | bytes 4194304 | tf_op jit(solution)/shard_map/all_to_all | solution.py:435
  85.1 3.6 %all-to-all-start = ((bf16[8,2,3,128,128]{4,3,2,1,0:T(8,128)(2,1)}), bf16[8,2,3,128,128]{4,3,2,1,0:T(8,128)(2,1)S(1)}, u32[]{:S(2)}, u32[]{:S(2)}) async-start(bf16[8,2,3,128,128]{4,3,2,1,0:T(8,128)(2,1)} %bitcast.8), calls=%async_computation | async-start | bytes 3145728 | tf_op jit(solution)/shard_map/all_to_all | solution.py:435
  88.7 0.1 slice.8
  88.7 0.2 copy.30
  88.9 0.1 copy.31
  89.0 0.6 reshape.74
  89.6 0.7 copy.33
  90.3 3.8 %place_served.2.refs_0_ = bf16[2,8,7,128,128]{4,3,2,1,0:T(8,128)(2,1)} custom-call(bf16[8,2,4,128,128]{4,3,2,1,0:T(8,128)(2,1)} %all_to_all.16.q_ref), custom_call_target="tpu_custom_call" | custom-call | bytes 4194304 | tf_op jit(solution)/shard_map/place_served/pallas_call | solution.py:259
  94.1 15.5 %all-to-all-done.q_ref = bf16[8,2,3,128,128]{4,3,2,1,0:T(8,128)(2,1)S(1)} async-done(((bf16[8,2,3,128,128]{4,3,2,1,0:T(8,128)(2,1)}), bf16[8,2,3,128,128]{4,3,2,1,0:T(8,128)(2,1)S(1)}, u32[]{:S(2)}, u32[]{:S(2)}) %all-to-all-start) | async-done | bytes 1572896 | tf_op jit(solution)/shard_map/all_to_all | solution.py:435
  109.6 0.0 copy-start
  109.6 1.1 copy-done
  110.8 3.4 %place_served.3 = bf16[2,8,7,128,128]{4,3,2,1,0:T(8,128)(2,1)} custom-call(bf16[8,2,3,128,128]{4,3,2,1,0:T(8,128)(2,1)} %copy-done, bf16[2,8,7,128,128]{4,3,2,1,0:T(8,128)(2,1)} %place_served.2.refs_0_), custom_call_target="tpu_custom_call", output_to_operand_aliasing={{}: (1, {})} | custom-call | bytes 3145728 | tf_op jit(solution)/shard_map/place_served/pallas_call | solution.py:259
  114.1 0.0 all-gather.2.cloned.1.call-done
  114.1 3.5 %copy.40 = bf16[896,1536]{1,0:T(8,128)(2,1)} copy(bf16[896,1536]{1,0:T(8,128)(2,1)} %all-gather.2.cloned.1.call-done) | data formatting | bytes 5505024
  (2 shorter events, 0.0 us)
Async XLA Ops:
  7.2 107.0 %all-gather.2.cloned.1.call-start = ((), (), s32[]{:S(2)}) async-start(), calls=%async_computation.3 | async-start | bytes 3440640 | tf_op jit(solution)/shard_map/all_gather | solution.py:427
  13.3 7.0 %collective-permute-start = (f32[8,128]{1,0:T(8,128)}, f32[8,128]{1,0:T(8,128)S(1)}, u32[]{:S(2)}, u32[]{:S(2)}) collective-permute-start(f32[8,128]{1,0:T(8,128)} %get-tuple-element.28.refs_0_), channel_id=1, source_target_pairs={{0,1},{1,2},{2,3},{3,0},{4,5},{5,6},{6,7},{7,4},{8,9},{9,10},{10,1... | collective-permute-start | bytes 12296 | tf_op jit(solution)/shard_map/ppermute | solution.py:422
  16.3 4.8 %collective-permute-start.1 = (f32[8,128]{1,0:T(8,128)}, f32[8,128]{1,0:T(8,128)S(1)}, u32[]{:S(2)}, u32[]{:S(2)}) collective-permute-start(f32[8,128]{1,0:T(8,128)} %get-tuple-element.28.refs_0_), channel_id=1, source_target_pairs={{0,2},{1,3},{2,0},{3,1},{4,6},{5,7},{6,4},{7,5},{8,10},{9,11},{10,... | collective-permute-start | bytes 12296 | tf_op jit(solution)/shard_map/ppermute | solution.py:422
  18.9 3.8 %collective-permute-start.2 = (f32[8,128]{1,0:T(8,128)}, f32[8,128]{1,0:T(8,128)S(1)}, u32[]{:S(2)}, u32[]{:S(2)}) collective-permute-start(f32[8,128]{1,0:T(8,128)} %get-tuple-element.28.refs_0_), channel_id=1, source_target_pairs={{0,3},{1,0},{2,1},{3,2},{4,7},{5,4},{6,5},{7,6},{8,11},{9,8},{10,9... | collective-permute-start | bytes 12296 | tf_op jit(solution)/shard_map/ppermute | solution.py:422
  20.3 2.5 %copy-start.2 = (f32[8,128]{1,0:T(8,128)}, f32[8,128]{1,0:T(8,128)S(1)}, u32[]{:S(2)}) copy-start(f32[8,128]{1,0:T(8,128)S(1)} %collective-permute-done.refs_1_) | copy-start | bytes 12292
  21.1 1.7 %copy-start.3 = (f32[8,128]{1,0:T(8,128)}, f32[8,128]{1,0:T(8,128)S(1)}, u32[]{:S(2)}) copy-start(f32[8,128]{1,0:T(8,128)S(1)} %collective-permute-done.1.refs_2_) | copy-start | bytes 12292
  22.7 0.6 copy-start.4
  37.0 18.3 %copy-start.1 = (bf16[16,4,128,128]{3,2,1,0:T(8,128)(2,1)S(1)}, bf16[16,4,128,128]{3,2,1,0:T(8,128)(2,1)}, u32[]{:S(2)}) copy-start(bf16[16,4,128,128]{3,2,1,0:T(8,128)(2,1)} %get-tuple-element.37) | copy-start | bytes 6291460
  85.1 24.5 %all-to-all-start = ((bf16[8,2,3,128,128]{4,3,2,1,0:T(8,128)(2,1)}), bf16[8,2,3,128,128]{4,3,2,1,0:T(8,128)(2,1)S(1)}, u32[]{:S(2)}, u32[]{:S(2)}) async-start(bf16[8,2,3,128,128]{4,3,2,1,0:T(8,128)(2,1)} %bitcast.8), calls=%async_computation | async-start | bytes 3145728 | tf_op jit(solution)/shard_map/all_to_all | solution.py:435
  109.6 1.1 copy-start
Sparse Core Ops, SparseCore 0:
  27.1 57.7 all-gather.1

commit v3 on v0

--- a/solution.py
+++ b/solution.py
@@ -1,6 +1,11 @@
+import functools
+import math
+
 import jax
 import jax.numpy as jnp
 from jax import lax
+from jax.experimental import pallas as pl
+from jax.experimental.pallas import tpu as pltpu
 from jax.sharding import PartitionSpec as P
 
 D = 7168
@@ -57,7 +62,7 @@
     return (blocks / (row_scale[..., None] + SCALE_EPS)).reshape(weights.shape).astype(jnp.bfloat16)
 
 
-def body(
+def general_body(
     expert_master,
     expert_first,
     expert_second,
@@ -143,6 +148,536 @@
     )
 
 
+CHUNK = 32
+EXTRA = 16
+SPARE = 64
+F32 = jnp.float32
+BF16 = jnp.bfloat16
+VMEM_LIMIT = 56 * 1024 * 1024
+ANY = pl.BlockSpec(memory_space=pl.ANY)
+SMEM = pl.BlockSpec(memory_space=pltpu.SMEM)
+VMEM = pl.BlockSpec(memory_space=pltpu.VMEM)
+PARAMS = pltpu.CompilerParams(vmem_limit_bytes=VMEM_LIMIT)
+LIGHT = pltpu.CompilerParams(vmem_limit_bytes=1024 * 1024)
+
+
+def corrections(step_ref):
+    one, two = lax.fori_loop(
+        0, step_ref[0], lambda _, p: (p[0] * BETA_ONE, p[1] * BETA_TWO), (F32(1.0), F32(1.0))
+    )
+    rate = LEARN_RATE / (1.0 - jnp.full((1, TILE), one, F32))
+    corr = 1.0 / (1.0 - jnp.full((1, TILE), two, F32))
+    return rate, corr
+
+
+def adamw_tile(w, m, v, g, rate, corr):
+    g = g.astype(F32)
+    m1 = BETA_ONE * m.astype(F32) + (1.0 - BETA_ONE) * g
+    v1 = BETA_TWO * v.astype(F32) + (1.0 - BETA_TWO) * g * g
+    x = v1 * corr
+    inv = pl.reciprocal(x * lax.rsqrt(x) + ADAM_EPS, approx=True)
+    w1 = (1.0 - LEARN_RATE * DECAY_RATE) * w - rate * m1 * inv
+    return w1, m1.astype(BF16), v1.astype(BF16)
+
+
+def sub_max(w1):
+    return jnp.max(jnp.abs(w1).reshape(w1.shape[0] // 8, 8, TILE), axis=0)
+
+
+def stack_max(parts):
+    parts = parts + [parts[-1]] * (8 - len(parts))
+    rows = [jnp.max(p, axis=0, keepdims=True) for p in parts]
+    return jnp.max(jnp.concatenate(rows, axis=0), axis=1, keepdims=True)
+
+
+def three_parts(x):
+    high = x.astype(BF16).astype(F32)
+    rest = x - high
+    middle = rest.astype(BF16).astype(F32)
+    return high, middle, rest - middle
+
+
+def copy_all(copies):
+    for c in copies:
+        c.start()
+
+
+def wait_all(copies):
+    for c in copies:
+        c.wait()
+
+
+def expert_kernel(partners, per_dest, n_alias, owner_ref, pos_ref, step_ref, lat_ref, *refs):
+    hbm = refs[:4]
+    outs = refs[4 + n_alias : 7 + n_alias]
+    n_dest = len(partners)
+    q_refs = refs[7 + n_alias : 7 + n_alias + n_dest]
+    w, m, v, g, extra, in_sem, out_sem, extra_sem = refs[7 + n_alias + n_dest :]
+    bufs = (w, m, v, g)
+    blocks = owner_ref.shape[0]
+    rows = w.shape[1]
+    tiles = rows // TILE
+    pos = pos_ref[0]
+
+    loads, stores = [], []
+    for d, k in enumerate(partners):
+        for j in range(per_dest):
+            i = d * per_dest + j
+            slot = (pos ^ k) * per_dest + j
+            block = jnp.int32(0)
+            for b in range(blocks):
+                block = jnp.where(owner_ref[b] == slot, b, block)
+            cols = pl.ds(pl.multiple_of(block * TILE, TILE), TILE)
+            loads.append(
+                [
+                    pltpu.make_async_copy(hbm[a].at[:, cols], bufs[a].at[i], in_sem.at[i, a])
+                    for a in range(4)
+                ]
+            )
+            stores.append(
+                [
+                    pltpu.make_async_copy(bufs[a].at[i], outs[a].at[:, cols], out_sem.at[i, a])
+                    for a in range(3)
+                ]
+                + [
+                    pltpu.make_async_copy(
+                        g.at[i], q_refs[d].at[pl.ds(j * rows, rows), :], out_sem.at[i, 3]
+                    )
+                ]
+            )
+            copy_all(loads[-1])
+    rate, corr = corrections(step_ref)
+    lane = lax.broadcasted_iota(jnp.int32, (8, TILE), 1)
+    extras = []
+    for d in range(n_dest):
+        side = lat_ref[...]
+        for j in range(per_dest):
+            i = d * per_dest + j
+            wait_all(loads[i])
+            parts = []
+            for t in range(tiles):
+                at = pl.ds(t * TILE, TILE)
+                w1, m1, v1 = adamw_tile(w[i, at, :], m[i, at, :], v[i, at, :], g[i, at, :], rate, corr)
+                w[i, at, :] = w1
+                m[i, at, :] = m1
+                v[i, at, :] = v1
+                parts.append(sub_max(w1))
+            copy_all(stores[i][:3])
+            top = stack_max(parts)
+            inv = 1.0 / (top + SCALE_EPS)
+            for t in range(tiles):
+                at = pl.ds(t * TILE, TILE)
+                g[i, at, :] = (w[i, at, :] * inv[t : t + 1, :]).astype(BF16)
+            stores[i][3].start()
+            for p, value in enumerate(three_parts(top)):
+                side = jnp.where(lane == SPARE + 3 * j + p, value, side)
+        extra[d] = jnp.concatenate([side, jnp.zeros_like(side)], axis=0).astype(BF16)
+        extras.append(
+            pltpu.make_async_copy(
+                extra.at[d], q_refs[d].at[pl.ds(per_dest * rows, EXTRA), :], extra_sem.at[d]
+            )
+        )
+        extras[-1].start()
+    for group in stores:
+        wait_all(group)
+    wait_all(extras)
+
+
+def expert_group(arrays, state, owner, pos, step, lat, partners, per_dest):
+    rows, cols = arrays[0].shape
+    n_alias = len(state)
+    n = len(partners) * per_dest
+    elems = rows * TILE * n
+    out = pl.pallas_call(
+        functools.partial(expert_kernel, partners, per_dest, n_alias),
+        in_specs=[SMEM] * 3 + [VMEM] + [ANY] * (4 + n_alias),
+        out_specs=[ANY] * (3 + len(partners)),
+        out_shape=[
+            jax.ShapeDtypeStruct((rows, cols), F32),
+            jax.ShapeDtypeStruct((rows, cols), BF16),
+            jax.ShapeDtypeStruct((rows, cols), BF16),
+        ]
+        + [jax.ShapeDtypeStruct((per_dest * rows + EXTRA, TILE), BF16)] * len(partners),
+        scratch_shapes=[
+            pltpu.VMEM((n, rows, TILE), F32),
+            pltpu.VMEM((n, rows, TILE), BF16),
+            pltpu.VMEM((n, rows, TILE), BF16),
+            pltpu.VMEM((n, rows, TILE), BF16),
+            pltpu.VMEM((len(partners), EXTRA, TILE), BF16),
+            pltpu.SemaphoreType.DMA((n, 4)),
+            pltpu.SemaphoreType.DMA((n, 4)),
+            pltpu.SemaphoreType.DMA((len(partners),)),
+        ],
+        input_output_aliases={8 + i: i for i in range(n_alias)},
+        compiler_params=PARAMS,
+        cost_estimate=pl.CostEstimate(
+            flops=30 * elems, bytes_accessed=20 * elems, transcendentals=2 * elems
+        ),
+        name="expert_adamw",
+    )(owner, pos, step, lat, *arrays, *state)
+    return out[:3], out[3:]
+
+
+def place_kernel(src_ref, q_ref, *refs):
+    served, sem = refs[-2:]
+    per_dest, _, rows, _ = served.shape
+    src = src_ref[0]
+    copies = [
+        pltpu.make_async_copy(q_ref.at[pl.ds(j * rows, rows), :], served.at[j, src], sem.at[j])
+        for j in range(per_dest)
+    ]
+    copy_all(copies)
+    wait_all(copies)
+
+
+def place_rows(placed, src, q, dp_count, per_dest):
+    rows = (q.shape[0] - EXTRA) // per_dest
+    return pl.pallas_call(
+        place_kernel,
+        in_specs=[SMEM] + [ANY] * (1 + len(placed)),
+        out_specs=ANY,
+        out_shape=jax.ShapeDtypeStruct((per_dest, dp_count, rows, TILE), BF16),
+        scratch_shapes=[pltpu.SemaphoreType.DMA((per_dest,))],
+        input_output_aliases={2: 0} if placed else {},
+        compiler_params=LIGHT,
+        cost_estimate=pl.CostEstimate(flops=0, bytes_accessed=4 * q.size, transcendentals=0),
+        name="place_served",
+    )(src, q, *placed)
+
+
+def scales_kernel(order, tiles, lat_tiles, pos_ref, *refs):
+    n = len(order)
+    q_refs = refs[:n]
+    exp_ref, lat_ref, extra, rows_ref, sem = refs[n:]
+    at = q_refs[0].shape[0] - EXTRA
+    per_dest = at // (tiles * TILE)
+    copies = [
+        pltpu.make_async_copy(q.at[pl.ds(at, EXTRA), :], extra.at[i], sem.at[i])
+        for i, q in enumerate(q_refs)
+    ]
+    copy_all(copies)
+    rows_ref[...] = jnp.zeros_like(rows_ref)
+    lane = lax.broadcasted_iota(jnp.int32, (8, TILE), 1)
+    sub = lax.broadcasted_iota(jnp.int32, (8, TILE), 0)
+    flat = jnp.zeros((8, exp_ref.shape[1]), F32)
+    wide = lax.broadcasted_iota(jnp.int32, flat.shape, 1)
+    deep = lax.broadcasted_iota(jnp.int32, flat.shape, 0)
+    for i, k in enumerate(order):
+        copies[i].wait()
+        src = pos_ref[0] ^ k
+        x = extra[i].astype(F32)[0:8, :]
+        lat = x + pltpu.roll(x, TILE - 16, 1) + pltpu.roll(x, TILE - 32, 1)
+        rows_ref[pl.ds(src * lat_tiles, lat_tiles), :] = lat[0:lat_tiles, :]
+        for j in range(per_dest):
+            first = SPARE + 3 * j
+            top = x[:, first : first + 1] + x[:, first + 1 : first + 2] + x[:, first + 2 : first + 3]
+            hit = (wide == (j * n + src) * tiles + deep) & (deep < tiles)
+            flat = jnp.where(hit, top, flat)
+    exp_ref[...] = jnp.max(flat, axis=0, keepdims=True)
+    blocks, height = lat_ref.shape
+    lat_ref[...] = jnp.transpose(rows_ref[...])[0:blocks, 0:height]
+
+
+def all_scales(pos, received, order, tiles, lat_tiles, lat_blocks):
+    n = len(order)
+    per_dest = (received[0].shape[0] - EXTRA) // (tiles * TILE)
+    expert, latent = pl.pallas_call(
+        functools.partial(scales_kernel, order, tiles, lat_tiles),
+        in_specs=[SMEM] + [ANY] * n,
+        out_specs=[VMEM, VMEM],
+        out_shape=[
+            jax.ShapeDtypeStruct((1, per_dest * n * tiles), F32),
+            jax.ShapeDtypeStruct((lat_blocks, n * lat_tiles), F32),
+        ],
+        scratch_shapes=[
+            pltpu.VMEM((n, EXTRA, TILE), BF16),
+            pltpu.VMEM((TILE, TILE), F32),
+            pltpu.SemaphoreType.DMA((n,)),
+        ],
+        compiler_params=LIGHT,
+        cost_estimate=pl.CostEstimate(
+            flops=1000000, bytes_accessed=100000, transcendentals=0
+        ),
+        name="all_scales",
+    )(pos, *received)
+    return expert, latent.T
+
+
+def spread_copy_kernel(pieces, x_ref, o_ref, sem):
+    rows = x_ref.shape[0] // pieces
+    copies = [
+        pltpu.make_async_copy(
+            x_ref.at[pl.ds(i * rows, rows), :], o_ref.at[pl.ds(i * rows, rows), :], sem.at[i]
+        )
+        for i in range(pieces)
+    ]
+    copy_all(copies)
+    wait_all(copies)
+
+
+def spread_copy(x):
+    pieces = x.shape[0] // TILE
+    return pl.pallas_call(
+        functools.partial(spread_copy_kernel, pieces),
+        in_specs=[ANY],
+        out_specs=ANY,
+        out_shape=jax.ShapeDtypeStruct(x.shape, x.dtype),
+        scratch_shapes=[pltpu.SemaphoreType.DMA((pieces,))],
+        compiler_params=pltpu.CompilerParams(vmem_limit_bytes=VMEM_LIMIT + 4 * 1024 * 1024),
+        cost_estimate=pl.CostEstimate(flops=0, bytes_accessed=4 * x.size, transcendentals=0),
+        name="latent_copy",
+    )(x)
+
+
+SLABS = 4
+
+
+def latent_kernel(chunks, step_ref, *refs):
+    hbm, outs, top_ref = refs[:4], refs[4:7], refs[7]
+    w, m, v, g, in_sem, out_sem = refs[8:]
+    bufs = (w, m, v, g)
+    width = w.shape[1] // SLABS
+    loads, stores = [], []
+    for i in range(SLABS):
+        cols = pl.ds(i * width, width)
+        loads.append(
+            [
+                pltpu.make_async_copy(hbm[a].at[:, cols], bufs[a].at[:, cols], in_sem.at[i, a])
+                for a in range(4)
+            ]
+        )
+        stores.append(
+            [
+                pltpu.make_async_copy(bufs[a].at[:, cols], outs[a].at[:, cols], out_sem.at[i, a])
+                for a in range(3)
+            ]
+        )
+        copy_all(loads[i])
+    rate, corr = corrections(step_ref)
+    lane = lax.broadcasted_iota(jnp.int32, (8, TILE), 1)
+    tops = jnp.zeros((8, TILE), F32)
+    for i in range(SLABS):
+        wait_all(loads[i])
+        for b in range(i * width // TILE, (i + 1) * width // TILE):
+            cols = pl.ds(b * TILE, TILE)
+            w1, m1, v1 = adamw_tile(w[:, cols], m[:, cols], v[:, cols], g[:, cols], rate, corr)
+            w[:, cols] = w1
+            m[:, cols] = m1
+            v[:, cols] = v1
+            parts = [sub_max(w1[c * CHUNK : (c + 1) * CHUNK]) for c in range(chunks)]
+            tops = jnp.where(lane == b, stack_max(parts), tops)
+        copy_all(stores[i])
+    top_ref[...] = tops
+    for group in stores:
+        wait_all(group)
+
+
+def latent_update(arrays, step):
+    rows, cols = arrays[0].shape
+    elems = rows * cols
+    return pl.pallas_call(
+        functools.partial(latent_kernel, rows // CHUNK),
+        in_specs=[SMEM] + [ANY] * 4,
+        out_specs=[ANY] * 3 + [VMEM],
+        out_shape=[
+            jax.ShapeDtypeStruct((rows, cols), F32),
+            jax.ShapeDtypeStruct((rows, cols), BF16),
+            jax.ShapeDtypeStruct((rows, cols), BF16),
+            jax.ShapeDtypeStruct((8, TILE), F32),
+        ],
+        scratch_shapes=[
+            pltpu.VMEM((rows, cols), F32),
+            pltpu.VMEM((rows, cols), BF16),
+            pltpu.VMEM((rows, cols), BF16),
+            pltpu.VMEM((rows, cols), BF16),
+            pltpu.SemaphoreType.DMA((SLABS, 4)),
+            pltpu.SemaphoreType.DMA((SLABS, 3)),
+        ],
+        compiler_params=PARAMS,
+        cost_estimate=pl.CostEstimate(
+            flops=30 * elems, bytes_accessed=18 * elems, transcendentals=2 * elems
+        ),
+        name="latent_adamw",
+    )(step, *arrays)
+
+
+def latent_quant_kernel(chunks, peers, pos_ref, w1_ref, *refs):
+    q_ref, side_ref, w, q, ext, tops_ref, in_sem, out_sem = refs[peers:]
+    per_tile = TILE // CHUNK
+    width = w.shape[1] // SLABS
+    pos = pos_ref[0]
+    slabs = [pl.ds(i * width, width) for i in range(SLABS)]
+    loads = [
+        pltpu.make_async_copy(w1_ref.at[:, c], w.at[:, c], in_sem.at[i]) for i, c in enumerate(slabs)
+    ]
+    stores = [
+        pltpu.make_async_copy(q.at[:, c], q_ref.at[:, c], out_sem.at[i]) for i, c in enumerate(slabs)
+    ]
+    copy_all(loads)
+    for s in range(peers):
+        at = lax.rem(pos + peers - s, peers) * chunks
+        ext[pl.ds(at, chunks), :] = refs[s][0:chunks, :]
+    tops_ref[...] = jnp.zeros_like(tops_ref)
+    for t in range(peers * chunks // per_tile):
+        tops_ref[t : t + 1, :] = jnp.max(
+            ext[t * per_tile : (t + 1) * per_tile, :], axis=0, keepdims=True
+        )
+    lane = lax.broadcasted_iota(jnp.int32, (8, TILE), 1)
+    side = jnp.zeros((8, TILE), F32)
+    for p, value in enumerate(three_parts(tops_ref[...])):
+        value = pltpu.roll(value, 16 * p, 1) if p else value
+        side = jnp.where((lane >= 16 * p) & (lane < 16 * p + 16), value, side)
+    side_ref[...] = side
+
+    rows = [tops_ref[pl.ds((pos * chunks + c) // per_tile, 1), :] for c in range(chunks)]
+    rows += [rows[-1]] * (8 - chunks)
+    mine = jnp.concatenate(rows, axis=0)
+    for i in range(SLABS):
+        loads[i].wait()
+        for b in range(i * width // TILE, (i + 1) * width // TILE):
+            top = jnp.max(jnp.where(lane == b, mine, 0.0), axis=1, keepdims=True)
+            inv = 1.0 / (top + SCALE_EPS)
+            cols = pl.ds(b * TILE, TILE)
+            for c in range(chunks):
+                span = pl.ds(c * CHUNK, CHUNK)
+                q[span, cols] = (w[span, cols] * inv[c : c + 1, :]).astype(BF16)
+        stores[i].start()
+    wait_all(stores)
+
+
+def latent_quant(w1, maxima, pos):
+    rows, cols = w1.shape
+    chunks = rows // CHUNK
+    peers = len(maxima)
+    return pl.pallas_call(
+        functools.partial(latent_quant_kernel, chunks, peers),
+        in_specs=[SMEM, ANY] + [VMEM] * peers,
+        out_specs=[ANY, VMEM],
+        out_shape=[
+            jax.ShapeDtypeStruct((rows, cols), BF16),
+            jax.ShapeDtypeStruct((8, TILE), F32),
+        ],
+        scratch_shapes=[
+            pltpu.VMEM((rows, cols), F32),
+            pltpu.VMEM((rows, cols), BF16),
+            pltpu.VMEM((8 * peers, TILE), F32),
+            pltpu.VMEM((8, TILE), F32),
+            pltpu.SemaphoreType.DMA((SLABS,)),
+            pltpu.SemaphoreType.DMA((SLABS,)),
+        ],
+        compiler_params=PARAMS,
+        cost_estimate=pl.CostEstimate(
+            flops=2 * rows * cols, bytes_accessed=6 * rows * cols, transcendentals=0
+        ),
+        name="latent_quant",
+    )(pos, w1, *maxima)
+
+
+def fast_fits(expert_shape, latent_shape, dp_count, exp_axis):
+    exp_count, rows, cols = expert_shape
+    latent_rows, latent_cols = latent_shape
+    return (
+        exp_count == 1
+        and rows % TILE == 0
+        and rows <= 8 * TILE
+        and cols % (TILE * dp_count) == 0
+        and cols // TILE // dp_count <= 20
+        and dp_count >= 4
+        and dp_count & (dp_count - 1) == 0
+        and dp_count * latent_rows * exp_axis <= TILE * TILE
+        and latent_rows % CHUNK == 0
+        and latent_rows <= 8 * CHUNK
+        and latent_rows * exp_axis % TILE == 0
+        and latent_rows * exp_axis <= 8 * TILE
+        and latent_cols % (SLABS * TILE) == 0
+        and latent_cols <= 16 * TILE
+    )
+
+
+def partner_groups(dp_count):
+    hops = lambda k: bin(k >> 1).count("1")
+    stage = lambda k: 3 if k < 2 else (1 if hops(k) > 1 else (2 if k & 1 else 0))
+    order = sorted(range(dp_count), key=lambda k: (stage(k), -k))
+    first = [k for k in order if stage(k) == 0]
+    second = [k for k in order if stage(k) == 1]
+    return [g for g in (first, second, [k for k in order if stage(k) > 1]) if g]
+
+
+def fast_body(
+    expert_master,
+    expert_first,
+    expert_second,
+    expert_grad,
+    latent_master,
+    latent_first,
+    latent_second,
+    latent_grad,
+    step_count,
+    column_owner,
+):
+    dp_count = lax.axis_size("dp")
+    dp_pos = lax.axis_index("dp").astype(jnp.int32)
+    exp_axis = lax.axis_size("expert")
+    exp_pos = lax.axis_index("expert").astype(jnp.int32)
+    _, rows, cols = expert_master.shape
+    block_count = cols // TILE
+    per_dest = block_count // dp_count
+    tiles = rows // TILE
+
+    latent_new, latent_one, latent_two, chunk_top = latent_update(
+        (latent_master, latent_first, latent_second, latent_grad), step_count
+    )
+    maxima = [chunk_top] + [
+        lax.ppermute(chunk_top, "expert", [(i, (i + s) % exp_axis) for i in range(exp_axis)])
+        for s in range(1, exp_axis)
+    ]
+    latent_q, side = latent_quant(latent_new, maxima, exp_pos.reshape(1))
+    latent_served = spread_copy(lax.all_gather(latent_q, "expert", axis=0, tiled=True))
+
+    arrays = tuple(
+        a.reshape(rows, cols) for a in (expert_master, expert_first, expert_second, expert_grad)
+    )
+    state, arrived = (), []
+    for partners in partner_groups(dp_count):
+        state, sent = expert_group(
+            arrays, state, column_owner, dp_pos.reshape(1), step_count, side, partners, per_dest
+        )
+        for k, q in zip(partners, sent):
+            pairs = [(i, i ^ k) for i in range(dp_count)]
+            arrived.append((k, lax.ppermute(q, "dp", pairs) if k else q))
+    placed = ()
+    for k, q in arrived[-1:] + arrived[:-1]:
+        placed = (place_rows(placed, (dp_pos ^ k).reshape(1), q, dp_count, per_dest),)
+    expert_served = placed[0].reshape(1, block_count * rows, TILE)
+    expert_scales, latent_scales = all_scales(
+        dp_pos.reshape(1),
+        [q for _, q in arrived],
+        [k for k, _ in arrived],
+        tiles,
+        latent_served.shape[0] // TILE,
+        latent_new.shape[1] // TILE,
+    )
+
+    return (
+        state[0][None],
+        state[1][None],
+        state[2][None],
+        expert_served,
+        expert_scales,
+        latent_new,
+        latent_one,
+        latent_two,
+        latent_served,
+        latent_scales,
+    )
+
+
+def body(*args):
+    if fast_fits(args[0].shape, args[4].shape, lax.axis_size("dp"), lax.axis_size("expert")):
+        return fast_body(*args)
+    return general_body(*args)
+
+
 def solution(mesh):
     placed = (
         P("expert", "dp", None),

time: 241 us -> 175 us (0.73)
  Pallas kernels: 0 us -> 119 us
  local copies, waits for them, and re-layouts: 81.6 us -> 2 us
  other arithmetic: 51.2 us -> 0 us
  waiting for transfers between devices: 61.3 us -> 25.2 us
  blocking collectives: 24.5 us -> 0 us
  starting transfers between devices: 5.66 us -> 13.7 us
    pallas_call x0 -> x15, Pallas kernels: none -> 119 us  [the longest x1 84.5 us: spread_copy(): pl.pallas_call(functools.partial(spread_copy_kernel, pieces), in_specs=[A...]
    all_to_all x1 -> x0, waiting for transfers between devices: 59.1 us -> none  [body(): lax.all_to_all(jnp.where(usable_slot[None, None, :, None], picked, jnp.ze...]
    unnamed x24 -> x10, local copies, waits for them, and re-layouts: 51.1 us -> 2 us
    convert_element_type x4 -> x0, other arithmetic: 28.4 us -> none  [the longest x2 16.7 us: adamw_step(): second_new.astype(jnp.bfloat16)]
    pmax x1 -> x0, blocking collectives: 24.5 us -> none  [body(): block_map = lax.pmax(place_tiles(block_tiles, block_offset // TILE), 'dp')]
    ppermute x0 -> x10, waiting for transfers between devices: none -> 18.9 us  [the longest x7 16.5 us: fast_body(): arrived.append((k, lax.ppermute(q, 'dp', pairs) if k else q))]
    gather x3 -> x0, local copies, waits for them, and re-layouts: 14.8 us -> none  [the longest x1 7.07 us: body(): ordered = jnp.take(received, pick_index, axis=2)]
    ppermute x0 -> x10, starting transfers between devices: none -> 13.6 us  [the longest x3 7.01 us: fast_body(): lax.ppermute(chunk_top, 'expert', [(i, (i + s) % exp_axis) for i in range...]
  transfers between devices with their start and end apart: 2 -> 11, of which waited for: 2 -> 5; matrix products, arithmetic and copies ran while one was open for 19% -> 0% of each run, Pallas kernels for 0% -> 15%
where the time goes in v3:
time: 175 us
  Pallas kernels  119 us (68%)
  waiting for transfers between devices  25.2 us (14%)
  between operations  14.9 us (9%)
  starting transfers between devices  13.7 us (8%)
  local copies, waits for them, and re-layouts  2 us (1%)
    pallas_call x1, Pallas kernels, spread_copy(): pl.pallas_call(functools.partial(spread_copy_kernel, pieces), in_specs=[A...  84.5 us
    pallas_call x3, Pallas kernels, expert_group(): pl.pallas_call(functools.partial(expert_kernel, partners, per_dest, n_ali...  19 us
    ppermute x7, waiting for transfers between devices, fast_body(): arrived.append((k, lax.ppermute(q, 'dp', pairs) if k else q))  16.5 us
    ppermute x3, starting transfers between devices, fast_body(): lax.ppermute(chunk_top, 'expert', [(i, (i + s) % exp_axis) for i in range...  7.01 us
    ppermute x7, starting transfers between devices, fast_body(): arrived.append((k, lax.ppermute(q, 'dp', pairs) if k else q))  6.64 us
    pallas_call x8, Pallas kernels, place_rows(): pl.pallas_call(place_kernel, in_specs=[SMEM] + [ANY] * (1 + len(placed)),...  6.27 us
    all_gather x1, waiting for transfers between devices, fast_body(): lax.all_gather(latent_q, 'expert', axis=0, tiled=True)  6.2 us
    pallas_call x1, Pallas kernels, latent_update(): pl.pallas_call(functools.partial(latent_kernel, rows // CHUNK), in_specs=...  4.19 us
  transfers between devices with their start and end apart: 11, of which 5 were waited for; matrix products, arithmetic and copies ran while one was open for 0% of the time, Pallas kernels for 15%

profile of v3, /device:TPU:0, one launch (start us, length us, event | category | flops | bytes accessed | tf_op | source)
XLA Modules:
  0.0 175.1 jit_solution(6613268429744251909)
XLA Ops:
  7.2 0.0 all-gather.2.cloned.1.call-start
  7.9 4.2 %latent_adamw.1 = (f32[224,1536]{1,0:T(8,128)}, bf16[224,1536]{1,0:T(8,128)(2,1)}, bf16[224,1536]{1,0:T(8,128)(2,1)}, f32[8,128]{1,0:T(8,128)}) custom-call(s32[1]{0:T(128)S(6)} %copy.46.step_ref, f32[224,1536]{1,0:T(8,128)} %refs_0_.1, bf16[224,1536]{1,0:T(8,128)(2,1)} %refs_1_.1, bf16[224,1536]{1,0:T(8,128)(2,1)} %refs_2_.1, bf16[224,1536]{1,0:T(8,128)(2,1)} %refs_3_.1), custom_call_target="tpu_custom_call" | custom-call | flops 10321920 | bytes 6193152 | tf_op jit(solution)/shard_map/latent_adamw/pallas_call | solution.py:478
  12.1 3.1 %collective-permute-start = (f32[8,128]{1,0:T(8,128)}, f32[8,128]{1,0:T(8,128)S(1)}, u32[]{:S(2)}, u32[]{:S(2)}) collective-permute-start(f32[8,128]{1,0:T(8,128)} %get-tuple-element.36.refs_0_), channel_id=1, source_target_pairs={{0,1},{1,2},{2,3},{3,0},{4,5},{5,6},{6,7},{7,4},{8,9},{9,10},{10,1... | collective-permute-start | bytes 12296 | tf_op jit(solution)/shard_map/ppermute | solution.py:631
  15.1 2.6 %collective-permute-start.1 = (f32[8,128]{1,0:T(8,128)}, f32[8,128]{1,0:T(8,128)S(1)}, u32[]{:S(2)}, u32[]{:S(2)}) collective-permute-start(f32[8,128]{1,0:T(8,128)} %get-tuple-element.36.refs_0_), channel_id=1, source_target_pairs={{0,2},{1,3},{2,0},{3,1},{4,6},{5,7},{6,4},{7,5},{8,10},{9,11},{10,... | collective-permute-start | bytes 12296 | tf_op jit(solution)/shard_map/ppermute | solution.py:631
  17.7 1.3 collective-permute-start.2
  19.1 0.0 collective-permute-done.refs_1_
  19.1 0.0 copy-start.2
  19.1 0.8 collective-permute-done.1.refs_2_
  19.9 0.0 copy-start.3
  19.9 1.6 collective-permute-done.2.refs_3_
  21.6 0.0 copy-start.4
  21.6 0.0 copy-done.2
  21.6 0.0 copy-done.3
  21.6 0.6 copy-done.4
  22.1 3.5 %latent_quant.1 = (bf16[224,1536]{1,0:T(8,128)(2,1)}, f32[8,128]{1,0:T(8,128)}) custom-call(s32[1]{0:T(128)} %bitcast.1.pos_ref, f32[224,1536]{1,0:T(8,128)} %get-tuple-element.30.w1_ref, f32[8,128]{1,0:T(8,128)} %get-tuple-element.36.refs_0_, f32[8,128]{1,0:T(8,128)} %copy-done.2, f32[8,128]{1,0:T(8,128)} %copy-done.3, f32[8,128]{1,0:T(8,128)} %copy-done.4), custom_call_target="tpu_custom_call" | custom-call | flops 688128 | bytes 2064384 | tf_op jit(solution)/shard_map/latent_quant/pallas_call | solution.py:552
  25.7 0.0 all-gather.2.cloned.1.call-update
  25.7 5.0 %expert_adamw.3 = (f32[896,2048]{1,0:T(8,128)}, bf16[896,2048]{1,0:T(8,128)(2,1)}, bf16[896,2048]{1,0:T(8,128)(2,1)}, bf16[1808,128]{1,0:T(8,128)(2,1)}, bf16[1808,128]{1,0:T(8,128)(2,1)}) custom-call(s32[16]{0:T(128)} %owner_ref.5, s32[1]{0:T(128)} %bitcast.pos_ref.src_ref, s32[1]{0:T(128)S(6)} %copy.46.step_ref, f32[8,128]{1,0:T(8,128)} %get-tuple-element.37.lat_ref, ...), custom_call_target="tpu_custom_call" | custom-call | flops 13762560 | bytes 9175040 | tf_op jit(solution)/shard_map/expert_adamw/pallas_call | solution.py:291
  30.7 1.6 collective-permute-start.8
  32.3 1.5 collective-permute-start.9
  33.8 5.2 %expert_adamw.4 = (f32[896,2048]{1,0:T(8,128)}, bf16[896,2048]{1,0:T(8,128)(2,1)}, bf16[896,2048]{1,0:T(8,128)(2,1)}, bf16[1808,128]{1,0:T(8,128)(2,1)}, bf16[1808,128]{1,0:T(8,128)(2,1)}) custom-call(s32[16]{0:T(128)} %owner_ref.5, s32[1]{0:T(128)} %bitcast.pos_ref.src_ref, ...), custom_call_target="tpu_custom_call", output_to_operand_aliasing={{0}: (8, {}), {1}: (9, {}), {2}: (10, {})} | custom-call | flops 13762560 | bytes 9175040 | tf_op jit(solution)/shard_map/expert_adamw/pallas_call | solution.py:291
  39.0 1.0 collective-permute-start.6
  40.0 0.0 collective-permute-start.7
  40.0 8.8 %expert_adamw.5 = (f32[896,2048]{1,0:T(8,128)}, bf16[896,2048]{1,0:T(8,128)(2,1)}, bf16[896,2048]{1,0:T(8,128)(2,1)}, bf16[1808,128]{1,0:T(8,128)(2,1)}, bf16[18...) custom-call(s32[16]{0:T(128)} %owner_ref.5, ...), custom_call_target="tpu_custom_call", output_to_operand_aliasing={{0}: (8, {}), {1}: (9, {}), {2}: (10, {})} | custom-call | flops 27525120 | bytes 18350080 | tf_op jit(solution)/shard_map/expert_adamw/pallas_call | solution.py:291
  48.7 2.5 %collective-permute-start.5 = (bf16[1808,128]{1,0:T(8,128)(2,1)}, bf16[1808,128]{1,0:T(8,128)(2,1)S(1)}, u32[]{:S(2)}, u32[]{:S(2)}) collective-permute-start(bf16[1808,128]{1,0:T(8,128)(2,1)} %get-tuple-element.49), channel_id=1, source_target_pairs={{0,20},{4,16},{8,28},{12,24},{16,4},{20,0},{24,12},{28,8},{1,21},{... | collective-permute-start | bytes 1388552 | tf_op jit(solution)/shard_map/ppermute | solution.py:647
  51.2 0.0 collective-permute-done.8.q_ref.refs_1_
  51.2 0.1 collective-permute-start.4
  51.3 11.3 %collective-permute-done.9.q_ref.refs_0_ = bf16[1808,128]{1,0:T(8,128)(2,1)S(1)} collective-permute-done((bf16[1808,128]{1,0:T(8,128)(2,1)}, bf16[1808,128]{1,0:T(8,128)(2,1)S(1)}, u32[]{:S(2)}, u32[]{:S(2)}) %collective-permute-start.9) | collective-permute-done | bytes 462880 | tf_op jit(solution)/shard_map/ppermute | solution.py:647
  62.7 0.0 collective-permute-start.3
  62.7 0.0 copy-start
  62.7 1.0 copy-done
  63.7 0.8 place_served.8.refs_0_
  64.5 0.8 place_served.9.refs_0_
  65.3 0.8 place_served.10.refs_0_
  66.1 0.0 collective-permute-done.7.q_ref.refs_2_
  66.1 0.8 place_served.11.refs_0_
  66.9 0.0 collective-permute-done.6.q_ref.refs_3_
  66.9 0.8 place_served.12.refs_0_
  67.7 5.1 %collective-permute-done.5.q_ref.refs_4_ = bf16[1808,128]{1,0:T(8,128)(2,1)S(1)} collective-permute-done((bf16[1808,128]{1,0:T(8,128)(2,1)}, bf16[1808,128]{1,0:T(8,128)(2,1)S(1)}, u32[]{:S(2)}, u32[]{:S(2)}) %collective-permute-start.5) | collective-permute-done | bytes 462880 | tf_op jit(solution)/shard_map/ppermute | solution.py:647
  72.8 0.8 place_served.13.refs_0_
  73.6 0.0 collective-permute-done.4.q_ref.refs_5_
  73.6 0.8 place_served.14.refs_0_
  74.4 0.0 collective-permute-done.3.q_ref.refs_6_
  74.4 0.0 copy-start.1
  74.4 0.8 place_served.15
  75.2 0.4 copy-done.1
  75.6 1.9 %all_scales.1 = (f32[1,112]{1,0:T(1,128)}, f32[12,56]{1,0:T(8,128)}) custom-call(s32[1]{0:T(128)} %bitcast.pos_ref.src_ref, bf16[1808,128]{1,0:T(8,128)(2,1)S(1)} %collective-permute-done.9.q_ref.refs_0_, bf16[1808,128]{1,0:T(8,128)(2,1)S(1)} %collective-permute-done.8.q_ref.refs_1_, bf16[1808,128]{1,0:T(8,128)(2,1)S(1)} %collective-permute-done.7.q_ref.refs_2_, ...), custom_call_target="tpu_custom_call" | custom-call | flops 1000000 | bytes 100000 | tf_op jit(solution)/shard_map/all_scales/pallas_call | solution.py:384
  77.5 6.2 %all-gather.2.cloned.1.call-done.x_ref = bf16[896,1536]{1,0:T(8,128)(2,1)} async-done(((bf16[224,1536]{1,0:T(8,128)(2,1)}), bf16[896,1536]{1,0:T(8,128)(2,1)}) %all-gather.2.cloned.1.call-update) | async-done | bytes 2752528 | tf_op jit(solution)/shard_map/all_gather | solution.py:635
  83.7 84.5 %latent_copy.1 = bf16[896,1536]{1,0:T(8,128)(2,1)} custom-call(bf16[896,1536]{1,0:T(8,128)(2,1)} %all-gather.2.cloned.1.call-done.x_ref), custom_call_target="tpu_custom_call" | custom-call | bytes 5505024 | tf_op jit(solution)/shard_map/latent_copy/pallas_call | solution.py:420
Async XLA Ops:
  7.2 76.5 %all-gather.2.cloned.1.call-start = ((), (), s32[]{:S(2)}) async-start(), calls=%async_computation | async-start | bytes 3440640 | tf_op jit(solution)/shard_map/all_gather | solution.py:635
  12.1 7.0 %collective-permute-start = (f32[8,128]{1,0:T(8,128)}, f32[8,128]{1,0:T(8,128)S(1)}, u32[]{:S(2)}, u32[]{:S(2)}) collective-permute-start(f32[8,128]{1,0:T(8,128)} %get-tuple-element.36.refs_0_), channel_id=1, source_target_pairs={{0,1},{1,2},{2,3},{3,0},{4,5},{5,6},{6,7},{7,4},{8,9},{9,10},{10,1... | collective-permute-start | bytes 12296 | tf_op jit(solution)/shard_map/ppermute | solution.py:631
  15.1 4.8 %collective-permute-start.1 = (f32[8,128]{1,0:T(8,128)}, f32[8,128]{1,0:T(8,128)S(1)}, u32[]{:S(2)}, u32[]{:S(2)}) collective-permute-start(f32[8,128]{1,0:T(8,128)} %get-tuple-element.36.refs_0_), channel_id=1, source_target_pairs={{0,2},{1,3},{2,0},{3,1},{4,6},{5,7},{6,4},{7,5},{8,10},{9,11},{10,... | collective-permute-start | bytes 12296 | tf_op jit(solution)/shard_map/ppermute | solution.py:631
  17.7 3.8 %collective-permute-start.2 = (f32[8,128]{1,0:T(8,128)}, f32[8,128]{1,0:T(8,128)S(1)}, u32[]{:S(2)}, u32[]{:S(2)}) collective-permute-start(f32[8,128]{1,0:T(8,128)} %get-tuple-element.36.refs_0_), channel_id=1, source_target_pairs={{0,3},{1,0},{2,1},{3,2},{4,7},{5,4},{6,5},{7,6},{8,11},{9,8},{10,9... | collective-permute-start | bytes 12296 | tf_op jit(solution)/shard_map/ppermute | solution.py:631
  19.1 2.5 %copy-start.2 = (f32[8,128]{1,0:T(8,128)}, f32[8,128]{1,0:T(8,128)S(1)}, u32[]{:S(2)}) copy-start(f32[8,128]{1,0:T(8,128)S(1)} %collective-permute-done.refs_1_) | copy-start | bytes 12292
  19.9 1.7 copy-start.3
  21.6 0.6 copy-start.4
  30.7 20.5 %collective-permute-start.8 = (bf16[1808,128]{1,0:T(8,128)(2,1)}, bf16[1808,128]{1,0:T(8,128)(2,1)S(1)}, u32[]{:S(2)}, u32[]{:S(2)}) collective-permute-start(bf16[1808,128]{1,0:T(8,128)(2,1)} %get-tuple-element.52), channel_id=1, source_target_pairs={{0,8},{4,12},{8,0},{12,4},{16,24},{20,28},{24,16},{28,20},{1,9},{5... | collective-permute-start | bytes 1388552 | tf_op jit(solution)/shard_map/ppermute | solution.py:647
  32.3 30.4 %collective-permute-start.9 = (bf16[1808,128]{1,0:T(8,128)(2,1)}, bf16[1808,128]{1,0:T(8,128)(2,1)S(1)}, u32[]{:S(2)}, u32[]{:S(2)}) collective-permute-start(bf16[1808,128]{1,0:T(8,128)(2,1)} %get-tuple-element.53), channel_id=1, source_target_pairs={{0,16},{4,20},{8,24},{12,28},{16,0},{20,4},{24,8},{28,12},{1,17},{... | collective-permute-start | bytes 1388552 | tf_op jit(solution)/shard_map/ppermute | solution.py:647
  39.0 27.9 %collective-permute-start.6 = (bf16[1808,128]{1,0:T(8,128)(2,1)}, bf16[1808,128]{1,0:T(8,128)(2,1)S(1)}, u32[]{:S(2)}, u32[]{:S(2)}) collective-permute-start(bf16[1808,128]{1,0:T(8,128)(2,1)} %get-tuple-element.50), channel_id=1, source_target_pairs={{0,24},{4,28},{8,16},{12,20},{16,8},{20,12},{24,0},{28,4},{1,25},{... | collective-permute-start | bytes 1388552 | tf_op jit(solution)/shard_map/ppermute | solution.py:647
  40.0 26.1 %collective-permute-start.7 = (bf16[1808,128]{1,0:T(8,128)(2,1)}, bf16[1808,128]{1,0:T(8,128)(2,1)S(1)}, u32[]{:S(2)}, u32[]{:S(2)}) collective-permute-start(bf16[1808,128]{1,0:T(8,128)(2,1)} %get-tuple-element.51), channel_id=1, source_target_pairs={{0,28},{4,24},{8,20},{12,16},{16,12},{20,8},{24,4},{28,0},{1,29},{... | collective-permute-start | bytes 1388552 | tf_op jit(solution)/shard_map/ppermute | solution.py:647
  48.7 24.1 %collective-permute-start.5 = (bf16[1808,128]{1,0:T(8,128)(2,1)}, bf16[1808,128]{1,0:T(8,128)(2,1)S(1)}, u32[]{:S(2)}, u32[]{:S(2)}) collective-permute-start(bf16[1808,128]{1,0:T(8,128)(2,1)} %get-tuple-element.49), channel_id=1, source_target_pairs={{0,20},{4,16},{8,28},{12,24},{16,4},{20,0},{24,12},{28,8},{1,21},{... | collective-permute-start | bytes 1388552 | tf_op jit(solution)/shard_map/ppermute | solution.py:647
  51.2 22.4 %collective-permute-start.4 = (bf16[1808,128]{1,0:T(8,128)(2,1)}, bf16[1808,128]{1,0:T(8,128)(2,1)S(1)}, u32[]{:S(2)}, u32[]{:S(2)}) collective-permute-start(bf16[1808,128]{1,0:T(8,128)(2,1)} %get-tuple-element.48), channel_id=1, source_target_pairs={{0,12},{4,8},{8,4},{12,0},{16,28},{20,24},{24,20},{28,16},{1,13},{... | collective-permute-start | bytes 1388552 | tf_op jit(solution)/shard_map/ppermute | solution.py:647
  62.7 11.7 %collective-permute-start.3 = (bf16[1808,128]{1,0:T(8,128)(2,1)}, bf16[1808,128]{1,0:T(8,128)(2,1)S(1)}, u32[]{:S(2)}, u32[]{:S(2)}) collective-permute-start(bf16[1808,128]{1,0:T(8,128)(2,1)} %get-tuple-element.47), channel_id=1, source_target_pairs={{0,4},{4,0},{8,12},{12,8},{16,20},{20,16},{24,28},{28,24},{1,5},{5... | collective-permute-start | bytes 1388552 | tf_op jit(solution)/shard_map/ppermute | solution.py:647
  62.7 1.0 copy-start
  74.4 1.2 copy-start.1
Sparse Core Ops, SparseCore 0:
  25.8 57.8 all-gather.1

commit v4 on v3

--- a/solution.py
+++ b/solution.py
@@ -150,7 +150,6 @@
 
 CHUNK = 32
 EXTRA = 16
-SPARE = 64
 F32 = jnp.float32
 BF16 = jnp.bfloat16
 VMEM_LIMIT = 56 * 1024 * 1024
@@ -207,7 +206,8 @@
         c.wait()
 
 
-def expert_kernel(partners, per_dest, n_alias, owner_ref, pos_ref, step_ref, lat_ref, *refs):
+def expert_kernel(partners, per_dest, n_alias, n_after, owner_ref, pos_ref, step_ref, *refs):
+    refs = refs[: 4 + n_alias] + refs[4 + n_alias + n_after :]
     hbm = refs[:4]
     outs = refs[4 + n_alias : 7 + n_alias]
     n_dest = len(partners)
@@ -250,7 +250,7 @@
     lane = lax.broadcasted_iota(jnp.int32, (8, TILE), 1)
     extras = []
     for d in range(n_dest):
-        side = lat_ref[...]
+        side = jnp.zeros((8, TILE), F32)
         for j in range(per_dest):
             i = d * per_dest + j
             wait_all(loads[i])
@@ -270,7 +270,7 @@
                 g[i, at, :] = (w[i, at, :] * inv[t : t + 1, :]).astype(BF16)
             stores[i][3].start()
             for p, value in enumerate(three_parts(top)):
-                side = jnp.where(lane == SPARE + 3 * j + p, value, side)
+                side = jnp.where(lane == 3 * j + p, value, side)
         extra[d] = jnp.concatenate([side, jnp.zeros_like(side)], axis=0).astype(BF16)
         extras.append(
             pltpu.make_async_copy(
@@ -283,14 +283,14 @@
     wait_all(extras)
 
 
-def expert_group(arrays, state, owner, pos, step, lat, partners, per_dest):
+def expert_group(arrays, state, owner, pos, step, after, partners, per_dest):
     rows, cols = arrays[0].shape
     n_alias = len(state)
     n = len(partners) * per_dest
     elems = rows * TILE * n
     out = pl.pallas_call(
-        functools.partial(expert_kernel, partners, per_dest, n_alias),
-        in_specs=[SMEM] * 3 + [VMEM] + [ANY] * (4 + n_alias),
+        functools.partial(expert_kernel, partners, per_dest, n_alias, len(after)),
+        in_specs=[SMEM] * 3 + [ANY] * (4 + n_alias + len(after)),
         out_specs=[ANY] * (3 + len(partners)),
         out_shape=[
             jax.ShapeDtypeStruct((rows, cols), F32),
@@ -308,13 +308,11 @@
             pltpu.SemaphoreType.DMA((n, 4)),
             pltpu.SemaphoreType.DMA((len(partners),)),
         ],
-        input_output_aliases={8 + i: i for i in range(n_alias)},
+        input_output_aliases={7 + i: i for i in range(n_alias)},
         compiler_params=PARAMS,
-        cost_estimate=pl.CostEstimate(
-            flops=30 * elems, bytes_accessed=20 * elems, transcendentals=2 * elems
-        ),
+        cost_estimate=pl.CostEstimate(flops=elems, bytes_accessed=elems, transcendentals=0),
         name="expert_adamw",
-    )(owner, pos, step, lat, *arrays, *state)
+    )(owner, pos, step, *arrays, *state, *after)
     return out[:3], out[3:]
 
 
@@ -345,20 +343,27 @@
     )(src, q, *placed)
 
 
-def scales_kernel(order, tiles, lat_tiles, pos_ref, *refs):
+def scales_kernel(order, tiles, chunks, pos_ref, maxima_ref, *refs):
     n = len(order)
     q_refs = refs[:n]
-    exp_ref, lat_ref, extra, rows_ref, sem = refs[n:]
+    exp_ref, lat_ref, extra, rows_ref, tops_ref, sem = refs[n:]
     at = q_refs[0].shape[0] - EXTRA
     per_dest = at // (tiles * TILE)
+    per_tile = TILE // CHUNK
     copies = [
         pltpu.make_async_copy(q.at[pl.ds(at, EXTRA), :], extra.at[i], sem.at[i])
         for i, q in enumerate(q_refs)
     ]
     copy_all(copies)
-    rows_ref[...] = jnp.zeros_like(rows_ref)
-    lane = lax.broadcasted_iota(jnp.int32, (8, TILE), 1)
-    sub = lax.broadcasted_iota(jnp.int32, (8, TILE), 0)
+    for d in range(maxima_ref.shape[0] // 8):
+        rows_ref[d * chunks : (d + 1) * chunks, :] = maxima_ref[8 * d : 8 * d + chunks, :]
+    blocks, height = lat_ref.shape
+    tops = rows_ref[pl.ds(0, height, stride=per_tile), :]
+    for r in range(1, per_tile):
+        tops = jnp.maximum(tops, rows_ref[pl.ds(r, height, stride=per_tile), :])
+    tops_ref[...] = jnp.zeros_like(tops_ref)
+    tops_ref[0:height, :] = tops
+    lat_ref[...] = jnp.transpose(tops_ref[...])[0:blocks, 0:height]
     flat = jnp.zeros((8, exp_ref.shape[1]), F32)
     wide = lax.broadcasted_iota(jnp.int32, flat.shape, 1)
     deep = lax.broadcasted_iota(jnp.int32, flat.shape, 0)
@@ -366,75 +371,137 @@
         copies[i].wait()
         src = pos_ref[0] ^ k
         x = extra[i].astype(F32)[0:8, :]
-        lat = x + pltpu.roll(x, TILE - 16, 1) + pltpu.roll(x, TILE - 32, 1)
-        rows_ref[pl.ds(src * lat_tiles, lat_tiles), :] = lat[0:lat_tiles, :]
         for j in range(per_dest):
-            first = SPARE + 3 * j
+            first = 3 * j
             top = x[:, first : first + 1] + x[:, first + 1 : first + 2] + x[:, first + 2 : first + 3]
             hit = (wide == (j * n + src) * tiles + deep) & (deep < tiles)
             flat = jnp.where(hit, top, flat)
     exp_ref[...] = jnp.max(flat, axis=0, keepdims=True)
-    blocks, height = lat_ref.shape
-    lat_ref[...] = jnp.transpose(rows_ref[...])[0:blocks, 0:height]
-
-
-def all_scales(pos, received, order, tiles, lat_tiles, lat_blocks):
+
+
+def all_scales(pos, maxima, received, order, tiles, chunks, lat_blocks):
     n = len(order)
     per_dest = (received[0].shape[0] - EXTRA) // (tiles * TILE)
+    lat_rows = maxima.shape[0] // 8 * chunks
     expert, latent = pl.pallas_call(
-        functools.partial(scales_kernel, order, tiles, lat_tiles),
-        in_specs=[SMEM] + [ANY] * n,
+        functools.partial(scales_kernel, order, tiles, chunks),
+        in_specs=[SMEM, VMEM] + [ANY] * n,
         out_specs=[VMEM, VMEM],
         out_shape=[
             jax.ShapeDtypeStruct((1, per_dest * n * tiles), F32),
-            jax.ShapeDtypeStruct((lat_blocks, n * lat_tiles), F32),
+            jax.ShapeDtypeStruct((lat_blocks, lat_rows * CHUNK // TILE), F32),
         ],
         scratch_shapes=[
             pltpu.VMEM((n, EXTRA, TILE), BF16),
+            pltpu.VMEM((lat_rows, TILE), F32),
             pltpu.VMEM((TILE, TILE), F32),
             pltpu.SemaphoreType.DMA((n,)),
         ],
         compiler_params=LIGHT,
-        cost_estimate=pl.CostEstimate(
-            flops=1000000, bytes_accessed=100000, transcendentals=0
-        ),
+        cost_estimate=pl.CostEstimate(flops=1000000, bytes_accessed=100000, transcendentals=0),
         name="all_scales",
-    )(pos, *received)
+    )(pos, maxima, *received)
     return expert, latent.T
 
 
-def spread_copy_kernel(pieces, x_ref, o_ref, sem):
-    rows = x_ref.shape[0] // pieces
-    copies = [
-        pltpu.make_async_copy(
-            x_ref.at[pl.ds(i * rows, rows), :], o_ref.at[pl.ds(i * rows, rows), :], sem.at[i]
+def whole_tile(pos, rows):
+    return pl.multiple_of(lax.rem(pos * (TILE - rows % TILE), TILE), CHUNK)
+
+
+def full_kernel(pieces, rows, x_ref, tops_ref, *refs):
+    out_ref, tops_out, buf, in_sem, out_sem = refs[-5:]
+    tops_out[...] = tops_ref[...]
+    loads, stores = [], []
+    for i in range(pieces):
+        lead = i * (TILE - rows % TILE) % TILE
+        at = pl.ds(i * TILE, TILE)
+        loads.append(pltpu.make_async_copy(x_ref.at[at, :], buf.at[at, :], in_sem.at[i]))
+        stores.append(
+            pltpu.make_async_copy(
+                buf.at[at, :], out_ref.at[pl.ds(i * rows + lead, TILE), :], out_sem.at[i]
+            )
         )
-        for i in range(pieces)
-    ]
-    copy_all(copies)
-    wait_all(copies)
-
-
-def spread_copy(x):
+    copy_all(loads)
+    for i in range(pieces):
+        loads[i].wait()
+        stores[i].start()
+    wait_all(stores)
+
+
+def place_full(out, x, tops, rows):
     pieces = x.shape[0] // TILE
     return pl.pallas_call(
-        functools.partial(spread_copy_kernel, pieces),
-        in_specs=[ANY],
+        functools.partial(full_kernel, pieces, rows),
+        in_specs=[ANY, VMEM] + [ANY] * len(out),
+        out_specs=[ANY, VMEM],
+        out_shape=[
+            jax.ShapeDtypeStruct((pieces * rows, x.shape[1]), BF16),
+            jax.ShapeDtypeStruct(tops.shape, tops.dtype),
+        ],
+        scratch_shapes=[
+            pltpu.VMEM(x.shape, BF16),
+            pltpu.SemaphoreType.DMA((pieces,)),
+            pltpu.SemaphoreType.DMA((pieces,)),
+        ],
+        input_output_aliases={2: 0} if out else {},
+        compiler_params=PARAMS,
+        cost_estimate=pl.CostEstimate(flops=0, bytes_accessed=4 * x.size, transcendentals=0),
+        name="place_whole",
+    )(x, tops, *out)
+
+
+def rest_kernel(deltas, rows, pos_ref, *refs):
+    x_refs = refs[: len(deltas)]
+    out_ref, buf, in_sem, out_sem = refs[-4:]
+    span = rows - TILE
+    loads = [
+        pltpu.make_async_copy(x_refs[i], buf.at[i], in_sem.at[i]) for i in range(len(deltas))
+    ]
+    copy_all(loads)
+    stores = []
+    for i, delta in enumerate(deltas):
+        peer = pos_ref[0] ^ delta
+        lead = whole_tile(peer, rows)
+        loads[i].wait()
+        for c in range(span // CHUNK):
+            at = peer * rows + c * CHUNK + jnp.where(c * CHUNK < lead, 0, TILE)
+            stores.append(
+                pltpu.make_async_copy(
+                    buf.at[i, pl.ds(c * CHUNK, CHUNK), :],
+                    out_ref.at[pl.ds(pl.multiple_of(at, CHUNK), CHUNK), :],
+                    out_sem.at[i, c],
+                )
+            )
+            stores[-1].start()
+    wait_all(stores)
+
+
+def place_rest(out, pos, xs, deltas, rows, peers):
+    span, cols = xs[0].shape
+    n = len(xs)
+    return pl.pallas_call(
+        functools.partial(rest_kernel, deltas, rows),
+        in_specs=[SMEM] + [ANY] * (n + len(out)),
         out_specs=ANY,
-        out_shape=jax.ShapeDtypeStruct(x.shape, x.dtype),
-        scratch_shapes=[pltpu.SemaphoreType.DMA((pieces,))],
-        compiler_params=pltpu.CompilerParams(vmem_limit_bytes=VMEM_LIMIT + 4 * 1024 * 1024),
-        cost_estimate=pl.CostEstimate(flops=0, bytes_accessed=4 * x.size, transcendentals=0),
-        name="latent_copy",
-    )(x)
+        out_shape=jax.ShapeDtypeStruct((peers * rows, cols), BF16),
+        scratch_shapes=[
+            pltpu.VMEM((n, span, cols), BF16),
+            pltpu.SemaphoreType.DMA((n,)),
+            pltpu.SemaphoreType.DMA((n, span // CHUNK)),
+        ],
+        input_output_aliases={1 + n: 0} if out else {},
+        compiler_params=pltpu.CompilerParams(vmem_limit_bytes=4 * 1024 * 1024),
+        cost_estimate=pl.CostEstimate(flops=0, bytes_accessed=4 * n * span * cols, transcendentals=0),
+        name="place_rest",
+    )(pos, *xs, *out)
 
 
 SLABS = 4
 
 
-def latent_kernel(chunks, step_ref, *refs):
-    hbm, outs, top_ref = refs[:4], refs[4:7], refs[7]
-    w, m, v, g, in_sem, out_sem = refs[8:]
+def latent_kernel(chunks, step_ref, pos_ref, *refs):
+    hbm, outs, top_ref = refs[:4], refs[4:8], refs[8]
+    w, m, v, g, q, in_sem, out_sem = refs[9:]
     bufs = (w, m, v, g)
     width = w.shape[1] // SLABS
     loads, stores = [], []
@@ -448,41 +515,51 @@
         )
         stores.append(
             [
-                pltpu.make_async_copy(bufs[a].at[:, cols], outs[a].at[:, cols], out_sem.at[i, a])
-                for a in range(3)
+                pltpu.make_async_copy(src.at[:, cols], outs[a].at[:, cols], out_sem.at[i, a])
+                for a, src in enumerate((w, m, v, q))
             ]
         )
         copy_all(loads[i])
     rate, corr = corrections(step_ref)
     lane = lax.broadcasted_iota(jnp.int32, (8, TILE), 1)
+    lead = whole_tile(pos_ref[0], w.shape[0])
+    sub = lax.broadcasted_iota(jnp.int32, (8, 1), 0) * CHUNK
+    inside = (sub >= lead) & (sub < lead + TILE)
     tops = jnp.zeros((8, TILE), F32)
     for i in range(SLABS):
         wait_all(loads[i])
-        for b in range(i * width // TILE, (i + 1) * width // TILE):
+        blocks = range(i * width // TILE, (i + 1) * width // TILE)
+        slab_tops = []
+        for b in blocks:
             cols = pl.ds(b * TILE, TILE)
             w1, m1, v1 = adamw_tile(w[:, cols], m[:, cols], v[:, cols], g[:, cols], rate, corr)
             w[:, cols] = w1
             m[:, cols] = m1
             v[:, cols] = v1
-            parts = [sub_max(w1[c * CHUNK : (c + 1) * CHUNK]) for c in range(chunks)]
-            tops = jnp.where(lane == b, stack_max(parts), tops)
+            slab_tops.append(stack_max([sub_max(w1[c * CHUNK : (c + 1) * CHUNK]) for c in range(chunks)]))
+        for b, top in zip(blocks, slab_tops):
+            cols = pl.ds(b * TILE, TILE)
+            tops = jnp.where(lane == b, top, tops)
+            whole = jnp.max(jnp.where(inside, top, 0.0), axis=0, keepdims=True)
+            q[:, cols] = (w[pl.ds(lead, TILE), cols] * (1.0 / (whole + SCALE_EPS))).astype(BF16)
         copy_all(stores[i])
     top_ref[...] = tops
     for group in stores:
         wait_all(group)
 
 
-def latent_update(arrays, step):
+def latent_update(arrays, step, pos):
     rows, cols = arrays[0].shape
     elems = rows * cols
     return pl.pallas_call(
         functools.partial(latent_kernel, rows // CHUNK),
-        in_specs=[SMEM] + [ANY] * 4,
-        out_specs=[ANY] * 3 + [VMEM],
+        in_specs=[SMEM] * 2 + [ANY] * 4,
+        out_specs=[ANY] * 4 + [VMEM],
         out_shape=[
             jax.ShapeDtypeStruct((rows, cols), F32),
             jax.ShapeDtypeStruct((rows, cols), BF16),
             jax.ShapeDtypeStruct((rows, cols), BF16),
+            jax.ShapeDtypeStruct((TILE, cols), BF16),
             jax.ShapeDtypeStruct((8, TILE), F32),
         ],
         scratch_shapes=[
@@ -490,87 +567,85 @@
             pltpu.VMEM((rows, cols), BF16),
             pltpu.VMEM((rows, cols), BF16),
             pltpu.VMEM((rows, cols), BF16),
+            pltpu.VMEM((TILE, cols), BF16),
             pltpu.SemaphoreType.DMA((SLABS, 4)),
-            pltpu.SemaphoreType.DMA((SLABS, 3)),
+            pltpu.SemaphoreType.DMA((SLABS, 4)),
         ],
         compiler_params=PARAMS,
         cost_estimate=pl.CostEstimate(
             flops=30 * elems, bytes_accessed=18 * elems, transcendentals=2 * elems
         ),
         name="latent_adamw",
-    )(step, *arrays)
-
-
-def latent_quant_kernel(chunks, peers, pos_ref, w1_ref, *refs):
-    q_ref, side_ref, w, q, ext, tops_ref, in_sem, out_sem = refs[peers:]
+    )(step, pos, *arrays)
+
+
+def latent_rest_kernel(chunks, pos_ref, w1_ref, own_ref, prev_ref, next_ref, after_ref, *refs):
+    q_ref, w, q, ext, in_sem, out_sem = refs
     per_tile = TILE // CHUNK
-    width = w.shape[1] // SLABS
-    pos = pos_ref[0]
-    slabs = [pl.ds(i * width, width) for i in range(SLABS)]
-    loads = [
-        pltpu.make_async_copy(w1_ref.at[:, c], w.at[:, c], in_sem.at[i]) for i, c in enumerate(slabs)
+    rows, cols = w1_ref.shape
+    width = cols // SLABS
+    lead = whole_tile(pos_ref[0], rows)
+    loads, stores = [], []
+    for i in range(SLABS):
+        at = pl.ds(i * width, width)
+        group = []
+        for c in range(chunks - per_tile):
+            first = pl.multiple_of(c * CHUNK + jnp.where(c * CHUNK < lead, 0, TILE), CHUNK)
+            group.append(
+                pltpu.make_async_copy(
+                    w1_ref.at[pl.ds(first, CHUNK), at],
+                    w.at[pl.ds(c * CHUNK, CHUNK), at],
+                    in_sem.at[i, c],
+                )
+            )
+        copy_all(group)
+        loads.append(group)
+        stores.append(pltpu.make_async_copy(q.at[:, at], q_ref.at[:, at], out_sem.at[i]))
+    ext[0:chunks, :] = prev_ref[0:chunks, :]
+    ext[chunks : 2 * chunks, :] = own_ref[0:chunks, :]
+    ext[2 * chunks : 3 * chunks, :] = next_ref[0:chunks, :]
+    first = chunks + lead // CHUNK
+    above = jnp.max(ext[pl.ds(first - per_tile, per_tile), :], axis=0, keepdims=True)
+    below = jnp.max(ext[pl.ds(first + per_tile, per_tile), :], axis=0, keepdims=True)
+    both = jnp.concatenate([above] * 4 + [below] * 4, axis=0)
+    lane = lax.broadcasted_iota(jnp.int32, (8, TILE), 1)
+    tops = [
+        jnp.max(jnp.where(lane == b, both, 0.0), axis=1, keepdims=True) for b in range(cols // TILE)
     ]
-    stores = [
-        pltpu.make_async_copy(q.at[:, c], q_ref.at[:, c], out_sem.at[i]) for i, c in enumerate(slabs)
-    ]
-    copy_all(loads)
-    for s in range(peers):
-        at = lax.rem(pos + peers - s, peers) * chunks
-        ext[pl.ds(at, chunks), :] = refs[s][0:chunks, :]
-    tops_ref[...] = jnp.zeros_like(tops_ref)
-    for t in range(peers * chunks // per_tile):
-        tops_ref[t : t + 1, :] = jnp.max(
-            ext[t * per_tile : (t + 1) * per_tile, :], axis=0, keepdims=True
-        )
-    lane = lax.broadcasted_iota(jnp.int32, (8, TILE), 1)
-    side = jnp.zeros((8, TILE), F32)
-    for p, value in enumerate(three_parts(tops_ref[...])):
-        value = pltpu.roll(value, 16 * p, 1) if p else value
-        side = jnp.where((lane >= 16 * p) & (lane < 16 * p + 16), value, side)
-    side_ref[...] = side
-
-    rows = [tops_ref[pl.ds((pos * chunks + c) // per_tile, 1), :] for c in range(chunks)]
-    rows += [rows[-1]] * (8 - chunks)
-    mine = jnp.concatenate(rows, axis=0)
+    invs = [1.0 / (top + SCALE_EPS) for top in tops]
     for i in range(SLABS):
-        loads[i].wait()
+        wait_all(loads[i])
         for b in range(i * width // TILE, (i + 1) * width // TILE):
-            top = jnp.max(jnp.where(lane == b, mine, 0.0), axis=1, keepdims=True)
-            inv = 1.0 / (top + SCALE_EPS)
-            cols = pl.ds(b * TILE, TILE)
-            for c in range(chunks):
+            at = pl.ds(b * TILE, TILE)
+            for c in range(chunks - per_tile):
                 span = pl.ds(c * CHUNK, CHUNK)
-                q[span, cols] = (w[span, cols] * inv[c : c + 1, :]).astype(BF16)
+                inv = jnp.where(c * CHUNK < lead, invs[b][0:1, :], invs[b][4:5, :])
+                q[span, at] = (w[span, at] * inv).astype(BF16)
         stores[i].start()
     wait_all(stores)
 
 
-def latent_quant(w1, maxima, pos):
+def latent_rest(w1, own, above, below, pos, after):
     rows, cols = w1.shape
     chunks = rows // CHUNK
-    peers = len(maxima)
     return pl.pallas_call(
-        functools.partial(latent_quant_kernel, chunks, peers),
-        in_specs=[SMEM, ANY] + [VMEM] * peers,
-        out_specs=[ANY, VMEM],
-        out_shape=[
-            jax.ShapeDtypeStruct((rows, cols), BF16),
-            jax.ShapeDtypeStruct((8, TILE), F32),
-        ],
+        functools.partial(latent_rest_kernel, chunks),
+        in_specs=[SMEM, ANY] + [VMEM] * 3 + [ANY],
+        out_specs=ANY,
+        out_shape=jax.ShapeDtypeStruct((rows - TILE, cols), BF16),
         scratch_shapes=[
-            pltpu.VMEM((rows, cols), F32),
-            pltpu.VMEM((rows, cols), BF16),
-            pltpu.VMEM((8 * peers, TILE), F32),
-            pltpu.VMEM((8, TILE), F32),
-            pltpu.SemaphoreType.DMA((SLABS,)),
+            pltpu.VMEM((rows - TILE, cols), F32),
+            pltpu.VMEM((rows - TILE, cols), BF16),
+            pltpu.VMEM((24, TILE), F32),
+            pltpu.SemaphoreType.DMA((SLABS, chunks)),
             pltpu.SemaphoreType.DMA((SLABS,)),
         ],
         compiler_params=PARAMS,
         cost_estimate=pl.CostEstimate(
-            flops=2 * rows * cols, bytes_accessed=6 * rows * cols, transcendentals=0
+            flops=rows * cols, bytes_accessed=3 * rows * cols, transcendentals=0
         ),
-        name="latent_quant",
-    )(pos, w1, *maxima)
+        name="latent_rest",
+    )(pos, w1, own, above, below, after)
 
 
 def fast_fits(expert_shape, latent_shape, dp_count, exp_axis):
@@ -586,11 +661,11 @@
         and dp_count & (dp_count - 1) == 0
         and dp_count * latent_rows * exp_axis <= TILE * TILE
         and latent_rows % CHUNK == 0
-        and latent_rows <= 8 * CHUNK
+        and 2 * TILE - CHUNK <= latent_rows < 2 * TILE
         and latent_rows * exp_axis % TILE == 0
-        and latent_rows * exp_axis <= 8 * TILE
+        and exp_axis & (exp_axis - 1) == 0
         and latent_cols % (SLABS * TILE) == 0
-        and latent_cols <= 16 * TILE
+        and latent_cols <= TILE * TILE
     )
 
 
@@ -598,9 +673,7 @@
     hops = lambda k: bin(k >> 1).count("1")
     stage = lambda k: 3 if k < 2 else (1 if hops(k) > 1 else (2 if k & 1 else 0))
     order = sorted(range(dp_count), key=lambda k: (stage(k), -k))
-    first = [k for k in order if stage(k) == 0]
-    second = [k for k in order if stage(k) == 1]
-    return [g for g in (first, second, [k for k in order if stage(k) > 1]) if g]
+    return [g for g in ([k for k in order if stage(k) == n] for n in range(4)) if g]
 
 
 def fast_body(
@@ -624,37 +697,62 @@
     per_dest = block_count // dp_count
     tiles = rows // TILE
 
-    latent_new, latent_one, latent_two, chunk_top = latent_update(
-        (latent_master, latent_first, latent_second, latent_grad), step_count
-    )
-    maxima = [chunk_top] + [
-        lax.ppermute(chunk_top, "expert", [(i, (i + s) % exp_axis) for i in range(exp_axis)])
-        for s in range(1, exp_axis)
-    ]
-    latent_q, side = latent_quant(latent_new, maxima, exp_pos.reshape(1))
-    latent_served = spread_copy(lax.all_gather(latent_q, "expert", axis=0, tiled=True))
-
+    expert_at = exp_pos.reshape(1)
+    latent_new, latent_one, latent_two, whole, chunk_top = latent_update(
+        (latent_master, latent_first, latent_second, latent_grad), step_count, expert_at
+    )
+    latent_rows = latent_new.shape[0]
+    whole = lax.all_gather(whole, "expert", axis=0, tiled=True)
+    above = lax.ppermute(chunk_top, "expert", [(i, i + 1) for i in range(exp_axis - 1)])
+    below = lax.ppermute(chunk_top, "expert", [(i + 1, i) for i in range(exp_axis - 1)])
     arrays = tuple(
         a.reshape(rows, cols) for a in (expert_master, expert_first, expert_second, expert_grad)
     )
-    state, arrived = (), []
-    for partners in partner_groups(dp_count):
+    state, arrived, after = (), [], ()
+    for n, partners in enumerate(partner_groups(dp_count)):
         state, sent = expert_group(
-            arrays, state, column_owner, dp_pos.reshape(1), step_count, side, partners, per_dest
+            arrays, state, column_owner, dp_pos.reshape(1), step_count, after, partners, per_dest
         )
+        if n == 0:
+            rest = {
+                0: latent_rest(latent_new, chunk_top, above, below, expert_at, sent[0])
+            }
+            bit = exp_axis // 2
+            while bit:
+                pairs = [(i, i ^ bit) for i in range(exp_axis)]
+                moved = {d ^ bit: lax.ppermute(x, "expert", pairs) for d, x in rest.items()}
+                rest.update(moved)
+                bit //= 2
         for k, q in zip(partners, sent):
             pairs = [(i, i ^ k) for i in range(dp_count)]
             arrived.append((k, lax.ppermute(q, "dp", pairs) if k else q))
+        if n == 0:
+            after = (rest[0],)
+        elif n == 1:
+            after = tuple(q[-EXTRA:] for _, q in arrived[: len(partners)])
+        else:
+            after = (rest[exp_axis - 1][:EXTRA, :TILE],)
     placed = ()
     for k, q in arrived[-1:] + arrived[:-1]:
         placed = (place_rows(placed, (dp_pos ^ k).reshape(1), q, dp_count, per_dest),)
     expert_served = placed[0].reshape(1, block_count * rows, TILE)
+    deltas = list(rest)
+    near, last = deltas[:-1], deltas[-1:]
+    latent_served = place_rest(
+        (), expert_at, [rest[d] for d in near], near, latent_rows, exp_axis
+    )
+    latent_served, tops = place_full((latent_served,), whole, chunk_top, latent_rows)
+    latent_served = place_rest(
+        (latent_served,), expert_at, [rest[d] for d in last], last, latent_rows, exp_axis
+    )
+    maxima = lax.all_gather(tops, ("dp", "expert"), axis=0, tiled=True)
     expert_scales, latent_scales = all_scales(
         dp_pos.reshape(1),
+        maxima,
         [q for _, q in arrived],
         [k for k, _ in arrived],
         tiles,
-        latent_served.shape[0] // TILE,
+        latent_rows // CHUNK,
         latent_new.shape[1] // TILE,
     )
 

time: 175 us -> 184 us (1.051)
  Pallas kernels: 119 us -> 40.7 us
  blocking collectives: 0 us -> 67.3 us
  waiting for transfers between devices: 25.2 us -> 34.1 us
  starting transfers between devices: 13.7 us -> 21 us
  local copies, waits for them, and re-layouts: 2 us -> 5.03 us
    pallas_call x3 -> x5, Pallas kernels: 90 us -> 10.1 us  [the longest x1 3.52 us: place_full(): pl.pallas_call(functools.partial(full_kernel, pieces, rows), in_specs=[AN...]
    all_gather x0 -> x1, blocking collectives: none -> 67.3 us  [fast_body(): maxima = lax.all_gather(tops, ('dp', 'expert'), axis=0, tiled=True)]
    ppermute x3 -> x5, waiting for transfers between devices: 2.46 us -> 27.1 us  [the longest x3 27.1 us: fast_body(): moved = {d ^ bit: lax.ppermute(x, 'expert', pairs) for d, x in rest.items()}]
    ppermute x7, waiting for transfers between devices: 16.5 us -> 6.98 us  [fast_body(): arrived.append((k, lax.ppermute(q, 'dp', pairs) if k else q))]
    all_gather x1, waiting for transfers between devices: 6.2 us -> 0.02 us  [fast_body(): whole = lax.all_gather(whole, 'expert', axis=0, tiled=True)]
    ppermute x3 -> x5, starting transfers between devices: 7.01 us -> 12.1 us  [the longest x3 5.84 us: fast_body(): moved = {d ^ bit: lax.ppermute(x, 'expert', pairs) for d, x in rest.items()}]
    ppermute x7, starting transfers between devices: 6.64 us -> 8.86 us  [fast_body(): arrived.append((k, lax.ppermute(q, 'dp', pairs) if k else q))]
    pallas_call x3 -> x4, Pallas kernels: 19 us -> 19.9 us  [expert_group(): pl.pallas_call(functools.partial(expert_kernel, partners, per_dest, n_ali...]
  transfers between devices with their start and end apart: 11 -> 13, of which waited for: 5 -> 2; matrix products, arithmetic and copies ran while one was open for 0% -> 1% of each run, Pallas kernels for 15% -> 16%
where the time goes in v4:
time: 184 us; the launch traced here: 183 us
  blocking collectives  67.3 us (37%)
  Pallas kernels  40.7 us (22%)
  waiting for transfers between devices  34.1 us (19%)
  starting transfers between devices  21 us (11%)
  between operations  15 us (8%)
  local copies, waits for them, and re-layouts  5.03 us (3%)
    all_gather x1, blocking collectives, fast_body(): maxima = lax.all_gather(tops, ('dp', 'expert'), axis=0, tiled=True)  67.3 us
    ppermute x3, waiting for transfers between devices, fast_body(): moved = {d ^ bit: lax.ppermute(x, 'expert', pairs) for d, x in rest.items()}  27.1 us
    pallas_call x4, Pallas kernels, expert_group(): pl.pallas_call(functools.partial(expert_kernel, partners, per_dest, n_ali...  19.9 us
    ppermute x7, starting transfers between devices, fast_body(): arrived.append((k, lax.ppermute(q, 'dp', pairs) if k else q))  8.86 us
    ppermute x7, waiting for transfers between devices, fast_body(): arrived.append((k, lax.ppermute(q, 'dp', pairs) if k else q))  6.98 us
    pallas_call x8, Pallas kernels, place_rows(): pl.pallas_call(place_kernel, in_specs=[SMEM] + [ANY] * (1 + len(placed)),...  6.28 us
    ppermute x3, starting transfers between devices, fast_body(): moved = {d ^ bit: lax.ppermute(x, 'expert', pairs) for d, x in rest.items()}  5.84 us
    ppermute x1, starting transfers between devices, fast_body(): lax.ppermute(chunk_top, 'expert', [(i, i + 1) for i in range(exp_axis - 1)])  4.96 us
  transfers between devices with their start and end apart: 13, of which 2 were waited for; matrix products, arithmetic and copies ran while one was open for 1% of the time, Pallas kernels for 16%

profile of v4, /device:TPU:0, one launch (start us, length us, event | category | flops | bytes accessed | tf_op | source)
XLA Modules:
  0.0 183.1 jit_solution(12988324179081535112)
XLA Ops:
  7.2 0.0 all-gather.2.cloned.1.call-start
  7.9 4.3 %latent_adamw.1 = (f32[224,1536]{1,0:T(8,128)}, bf16[224,1536]{1,0:T(8,128)(2,1)}, bf16[224,1536]{1,0:T(8,128)(2,1)}, bf16[128,1536]{1,0:T(8,128)(2,1)}, f32[8,128]{1,0:T(8,128)}) custom-call(s32[1]{0:T(128)S(6)} %copy.56.step_ref, s32[1]{0:T(128)} %bitcast.5.pos_ref, f32[224,1536]{1,0:T(8,128)} %refs_0_.1, bf16[224,1536]{1,0:T(8,128)(2,1)} %refs_1_.1, ...), custom_call_target="tpu_custom_call" | custom-call | flops 10321920 | bytes 6193152 | tf_op jit(solution)/shard_map/latent_adamw/pallas_call | solution.py:554
  12.2 0.0 all-gather.2.cloned.1.call-update
  12.2 5.0 %collective-permute-start = (f32[8,128]{1,0:T(8,128)}, f32[8,128]{1,0:T(8,128)S(1)}, u32[]{:S(2)}, u32[]{:S(2)}) collective-permute-start(f32[8,128]{1,0:T(8,128)} %get-tuple-element.43.own_ref.tops_ref), channel_id=1, source_target_pairs={{0,1},{1,2},{2,3},{4,5},{5,6},{6,7},{8,9},{9,10},{10,11},{12,13},{... | collective-permute-start | bytes 12296 | tf_op jit(solution)/shard_map/ppermute | solution.py:706
  17.2 1.3 collective-permute-start.1
  18.5 5.0 %expert_adamw.4 = (f32[896,2048]{1,0:T(8,128)}, bf16[896,2048]{1,0:T(8,128)(2,1)}, bf16[896,2048]{1,0:T(8,128)(2,1)}, bf16[1808,128]{1,0:T(8,128)(2,1)}, bf16[1808,128]{1,0:T(8,128)(2,1)}) custom-call(s32[16]{0:T(128)} %owner_ref.7, s32[1]{0:T(128)} %bitcast.pos_ref.src_ref, s32[1]{0:T(128)S(6)} %copy.56.step_ref, f32[896,2048]{1,0:T(8,128)} %bitcast.19, ...), custom_call_target="tpu_custom_call" | custom-call | flops 458752 | bytes 458752 | tf_op jit(solution)/shard_map/expert_adamw/pallas_call | solution.py:291
  23.5 0.0 collective-permute-done.prev_ref
  23.5 0.0 collective-permute-done.1.next_ref
  23.5 0.6 copy-done.9
  24.1 0.0 copy-done.10
  24.1 2.7 %latent_rest.1.refs_7_.refs_0_ = bf16[96,1536]{1,0:T(8,128)(2,1)} custom-call(s32[1]{0:T(128)} %bitcast.5.pos_ref, f32[224,1536]{1,0:T(8,128)} %get-tuple-element.34.w1_ref, f32[8,128]{1,0:T(8,128)} %get-tuple-element.43.own_ref.tops_ref, f32[8,128]{1,0:T(8,128)} %copy-done.9, f32[8,128]{1,0:T(8,128)} %copy-done.10, ...), custom_call_target="tpu_custom_call" | custom-call | flops 344064 | bytes 1032192 | tf_op jit(solution)/shard_map/latent_rest/pallas_call | solution.py:631
  26.8 3.8 %collective-permute-start.4 = (bf16[96,1536]{1,0:T(8,128)(2,1)}, bf16[96,1536]{1,0:T(8,128)(2,1)S(1)}, u32[]{:S(2)}, u32[]{:S(2)}) collective-permute-start(bf16[96,1536]{1,0:T(8,128)(2,1)} %latent_rest.1.refs_7_.refs_0_), channel_id=1, source_target_pairs={{0,2},{1,3},{2,0},{3,1},{4,6},{5,7},{6,4},{7,5},{8,10},{9,11},{10,... | collective-permute-start | bytes 884744 | tf_op jit(solution)/shard_map/ppermute | solution.py:723
  30.7 1.5 collective-permute-start.2
  32.2 1.5 collective-permute-start.3
  33.7 27.1 %collective-permute-done.4.refs_1_ = bf16[96,1536]{1,0:T(8,128)(2,1)S(1)} collective-permute-done((bf16[96,1536]{1,0:T(8,128)(2,1)}, bf16[96,1536]{1,0:T(8,128)(2,1)S(1)}, u32[]{:S(2)}, u32[]{:S(2)}) %collective-permute-start.4) | collective-permute-done | bytes 294944 | tf_op jit(solution)/shard_map/ppermute | solution.py:723
  60.8 0.0 collective-permute-start.5
  60.8 2.0 %collective-permute-start.11 = (bf16[96,1536]{1,0:T(8,128)(2,1)}, bf16[96,1536]{1,0:T(8,128)(2,1)S(1)}, u32[]{:S(2)}, u32[]{:S(2)}) collective-permute-start(bf16[96,1536]{1,0:T(8,128)(2,1)} %latent_rest.1.refs_7_.refs_0_), channel_id=1, source_target_pairs={{0,1},{1,0},{2,3},{3,2},{4,5},{5,4},{6,7},{7,6},{8,9},{9,8},{10,11... | collective-permute-start | bytes 884744 | tf_op jit(solution)/shard_map/ppermute | solution.py:723
  62.8 4.9 %expert_adamw.5 = (f32[896,2048]{1,0:T(8,128)}, bf16[896,2048]{1,0:T(8,128)(2,1)}, bf16[896,2048]{1,0:T(8,128)(2,1)}, bf16[1808,128]{1,0:T(8,128)(2,1)}, bf16[1808,128]{1,0:T(8,128)(2,1)}) custom-call(s32[16]{0:T(128)} %owner_ref.7, s32[1]{0:T(128)} %bitcast.pos_ref.src_ref, ...), custom_call_target="tpu_custom_call", output_to_operand_aliasing={{0}: (7, {}), {1}: (8, {}), {2}: (9, {})} | custom-call | flops 458752 | bytes 458752 | tf_op jit(solution)/shard_map/expert_adamw/pallas_call | solution.py:291
  67.8 2.5 %collective-permute-start.9 = (bf16[1808,128]{1,0:T(8,128)(2,1)}, bf16[1808,128]{1,0:T(8,128)(2,1)S(1)}, u32[]{:S(2)}, u32[]{:S(2)}) collective-permute-start(bf16[1808,128]{1,0:T(8,128)(2,1)} %get-tuple-element.58), channel_id=1, source_target_pairs={{0,24},{4,28},{8,16},{12,20},{16,8},{20,12},{24,0},{28,4},{1,25},{... | collective-permute-start | bytes 1388552 | tf_op jit(solution)/shard_map/ppermute | solution.py:728
  70.2 0.6 slice.12.refs_7_
  70.8 0.6 slice.13.refs_8_
  71.4 5.0 %expert_adamw.6 = (f32[896,2048]{1,0:T(8,128)}, bf16[896,2048]{1,0:T(8,128)(2,1)}, bf16[896,2048]{1,0:T(8,128)(2,1)}, bf16[1808,128]{1,0:T(8,128)(2,1)}, bf16[1808,128]{1,0:T(8,128)(2,1)}) custom-call(s32[16]{0:T(128)} %owner_ref.7, s32[1]{0:T(128)} %bitcast.pos_ref.src_ref, ...), custom_call_target="tpu_custom_call", output_to_operand_aliasing={{0}: (7, {}), {1}: (8, {}), {2}: (9, {})} | custom-call | flops 458752 | bytes 458752 | tf_op jit(solution)/shard_map/expert_adamw/pallas_call | solution.py:291
  76.4 1.8 collective-permute-start.7
  78.2 0.1 collective-permute-start.8
  78.3 0.6 slice.14.refs_7_
  78.9 5.1 %expert_adamw.7 = (f32[896,2048]{1,0:T(8,128)}, bf16[896,2048]{1,0:T(8,128)(2,1)}, bf16[896,2048]{1,0:T(8,128)(2,1)}, bf16[1808,128]{1,0:T(8,128)(2,1)}, bf16[1808,128]{1,0:T(8,128)(2,1)}) custom-call(s32[16]{0:T(128)} %owner_ref.7, s32[1]{0:T(128)} %bitcast.pos_ref.src_ref, ...), custom_call_target="tpu_custom_call", output_to_operand_aliasing={{0}: (7, {}), {1}: (8, {}), {2}: (9, {})} | custom-call | flops 458752 | bytes 458752 | tf_op jit(solution)/shard_map/expert_adamw/pallas_call | solution.py:291
  84.0 0.0 copy-start.7
  84.0 0.7 copy-done.7
  84.7 1.5 collective-permute-start.6
  86.2 1.0 copy-done.6
  87.2 1.0 copy-done.8
  88.1 1.2 place_rest.2.refs_0_
  89.3 0.8 place_served.8.refs_0_
  90.1 0.8 place_served.9.refs_0_
  90.9 0.8 place_served.10.refs_0_
  91.7 0.0 collective-permute-done.10.q_ref.refs_2_
  91.7 0.8 place_served.11.refs_0_
  92.5 0.8 place_served.12.refs_0_
  93.3 7.0 %collective-permute-done.8.q_ref.refs_4_ = bf16[1808,128]{1,0:T(8,128)(2,1)S(1)} collective-permute-done((bf16[1808,128]{1,0:T(8,128)(2,1)}, bf16[1808,128]{1,0:T(8,128)(2,1)S(1)}, u32[]{:S(2)}, u32[]{:S(2)}) %collective-permute-start.8) | collective-permute-done | bytes 462880 | tf_op jit(solution)/shard_map/ppermute | solution.py:728
  100.3 0.8 place_served.13.refs_0_
  101.1 0.8 place_served.14.refs_0_
  101.9 0.0 collective-permute-done.6.q_ref.refs_6_
  101.9 0.8 place_served.15
  102.7 0.0 all-gather.2.cloned.1.call-done.x_ref
  102.7 3.5 %place_whole.1 = (bf16[896,1536]{1,0:T(8,128)(2,1)}, f32[8,128]{1,0:T(8,128)}) custom-call(bf16[512,1536]{1,0:T(8,128)(2,1)} %all-gather.2.cloned.1.call-done.x_ref, f32[8,128]{1,0:T(8,128)} %get-tuple-element.43.own_ref.tops_ref, bf16[896,1536]{1,0:T(8,128)(2,1)} %place_rest.2.refs_0_), custom_call_target="tpu_custom_call", output_to_operand_aliasing={{0}: (2, {})} | custom-call | bytes 3145728 | tf_op jit(solution)/shard_map/place_whole/pallas_call | solution.py:433
  106.3 67.3 %all_gather.7.maxima_ref = f32[256,128]{1,0:T(8,128)S(1)} all-gather(f32[8,128]{1,0:T(8,128)} %get-tuple-element.62), channel_id=1, replica_groups=mesh['dp'=8,'expert'=4] {'dp','expert'}, dimensions={0}, use_global_device_ids=true | all-gather | bytes 135168 | tf_op jit(solution)/shard_map/all_gather | solution.py:748
  173.6 1.9 %all_scales.1 = (f32[1,112]{1,0:T(1,128)}, f32[12,56]{1,0:T(8,128)}) custom-call(s32[1]{0:T(128)} %bitcast.pos_ref.src_ref, f32[256,128]{1,0:T(8,128)S(1)} %all_gather.7.maxima_ref, bf16[1808,128]{1,0:T(8,128)(2,1)S(1)} %collective-permute-done.2.q_ref.refs_0_, bf16[1808,128]{1,0:T(8,128)(2,1)S(1)} %collective-permute-done.3.q_ref.refs_1_, ...), custom_call_target="tpu_custom_call" | custom-call | flops 1000000 | bytes 100000 | tf_op jit(solution)/shard_map/all_scales/pallas_call | solution.py:386
  175.4 0.8 place_rest.3
  (23 shorter events, 0.0 us)
Async XLA Ops:
  7.2 95.6 %all-gather.2.cloned.1.call-start = ((), (), s32[]{:S(2)}) async-start(), calls=%async_computation | async-start | bytes 1966080 | tf_op jit(solution)/shard_map/all_gather | solution.py:705
  12.2 11.2 %collective-permute-start = (f32[8,128]{1,0:T(8,128)}, f32[8,128]{1,0:T(8,128)S(1)}, u32[]{:S(2)}, u32[]{:S(2)}) collective-permute-start(f32[8,128]{1,0:T(8,128)} %get-tuple-element.43.own_ref.tops_ref), channel_id=1, source_target_pairs={{0,1},{1,2},{2,3},{4,5},{5,6},{6,7},{8,9},{9,10},{10,11},{12,13},{... | collective-permute-start | bytes 12296 | tf_op jit(solution)/shard_map/ppermute | solution.py:706
  17.2 6.3 %collective-permute-start.1 = (f32[8,128]{1,0:T(8,128)}, f32[8,128]{1,0:T(8,128)S(1)}, u32[]{:S(2)}, u32[]{:S(2)}) collective-permute-start(f32[8,128]{1,0:T(8,128)} %get-tuple-element.43.own_ref.tops_ref), channel_id=1, source_target_pairs={{1,0},{2,1},{3,2},{5,4},{6,5},{7,6},{9,8},{10,9},{11,10},{13,12},{... | collective-permute-start | bytes 12296 | tf_op jit(solution)/shard_map/ppermute | solution.py:707
  23.5 0.6 copy-start.9
  23.5 0.6 copy-start.10
  26.8 33.9 %collective-permute-start.4 = (bf16[96,1536]{1,0:T(8,128)(2,1)}, bf16[96,1536]{1,0:T(8,128)(2,1)S(1)}, u32[]{:S(2)}, u32[]{:S(2)}) collective-permute-start(bf16[96,1536]{1,0:T(8,128)(2,1)} %latent_rest.1.refs_7_.refs_0_), channel_id=1, source_target_pairs={{0,2},{1,3},{2,0},{3,1},{4,6},{5,7},{6,4},{7,5},{8,10},{9,11},{10,... | collective-permute-start | bytes 884744 | tf_op jit(solution)/shard_map/ppermute | solution.py:723
  30.7 39.6 %collective-permute-start.2 = (bf16[1808,128]{1,0:T(8,128)(2,1)}, bf16[1808,128]{1,0:T(8,128)(2,1)S(1)}, u32[]{:S(2)}, u32[]{:S(2)}) collective-permute-start(bf16[1808,128]{1,0:T(8,128)(2,1)} %get-tuple-element.44.after_ref), channel_id=1, source_target_pairs={{0,16},{4,20},{8,24},{12,28},{16,0},{20,4},{24,8},{28,12},{1,17},{... | collective-permute-start | bytes 1388552 | tf_op jit(solution)/shard_map/ppermute | solution.py:728
  32.2 38.6 %collective-permute-start.3 = (bf16[1808,128]{1,0:T(8,128)(2,1)}, bf16[1808,128]{1,0:T(8,128)(2,1)S(1)}, u32[]{:S(2)}, u32[]{:S(2)}) collective-permute-start(bf16[1808,128]{1,0:T(8,128)(2,1)} %get-tuple-element.48), channel_id=1, source_target_pairs={{0,8},{4,12},{8,0},{12,4},{16,24},{20,28},{24,16},{28,20},{1,9},{5... | collective-permute-start | bytes 1388552 | tf_op jit(solution)/shard_map/ppermute | solution.py:728
  60.8 7.0 %copy-start.5 = (bf16[96,1536]{1,0:T(8,128)(2,1)}, bf16[96,1536]{1,0:T(8,128)(2,1)S(1)}, u32[]{:S(2)}) copy-start(bf16[96,1536]{1,0:T(8,128)(2,1)S(1)} %collective-permute-done.4.refs_1_) | copy-start | bytes 884740
  60.8 17.4 %collective-permute-start.5 = (bf16[96,1536]{1,0:T(8,128)(2,1)S(1)}, bf16[96,1536]{1,0:T(8,128)(2,1)S(1)}, u32[]{:S(2)}, u32[]{:S(2)}) collective-permute-start(bf16[96,1536]{1,0:T(8,128)(2,1)S(1)} %collective-permute-done.4.refs_1_), channel_id=1, source_target_pairs={{0,1},{1,0},{2,3},{3,2},{4,5},{5,4},{6,7},{7,6},{8,9},{9,8},{10,11... | collective-permute-start | bytes 884744 | tf_op jit(solution)/shard_map/ppermute | solution.py:723
  60.8 23.2 %collective-permute-start.11 = (bf16[96,1536]{1,0:T(8,128)(2,1)}, bf16[96,1536]{1,0:T(8,128)(2,1)S(1)}, u32[]{:S(2)}, u32[]{:S(2)}) collective-permute-start(bf16[96,1536]{1,0:T(8,128)(2,1)} %latent_rest.1.refs_7_.refs_0_), channel_id=1, source_target_pairs={{0,1},{1,0},{2,3},{3,2},{4,5},{5,4},{6,7},{7,6},{8,9},{9,8},{10,11... | collective-permute-start | bytes 884744 | tf_op jit(solution)/shard_map/ppermute | solution.py:723
  67.8 24.8 %collective-permute-start.9 = (bf16[1808,128]{1,0:T(8,128)(2,1)}, bf16[1808,128]{1,0:T(8,128)(2,1)S(1)}, u32[]{:S(2)}, u32[]{:S(2)}) collective-permute-start(bf16[1808,128]{1,0:T(8,128)(2,1)} %get-tuple-element.58), channel_id=1, source_target_pairs={{0,24},{4,28},{8,16},{12,20},{16,8},{20,12},{24,0},{28,4},{1,25},{... | collective-permute-start | bytes 1388552 | tf_op jit(solution)/shard_map/ppermute | solution.py:728
  70.2 21.5 %collective-permute-start.10 = (bf16[1808,128]{1,0:T(8,128)(2,1)}, bf16[1808,128]{1,0:T(8,128)(2,1)S(1)}, u32[]{:S(2)}, u32[]{:S(2)}) collective-permute-start(bf16[1808,128]{1,0:T(8,128)(2,1)} %get-tuple-element.59), channel_id=1, source_target_pairs={{0,28},{4,24},{8,20},{12,16},{16,12},{20,8},{24,4},{28,0},{1,29},{... | collective-permute-start | bytes 1388552 | tf_op jit(solution)/shard_map/ppermute | solution.py:728
  76.4 24.7 %collective-permute-start.7 = (bf16[1808,128]{1,0:T(8,128)(2,1)}, bf16[1808,128]{1,0:T(8,128)(2,1)S(1)}, u32[]{:S(2)}, u32[]{:S(2)}) collective-permute-start(bf16[1808,128]{1,0:T(8,128)(2,1)} %get-tuple-element.56), channel_id=1, source_target_pairs={{0,12},{4,8},{8,4},{12,0},{16,28},{20,24},{24,20},{28,16},{1,13},{... | collective-permute-start | bytes 1388552 | tf_op jit(solution)/shard_map/ppermute | solution.py:728
  78.2 5.8 %copy-start.3 = (bf16[96,1536]{1,0:T(8,128)(2,1)}, bf16[96,1536]{1,0:T(8,128)(2,1)S(1)}, u32[]{:S(2)}) copy-start(bf16[96,1536]{1,0:T(8,128)(2,1)S(1)} %collective-permute-done.5.refs_0_) | copy-start | bytes 884740
  78.2 22.1 %collective-permute-start.8 = (bf16[1808,128]{1,0:T(8,128)(2,1)}, bf16[1808,128]{1,0:T(8,128)(2,1)S(1)}, u32[]{:S(2)}, u32[]{:S(2)}) collective-permute-start(bf16[1808,128]{1,0:T(8,128)(2,1)} %get-tuple-element.57), channel_id=1, source_target_pairs={{0,20},{4,16},{8,28},{12,24},{16,4},{20,0},{24,12},{28,8},{1,21},{... | collective-permute-start | bytes 1388552 | tf_op jit(solution)/shard_map/ppermute | solution.py:728
  78.9 7.3 %copy-start = (bf16[96,1536]{1,0:T(8,128)(2,1)S(1)}, bf16[96,1536]{1,0:T(8,128)(2,1)}, u32[]{:S(2)}) copy-start(bf16[96,1536]{1,0:T(8,128)(2,1)} %latent_rest.1.refs_7_.refs_0_) | copy-start | bytes 884740
  84.0 0.7 copy-start.7
  84.7 17.2 %collective-permute-start.6 = (bf16[1808,128]{1,0:T(8,128)(2,1)}, bf16[1808,128]{1,0:T(8,128)(2,1)S(1)}, u32[]{:S(2)}, u32[]{:S(2)}) collective-permute-start(bf16[1808,128]{1,0:T(8,128)(2,1)} %get-tuple-element.55), channel_id=1, source_target_pairs={{0,4},{4,0},{8,12},{12,8},{16,20},{20,16},{24,28},{28,24},{1,5},{5... | collective-permute-start | bytes 1388552 | tf_op jit(solution)/shard_map/ppermute | solution.py:728
  86.2 1.0 copy-start.6
  87.2 1.0 copy-start.8
  88.1 1.2 copy-start.1
  102.7 72.7 %copy-start.4 = (bf16[96,1536]{1,0:T(8,128)(2,1)S(1)}, bf16[96,1536]{1,0:T(8,128)(2,1)}, u32[]{:S(2)}) copy-start(bf16[96,1536]{1,0:T(8,128)(2,1)} %copy-done.3) | copy-start | bytes 884740
  102.7 70.8 %copy-start.2 = (bf16[1808,128]{1,0:T(8,128)(2,1)S(1)}, bf16[1808,128]{1,0:T(8,128)(2,1)}, u32[]{:S(2)}) copy-start(bf16[1808,128]{1,0:T(8,128)(2,1)} %get-tuple-element.60.q_ref.refs_7_) | copy-start | bytes 1388548
Sparse Core Ops, SparseCore 0:
  12.4 52.5 all-gather.1

commit v5 on v4

--- a/solution.py
+++ b/solution.py
@@ -150,6 +150,7 @@
 
 CHUNK = 32
 EXTRA = 16
+SPARE = 64
 F32 = jnp.float32
 BF16 = jnp.bfloat16
 VMEM_LIMIT = 56 * 1024 * 1024
@@ -206,7 +207,7 @@
         c.wait()
 
 
-def expert_kernel(partners, per_dest, n_alias, n_after, owner_ref, pos_ref, step_ref, *refs):
+def expert_kernel(partners, per_dest, n_alias, n_after, owner_ref, pos_ref, step_ref, side_ref, *refs):
     refs = refs[: 4 + n_alias] + refs[4 + n_alias + n_after :]
     hbm = refs[:4]
     outs = refs[4 + n_alias : 7 + n_alias]
@@ -250,7 +251,7 @@
     lane = lax.broadcasted_iota(jnp.int32, (8, TILE), 1)
     extras = []
     for d in range(n_dest):
-        side = jnp.zeros((8, TILE), F32)
+        side = side_ref[...]
         for j in range(per_dest):
             i = d * per_dest + j
             wait_all(loads[i])
@@ -283,14 +284,14 @@
     wait_all(extras)
 
 
-def expert_group(arrays, state, owner, pos, step, after, partners, per_dest):
+def expert_group(arrays, state, owner, pos, step, side, after, partners, per_dest):
     rows, cols = arrays[0].shape
     n_alias = len(state)
     n = len(partners) * per_dest
     elems = rows * TILE * n
     out = pl.pallas_call(
         functools.partial(expert_kernel, partners, per_dest, n_alias, len(after)),
-        in_specs=[SMEM] * 3 + [ANY] * (4 + n_alias + len(after)),
+        in_specs=[SMEM] * 3 + [VMEM] + [ANY] * (4 + n_alias + len(after)),
         out_specs=[ANY] * (3 + len(partners)),
         out_shape=[
             jax.ShapeDtypeStruct((rows, cols), F32),
@@ -308,11 +309,11 @@
             pltpu.SemaphoreType.DMA((n, 4)),
             pltpu.SemaphoreType.DMA((len(partners),)),
         ],
-        input_output_aliases={7 + i: i for i in range(n_alias)},
+        input_output_aliases={8 + i: i for i in range(n_alias)},
         compiler_params=PARAMS,
         cost_estimate=pl.CostEstimate(flops=elems, bytes_accessed=elems, transcendentals=0),
         name="expert_adamw",
-    )(owner, pos, step, *arrays, *state, *after)
+    )(owner, pos, step, side, *arrays, *state, *after)
     return out[:3], out[3:]
 
 
@@ -343,27 +344,18 @@
     )(src, q, *placed)
 
 
-def scales_kernel(order, tiles, chunks, pos_ref, maxima_ref, *refs):
+def scales_kernel(order, tiles, lat_tiles, n_late, pos_ref, *refs):
     n = len(order)
-    q_refs = refs[:n]
-    exp_ref, lat_ref, extra, rows_ref, tops_ref, sem = refs[n:]
+    late, q_refs = refs[:n_late], refs[n_late : n_late + n]
+    exp_ref, lat_ref, extra, rows_ref, sem = refs[n_late + n :]
     at = q_refs[0].shape[0] - EXTRA
     per_dest = at // (tiles * TILE)
-    per_tile = TILE // CHUNK
     copies = [
         pltpu.make_async_copy(q.at[pl.ds(at, EXTRA), :], extra.at[i], sem.at[i])
         for i, q in enumerate(q_refs)
     ]
     copy_all(copies)
-    for d in range(maxima_ref.shape[0] // 8):
-        rows_ref[d * chunks : (d + 1) * chunks, :] = maxima_ref[8 * d : 8 * d + chunks, :]
-    blocks, height = lat_ref.shape
-    tops = rows_ref[pl.ds(0, height, stride=per_tile), :]
-    for r in range(1, per_tile):
-        tops = jnp.maximum(tops, rows_ref[pl.ds(r, height, stride=per_tile), :])
-    tops_ref[...] = jnp.zeros_like(tops_ref)
-    tops_ref[0:height, :] = tops
-    lat_ref[...] = jnp.transpose(tops_ref[...])[0:blocks, 0:height]
+    rows_ref[...] = jnp.zeros_like(rows_ref)
     flat = jnp.zeros((8, exp_ref.shape[1]), F32)
     wide = lax.broadcasted_iota(jnp.int32, flat.shape, 1)
     deep = lax.broadcasted_iota(jnp.int32, flat.shape, 0)
@@ -371,36 +363,39 @@
         copies[i].wait()
         src = pos_ref[0] ^ k
         x = extra[i].astype(F32)[0:8, :]
+        side = late[i][...] if i < n_late else x
+        lat = sum(pltpu.roll(side, TILE - SPARE - 16 * p, 1) for p in range(3))
+        rows_ref[pl.ds(src * lat_tiles, lat_tiles), :] = lat[0:lat_tiles, :]
         for j in range(per_dest):
             first = 3 * j
             top = x[:, first : first + 1] + x[:, first + 1 : first + 2] + x[:, first + 2 : first + 3]
             hit = (wide == (j * n + src) * tiles + deep) & (deep < tiles)
             flat = jnp.where(hit, top, flat)
     exp_ref[...] = jnp.max(flat, axis=0, keepdims=True)
-
-
-def all_scales(pos, maxima, received, order, tiles, chunks, lat_blocks):
+    blocks, height = lat_ref.shape
+    lat_ref[...] = jnp.transpose(rows_ref[...])[0:blocks, 0:height]
+
+
+def all_scales(pos, late, received, order, tiles, lat_tiles, lat_blocks):
     n = len(order)
     per_dest = (received[0].shape[0] - EXTRA) // (tiles * TILE)
-    lat_rows = maxima.shape[0] // 8 * chunks
     expert, latent = pl.pallas_call(
-        functools.partial(scales_kernel, order, tiles, chunks),
-        in_specs=[SMEM, VMEM] + [ANY] * n,
+        functools.partial(scales_kernel, order, tiles, lat_tiles, len(late)),
+        in_specs=[SMEM] + [VMEM] * len(late) + [ANY] * n,
         out_specs=[VMEM, VMEM],
         out_shape=[
             jax.ShapeDtypeStruct((1, per_dest * n * tiles), F32),
-            jax.ShapeDtypeStruct((lat_blocks, lat_rows * CHUNK // TILE), F32),
+            jax.ShapeDtypeStruct((lat_blocks, n * lat_tiles), F32),
         ],
         scratch_shapes=[
             pltpu.VMEM((n, EXTRA, TILE), BF16),
-            pltpu.VMEM((lat_rows, TILE), F32),
             pltpu.VMEM((TILE, TILE), F32),
             pltpu.SemaphoreType.DMA((n,)),
         ],
         compiler_params=LIGHT,
         cost_estimate=pl.CostEstimate(flops=1000000, bytes_accessed=100000, transcendentals=0),
         name="all_scales",
-    )(pos, maxima, *received)
+    )(pos, *late, *received)
     return expert, latent.T
 
 
@@ -408,9 +403,8 @@
     return pl.multiple_of(lax.rem(pos * (TILE - rows % TILE), TILE), CHUNK)
 
 
-def full_kernel(pieces, rows, x_ref, tops_ref, *refs):
-    out_ref, tops_out, buf, in_sem, out_sem = refs[-5:]
-    tops_out[...] = tops_ref[...]
+def full_kernel(pieces, rows, x_ref, *refs):
+    out_ref, buf, in_sem, out_sem = refs[-4:]
     loads, stores = [], []
     for i in range(pieces):
         lead = i * (TILE - rows % TILE) % TILE
@@ -428,41 +422,40 @@
     wait_all(stores)
 
 
-def place_full(out, x, tops, rows):
+def place_full(out, x, rows):
     pieces = x.shape[0] // TILE
     return pl.pallas_call(
         functools.partial(full_kernel, pieces, rows),
-        in_specs=[ANY, VMEM] + [ANY] * len(out),
-        out_specs=[ANY, VMEM],
-        out_shape=[
-            jax.ShapeDtypeStruct((pieces * rows, x.shape[1]), BF16),
-            jax.ShapeDtypeStruct(tops.shape, tops.dtype),
-        ],
+        in_specs=[ANY] * (1 + len(out)),
+        out_specs=ANY,
+        out_shape=jax.ShapeDtypeStruct((pieces * rows, x.shape[1]), BF16),
         scratch_shapes=[
             pltpu.VMEM(x.shape, BF16),
             pltpu.SemaphoreType.DMA((pieces,)),
             pltpu.SemaphoreType.DMA((pieces,)),
         ],
-        input_output_aliases={2: 0} if out else {},
+        input_output_aliases={1: 0} if out else {},
         compiler_params=PARAMS,
         cost_estimate=pl.CostEstimate(flops=0, bytes_accessed=4 * x.size, transcendentals=0),
         name="place_whole",
-    )(x, tops, *out)
-
-
-def rest_kernel(deltas, rows, pos_ref, *refs):
-    x_refs = refs[: len(deltas)]
-    out_ref, buf, in_sem, out_sem = refs[-4:]
+    )(x, *out)
+
+
+def rest_kernel(deltas, rows, n_after, forward, pos_ref, *refs):
+    n = len(deltas)
+    x_refs, out_ref = refs[:n], refs[-4 - forward]
+    buf, in_sem, out_sem = refs[-3:]
     span = rows - TILE
-    loads = [
-        pltpu.make_async_copy(x_refs[i], buf.at[i], in_sem.at[i]) for i in range(len(deltas))
-    ]
+    loads = [pltpu.make_async_copy(x_refs[i], buf.at[i], in_sem.at[i]) for i in range(n)]
     copy_all(loads)
     stores = []
-    for i, delta in enumerate(deltas):
-        peer = pos_ref[0] ^ delta
+    for i in reversed(range(n)):
+        peer = pos_ref[0] ^ deltas[i]
         lead = whole_tile(peer, rows)
         loads[i].wait()
+        if forward and i == n - 1:
+            stores.append(pltpu.make_async_copy(buf.at[i], refs[-4], out_sem.at[n, 0]))
+            stores[-1].start()
         for c in range(span // CHUNK):
             at = peer * rows + c * CHUNK + jnp.where(c * CHUNK < lead, 0, TILE)
             stores.append(
@@ -476,24 +469,26 @@
     wait_all(stores)
 
 
-def place_rest(out, pos, xs, deltas, rows, peers):
+def place_rest(out, pos, xs, deltas, rows, peers, after=(), forward=False):
     span, cols = xs[0].shape
     n = len(xs)
+    shapes = [jax.ShapeDtypeStruct((peers * rows, cols), BF16)]
+    shapes += [jax.ShapeDtypeStruct((span, cols), BF16)] * forward
     return pl.pallas_call(
-        functools.partial(rest_kernel, deltas, rows),
-        in_specs=[SMEM] + [ANY] * (n + len(out)),
-        out_specs=ANY,
-        out_shape=jax.ShapeDtypeStruct((peers * rows, cols), BF16),
+        functools.partial(rest_kernel, deltas, rows, len(after), int(forward)),
+        in_specs=[SMEM] + [ANY] * (n + len(out) + len(after)),
+        out_specs=[ANY] * len(shapes),
+        out_shape=shapes,
         scratch_shapes=[
             pltpu.VMEM((n, span, cols), BF16),
             pltpu.SemaphoreType.DMA((n,)),
-            pltpu.SemaphoreType.DMA((n, span // CHUNK)),
+            pltpu.SemaphoreType.DMA((n + 1, span // CHUNK)),
         ],
         input_output_aliases={1 + n: 0} if out else {},
         compiler_params=pltpu.CompilerParams(vmem_limit_bytes=4 * 1024 * 1024),
         cost_estimate=pl.CostEstimate(flops=0, bytes_accessed=4 * n * span * cols, transcendentals=0),
         name="place_rest",
-    )(pos, *xs, *out)
+    )(pos, *xs, *out, *after)
 
 
 SLABS = 4
@@ -579,12 +574,13 @@
     )(step, pos, *arrays)
 
 
-def latent_rest_kernel(chunks, pos_ref, w1_ref, own_ref, prev_ref, next_ref, after_ref, *refs):
-    q_ref, w, q, ext, in_sem, out_sem = refs
+def latent_rest_kernel(chunks, peers, pos_ref, w1_ref, *refs):
+    q_ref, side_ref, w, q, ext, tops_ref, in_sem, out_sem = refs[-8:]
     per_tile = TILE // CHUNK
     rows, cols = w1_ref.shape
     width = cols // SLABS
-    lead = whole_tile(pos_ref[0], rows)
+    pos = pos_ref[0]
+    lead = whole_tile(pos, rows)
     loads, stores = [], []
     for i in range(SLABS):
         at = pl.ds(i * width, width)
@@ -601,14 +597,24 @@
         copy_all(group)
         loads.append(group)
         stores.append(pltpu.make_async_copy(q.at[:, at], q_ref.at[:, at], out_sem.at[i]))
-    ext[0:chunks, :] = prev_ref[0:chunks, :]
-    ext[chunks : 2 * chunks, :] = own_ref[0:chunks, :]
-    ext[2 * chunks : 3 * chunks, :] = next_ref[0:chunks, :]
-    first = chunks + lead // CHUNK
-    above = jnp.max(ext[pl.ds(first - per_tile, per_tile), :], axis=0, keepdims=True)
-    below = jnp.max(ext[pl.ds(first + per_tile, per_tile), :], axis=0, keepdims=True)
+    for s in range(peers):
+        peer = lax.rem(pos + peers - s, peers)
+        ext[pl.ds(peer * chunks, chunks), :] = refs[s][0:chunks, :]
+    tops_ref[...] = jnp.zeros_like(tops_ref)
+    for t in range(peers * chunks // per_tile):
+        tops_ref[t : t + 1, :] = jnp.max(
+            ext[t * per_tile : (t + 1) * per_tile, :], axis=0, keepdims=True
+        )
+    lane = lax.broadcasted_iota(jnp.int32, (8, TILE), 1)
+    side = jnp.zeros((8, TILE), F32)
+    for p, value in enumerate(three_parts(tops_ref[...])):
+        at = SPARE + 16 * p
+        side = jnp.where((lane >= at) & (lane < at + 16), pltpu.roll(value, at, 1), side)
+    side_ref[...] = side
+    start = pos * chunks
+    above = tops_ref[pl.ds(start // per_tile, 1), :]
+    below = tops_ref[pl.ds((start + lead // CHUNK + per_tile) // per_tile, 1), :]
     both = jnp.concatenate([above] * 4 + [below] * 4, axis=0)
-    lane = lax.broadcasted_iota(jnp.int32, (8, TILE), 1)
     tops = [
         jnp.max(jnp.where(lane == b, both, 0.0), axis=1, keepdims=True) for b in range(cols // TILE)
     ]
@@ -625,18 +631,23 @@
     wait_all(stores)
 
 
-def latent_rest(w1, own, above, below, pos, after):
+def latent_rest(w1, maxima, pos, after):
     rows, cols = w1.shape
     chunks = rows // CHUNK
+    peers = len(maxima)
     return pl.pallas_call(
-        functools.partial(latent_rest_kernel, chunks),
-        in_specs=[SMEM, ANY] + [VMEM] * 3 + [ANY],
-        out_specs=ANY,
-        out_shape=jax.ShapeDtypeStruct((rows - TILE, cols), BF16),
+        functools.partial(latent_rest_kernel, chunks, peers),
+        in_specs=[SMEM, ANY] + [VMEM] * peers + [ANY],
+        out_specs=[ANY, VMEM],
+        out_shape=[
+            jax.ShapeDtypeStruct((rows - TILE, cols), BF16),
+            jax.ShapeDtypeStruct((8, TILE), F32),
+        ],
         scratch_shapes=[
             pltpu.VMEM((rows - TILE, cols), F32),
             pltpu.VMEM((rows - TILE, cols), BF16),
-            pltpu.VMEM((24, TILE), F32),
+            pltpu.VMEM((8 * peers, TILE), F32),
+            pltpu.VMEM((8, TILE), F32),
             pltpu.SemaphoreType.DMA((SLABS, chunks)),
             pltpu.SemaphoreType.DMA((SLABS,)),
         ],
@@ -645,7 +656,7 @@
             flops=rows * cols, bytes_accessed=3 * rows * cols, transcendentals=0
         ),
         name="latent_rest",
-    )(pos, w1, own, above, below, after)
+    )(pos, w1, *maxima, after)
 
 
 def fast_fits(expert_shape, latent_shape, dp_count, exp_axis):
@@ -656,16 +667,17 @@
         and rows % TILE == 0
         and rows <= 8 * TILE
         and cols % (TILE * dp_count) == 0
-        and cols // TILE // dp_count <= 20
+        and cols // TILE // dp_count <= 16
         and dp_count >= 4
         and dp_count & (dp_count - 1) == 0
         and dp_count * latent_rows * exp_axis <= TILE * TILE
         and latent_rows % CHUNK == 0
         and 2 * TILE - CHUNK <= latent_rows < 2 * TILE
         and latent_rows * exp_axis % TILE == 0
-        and exp_axis & (exp_axis - 1) == 0
+        and latent_rows * exp_axis <= 8 * TILE
+        and exp_axis == 4
         and latent_cols % (SLABS * TILE) == 0
-        and latent_cols <= TILE * TILE
+        and latent_cols <= 16 * TILE
     )
 
 
@@ -703,56 +715,53 @@
     )
     latent_rows = latent_new.shape[0]
     whole = lax.all_gather(whole, "expert", axis=0, tiled=True)
-    above = lax.ppermute(chunk_top, "expert", [(i, i + 1) for i in range(exp_axis - 1)])
-    below = lax.ppermute(chunk_top, "expert", [(i + 1, i) for i in range(exp_axis - 1)])
+    maxima = [chunk_top] + [
+        lax.ppermute(chunk_top, "expert", [(i, (i + s) % exp_axis) for i in range(exp_axis)])
+        for s in range(1, exp_axis)
+    ]
+
     arrays = tuple(
         a.reshape(rows, cols) for a in (expert_master, expert_first, expert_second, expert_grad)
     )
+    def swap(x, axis, k):
+        return lax.ppermute(x, axis, [(i, i ^ k) for i in range(lax.axis_size(axis))])
+
     state, arrived, after = (), [], ()
-    for n, partners in enumerate(partner_groups(dp_count)):
+    side = jnp.zeros((8, TILE), F32)
+    groups = partner_groups(dp_count)
+    for n, partners in enumerate(groups):
         state, sent = expert_group(
-            arrays, state, column_owner, dp_pos.reshape(1), step_count, after, partners, per_dest
+            arrays, state, column_owner, dp_pos.reshape(1), step_count, side, after, partners, per_dest
         )
+        arrived += [(k, swap(q, "dp", k) if k else q) for k, q in zip(partners, sent)]
         if n == 0:
-            rest = {
-                0: latent_rest(latent_new, chunk_top, above, below, expert_at, sent[0])
-            }
-            bit = exp_axis // 2
-            while bit:
-                pairs = [(i, i ^ bit) for i in range(exp_axis)]
-                moved = {d ^ bit: lax.ppermute(x, "expert", pairs) for d, x in rest.items()}
-                rest.update(moved)
-                bit //= 2
-        for k, q in zip(partners, sent):
-            pairs = [(i, i ^ k) for i in range(dp_count)]
-            arrived.append((k, lax.ppermute(q, "dp", pairs) if k else q))
-        if n == 0:
-            after = (rest[0],)
+            rest, side = latent_rest(latent_new, maxima, expert_at, sent[0])
+            far, near = swap(rest, "expert", 2), swap(rest, "expert", 1)
+            late = [swap(side, "dp", k) for k in partners]
+            after = ()
         elif n == 1:
-            after = tuple(q[-EXTRA:] for _, q in arrived[: len(partners)])
+            after = tuple(q[-EXTRA:] for _, q in arrived[: len(groups[0])])
         else:
-            after = (rest[exp_axis - 1][:EXTRA, :TILE],)
+            after = ()
+    latent_served, far_again = place_rest(
+        (), expert_at, [rest, far], [0, 2], latent_rows, exp_axis, (sent[-1][-EXTRA:],), True
+    )
+    last = swap(far_again, "expert", 1)
+    (latent_served,) = place_rest((latent_served,), expert_at, [near], [1], latent_rows, exp_axis)
+    latent_served = place_full((latent_served,), whole, latent_rows)
+    (latent_served,) = place_rest((latent_served,), expert_at, [last], [3], latent_rows, exp_axis)
+
     placed = ()
     for k, q in arrived[-1:] + arrived[:-1]:
         placed = (place_rows(placed, (dp_pos ^ k).reshape(1), q, dp_count, per_dest),)
     expert_served = placed[0].reshape(1, block_count * rows, TILE)
-    deltas = list(rest)
-    near, last = deltas[:-1], deltas[-1:]
-    latent_served = place_rest(
-        (), expert_at, [rest[d] for d in near], near, latent_rows, exp_axis
-    )
-    latent_served, tops = place_full((latent_served,), whole, chunk_top, latent_rows)
-    latent_served = place_rest(
-        (latent_served,), expert_at, [rest[d] for d in last], last, latent_rows, exp_axis
-    )
-    maxima = lax.all_gather(tops, ("dp", "expert"), axis=0, tiled=True)
     expert_scales, latent_scales = all_scales(
         dp_pos.reshape(1),
-        maxima,
+        late,
         [q for _, q in arrived],
         [k for k, _ in arrived],
         tiles,
-        latent_rows // CHUNK,
+        latent_rows * exp_axis // TILE,
         latent_new.shape[1] // TILE,
     )
 

time: 184 us -> 96 us (0.52)
  blocking collectives: 67.3 us -> 0 us
  waiting for transfers between devices: 34.1 us -> 15.2 us
  starting transfers between devices: 21 us -> 18.9 us
    all_gather x1 -> x0, blocking collectives: 67.3 us -> none  [fast_body(): maxima = lax.all_gather(tops, ('dp', 'expert'), axis=0, tiled=True)]
    ppermute x12 -> x15, waiting for transfers between devices: 34.1 us -> 15.2 us  [the longest x12 12.8 us: swap(): lax.ppermute(x, axis, [(i, i ^ k) for i in range(lax.axis_size(axis))])]
    pallas_call x4 -> x5, Pallas kernels: 6.61 us -> 8.94 us  [the longest x3 3.69 us: place_rest(): pl.pallas_call(functools.partial(rest_kernel, deltas, rows, len(after), i...]
    ppermute x12 -> x15, starting transfers between devices: 21 us -> 18.8 us  [the longest x12 13.3 us: swap(): lax.ppermute(x, axis, [(i, i ^ k) for i in range(lax.axis_size(axis))])]
  transfers between devices with their start and end apart: 13 -> 16, of which waited for: 2 -> 4; matrix products, arithmetic and copies ran while one was open for 1% -> 3% of each run, Pallas kernels for 16% -> 38%
where the time goes in v5:
time: 96 us; the launch traced here: 95.5 us
  Pallas kernels  42 us (44%)
  starting transfers between devices  18.9 us (20%)
  waiting for transfers between devices  15.2 us (16%)
  between operations  15 us (16%)
  local copies, waits for them, and re-layouts  4.46 us (5%)
    pallas_call x4, Pallas kernels, expert_group(): pl.pallas_call(functools.partial(expert_kernel, partners, per_dest, n_ali...  20.3 us
    ppermute x12, starting transfers between devices, swap(): lax.ppermute(x, axis, [(i, i ^ k) for i in range(lax.axis_size(axis))])  13.3 us
    ppermute x12, waiting for transfers between devices, swap(): lax.ppermute(x, axis, [(i, i ^ k) for i in range(lax.axis_size(axis))])  12.8 us
    pallas_call x8, Pallas kernels, place_rows(): pl.pallas_call(place_kernel, in_specs=[SMEM] + [ANY] * (1 + len(placed)),...  6.28 us
    ppermute x3, starting transfers between devices, fast_body(): lax.ppermute(chunk_top, 'expert', [(i, (i + s) % exp_axis) for i in range...  5.51 us
    pallas_call x1, Pallas kernels, latent_update(): pl.pallas_call(functools.partial(latent_kernel, rows // CHUNK), in_specs=...  4.32 us
    pallas_call x3, Pallas kernels, place_rest(): pl.pallas_call(functools.partial(rest_kernel, deltas, rows, len(after), i...  3.69 us
    pallas_call x1, Pallas kernels, latent_rest(): pl.pallas_call(functools.partial(latent_rest_kernel, chunks, peers), in_s...  3.38 us
  transfers between devices with their start and end apart: 16, of which 4 were waited for; matrix products, arithmetic and copies ran while one was open for 3% of the time, Pallas kernels for 38%

profile of v5, /device:TPU:0, one launch (start us, length us, event | category | flops | bytes accessed | tf_op | source)
XLA Modules:
  0.0 95.5 jit_solution(10440949797744479016)
XLA Ops:
  7.2 0.0 all-gather.2.cloned.1.call-start
  7.9 4.3 %latent_adamw.1 = (f32[224,1536]{1,0:T(8,128)}, bf16[224,1536]{1,0:T(8,128)(2,1)}, bf16[224,1536]{1,0:T(8,128)(2,1)}, bf16[128,1536]{1,0:T(8,128)(2,1)}, f32[8,128]{1,0:T(8,128)}) custom-call(s32[1]{0:T(128)S(6)} %copy.58.step_ref, s32[1]{0:T(128)} %bitcast.1.pos_ref, f32[224,1536]{1,0:T(8,128)} %refs_0_.1, bf16[224,1536]{1,0:T(8,128)(2,1)} %refs_1_.1, ...), custom_call_target="tpu_custom_call" | custom-call | flops 10321920 | bytes 6193152 | tf_op jit(solution)/shard_map/latent_adamw/pallas_call | solution.py:549
  12.2 0.0 all-gather.2.cloned.1.call-update
  12.2 0.6 broadcast_in_dim.12.side_ref
  12.8 5.1 %expert_adamw.4 = (f32[896,2048]{1,0:T(8,128)}, bf16[896,2048]{1,0:T(8,128)(2,1)}, bf16[896,2048]{1,0:T(8,128)(2,1)}, bf16[1808,128]{1,0:T(8,128)(2,1)}, bf16[1808,128]{1,0:T(8,128)(2,1)}) custom-call(s32[16]{0:T(128)} %owner_ref.7, s32[1]{0:T(128)} %bitcast.pos_ref.src_ref, s32[1]{0:T(128)S(6)} %copy.58.step_ref, f32[8,128]{1,0:T(8,128)} %broadcast_in_dim.12.side_ref, ...), custom_call_target="tpu_custom_call" | custom-call | flops 458752 | bytes 458752 | tf_op jit(solution)/shard_map/expert_adamw/pallas_call | solution.py:292
  17.9 3.0 %collective-permute-start.3 = (bf16[1808,128]{1,0:T(8,128)(2,1)}, bf16[1808,128]{1,0:T(8,128)(2,1)S(1)}, u32[]{:S(2)}, u32[]{:S(2)}) collective-permute-start(bf16[1808,128]{1,0:T(8,128)(2,1)} %get-tuple-element.43.refs_4_), channel_id=1, source_target_pairs={{0,16},{4,20},{8,24},{12,28},{16,0},{20,4},{24,8},{28,12},{1,17},{... | collective-permute-start | bytes 1388552 | tf_op jit(solution)/shard_map/ppermute | solution.py:727
  21.0 1.5 %collective-permute-start.4 = (bf16[1808,128]{1,0:T(8,128)(2,1)}, bf16[1808,128]{1,0:T(8,128)(2,1)S(1)}, u32[]{:S(2)}, u32[]{:S(2)}) collective-permute-start(bf16[1808,128]{1,0:T(8,128)(2,1)} %get-tuple-element.51), channel_id=1, source_target_pairs={{0,8},{4,12},{8,0},{12,4},{16,24},{20,28},{24,16},{28,20},{1,9},{5... | collective-permute-start | bytes 1388552 | tf_op jit(solution)/shard_map/ppermute | solution.py:727
  22.5 1.6 %collective-permute-start = (f32[8,128]{1,0:T(8,128)S(1)}, f32[8,128]{1,0:T(8,128)S(1)}, u32[]{:S(2)}, u32[]{:S(2)}) collective-permute-start(f32[8,128]{1,0:T(8,128)S(1)} %copy-done.4), channel_id=1, source_target_pairs={{0,1},{1,2},{2,3},{3,0},{4,5},{5,6},{6,7},{7,4},{8,9},{9,10},{10,1... | collective-permute-start | bytes 12296 | tf_op jit(solution)/shard_map/ppermute | solution.py:719
  24.0 2.6 %collective-permute-start.1 = (f32[8,128]{1,0:T(8,128)S(1)}, f32[8,128]{1,0:T(8,128)S(1)}, u32[]{:S(2)}, u32[]{:S(2)}) collective-permute-start(f32[8,128]{1,0:T(8,128)S(1)} %copy-done.4), channel_id=1, source_target_pairs={{0,2},{1,3},{2,0},{3,1},{4,6},{5,7},{6,4},{7,5},{8,10},{9,11},{10,... | collective-permute-start | bytes 12296 | tf_op jit(solution)/shard_map/ppermute | solution.py:719
  26.6 1.3 %collective-permute-start.2 = (f32[8,128]{1,0:T(8,128)S(1)}, f32[8,128]{1,0:T(8,128)S(1)}, u32[]{:S(2)}, u32[]{:S(2)}) collective-permute-start(f32[8,128]{1,0:T(8,128)S(1)} %copy-done.4), channel_id=1, source_target_pairs={{0,3},{1,0},{2,1},{3,2},{4,7},{5,4},{6,5},{7,6},{8,11},{9,8},{10,9... | collective-permute-start | bytes 12296 | tf_op jit(solution)/shard_map/ppermute | solution.py:719
  28.0 0.0 collective-permute-done.refs_1_
  28.0 0.6 collective-permute-done.1.refs_2_
  28.6 1.6 %collective-permute-done.2.refs_3_ = f32[8,128]{1,0:T(8,128)S(1)} collective-permute-done((f32[8,128]{1,0:T(8,128)S(1)}, f32[8,128]{1,0:T(8,128)S(1)}, u32[]{:S(2)}, u32[]{:S(2)}) %collective-permute-start.2) | collective-permute-done | bytes 4128 | tf_op jit(solution)/shard_map/ppermute | solution.py:719
  30.3 0.6 copy-done.7
  30.9 3.4 %latent_rest.1 = (bf16[96,1536]{1,0:T(8,128)(2,1)}, f32[8,128]{1,0:T(8,128)}) custom-call(s32[1]{0:T(128)} %bitcast.1.pos_ref, f32[224,1536]{1,0:T(8,128)} %get-tuple-element.36.w1_ref, f32[8,128]{1,0:T(8,128)} %get-tuple-element.42.refs_0_, f32[8,128]{1,0:T(8,128)} %copy-done.5, f32[8,128]{1,0:T(8,128)} %copy-done.6, f32[8,128]{1,0:T(8,128)} %copy-done.7, ...), custom_call_target="tpu_custom_call" | custom-call | flops 344064 | bytes 1032192 | tf_op jit(solution)/shard_map/latent_rest/pallas_call | solution.py:638
  34.3 1.1 %collective-permute-start.12 = (bf16[96,1536]{1,0:T(8,128)(2,1)}, bf16[96,1536]{1,0:T(8,128)(2,1)S(1)}, u32[]{:S(2)}, u32[]{:S(2)}) collective-permute-start(bf16[96,1536]{1,0:T(8,128)(2,1)} %get-tuple-element.67.refs_0_), channel_id=1, source_target_pairs={{0,2},{1,3},{2,0},{3,1},{4,6},{5,7},{6,4},{7,5},{8,10},{9,11},{10,... | collective-permute-start | bytes 884744 | tf_op jit(solution)/shard_map/ppermute | solution.py:727
  35.3 2.8 %collective-permute-start.14 = (bf16[96,1536]{1,0:T(8,128)(2,1)}, bf16[96,1536]{1,0:T(8,128)(2,1)S(1)}, u32[]{:S(2)}, u32[]{:S(2)}) collective-permute-start(bf16[96,1536]{1,0:T(8,128)(2,1)} %get-tuple-element.67.refs_0_), channel_id=1, source_target_pairs={{0,1},{1,0},{2,3},{3,2},{4,5},{5,4},{6,7},{7,6},{8,9},{9,8},{10,11... | collective-permute-start | bytes 884744 | tf_op jit(solution)/shard_map/ppermute | solution.py:727
  38.1 5.0 %expert_adamw.5 = (f32[896,2048]{1,0:T(8,128)}, bf16[896,2048]{1,0:T(8,128)(2,1)}, bf16[896,2048]{1,0:T(8,128)(2,1)}, bf16[1808,128]{1,0:T(8,128)(2,1)}, bf16[1808,128]{1,0:T(8,128)(2,1)}) custom-call(s32[16]{0:T(128)} %owner_ref.7, s32[1]{0:T(128)} %bitcast.pos_ref.src_ref, ...), custom_call_target="tpu_custom_call", output_to_operand_aliasing={{0}: (8, {}), {1}: (9, {}), {2}: (10, {})} | custom-call | flops 458752 | bytes 458752 | tf_op jit(solution)/shard_map/expert_adamw/pallas_call | solution.py:292
  43.1 0.5 collective-permute-start.8
  43.7 0.0 collective-permute-done.3.q_ref.refs_2_
  43.7 0.6 slice.12.refs_7_
  44.3 0.6 slice.13.refs_8_
  44.9 5.1 %expert_adamw.6 = (f32[896,2048]{1,0:T(8,128)}, bf16[896,2048]{1,0:T(8,128)(2,1)}, bf16[896,2048]{1,0:T(8,128)(2,1)}, bf16[1808,128]{1,0:T(8,128)(2,1)}, bf16[1808,128]{1,0:T(8,128)(2,1)}) custom-call(s32[16]{0:T(128)} %owner_ref.7, s32[1]{0:T(128)} %bitcast.pos_ref.src_ref, ...), custom_call_target="tpu_custom_call", output_to_operand_aliasing={{0}: (8, {}), {1}: (9, {}), {2}: (10, {})} | custom-call | flops 458752 | bytes 458752 | tf_op jit(solution)/shard_map/expert_adamw/pallas_call | solution.py:292
  50.0 2.7 %collective-permute-start.7 = (bf16[1808,128]{1,0:T(8,128)(2,1)}, bf16[1808,128]{1,0:T(8,128)(2,1)S(1)}, u32[]{:S(2)}, u32[]{:S(2)}) collective-permute-start(bf16[1808,128]{1,0:T(8,128)(2,1)} %get-tuple-element.60), channel_id=1, source_target_pairs={{0,20},{4,16},{8,28},{12,24},{16,4},{20,0},{24,12},{28,8},{1,21},{... | collective-permute-start | bytes 1388552 | tf_op jit(solution)/shard_map/ppermute | solution.py:727
  52.7 5.1 %expert_adamw.7 = (f32[896,2048]{1,0:T(8,128)}, bf16[896,2048]{1,0:T(8,128)(2,1)}, bf16[896,2048]{1,0:T(8,128)(2,1)}, bf16[1808,128]{1,0:T(8,128)(2,1)}, bf16[1808,128]{1,0:T(8,128)(2,1)}) custom-call(s32[16]{0:T(128)} %owner_ref.7, s32[1]{0:T(128)} %bitcast.pos_ref.src_ref, ...), custom_call_target="tpu_custom_call", output_to_operand_aliasing={{0}: (8, {}), {1}: (9, {}), {2}: (10, {})} | custom-call | flops 458752 | bytes 458752 | tf_op jit(solution)/shard_map/expert_adamw/pallas_call | solution.py:292
  57.8 5.1 %collective-permute-done.12.refs_1_ = bf16[96,1536]{1,0:T(8,128)(2,1)S(1)} collective-permute-done((bf16[96,1536]{1,0:T(8,128)(2,1)}, bf16[96,1536]{1,0:T(8,128)(2,1)S(1)}, u32[]{:S(2)}, u32[]{:S(2)}) %collective-permute-start.12) | collective-permute-done | bytes 294944 | tf_op jit(solution)/shard_map/ppermute | solution.py:727
  62.9 0.9 collective-permute-start.5
  63.7 0.7 slice.11.refs_2_
  64.4 1.1 %place_rest.3 = (bf16[896,1536]{1,0:T(8,128)(2,1)}, bf16[96,1536]{1,0:T(8,128)(2,1)}) custom-call(s32[1]{0:T(128)} %bitcast.1.pos_ref, bf16[96,1536]{1,0:T(8,128)(2,1)S(1)} %copy-done.2, bf16[96,1536]{1,0:T(8,128)(2,1)S(1)} %collective-permute-done.12.refs_1_, bf16[16,128]{1,0:T(8,128)(2,1)S(1)} %slice.11.refs_2_), custom_call_target="tpu_custom_call" | custom-call | bytes 1179648 | tf_op jit(solution)/shard_map/place_rest/pallas_call | solution.py:477
  65.6 0.1 collective-permute-start.13
  65.7 0.2 collective-permute-start.10
  65.8 7.7 %collective-permute-done.7.q_ref.refs_6_ = bf16[1808,128]{1,0:T(8,128)(2,1)S(1)} collective-permute-done((bf16[1808,128]{1,0:T(8,128)(2,1)}, bf16[1808,128]{1,0:T(8,128)(2,1)S(1)}, u32[]{:S(2)}, u32[]{:S(2)}) %collective-permute-start.7) | collective-permute-done | bytes 462880 | tf_op jit(solution)/shard_map/ppermute | solution.py:727
  73.6 0.5 collective-permute-start.11
  74.1 1.0 %copy-done = bf16[1808,128]{1,0:T(8,128)(2,1)S(1)} copy-done((bf16[1808,128]{1,0:T(8,128)(2,1)S(1)}, bf16[1808,128]{1,0:T(8,128)(2,1)}, u32[]{:S(2)}) %copy-start) | copy-done | bytes 462872
  75.1 0.8 place_served.8.refs_0_
  75.9 0.8 place_rest.4.refs_0_
  76.8 0.8 place_served.9.refs_0_
  77.6 0.8 place_served.10.refs_0_
  78.4 0.8 place_served.11.refs_0_
  79.2 0.8 place_served.12.refs_0_
  79.9 0.8 place_served.13.refs_0_
  80.8 0.8 place_served.14.refs_0_
  81.6 0.8 place_served.15
  82.4 0.4 copy-done.1
  82.7 1.9 %all_scales.1 = (f32[1,112]{1,0:T(1,128)}, f32[12,56]{1,0:T(8,128)}) custom-call(s32[1]{0:T(128)} %bitcast.pos_ref.src_ref, f32[8,128]{1,0:T(8,128)S(1)} %collective-permute-done.10.refs_0_, f32[8,128]{1,0:T(8,128)S(1)} %collective-permute-done.11.refs_1_, bf16[1808,128]{1,0:T(8,128)(2,1)S(1)} %collective-permute-done.3.q_ref.refs_2_, ...), custom_call_target="tpu_custom_call" | custom-call | flops 1000000 | bytes 100000 | tf_op jit(solution)/shard_map/all_scales/pallas_call | solution.py:382
  84.6 0.0 all-gather.2.cloned.1.call-done.x_ref
  84.6 2.2 %place_whole.1.refs_1_ = bf16[896,1536]{1,0:T(8,128)(2,1)} custom-call(bf16[512,1536]{1,0:T(8,128)(2,1)} %all-gather.2.cloned.1.call-done.x_ref, bf16[896,1536]{1,0:T(8,128)(2,1)} %place_rest.4.refs_0_), custom_call_target="tpu_custom_call", output_to_operand_aliasing={{}: (1, {})} | custom-call | bytes 3145728 | tf_op jit(solution)/shard_map/place_whole/pallas_call | solution.py:427
  86.9 1.7 %place_rest.5 = bf16[896,1536]{1,0:T(8,128)(2,1)} custom-call(s32[1]{0:T(128)} %bitcast.1.pos_ref, bf16[96,1536]{1,0:T(8,128)(2,1)} %collective-permute-done.13.refs_0_, bf16[896,1536]{1,0:T(8,128)(2,1)} %place_whole.1.refs_1_), custom_call_target="tpu_custom_call", output_to_operand_aliasing={{}: (2, {})} | custom-call | bytes 589824 | tf_op jit(solution)/shard_map/place_rest/pallas_call | solution.py:477
  (24 shorter events, 0.1 us)
Async XLA Ops:
  7.2 77.5 %all-gather.2.cloned.1.call-start = ((), (), s32[]{:S(2)}) async-start(), calls=%async_computation | async-start | bytes 1966080 | tf_op jit(solution)/shard_map/all_gather | solution.py:717
  12.8 9.6 %copy-start.4 = (f32[8,128]{1,0:T(8,128)S(1)}, f32[8,128]{1,0:T(8,128)}, u32[]{:S(2)}) copy-start(f32[8,128]{1,0:T(8,128)} %get-tuple-element.42.refs_0_) | copy-start | bytes 12292
  17.9 25.8 %collective-permute-start.3 = (bf16[1808,128]{1,0:T(8,128)(2,1)}, bf16[1808,128]{1,0:T(8,128)(2,1)S(1)}, u32[]{:S(2)}, u32[]{:S(2)}) collective-permute-start(bf16[1808,128]{1,0:T(8,128)(2,1)} %get-tuple-element.43.refs_4_), channel_id=1, source_target_pairs={{0,16},{4,20},{8,24},{12,28},{16,0},{20,4},{24,8},{28,12},{1,17},{... | collective-permute-start | bytes 1388552 | tf_op jit(solution)/shard_map/ppermute | solution.py:727
  21.0 23.3 %collective-permute-start.4 = (bf16[1808,128]{1,0:T(8,128)(2,1)}, bf16[1808,128]{1,0:T(8,128)(2,1)S(1)}, u32[]{:S(2)}, u32[]{:S(2)}) collective-permute-start(bf16[1808,128]{1,0:T(8,128)(2,1)} %get-tuple-element.51), channel_id=1, source_target_pairs={{0,8},{4,12},{8,0},{12,4},{16,24},{20,28},{24,16},{28,20},{1,9},{5... | collective-permute-start | bytes 1388552 | tf_op jit(solution)/shard_map/ppermute | solution.py:727
  22.5 5.6 %collective-permute-start = (f32[8,128]{1,0:T(8,128)S(1)}, f32[8,128]{1,0:T(8,128)S(1)}, u32[]{:S(2)}, u32[]{:S(2)}) collective-permute-start(f32[8,128]{1,0:T(8,128)S(1)} %copy-done.4), channel_id=1, source_target_pairs={{0,1},{1,2},{2,3},{3,0},{4,5},{5,6},{6,7},{7,4},{8,9},{9,10},{10,1... | collective-permute-start | bytes 12296 | tf_op jit(solution)/shard_map/ppermute | solution.py:719
  24.0 4.6 %collective-permute-start.1 = (f32[8,128]{1,0:T(8,128)S(1)}, f32[8,128]{1,0:T(8,128)S(1)}, u32[]{:S(2)}, u32[]{:S(2)}) collective-permute-start(f32[8,128]{1,0:T(8,128)S(1)} %copy-done.4), channel_id=1, source_target_pairs={{0,2},{1,3},{2,0},{3,1},{4,6},{5,7},{6,4},{7,5},{8,10},{9,11},{10,... | collective-permute-start | bytes 12296 | tf_op jit(solution)/shard_map/ppermute | solution.py:719
  26.6 3.7 %collective-permute-start.2 = (f32[8,128]{1,0:T(8,128)S(1)}, f32[8,128]{1,0:T(8,128)S(1)}, u32[]{:S(2)}, u32[]{:S(2)}) collective-permute-start(f32[8,128]{1,0:T(8,128)S(1)} %copy-done.4), channel_id=1, source_target_pairs={{0,3},{1,0},{2,1},{3,2},{4,7},{5,4},{6,5},{7,6},{8,11},{9,8},{10,9... | collective-permute-start | bytes 12296 | tf_op jit(solution)/shard_map/ppermute | solution.py:719
  28.0 2.3 %copy-start.5 = (f32[8,128]{1,0:T(8,128)}, f32[8,128]{1,0:T(8,128)S(1)}, u32[]{:S(2)}) copy-start(f32[8,128]{1,0:T(8,128)S(1)} %collective-permute-done.refs_1_) | copy-start | bytes 12292
  28.6 1.7 %copy-start.6 = (f32[8,128]{1,0:T(8,128)}, f32[8,128]{1,0:T(8,128)S(1)}, u32[]{:S(2)}) copy-start(f32[8,128]{1,0:T(8,128)S(1)} %collective-permute-done.1.refs_2_) | copy-start | bytes 12292
  30.3 0.6 copy-start.7
  34.3 28.6 %collective-permute-start.12 = (bf16[96,1536]{1,0:T(8,128)(2,1)}, bf16[96,1536]{1,0:T(8,128)(2,1)S(1)}, u32[]{:S(2)}, u32[]{:S(2)}) collective-permute-start(bf16[96,1536]{1,0:T(8,128)(2,1)} %get-tuple-element.67.refs_0_), channel_id=1, source_target_pairs={{0,2},{1,3},{2,0},{3,1},{4,6},{5,7},{6,4},{7,5},{8,10},{9,11},{10,... | collective-permute-start | bytes 884744 | tf_op jit(solution)/shard_map/ppermute | solution.py:727
  35.3 27.5 %collective-permute-start.14 = (bf16[96,1536]{1,0:T(8,128)(2,1)}, bf16[96,1536]{1,0:T(8,128)(2,1)S(1)}, u32[]{:S(2)}, u32[]{:S(2)}) collective-permute-start(bf16[96,1536]{1,0:T(8,128)(2,1)} %get-tuple-element.67.refs_0_), channel_id=1, source_target_pairs={{0,1},{1,0},{2,3},{3,2},{4,5},{5,4},{6,7},{7,6},{8,9},{9,8},{10,11... | collective-permute-start | bytes 884744 | tf_op jit(solution)/shard_map/ppermute | solution.py:727
  43.1 22.4 %collective-permute-start.8 = (bf16[1808,128]{1,0:T(8,128)(2,1)}, bf16[1808,128]{1,0:T(8,128)(2,1)S(1)}, u32[]{:S(2)}, u32[]{:S(2)}) collective-permute-start(bf16[1808,128]{1,0:T(8,128)(2,1)} %get-tuple-element.61), channel_id=1, source_target_pairs={{0,24},{4,28},{8,16},{12,20},{16,8},{20,12},{24,0},{28,4},{1,25},{... | collective-permute-start | bytes 1388552 | tf_op jit(solution)/shard_map/ppermute | solution.py:727
  43.7 22.0 %collective-permute-start.9 = (bf16[1808,128]{1,0:T(8,128)(2,1)}, bf16[1808,128]{1,0:T(8,128)(2,1)S(1)}, u32[]{:S(2)}, u32[]{:S(2)}) collective-permute-start(bf16[1808,128]{1,0:T(8,128)(2,1)} %get-tuple-element.62), channel_id=1, source_target_pairs={{0,28},{4,24},{8,20},{12,16},{16,12},{20,8},{24,4},{28,0},{1,29},{... | collective-permute-start | bytes 1388552 | tf_op jit(solution)/shard_map/ppermute | solution.py:727
  50.0 23.6 %collective-permute-start.7 = (bf16[1808,128]{1,0:T(8,128)(2,1)}, bf16[1808,128]{1,0:T(8,128)(2,1)S(1)}, u32[]{:S(2)}, u32[]{:S(2)}) collective-permute-start(bf16[1808,128]{1,0:T(8,128)(2,1)} %get-tuple-element.60), channel_id=1, source_target_pairs={{0,20},{4,16},{8,28},{12,24},{16,4},{20,0},{24,12},{28,8},{1,21},{... | collective-permute-start | bytes 1388552 | tf_op jit(solution)/shard_map/ppermute | solution.py:727
  52.7 11.7 %copy-start.2 = (bf16[96,1536]{1,0:T(8,128)(2,1)S(1)}, bf16[96,1536]{1,0:T(8,128)(2,1)}, u32[]{:S(2)}) copy-start(bf16[96,1536]{1,0:T(8,128)(2,1)} %get-tuple-element.67.refs_0_) | copy-start | bytes 884740
  52.7 13.0 %copy-start.3 = (f32[8,128]{1,0:T(8,128)S(1)}, f32[8,128]{1,0:T(8,128)}, u32[]{:S(2)}) copy-start(f32[8,128]{1,0:T(8,128)} %get-tuple-element.44.side_ref) | copy-start | bytes 12292
  62.9 17.9 %collective-permute-start.6 = (bf16[1808,128]{1,0:T(8,128)(2,1)}, bf16[1808,128]{1,0:T(8,128)(2,1)S(1)}, u32[]{:S(2)}, u32[]{:S(2)}) collective-permute-start(bf16[1808,128]{1,0:T(8,128)(2,1)} %get-tuple-element.59), channel_id=1, source_target_pairs={{0,12},{4,8},{8,4},{12,0},{16,28},{20,24},{24,20},{28,16},{1,13},{... | collective-permute-start | bytes 1388552 | tf_op jit(solution)/shard_map/ppermute | solution.py:727
  62.9 18.7 %collective-permute-start.5 = (bf16[1808,128]{1,0:T(8,128)(2,1)}, bf16[1808,128]{1,0:T(8,128)(2,1)S(1)}, u32[]{:S(2)}, u32[]{:S(2)}) collective-permute-start(bf16[1808,128]{1,0:T(8,128)(2,1)} %get-tuple-element.58), channel_id=1, source_target_pairs={{0,4},{4,0},{8,12},{12,8},{16,20},{20,16},{24,28},{28,24},{1,5},{5... | collective-permute-start | bytes 1388552 | tf_op jit(solution)/shard_map/ppermute | solution.py:727
  65.6 21.3 %collective-permute-start.13 = (bf16[96,1536]{1,0:T(8,128)(2,1)}, bf16[96,1536]{1,0:T(8,128)(2,1)}, u32[]{:S(2)}, u32[]{:S(2)}) collective-permute-start(bf16[96,1536]{1,0:T(8,128)(2,1)} %get-tuple-element.68), channel_id=1, source_target_pairs={{0,1},{1,0},{2,3},{3,2},{4,5},{5,4},{6,7},{7,6},{8,9},{9,8},{10,11... | collective-permute-start | bytes 884744 | tf_op jit(solution)/shard_map/ppermute | solution.py:727
  65.7 16.7 %collective-permute-start.10 = (f32[8,128]{1,0:T(8,128)S(1)}, f32[8,128]{1,0:T(8,128)S(1)}, u32[]{:S(2)}, u32[]{:S(2)}) collective-permute-start(f32[8,128]{1,0:T(8,128)S(1)} %copy-done.3), channel_id=1, source_target_pairs={{0,16},{4,20},{8,24},{12,28},{16,0},{20,4},{24,8},{28,12},{1,17},{... | collective-permute-start | bytes 12296 | tf_op jit(solution)/shard_map/ppermute | solution.py:727
  73.6 8.8 %collective-permute-start.11 = (f32[8,128]{1,0:T(8,128)S(1)}, f32[8,128]{1,0:T(8,128)S(1)}, u32[]{:S(2)}, u32[]{:S(2)}) collective-permute-start(f32[8,128]{1,0:T(8,128)S(1)} %copy-done.3), channel_id=1, source_target_pairs={{0,8},{4,12},{8,0},{12,4},{16,24},{20,28},{24,16},{28,20},{1,9},{5... | collective-permute-start | bytes 12296 | tf_op jit(solution)/shard_map/ppermute | solution.py:727
  74.1 1.0 %copy-start = (bf16[1808,128]{1,0:T(8,128)(2,1)S(1)}, bf16[1808,128]{1,0:T(8,128)(2,1)}, u32[]{:S(2)}) copy-start(bf16[1808,128]{1,0:T(8,128)(2,1)} %get-tuple-element.63.q_ref.refs_9_) | copy-start | bytes 1388548
  81.6 1.2 %copy-start.1 = (bf16[1808,128]{1,0:T(8,128)(2,1)S(1)}, bf16[1808,128]{1,0:T(8,128)(2,1)}, u32[]{:S(2)}) copy-start(bf16[1808,128]{1,0:T(8,128)(2,1)} %get-tuple-element.63.q_ref.refs_9_) | copy-start | bytes 1388548
Sparse Core Ops, SparseCore 0:
  12.3 52.6 all-gather.1

commit v6 on v5

--- a/solution.py
+++ b/solution.py
@@ -207,18 +207,18 @@
         c.wait()
 
 
-def expert_kernel(partners, per_dest, n_alias, n_after, owner_ref, pos_ref, step_ref, side_ref, *refs):
-    refs = refs[: 4 + n_alias] + refs[4 + n_alias + n_after :]
-    hbm = refs[:4]
-    outs = refs[4 + n_alias : 7 + n_alias]
+def expert_kernel(partners, per_dest, n_alias, n_skip, has_side, owner_ref, pos_ref, step_ref, side_ref, *refs):
+    hbm, refs = refs[:4], refs[4 + n_alias + n_skip :]
     n_dest = len(partners)
-    q_refs = refs[7 + n_alias : 7 + n_alias + n_dest]
-    w, m, v, g, extra, in_sem, out_sem, extra_sem = refs[7 + n_alias + n_dest :]
+    outs, q_refs, served_ref = refs[:3], refs[3 : 3 + n_dest], refs[3 + n_dest]
+    w, m, v, g, extra, in_sem, out_sem, extra_sem = refs[-8:]
     bufs = (w, m, v, g)
     blocks = owner_ref.shape[0]
     rows = w.shape[1]
     tiles = rows // TILE
     pos = pos_ref[0]
+    if has_side:
+        refs[-9][...] = side_ref[...]
 
     loads, stores = [], []
     for d, k in enumerate(partners):
@@ -235,22 +235,19 @@
                     for a in range(4)
                 ]
             )
+            target = q_refs[d].at[pl.ds(j * rows, rows), :] if k else served_ref.at[j, pos]
             stores.append(
                 [
                     pltpu.make_async_copy(bufs[a].at[i], outs[a].at[:, cols], out_sem.at[i, a])
                     for a in range(3)
                 ]
-                + [
-                    pltpu.make_async_copy(
-                        g.at[i], q_refs[d].at[pl.ds(j * rows, rows), :], out_sem.at[i, 3]
-                    )
-                ]
+                + [pltpu.make_async_copy(g.at[i], target, out_sem.at[i, 3])]
             )
             copy_all(loads[-1])
     rate, corr = corrections(step_ref)
     lane = lax.broadcasted_iota(jnp.int32, (8, TILE), 1)
     extras = []
-    for d in range(n_dest):
+    for d, k in enumerate(partners):
         side = side_ref[...]
         for j in range(per_dest):
             i = d * per_dest + j
@@ -273,9 +270,10 @@
             for p, value in enumerate(three_parts(top)):
                 side = jnp.where(lane == 3 * j + p, value, side)
         extra[d] = jnp.concatenate([side, jnp.zeros_like(side)], axis=0).astype(BF16)
+        first = per_dest * rows if k else 0
         extras.append(
             pltpu.make_async_copy(
-                extra.at[d], q_refs[d].at[pl.ds(per_dest * rows, EXTRA), :], extra_sem.at[d]
+                extra.at[d], q_refs[d].at[pl.ds(first, EXTRA), :], extra_sem.at[d]
             )
         )
         extras[-1].start()
@@ -284,21 +282,31 @@
     wait_all(extras)
 
 
-def expert_group(arrays, state, owner, pos, step, side, after, partners, per_dest):
+def expert_group(arrays, state, owner, pos, step, side, carry, after, partners, per_dest):
     rows, cols = arrays[0].shape
     n_alias = len(state)
     n = len(partners) * per_dest
     elems = rows * TILE * n
+    sides = [jax.ShapeDtypeStruct(side.shape, side.dtype)] * (len(carry) > 0)
+    aliases = {8 + i: i for i in range(n_alias)}
+    aliases.update({8 + n_alias + i: 3 + len(partners) + i for i in range(len(carry))})
     out = pl.pallas_call(
-        functools.partial(expert_kernel, partners, per_dest, n_alias, len(after)),
-        in_specs=[SMEM] * 3 + [VMEM] + [ANY] * (4 + n_alias + len(after)),
-        out_specs=[ANY] * (3 + len(partners)),
+        functools.partial(
+            expert_kernel, partners, per_dest, n_alias, len(carry) + len(after), len(sides)
+        ),
+        in_specs=[SMEM] * 3 + [VMEM] + [ANY] * (4 + n_alias + len(carry) + len(after)),
+        out_specs=[ANY] * (3 + len(partners) + len(carry)) + [VMEM] * len(sides),
         out_shape=[
             jax.ShapeDtypeStruct((rows, cols), F32),
             jax.ShapeDtypeStruct((rows, cols), BF16),
             jax.ShapeDtypeStruct((rows, cols), BF16),
         ]
-        + [jax.ShapeDtypeStruct((per_dest * rows + EXTRA, TILE), BF16)] * len(partners),
+        + [
+            jax.ShapeDtypeStruct((per_dest * rows * (k > 0) + EXTRA, TILE), BF16)
+            for k in partners
+        ]
+        + [jax.ShapeDtypeStruct(x.shape, x.dtype) for x in carry]
+        + sides,
         scratch_shapes=[
             pltpu.VMEM((n, rows, TILE), F32),
             pltpu.VMEM((n, rows, TILE), BF16),
@@ -309,59 +317,83 @@
             pltpu.SemaphoreType.DMA((n, 4)),
             pltpu.SemaphoreType.DMA((len(partners),)),
         ],
-        input_output_aliases={8 + i: i for i in range(n_alias)},
+        input_output_aliases=aliases,
         compiler_params=PARAMS,
         cost_estimate=pl.CostEstimate(flops=elems, bytes_accessed=elems, transcendentals=0),
         name="expert_adamw",
-    )(owner, pos, step, side, *arrays, *state, *after)
-    return out[:3], out[3:]
-
-
-def place_kernel(src_ref, q_ref, *refs):
-    served, sem = refs[-2:]
+    )(owner, pos, step, side, *arrays, *state, *carry, *after)
+    return out[:3], out[3 : 3 + len(partners)], out[3 + len(partners) :]
+
+
+def block_copies(served, payloads, srcs, sem):
     per_dest, _, rows, _ = served.shape
-    src = src_ref[0]
-    copies = [
-        pltpu.make_async_copy(q_ref.at[pl.ds(j * rows, rows), :], served.at[j, src], sem.at[j])
+    return [
+        pltpu.make_async_copy(q.at[pl.ds(j * rows, rows), :], served.at[j, src], sem.at[i, j])
+        for i, (q, src) in enumerate(zip(payloads, srcs))
         for j in range(per_dest)
     ]
+
+
+def place_kernel(partners, pos_ref, *refs):
+    n = len(partners)
+    served, sem = refs[-2:]
+    copies = block_copies(served, refs[:n], [pos_ref[0] ^ k for k in partners], sem)
     copy_all(copies)
     wait_all(copies)
 
 
-def place_rows(placed, src, q, dp_count, per_dest):
-    rows = (q.shape[0] - EXTRA) // per_dest
+def place_blocks(served, pos, payloads, partners, shape):
+    n = len(partners)
     return pl.pallas_call(
-        place_kernel,
-        in_specs=[SMEM] + [ANY] * (1 + len(placed)),
+        functools.partial(place_kernel, partners),
+        in_specs=[SMEM] + [ANY] * (n + len(served)),
         out_specs=ANY,
-        out_shape=jax.ShapeDtypeStruct((per_dest, dp_count, rows, TILE), BF16),
-        scratch_shapes=[pltpu.SemaphoreType.DMA((per_dest,))],
-        input_output_aliases={2: 0} if placed else {},
+        out_shape=jax.ShapeDtypeStruct(shape, BF16),
+        scratch_shapes=[pltpu.SemaphoreType.DMA((n, shape[0]))],
+        input_output_aliases={1 + n: 0} if served else {},
         compiler_params=LIGHT,
-        cost_estimate=pl.CostEstimate(flops=0, bytes_accessed=4 * q.size, transcendentals=0),
+        cost_estimate=pl.CostEstimate(
+            flops=0, bytes_accessed=4 * n * payloads[0].size, transcendentals=0
+        ),
         name="place_served",
-    )(src, q, *placed)
-
-
-def scales_kernel(order, tiles, lat_tiles, n_late, pos_ref, *refs):
+    )(pos, *payloads, *served)
+
+
+def finish_kernel(order, tiles, lat_tiles, n_late, to_place, deltas, rows, pos_ref, line_ref, *refs):
     n = len(order)
     late, q_refs = refs[:n_late], refs[n_late : n_late + n]
-    exp_ref, lat_ref, extra, rows_ref, sem = refs[n_late + n :]
-    at = q_refs[0].shape[0] - EXTRA
-    per_dest = at // (tiles * TILE)
+    n_rest = len(deltas)
+    rest = refs[n_late + n : n_late + n + n_rest]
+    outs = refs[n_late + n + n_rest + 2 :]
+    served, latent, exp_ref, lat_ref, extra, rows_ref, buf, place_sem, sem, in_sem, out_sem = outs
+    pos = pos_ref[0]
+    per_dest = served.shape[0]
+    blocks_copies = block_copies(
+        served, [q_refs[i] for i in to_place], [pos ^ order[i] for i in to_place], place_sem
+    )
     copies = [
-        pltpu.make_async_copy(q.at[pl.ds(at, EXTRA), :], extra.at[i], sem.at[i])
+        pltpu.make_async_copy(
+            q.at[pl.ds(q.shape[0] - EXTRA, EXTRA), :], extra.at[i], sem.at[i]
+        )
         for i, q in enumerate(q_refs)
     ]
+    rest_loads = [pltpu.make_async_copy(rest[i], buf.at[i], in_sem.at[i]) for i in range(n_rest)]
+    copy_all(rest_loads)
     copy_all(copies)
+    copy_all(blocks_copies)
+    rest_copies = []
+    for i, delta in enumerate(deltas):
+        rest_loads[i].wait()
+        group = rest_stores(buf, i, line_ref[0] ^ delta, rows, latent, out_sem)
+        copy_all(group)
+        rest_copies += group
     rows_ref[...] = jnp.zeros_like(rows_ref)
     flat = jnp.zeros((8, exp_ref.shape[1]), F32)
     wide = lax.broadcasted_iota(jnp.int32, flat.shape, 1)
     deep = lax.broadcasted_iota(jnp.int32, flat.shape, 0)
     for i, k in enumerate(order):
         copies[i].wait()
-        src = pos_ref[0] ^ k
+        src = pos ^ k
         x = extra[i].astype(F32)[0:8, :]
         side = late[i][...] if i < n_late else x
         lat = sum(pltpu.roll(side, TILE - SPARE - 16 * p, 1) for p in range(3))
@@ -374,29 +406,45 @@
     exp_ref[...] = jnp.max(flat, axis=0, keepdims=True)
     blocks, height = lat_ref.shape
     lat_ref[...] = jnp.transpose(rows_ref[...])[0:blocks, 0:height]
-
-
-def all_scales(pos, late, received, order, tiles, lat_tiles, lat_blocks):
+    wait_all(blocks_copies)
+    wait_all(rest_copies)
+
+
+def finish(
+    served, latent, pos, line, late, received, rest, order, to_place, deltas, tiles, lat_tiles, lat_blocks
+):
     n = len(order)
-    per_dest = (received[0].shape[0] - EXTRA) // (tiles * TILE)
-    expert, latent = pl.pallas_call(
-        functools.partial(scales_kernel, order, tiles, lat_tiles, len(late)),
-        in_specs=[SMEM] + [VMEM] * len(late) + [ANY] * n,
-        out_specs=[VMEM, VMEM],
+    per_dest = served.shape[0]
+    span, cols = rest[0].shape
+    rows = TILE + span
+    ins = 2 + len(late) + n + len(rest)
+    served, latent, expert, scales = pl.pallas_call(
+        functools.partial(
+            finish_kernel, order, tiles, lat_tiles, len(late), to_place, deltas, rows
+        ),
+        in_specs=[SMEM] * 2 + [VMEM] * len(late) + [ANY] * (n + len(rest) + 2),
+        out_specs=[ANY, ANY, VMEM, VMEM],
         out_shape=[
+            jax.ShapeDtypeStruct(served.shape, served.dtype),
+            jax.ShapeDtypeStruct(latent.shape, latent.dtype),
             jax.ShapeDtypeStruct((1, per_dest * n * tiles), F32),
             jax.ShapeDtypeStruct((lat_blocks, n * lat_tiles), F32),
         ],
         scratch_shapes=[
             pltpu.VMEM((n, EXTRA, TILE), BF16),
             pltpu.VMEM((TILE, TILE), F32),
+            pltpu.VMEM((len(rest), span, cols), BF16),
+            pltpu.SemaphoreType.DMA((len(to_place), per_dest)),
             pltpu.SemaphoreType.DMA((n,)),
-        ],
-        compiler_params=LIGHT,
-        cost_estimate=pl.CostEstimate(flops=1000000, bytes_accessed=100000, transcendentals=0),
-        name="all_scales",
-    )(pos, *late, *received)
-    return expert, latent.T
+            pltpu.SemaphoreType.DMA((len(rest),)),
+            pltpu.SemaphoreType.DMA((len(rest), span // CHUNK)),
+        ],
+        input_output_aliases={ins: 0, ins + 1: 1},
+        compiler_params=pltpu.CompilerParams(vmem_limit_bytes=4 * 1024 * 1024),
+        cost_estimate=pl.CostEstimate(flops=1000000, bytes_accessed=1000000, transcendentals=0),
+        name="place_last",
+    )(pos, line, *late, *received, *rest, served, latent)
+    return served, latent, expert, scales.T
 
 
 def whole_tile(pos, rows):
@@ -441,54 +489,61 @@
     )(x, *out)
 
 
-def rest_kernel(deltas, rows, n_after, forward, pos_ref, *refs):
+def rest_stores(buf, i, peer, rows, out_ref, sem):
+    lead = whole_tile(peer, rows)
+    copies = []
+    for c in range((rows - TILE) // CHUNK):
+        at = peer * rows + c * CHUNK + jnp.where(c * CHUNK < lead, 0, TILE)
+        copies.append(
+            pltpu.make_async_copy(
+                buf.at[i, pl.ds(c * CHUNK, CHUNK), :],
+                out_ref.at[pl.ds(pl.multiple_of(at, CHUNK), CHUNK), :],
+                sem.at[i, c],
+            )
+        )
+    return copies
+
+
+def rest_kernel(deltas, rows, pos_ref, *refs):
     n = len(deltas)
-    x_refs, out_ref = refs[:n], refs[-4 - forward]
-    buf, in_sem, out_sem = refs[-3:]
-    span = rows - TILE
+    x_refs = refs[:n]
+    out_ref, again_ref, side_ref, buf, in_sem, out_sem = refs[-6:]
+    side_ref[...] = refs[n][...]
     loads = [pltpu.make_async_copy(x_refs[i], buf.at[i], in_sem.at[i]) for i in range(n)]
     copy_all(loads)
     stores = []
     for i in reversed(range(n)):
-        peer = pos_ref[0] ^ deltas[i]
-        lead = whole_tile(peer, rows)
         loads[i].wait()
-        if forward and i == n - 1:
-            stores.append(pltpu.make_async_copy(buf.at[i], refs[-4], out_sem.at[n, 0]))
+        if i == n - 1:
+            stores.append(pltpu.make_async_copy(buf.at[i], again_ref, out_sem.at[n, 0]))
             stores[-1].start()
-        for c in range(span // CHUNK):
-            at = peer * rows + c * CHUNK + jnp.where(c * CHUNK < lead, 0, TILE)
-            stores.append(
-                pltpu.make_async_copy(
-                    buf.at[i, pl.ds(c * CHUNK, CHUNK), :],
-                    out_ref.at[pl.ds(pl.multiple_of(at, CHUNK), CHUNK), :],
-                    out_sem.at[i, c],
-                )
-            )
-            stores[-1].start()
+        group = rest_stores(buf, i, pos_ref[0] ^ deltas[i], rows, out_ref, out_sem)
+        copy_all(group)
+        stores += group
     wait_all(stores)
 
 
-def place_rest(out, pos, xs, deltas, rows, peers, after=(), forward=False):
+def place_rest(pos, xs, deltas, side, after, rows, peers):
     span, cols = xs[0].shape
     n = len(xs)
-    shapes = [jax.ShapeDtypeStruct((peers * rows, cols), BF16)]
-    shapes += [jax.ShapeDtypeStruct((span, cols), BF16)] * forward
     return pl.pallas_call(
-        functools.partial(rest_kernel, deltas, rows, len(after), int(forward)),
-        in_specs=[SMEM] + [ANY] * (n + len(out) + len(after)),
-        out_specs=[ANY] * len(shapes),
-        out_shape=shapes,
+        functools.partial(rest_kernel, deltas, rows),
+        in_specs=[SMEM] + [ANY] * n + [VMEM, ANY],
+        out_specs=[ANY, ANY, VMEM],
+        out_shape=[
+            jax.ShapeDtypeStruct((peers * rows, cols), BF16),
+            jax.ShapeDtypeStruct((span, cols), BF16),
+            jax.ShapeDtypeStruct(side.shape, side.dtype),
+        ],
         scratch_shapes=[
             pltpu.VMEM((n, span, cols), BF16),
             pltpu.SemaphoreType.DMA((n,)),
             pltpu.SemaphoreType.DMA((n + 1, span // CHUNK)),
         ],
-        input_output_aliases={1 + n: 0} if out else {},
         compiler_params=pltpu.CompilerParams(vmem_limit_bytes=4 * 1024 * 1024),
         cost_estimate=pl.CostEstimate(flops=0, bytes_accessed=4 * n * span * cols, transcendentals=0),
         name="place_rest",
-    )(pos, *xs, *out, *after)
+    )(pos, *xs, side, after)
 
 
 SLABS = 4
@@ -575,7 +630,7 @@
 
 
 def latent_rest_kernel(chunks, peers, pos_ref, w1_ref, *refs):
-    q_ref, side_ref, w, q, ext, tops_ref, in_sem, out_sem = refs[-8:]
+    q_ref, again_ref, side_ref, w, q, ext, tops_ref, in_sem, out_sem = refs[-9:]
     per_tile = TILE // CHUNK
     rows, cols = w1_ref.shape
     width = cols // SLABS
@@ -596,7 +651,12 @@
             )
         copy_all(group)
         loads.append(group)
-        stores.append(pltpu.make_async_copy(q.at[:, at], q_ref.at[:, at], out_sem.at[i]))
+        stores.append(
+            [
+                pltpu.make_async_copy(q.at[:, at], out.at[:, at], out_sem.at[i, n])
+                for n, out in enumerate((q_ref, again_ref))
+            ]
+        )
     for s in range(peers):
         peer = lax.rem(pos + peers - s, peers)
         ext[pl.ds(peer * chunks, chunks), :] = refs[s][0:chunks, :]
@@ -627,8 +687,9 @@
                 span = pl.ds(c * CHUNK, CHUNK)
                 inv = jnp.where(c * CHUNK < lead, invs[b][0:1, :], invs[b][4:5, :])
                 q[span, at] = (w[span, at] * inv).astype(BF16)
-        stores[i].start()
-    wait_all(stores)
+        copy_all(stores[i])
+    for group in stores:
+        wait_all(group)
 
 
 def latent_rest(w1, maxima, pos, after):
@@ -638,8 +699,9 @@
     return pl.pallas_call(
         functools.partial(latent_rest_kernel, chunks, peers),
         in_specs=[SMEM, ANY] + [VMEM] * peers + [ANY],
-        out_specs=[ANY, VMEM],
+        out_specs=[ANY, ANY, VMEM],
         out_shape=[
+            jax.ShapeDtypeStruct((rows - TILE, cols), BF16),
             jax.ShapeDtypeStruct((rows - TILE, cols), BF16),
             jax.ShapeDtypeStruct((8, TILE), F32),
         ],
@@ -649,7 +711,7 @@
             pltpu.VMEM((8 * peers, TILE), F32),
             pltpu.VMEM((8, TILE), F32),
             pltpu.SemaphoreType.DMA((SLABS, chunks)),
-            pltpu.SemaphoreType.DMA((SLABS,)),
+            pltpu.SemaphoreType.DMA((SLABS, 2)),
         ],
         compiler_params=PARAMS,
         cost_estimate=pl.CostEstimate(
@@ -668,8 +730,7 @@
         and rows <= 8 * TILE
         and cols % (TILE * dp_count) == 0
         and cols // TILE // dp_count <= 16
-        and dp_count >= 4
-        and dp_count & (dp_count - 1) == 0
+        and dp_count == 8
         and dp_count * latent_rows * exp_axis <= TILE * TILE
         and latent_rows % CHUNK == 0
         and 2 * TILE - CHUNK <= latent_rows < 2 * TILE
@@ -685,7 +746,7 @@
     hops = lambda k: bin(k >> 1).count("1")
     stage = lambda k: 3 if k < 2 else (1 if hops(k) > 1 else (2 if k & 1 else 0))
     order = sorted(range(dp_count), key=lambda k: (stage(k), -k))
-    return [g for g in ([k for k in order if stage(k) == n] for n in range(4)) if g]
+    return [[k for k in order if stage(k) in n] for n in ((0,), (1,), (2, 3))]
 
 
 def fast_body(
@@ -709,7 +770,7 @@
     per_dest = block_count // dp_count
     tiles = rows // TILE
 
-    expert_at = exp_pos.reshape(1)
+    expert_at, dp_at = exp_pos.reshape(1), dp_pos.reshape(1)
     latent_new, latent_one, latent_two, whole, chunk_top = latent_update(
         (latent_master, latent_first, latent_second, latent_grad), step_count, expert_at
     )
@@ -726,44 +787,48 @@
     def swap(x, axis, k):
         return lax.ppermute(x, axis, [(i, i ^ k) for i in range(lax.axis_size(axis))])
 
-    state, arrived, after = (), [], ()
+    groups = partner_groups(dp_count)
+    order = [k for partners in groups for k in partners]
+    state, received, carry = (), [], ()
     side = jnp.zeros((8, TILE), F32)
-    groups = partner_groups(dp_count)
     for n, partners in enumerate(groups):
-        state, sent = expert_group(
-            arrays, state, column_owner, dp_pos.reshape(1), step_count, side, after, partners, per_dest
+        state, sent, carried = expert_group(
+            arrays, state, column_owner, dp_at, step_count, side, carry, (), partners, per_dest
         )
-        arrived += [(k, swap(q, "dp", k) if k else q) for k, q in zip(partners, sent)]
-        if n == 0:
-            rest, side = latent_rest(latent_new, maxima, expert_at, sent[0])
-            far, near = swap(rest, "expert", 2), swap(rest, "expert", 1)
-            late = [swap(side, "dp", k) for k in partners]
-            after = ()
-        elif n == 1:
-            after = tuple(q[-EXTRA:] for _, q in arrived[: len(groups[0])])
-        else:
-            after = ()
-    latent_served, far_again = place_rest(
-        (), expert_at, [rest, far], [0, 2], latent_rows, exp_axis, (sent[-1][-EXTRA:],), True
+        received += [swap(q, "dp", k) if k else q for k, q in zip(partners, sent)]
+        if n == 1:
+            rest, again, side = latent_rest(latent_new, maxima, expert_at, sent[0])
+            far = swap(rest, "expert", 2)
+            served = place_blocks(
+                (), dp_at, received[: len(groups[0])], groups[0], (per_dest, dp_count, rows, TILE)
+            )
+            carry = (served, again)
+    served, again, side = carried
+    near = swap(again, "expert", 1)
+    first, count = len(groups[0]), len(groups[0]) + len(groups[1])
+    served = place_blocks((served,), dp_at, received[first:count], groups[1], served.shape)
+    latent_served, far_again, side = place_rest(
+        expert_at, [rest, far], [0, 2], side, sent[-1], latent_rows, exp_axis
     )
     last = swap(far_again, "expert", 1)
-    (latent_served,) = place_rest((latent_served,), expert_at, [near], [1], latent_rows, exp_axis)
+    late = [swap(side, "dp", k) for k in groups[0] + groups[1]]
     latent_served = place_full((latent_served,), whole, latent_rows)
-    (latent_served,) = place_rest((latent_served,), expert_at, [last], [3], latent_rows, exp_axis)
-
-    placed = ()
-    for k, q in arrived[-1:] + arrived[:-1]:
-        placed = (place_rows(placed, (dp_pos ^ k).reshape(1), q, dp_count, per_dest),)
-    expert_served = placed[0].reshape(1, block_count * rows, TILE)
-    expert_scales, latent_scales = all_scales(
-        dp_pos.reshape(1),
+    served, latent_served, expert_scales, latent_scales = finish(
+        served,
+        latent_served,
+        dp_at,
+        expert_at,
         late,
-        [q for _, q in arrived],
-        [k for k, _ in arrived],
+        received,
+        [near, last],
+        order,
+        range(count, dp_count - 1),
+        [1, 3],
         tiles,
         latent_rows * exp_axis // TILE,
         latent_new.shape[1] // TILE,
     )
+    expert_served = served.reshape(1, block_count * rows, TILE)
 
     return (
         state[0][None],

time: 96 us -> 101 us (1.052)
  waiting for transfers between devices: 15.2 us -> 25.4 us
  Pallas kernels: 42 us -> 35.4 us
  starting transfers between devices: 18.9 us -> 22.2 us
  local copies, waits for them, and re-layouts: 4.46 us -> 2.57 us
    ppermute x12 -> x14, waiting for transfers between devices: 12.8 us -> 22.8 us  [swap(): lax.ppermute(x, axis, [(i, i ^ k) for i in range(lax.axis_size(axis))])]
    pallas_call x12 -> x4, Pallas kernels: 11.8 us -> 5.97 us  [the longest x1 2.96 us: finish(): pl.pallas_call(functools.partial(finish_kernel, order, tiles, lat_tiles,...]
    ppermute x12 -> x14, starting transfers between devices: 13.3 us -> 15.7 us  [swap(): lax.ppermute(x, axis, [(i, i ^ k) for i in range(lax.axis_size(axis))])]
    slice x3 -> x0, local copies, waits for them, and re-layouts: 1.87 us -> none  [the longest x2 1.19 us: fast_body(): after = tuple((q[-EXTRA:] for _, q in arrived[:len(groups[0])]))]
    pallas_call x4 -> x3, Pallas kernels: 20.3 us -> 19.4 us  [expert_group(): pl.pallas_call(functools.partial(expert_kernel, partners, per_dest, n_ali...]
  transfers between devices with their start and end apart: 16 -> 18, of which waited for: 4 -> 9; matrix products, arithmetic and copies ran while one was open for 3% -> 1% of each run, Pallas kernels for 38% -> 28%
where the time goes in v6:
time: 101 us; the launch traced here: 100 us
  Pallas kernels  35.4 us (35%)
  waiting for transfers between devices  25.4 us (25%)
  starting transfers between devices  22.2 us (22%)
  between operations  14.9 us (15%)
  local copies, waits for them, and re-layouts  2.57 us (3%)
    ppermute x14, waiting for transfers between devices, swap(): lax.ppermute(x, axis, [(i, i ^ k) for i in range(lax.axis_size(axis))])  22.8 us
    pallas_call x3, Pallas kernels, expert_group(): pl.pallas_call(functools.partial(expert_kernel, partners, per_dest, n_ali...  19.4 us
    ppermute x14, starting transfers between devices, swap(): lax.ppermute(x, axis, [(i, i ^ k) for i in range(lax.axis_size(axis))])  15.7 us
    ppermute x3, starting transfers between devices, fast_body(): lax.ppermute(chunk_top, 'expert', [(i, (i + s) % exp_axis) for i in range...  6.47 us
    pallas_call x1, Pallas kernels, latent_update(): pl.pallas_call(functools.partial(latent_kernel, rows // CHUNK), in_specs=...  4.33 us
    pallas_call x1, Pallas kernels, latent_rest(): pl.pallas_call(functools.partial(latent_rest_kernel, chunks, peers), in_s...  3.43 us
    pallas_call x1, Pallas kernels, finish(): pl.pallas_call(functools.partial(finish_kernel, order, tiles, lat_tiles,...  2.96 us
    ppermute x3, waiting for transfers between devices, fast_body(): lax.ppermute(chunk_top, 'expert', [(i, (i + s) % exp_axis) for i in range...  2.55 us
  transfers between devices with their start and end apart: 18, of which 9 were waited for; matrix products, arithmetic and copies ran while one was open for 1% of the time, Pallas kernels for 28%

profile of v6, /device:TPU:0, one launch (start us, length us, event | category | flops | bytes accessed | tf_op | source)
XLA Modules:
  0.0 100.4 jit_solution(5167148103164906937)
XLA Ops:
  7.2 0.0 all-gather.2.cloned.1.call-start
  7.9 4.3 %latent_adamw.1 = (f32[224,1536]{1,0:T(8,128)}, bf16[224,1536]{1,0:T(8,128)(2,1)}, bf16[224,1536]{1,0:T(8,128)(2,1)}, bf16[128,1536]{1,0:T(8,128)(2,1)}, f32[8,128]{1,0:T(8,128)}) custom-call(s32[1]{0:T(128)S(6)} %copy.44.step_ref, s32[1]{0:T(128)} %bitcast.1.pos_ref.line_ref, f32[224,1536]{1,0:T(8,128)} %refs_0_.1, bf16[224,1536]{1,0:T(8,128)(2,1)} %refs_1_.1, ...), custom_call_target="tpu_custom_call" | custom-call | flops 10321920 | bytes 6193152 | tf_op jit(solution)/shard_map/latent_adamw/pallas_call | solution.py:604
  12.2 0.0 all-gather.2.cloned.1.call-update
  12.2 0.6 broadcast_in_dim.12.side_ref
  12.8 5.1 %expert_adamw.3 = (f32[896,2048]{1,0:T(8,128)}, bf16[896,2048]{1,0:T(8,128)(2,1)}, bf16[896,2048]{1,0:T(8,128)(2,1)}, bf16[1808,128]{1,0:T(8,128)(2,1)}, bf16[1808,128]{1,0:T(8,128)(2,1)}) custom-call(s32[16]{0:T(128)} %owner_ref.5, s32[1]{0:T(128)} %bitcast.pos_ref, s32[1]{0:T(128)S(6)} %copy.44.step_ref, f32[8,128]{1,0:T(8,128)} %broadcast_in_dim.12.side_ref, ...), custom_call_target="tpu_custom_call" | custom-call | flops 458752 | bytes 458752 | tf_op jit(solution)/shard_map/expert_adamw/pallas_call | solution.py:293
  17.9 3.0 %collective-permute-start.3 = (bf16[1808,128]{1,0:T(8,128)(2,1)}, bf16[1808,128]{1,0:T(8,128)(2,1)S(1)}, u32[]{:S(2)}, u32[]{:S(2)}) collective-permute-start(bf16[1808,128]{1,0:T(8,128)(2,1)} %get-tuple-element.55), channel_id=1, source_target_pairs={{0,16},{4,20},{8,24},{12,28},{16,0},{20,4},{24,8},{28,12},{1,17},{... | collective-permute-start | bytes 1388552 | tf_op jit(solution)/shard_map/ppermute | solution.py:788
  21.0 1.5 %collective-permute-start.4 = (bf16[1808,128]{1,0:T(8,128)(2,1)}, bf16[1808,128]{1,0:T(8,128)(2,1)S(1)}, u32[]{:S(2)}, u32[]{:S(2)}) collective-permute-start(bf16[1808,128]{1,0:T(8,128)(2,1)} %get-tuple-element.56), channel_id=1, source_target_pairs={{0,8},{4,12},{8,0},{12,4},{16,24},{20,28},{24,16},{28,20},{1,9},{5... | collective-permute-start | bytes 1388552 | tf_op jit(solution)/shard_map/ppermute | solution.py:788
  22.5 1.6 %collective-permute-start = (f32[8,128]{1,0:T(8,128)S(1)}, f32[8,128]{1,0:T(8,128)S(1)}, u32[]{:S(2)}, u32[]{:S(2)}) collective-permute-start(f32[8,128]{1,0:T(8,128)S(1)} %copy-done.4), channel_id=1, source_target_pairs={{0,1},{1,2},{2,3},{3,0},{4,5},{5,6},{6,7},{7,4},{8,9},{9,10},{10,1... | collective-permute-start | bytes 12296 | tf_op jit(solution)/shard_map/ppermute | solution.py:780
  24.0 5.0 %expert_adamw.4 = (f32[896,2048]{1,0:T(8,128)}, bf16[896,2048]{1,0:T(8,128)(2,1)}, bf16[896,2048]{1,0:T(8,128)(2,1)}, bf16[1808,128]{1,0:T(8,128)(2,1)}, bf16[1808,128]{1,0:T(8,128)(2,1)}) custom-call(s32[16]{0:T(128)} %owner_ref.5, s32[1]{0:T(128)} %bitcast.pos_ref, ...), custom_call_target="tpu_custom_call", output_to_operand_aliasing={{0}: (8, {}), {1}: (9, {}), {2}: (10, {})} | custom-call | flops 458752 | bytes 458752 | tf_op jit(solution)/shard_map/expert_adamw/pallas_call | solution.py:293
  29.0 0.1 collective-permute-start.10
  29.1 2.7 %collective-permute-start.1 = (f32[8,128]{1,0:T(8,128)S(1)}, f32[8,128]{1,0:T(8,128)S(1)}, u32[]{:S(2)}, u32[]{:S(2)}) collective-permute-start(f32[8,128]{1,0:T(8,128)S(1)} %copy-done.4), channel_id=1, source_target_pairs={{0,2},{1,3},{2,0},{3,1},{4,6},{5,7},{6,4},{7,5},{8,10},{9,11},{10,... | collective-permute-start | bytes 12296 | tf_op jit(solution)/shard_map/ppermute | solution.py:780
  31.8 0.0 collective-permute-done.refs_1_
  31.8 1.4 %collective-permute-start.11 = (bf16[1808,128]{1,0:T(8,128)(2,1)}, bf16[1808,128]{1,0:T(8,128)(2,1)S(1)}, u32[]{:S(2)}, u32[]{:S(2)}) collective-permute-start(bf16[1808,128]{1,0:T(8,128)(2,1)} %get-tuple-element.65), channel_id=1, source_target_pairs={{0,24},{4,28},{8,16},{12,20},{16,8},{20,12},{24,0},{28,4},{1,25},{... | collective-permute-start | bytes 1388552 | tf_op jit(solution)/shard_map/ppermute | solution.py:788
  33.2 0.6 collective-permute-done.1.refs_2_
  33.8 2.2 %collective-permute-start.2 = (f32[8,128]{1,0:T(8,128)S(1)}, f32[8,128]{1,0:T(8,128)S(1)}, u32[]{:S(2)}, u32[]{:S(2)}) collective-permute-start(f32[8,128]{1,0:T(8,128)S(1)} %copy-done.4), channel_id=1, source_target_pairs={{0,3},{1,0},{2,1},{3,2},{4,7},{5,4},{6,5},{7,6},{8,11},{9,8},{10,9... | collective-permute-start | bytes 12296 | tf_op jit(solution)/shard_map/ppermute | solution.py:780
  36.1 1.9 %collective-permute-done.2.refs_3_ = f32[8,128]{1,0:T(8,128)S(1)} collective-permute-done((f32[8,128]{1,0:T(8,128)S(1)}, f32[8,128]{1,0:T(8,128)S(1)}, u32[]{:S(2)}, u32[]{:S(2)}) %collective-permute-start.2) | collective-permute-done | bytes 4128 | tf_op jit(solution)/shard_map/ppermute | solution.py:780
  38.0 0.6 copy-done.7
  38.6 3.4 %latent_rest.1 = (bf16[96,1536]{1,0:T(8,128)(2,1)}, bf16[96,1536]{1,0:T(8,128)(2,1)}, f32[8,128]{1,0:T(8,128)}) custom-call(s32[1]{0:T(128)} %bitcast.1.pos_ref.line_ref, f32[224,1536]{1,0:T(8,128)} %get-tuple-element.40.w1_ref, f32[8,128]{1,0:T(8,128)} %get-tuple-element.46.refs_0_, f32[8,128]{1,0:T(8,128)} %copy-done.5, f32[8,128]{1,0:T(8,128)} %copy-done.6, ...), custom_call_target="tpu_custom_call" | custom-call | flops 344064 | bytes 1032192 | tf_op jit(solution)/shard_map/latent_rest/pallas_call | solution.py:699
  42.0 2.1 %collective-permute-start.5 = (bf16[96,1536]{1,0:T(8,128)(2,1)}, bf16[96,1536]{1,0:T(8,128)(2,1)S(1)}, u32[]{:S(2)}, u32[]{:S(2)}) collective-permute-start(bf16[96,1536]{1,0:T(8,128)(2,1)} %get-tuple-element.61.refs_0_), channel_id=1, source_target_pairs={{0,2},{1,3},{2,0},{3,1},{4,6},{5,7},{6,4},{7,5},{8,10},{9,11},{10,... | collective-permute-start | bytes 884744 | tf_op jit(solution)/shard_map/ppermute | solution.py:788
  44.2 0.0 collective-permute-done.3.refs_0_.refs_4_
  44.2 0.0 collective-permute-done.4.refs_1_.refs_5_
  44.2 0.9 place_served.2.refs_7_
  45.2 9.4 %expert_adamw.5 = (f32[896,2048]{1,0:T(8,128)}, bf16[896,2048]{1,0:T(8,128)(2,1)}, bf16[896,2048]{1,0:T(8,128)(2,1)}, bf16[1808,128]{1,0:T(8,128)(2,1)}, bf16[18...) custom-call(s32[16]{0:T(128)} %owner_ref.5, ...), custom_call_target="tpu_custom_call", output_to_operand_aliasing={{0}: (8, {}), {1}: (9, {}), {2}: (10, {}), {7}: (11, {}), {... | custom-call | flops 917504 | bytes 917504 | tf_op jit(solution)/shard_map/expert_adamw/pallas_call | solution.py:293
  54.5 0.1 collective-permute-start.12
  54.6 1.7 %collective-permute-start.13 = (bf16[1808,128]{1,0:T(8,128)(2,1)}, bf16[1808,128]{1,0:T(8,128)(2,1)S(1)}, u32[]{:S(2)}, u32[]{:S(2)}) collective-permute-start(bf16[1808,128]{1,0:T(8,128)(2,1)} %get-tuple-element.67), channel_id=1, source_target_pairs={{0,12},{4,8},{8,4},{12,0},{16,28},{20,24},{24,20},{28,16},{1,13},{... | collective-permute-start | bytes 1388552 | tf_op jit(solution)/shard_map/ppermute | solution.py:788
  56.3 8.5 %collective-permute-done.5.refs_1_ = bf16[96,1536]{1,0:T(8,128)(2,1)S(1)} collective-permute-done((bf16[96,1536]{1,0:T(8,128)(2,1)}, bf16[96,1536]{1,0:T(8,128)(2,1)S(1)}, u32[]{:S(2)}, u32[]{:S(2)}) %collective-permute-start.5) | collective-permute-done | bytes 294944 | tf_op jit(solution)/shard_map/ppermute | solution.py:788
  64.8 0.7 copy-done.1
  65.5 0.7 copy-done.3
  66.1 1.1 %place_rest.1 = (bf16[896,1536]{1,0:T(8,128)(2,1)}, bf16[96,1536]{1,0:T(8,128)(2,1)}, f32[8,128]{1,0:T(8,128)S(1)}) custom-call(s32[1]{0:T(128)} %bitcast.1.pos_ref.line_ref, bf16[96,1536]{1,0:T(8,128)(2,1)S(1)} %copy-done, bf16[96,1536]{1,0:T(8,128)(2,1)S(1)} %collective-permute-done.5.refs_1_, f32[8,128]{1,0:T(8,128)S(1)} %copy-done.3, ...), custom_call_target="tpu_custom_call" | custom-call | bytes 1179648 | tf_op jit(solution)/shard_map/place_rest/pallas_call | solution.py:529
  67.3 1.6 %collective-permute-start.6 = (f32[8,128]{1,0:T(8,128)S(1)}, f32[8,128]{1,0:T(8,128)S(1)}, u32[]{:S(2)}, u32[]{:S(2)}) collective-permute-start(f32[8,128]{1,0:T(8,128)S(1)} %get-tuple-element.64), channel_id=1, source_target_pairs={{0,16},{4,20},{8,24},{12,28},{16,0},{20,4},{24,8},{28,12},{1,17},{... | collective-permute-start | bytes 12296 | tf_op jit(solution)/shard_map/ppermute | solution.py:788
  68.8 1.4 %collective-permute-start.7 = (f32[8,128]{1,0:T(8,128)S(1)}, f32[8,128]{1,0:T(8,128)S(1)}, u32[]{:S(2)}, u32[]{:S(2)}) collective-permute-start(f32[8,128]{1,0:T(8,128)S(1)} %get-tuple-element.64), channel_id=1, source_target_pairs={{0,8},{4,12},{8,0},{12,4},{16,24},{20,28},{24,16},{28,20},{1,9},{5... | collective-permute-start | bytes 12296 | tf_op jit(solution)/shard_map/ppermute | solution.py:788
  70.3 0.7 collective-permute-done.6.refs_0_
  70.9 1.3 %collective-permute-start.8 = (f32[8,128]{1,0:T(8,128)S(1)}, f32[8,128]{1,0:T(8,128)S(1)}, u32[]{:S(2)}, u32[]{:S(2)}) collective-permute-start(f32[8,128]{1,0:T(8,128)S(1)} %get-tuple-element.64), channel_id=1, source_target_pairs={{0,28},{4,24},{8,20},{12,16},{16,12},{20,8},{24,4},{28,0},{1,29},{... | collective-permute-start | bytes 12296 | tf_op jit(solution)/shard_map/ppermute | solution.py:788
  72.2 0.2 collective-permute-done.7.refs_1_
  72.4 1.5 %collective-permute-start.9 = (f32[8,128]{1,0:T(8,128)S(1)}, f32[8,128]{1,0:T(8,128)S(1)}, u32[]{:S(2)}, u32[]{:S(2)}) collective-permute-start(f32[8,128]{1,0:T(8,128)S(1)} %get-tuple-element.64), channel_id=1, source_target_pairs={{0,24},{4,28},{8,16},{12,20},{16,8},{20,12},{24,0},{28,4},{1,25},{... | collective-permute-start | bytes 12296 | tf_op jit(solution)/shard_map/ppermute | solution.py:788
  73.9 1.0 %collective-permute-done.8.refs_2_ = f32[8,128]{1,0:T(8,128)S(1)} collective-permute-done((f32[8,128]{1,0:T(8,128)S(1)}, f32[8,128]{1,0:T(8,128)S(1)}, u32[]{:S(2)}, u32[]{:S(2)}) %collective-permute-start.8) | collective-permute-done | bytes 4128 | tf_op jit(solution)/shard_map/ppermute | solution.py:788
  74.9 0.0 collective-permute-start.16
  74.9 2.1 %collective-permute-done.9.refs_3_ = f32[8,128]{1,0:T(8,128)S(1)} collective-permute-done((f32[8,128]{1,0:T(8,128)S(1)}, f32[8,128]{1,0:T(8,128)S(1)}, u32[]{:S(2)}, u32[]{:S(2)}) %collective-permute-start.9) | collective-permute-done | bytes 4128 | tf_op jit(solution)/shard_map/ppermute | solution.py:788
  77.0 0.9 place_served.3.refs_14_
  77.9 0.0 copy-start.2
  77.9 0.0 all-gather.2.cloned.1.call-done.x_ref
  78.0 2.2 %place_whole.1.refs_15_ = bf16[896,1536]{1,0:T(8,128)(2,1)} custom-call(bf16[512,1536]{1,0:T(8,128)(2,1)} %all-gather.2.cloned.1.call-done.x_ref, bf16[896,1536]{1,0:T(8,128)(2,1)} %get-tuple-element.73.refs_0_), custom_call_target="tpu_custom_call", output_to_operand_aliasing={{}: (1, {})} | custom-call | bytes 3145728 | tf_op jit(solution)/shard_map/place_whole/pallas_call | solution.py:475
  80.2 4.8 %collective-permute-done.16.refs_13_ = bf16[96,1536]{1,0:T(8,128)(2,1)S(1)} collective-permute-done((bf16[96,1536]{1,0:T(8,128)(2,1)}, bf16[96,1536]{1,0:T(8,128)(2,1)S(1)}, u32[]{:S(2)}, u32[]{:S(2)}) %collective-permute-start.16) | collective-permute-done | bytes 294944 | tf_op jit(solution)/shard_map/ppermute | solution.py:788
  85.0 5.6 %collective-permute-done.15.refs_12_ = bf16[96,1536]{1,0:T(8,128)(2,1)} collective-permute-done((bf16[96,1536]{1,0:T(8,128)(2,1)}, bf16[96,1536]{1,0:T(8,128)(2,1)}, u32[]{:S(2)}, u32[]{:S(2)}) %collective-permute-start.15) | collective-permute-done | bytes 294944 | tf_op jit(solution)/shard_map/ppermute | solution.py:788
  90.6 0.0 collective-permute-done.12.refs_8_
  90.6 0.0 collective-permute-done.13.refs_9_
  90.6 0.0 collective-permute-done.14.refs_10_
  90.6 3.0 %place_last.1 = (bf16[2,8,896,128]{3,2,1,0:T(8,128)(2,1)}, bf16[896,1536]{1,0:T(8,128)(2,1)}, f32[1,112]{1,0:T(1,128)}, f32[12,56]{1,0:T(8,128)}) custom-call(s32[1]{0:T(128)} %bitcast.pos_ref, s32[1]{0:T(128)} %bitcast.1.pos_ref.line_ref, f32[8,128]{1,0:T(8,128)S(1)} %collective-permute-done.6.refs_0_, ...), custom_call_target="tpu_custom_call", output_to_operand_aliasing={{0}: (16, {}), {1}: (17, {})} | custom-call | flops 1000000 | bytes 1000000 | tf_op jit(solution)/shard_map/place_last/pallas_call | solution.py:421
  (16 shorter events, 0.0 us)
Async XLA Ops:
  7.2 70.8 %all-gather.2.cloned.1.call-start = ((), (), s32[]{:S(2)}) async-start(), calls=%async_computation | async-start | bytes 1966080 | tf_op jit(solution)/shard_map/all_gather | solution.py:778
  12.8 9.6 %copy-start.4 = (f32[8,128]{1,0:T(8,128)S(1)}, f32[8,128]{1,0:T(8,128)}, u32[]{:S(2)}) copy-start(f32[8,128]{1,0:T(8,128)} %get-tuple-element.46.refs_0_) | copy-start | bytes 12292
  17.9 26.2 %collective-permute-start.3 = (bf16[1808,128]{1,0:T(8,128)(2,1)}, bf16[1808,128]{1,0:T(8,128)(2,1)S(1)}, u32[]{:S(2)}, u32[]{:S(2)}) collective-permute-start(bf16[1808,128]{1,0:T(8,128)(2,1)} %get-tuple-element.55), channel_id=1, source_target_pairs={{0,16},{4,20},{8,24},{12,28},{16,0},{20,4},{24,8},{28,12},{1,17},{... | collective-permute-start | bytes 1388552 | tf_op jit(solution)/shard_map/ppermute | solution.py:788
  21.0 23.2 %collective-permute-start.4 = (bf16[1808,128]{1,0:T(8,128)(2,1)}, bf16[1808,128]{1,0:T(8,128)(2,1)S(1)}, u32[]{:S(2)}, u32[]{:S(2)}) collective-permute-start(bf16[1808,128]{1,0:T(8,128)(2,1)} %get-tuple-element.56), channel_id=1, source_target_pairs={{0,8},{4,12},{8,0},{12,4},{16,24},{20,28},{24,16},{28,20},{1,9},{5... | collective-permute-start | bytes 1388552 | tf_op jit(solution)/shard_map/ppermute | solution.py:788
  22.5 9.3 %collective-permute-start = (f32[8,128]{1,0:T(8,128)S(1)}, f32[8,128]{1,0:T(8,128)S(1)}, u32[]{:S(2)}, u32[]{:S(2)}) collective-permute-start(f32[8,128]{1,0:T(8,128)S(1)} %copy-done.4), channel_id=1, source_target_pairs={{0,1},{1,2},{2,3},{3,0},{4,5},{5,6},{6,7},{7,4},{8,9},{9,10},{10,1... | collective-permute-start | bytes 12296 | tf_op jit(solution)/shard_map/ppermute | solution.py:780
  29.0 38.2 %collective-permute-start.10 = (bf16[1808,128]{1,0:T(8,128)(2,1)}, bf16[1808,128]{1,0:T(8,128)(2,1)S(1)}, u32[]{:S(2)}, u32[]{:S(2)}) collective-permute-start(bf16[1808,128]{1,0:T(8,128)(2,1)} %get-tuple-element.50.refs_4_), channel_id=1, source_target_pairs={{0,28},{4,24},{8,20},{12,16},{16,12},{20,8},{24,4},{28,0},{1,29},{... | collective-permute-start | bytes 1388552 | tf_op jit(solution)/shard_map/ppermute | solution.py:788
  29.1 4.7 %collective-permute-start.1 = (f32[8,128]{1,0:T(8,128)S(1)}, f32[8,128]{1,0:T(8,128)S(1)}, u32[]{:S(2)}, u32[]{:S(2)}) collective-permute-start(f32[8,128]{1,0:T(8,128)S(1)} %copy-done.4), channel_id=1, source_target_pairs={{0,2},{1,3},{2,0},{3,1},{4,6},{5,7},{6,4},{7,5},{8,10},{9,11},{10,... | collective-permute-start | bytes 12296 | tf_op jit(solution)/shard_map/ppermute | solution.py:780
  31.8 6.2 %copy-start.5 = (f32[8,128]{1,0:T(8,128)}, f32[8,128]{1,0:T(8,128)S(1)}, u32[]{:S(2)}) copy-start(f32[8,128]{1,0:T(8,128)S(1)} %collective-permute-done.refs_1_) | copy-start | bytes 12292
  31.8 37.1 %collective-permute-start.11 = (bf16[1808,128]{1,0:T(8,128)(2,1)}, bf16[1808,128]{1,0:T(8,128)(2,1)S(1)}, u32[]{:S(2)}, u32[]{:S(2)}) collective-permute-start(bf16[1808,128]{1,0:T(8,128)(2,1)} %get-tuple-element.65), channel_id=1, source_target_pairs={{0,24},{4,28},{8,16},{12,20},{16,8},{20,12},{24,0},{28,4},{1,25},{... | collective-permute-start | bytes 1388552 | tf_op jit(solution)/shard_map/ppermute | solution.py:788
  33.8 4.2 %copy-start.6 = (f32[8,128]{1,0:T(8,128)}, f32[8,128]{1,0:T(8,128)S(1)}, u32[]{:S(2)}) copy-start(f32[8,128]{1,0:T(8,128)S(1)} %collective-permute-done.1.refs_2_) | copy-start | bytes 12292
  33.8 4.2 %collective-permute-start.2 = (f32[8,128]{1,0:T(8,128)S(1)}, f32[8,128]{1,0:T(8,128)S(1)}, u32[]{:S(2)}, u32[]{:S(2)}) collective-permute-start(f32[8,128]{1,0:T(8,128)S(1)} %copy-done.4), channel_id=1, source_target_pairs={{0,3},{1,0},{2,1},{3,2},{4,7},{5,4},{6,5},{7,6},{8,11},{9,8},{10,9... | collective-permute-start | bytes 12296 | tf_op jit(solution)/shard_map/ppermute | solution.py:780
  38.0 0.6 copy-start.7
  42.0 22.7 %collective-permute-start.5 = (bf16[96,1536]{1,0:T(8,128)(2,1)}, bf16[96,1536]{1,0:T(8,128)(2,1)S(1)}, u32[]{:S(2)}, u32[]{:S(2)}) collective-permute-start(bf16[96,1536]{1,0:T(8,128)(2,1)} %get-tuple-element.61.refs_0_), channel_id=1, source_target_pairs={{0,2},{1,3},{2,0},{3,1},{4,6},{5,7},{6,4},{7,5},{8,10},{9,11},{10,... | collective-permute-start | bytes 884744 | tf_op jit(solution)/shard_map/ppermute | solution.py:788
  45.1 19.6 %copy-start = (bf16[96,1536]{1,0:T(8,128)(2,1)S(1)}, bf16[96,1536]{1,0:T(8,128)(2,1)}, u32[]{:S(2)}) copy-start(bf16[96,1536]{1,0:T(8,128)(2,1)} %get-tuple-element.61.refs_0_) | copy-start | bytes 884740
  54.5 36.0 %collective-permute-start.12 = (bf16[1808,128]{1,0:T(8,128)(2,1)}, bf16[1808,128]{1,0:T(8,128)(2,1)S(1)}, u32[]{:S(2)}, u32[]{:S(2)}) collective-permute-start(bf16[1808,128]{1,0:T(8,128)(2,1)} %get-tuple-element.66), channel_id=1, source_target_pairs={{0,20},{4,16},{8,28},{12,24},{16,4},{20,0},{24,12},{28,8},{1,21},{... | collective-permute-start | bytes 1388552 | tf_op jit(solution)/shard_map/ppermute | solution.py:788
  54.6 36.0 %collective-permute-start.13 = (bf16[1808,128]{1,0:T(8,128)(2,1)}, bf16[1808,128]{1,0:T(8,128)(2,1)S(1)}, u32[]{:S(2)}, u32[]{:S(2)}) collective-permute-start(bf16[1808,128]{1,0:T(8,128)(2,1)} %get-tuple-element.67), channel_id=1, source_target_pairs={{0,12},{4,8},{8,4},{12,0},{16,28},{20,24},{24,20},{28,16},{1,13},{... | collective-permute-start | bytes 1388552 | tf_op jit(solution)/shard_map/ppermute | solution.py:788
  64.8 25.8 %collective-permute-start.14 = (bf16[1808,128]{1,0:T(8,128)(2,1)}, bf16[1808,128]{1,0:T(8,128)(2,1)S(1)}, u32[]{:S(2)}, u32[]{:S(2)}) collective-permute-start(bf16[1808,128]{1,0:T(8,128)(2,1)} %get-tuple-element.68), channel_id=1, source_target_pairs={{0,4},{4,0},{8,12},{12,8},{16,20},{20,16},{24,28},{28,24},{1,5},{5... | collective-permute-start | bytes 1388552 | tf_op jit(solution)/shard_map/ppermute | solution.py:788
  64.8 0.7 copy-start.1
  65.5 0.7 copy-start.3
  67.3 3.7 %collective-permute-start.6 = (f32[8,128]{1,0:T(8,128)S(1)}, f32[8,128]{1,0:T(8,128)S(1)}, u32[]{:S(2)}, u32[]{:S(2)}) collective-permute-start(f32[8,128]{1,0:T(8,128)S(1)} %get-tuple-element.64), channel_id=1, source_target_pairs={{0,16},{4,20},{8,24},{12,28},{16,0},{20,4},{24,8},{28,12},{1,17},{... | collective-permute-start | bytes 12296 | tf_op jit(solution)/shard_map/ppermute | solution.py:788
  68.8 3.6 %collective-permute-start.7 = (f32[8,128]{1,0:T(8,128)S(1)}, f32[8,128]{1,0:T(8,128)S(1)}, u32[]{:S(2)}, u32[]{:S(2)}) collective-permute-start(f32[8,128]{1,0:T(8,128)S(1)} %get-tuple-element.64), channel_id=1, source_target_pairs={{0,8},{4,12},{8,0},{12,4},{16,24},{20,28},{24,16},{28,20},{1,9},{5... | collective-permute-start | bytes 12296 | tf_op jit(solution)/shard_map/ppermute | solution.py:788
  70.9 4.0 %collective-permute-start.8 = (f32[8,128]{1,0:T(8,128)S(1)}, f32[8,128]{1,0:T(8,128)S(1)}, u32[]{:S(2)}, u32[]{:S(2)}) collective-permute-start(f32[8,128]{1,0:T(8,128)S(1)} %get-tuple-element.64), channel_id=1, source_target_pairs={{0,28},{4,24},{8,20},{12,16},{16,12},{20,8},{24,4},{28,0},{1,29},{... | collective-permute-start | bytes 12296 | tf_op jit(solution)/shard_map/ppermute | solution.py:788
  72.4 4.5 %collective-permute-start.9 = (f32[8,128]{1,0:T(8,128)S(1)}, f32[8,128]{1,0:T(8,128)S(1)}, u32[]{:S(2)}, u32[]{:S(2)}) collective-permute-start(f32[8,128]{1,0:T(8,128)S(1)} %get-tuple-element.64), channel_id=1, source_target_pairs={{0,24},{4,28},{8,16},{12,20},{16,8},{20,12},{24,0},{28,4},{1,25},{... | collective-permute-start | bytes 12296 | tf_op jit(solution)/shard_map/ppermute | solution.py:788
  74.9 10.1 %collective-permute-start.16 = (bf16[96,1536]{1,0:T(8,128)(2,1)}, bf16[96,1536]{1,0:T(8,128)(2,1)S(1)}, u32[]{:S(2)}, u32[]{:S(2)}) collective-permute-start(bf16[96,1536]{1,0:T(8,128)(2,1)} %get-tuple-element.70), channel_id=1, source_target_pairs={{0,1},{1,0},{2,3},{3,2},{4,5},{5,4},{6,7},{7,6},{8,9},{9,8},{10,11... | collective-permute-start | bytes 884744 | tf_op jit(solution)/shard_map/ppermute | solution.py:788
  77.0 13.6 %collective-permute-start.15 = (bf16[96,1536]{1,0:T(8,128)(2,1)}, bf16[96,1536]{1,0:T(8,128)(2,1)}, u32[]{:S(2)}, u32[]{:S(2)}) collective-permute-start(bf16[96,1536]{1,0:T(8,128)(2,1)} %get-tuple-element.69), channel_id=1, source_target_pairs={{0,1},{1,0},{2,3},{3,2},{4,5},{5,4},{6,7},{7,6},{8,9},{9,8},{10,11... | collective-permute-start | bytes 884744 | tf_op jit(solution)/shard_map/ppermute | solution.py:788
  77.9 12.7 %copy-start.2 = (bf16[16,128]{1,0:T(8,128)(2,1)S(1)}, bf16[16,128]{1,0:T(8,128)(2,1)}, u32[]{:S(2)}) copy-start(bf16[16,128]{1,0:T(8,128)(2,1)} %get-tuple-element.63.refs_3_.refs_11_) | copy-start | bytes 12292
Sparse Core Ops, SparseCore 0:
  12.4 49.8 all-gather.1

commit v7 on v6

--- a/solution.py
+++ b/solution.py
@@ -246,9 +246,15 @@
             copy_all(loads[-1])
     rate, corr = corrections(step_ref)
     lane = lax.broadcasted_iota(jnp.int32, (8, TILE), 1)
+    parts_of_maxima = jnp.zeros((8, TILE), F32)
+    for p, value in enumerate(three_parts(side_ref[...])):
+        at = SPARE + 16 * p
+        parts_of_maxima = jnp.where(
+            (lane >= at) & (lane < at + 16), pltpu.roll(value, at, 1), parts_of_maxima
+        )
     extras = []
     for d, k in enumerate(partners):
-        side = side_ref[...]
+        side = parts_of_maxima
         for j in range(per_dest):
             i = d * per_dest + j
             wait_all(loads[i])
@@ -336,7 +342,8 @@
 
 def place_kernel(partners, pos_ref, *refs):
     n = len(partners)
-    served, sem = refs[-2:]
+    served, token, sem = refs[-3:]
+    token[...] = jnp.zeros_like(token)
     copies = block_copies(served, refs[:n], [pos_ref[0] ^ k for k in partners], sem)
     copy_all(copies)
     wait_all(copies)
@@ -347,8 +354,8 @@
     return pl.pallas_call(
         functools.partial(place_kernel, partners),
         in_specs=[SMEM] + [ANY] * (n + len(served)),
-        out_specs=ANY,
-        out_shape=jax.ShapeDtypeStruct(shape, BF16),
+        out_specs=[ANY, VMEM],
+        out_shape=[jax.ShapeDtypeStruct(shape, BF16), jax.ShapeDtypeStruct((8, TILE), F32)],
         scratch_shapes=[pltpu.SemaphoreType.DMA((n, shape[0]))],
         input_output_aliases={1 + n: 0} if served else {},
         compiler_params=LIGHT,
@@ -359,13 +366,10 @@
     )(pos, *payloads, *served)
 
 
-def finish_kernel(order, tiles, lat_tiles, n_late, to_place, deltas, rows, pos_ref, line_ref, *refs):
+def collect_kernel(order, tiles, to_place, pos_ref, *refs):
     n = len(order)
-    late, q_refs = refs[:n_late], refs[n_late : n_late + n]
-    n_rest = len(deltas)
-    rest = refs[n_late + n : n_late + n + n_rest]
-    outs = refs[n_late + n + n_rest + 2 :]
-    served, latent, exp_ref, lat_ref, extra, rows_ref, buf, place_sem, sem, in_sem, out_sem = outs
+    q_refs = refs[:n]
+    served, exp_ref, maxima_ref, extra, place_sem, sem = refs[n + 1 :]
     pos = pos_ref[0]
     per_dest = served.shape[0]
     blocks_copies = block_copies(
@@ -377,17 +381,8 @@
         )
         for i, q in enumerate(q_refs)
     ]
-    rest_loads = [pltpu.make_async_copy(rest[i], buf.at[i], in_sem.at[i]) for i in range(n_rest)]
-    copy_all(rest_loads)
     copy_all(copies)
     copy_all(blocks_copies)
-    rest_copies = []
-    for i, delta in enumerate(deltas):
-        rest_loads[i].wait()
-        group = rest_stores(buf, i, line_ref[0] ^ delta, rows, latent, out_sem)
-        copy_all(group)
-        rest_copies += group
-    rows_ref[...] = jnp.zeros_like(rows_ref)
     flat = jnp.zeros((8, exp_ref.shape[1]), F32)
     wide = lax.broadcasted_iota(jnp.int32, flat.shape, 1)
     deep = lax.broadcasted_iota(jnp.int32, flat.shape, 0)
@@ -395,64 +390,103 @@
         copies[i].wait()
         src = pos ^ k
         x = extra[i].astype(F32)[0:8, :]
-        side = late[i][...] if i < n_late else x
-        lat = sum(pltpu.roll(side, TILE - SPARE - 16 * p, 1) for p in range(3))
-        rows_ref[pl.ds(src * lat_tiles, lat_tiles), :] = lat[0:lat_tiles, :]
+        lat = sum(pltpu.roll(x, TILE - SPARE - 16 * p, 1) for p in range(3))
+        maxima_ref[pl.ds(pl.multiple_of(8 * src, 8), 8), :] = lat
         for j in range(per_dest):
             first = 3 * j
             top = x[:, first : first + 1] + x[:, first + 1 : first + 2] + x[:, first + 2 : first + 3]
             hit = (wide == (j * n + src) * tiles + deep) & (deep < tiles)
             flat = jnp.where(hit, top, flat)
     exp_ref[...] = jnp.max(flat, axis=0, keepdims=True)
-    blocks, height = lat_ref.shape
-    lat_ref[...] = jnp.transpose(rows_ref[...])[0:blocks, 0:height]
     wait_all(blocks_copies)
-    wait_all(rest_copies)
-
-
-def finish(
-    served, latent, pos, line, late, received, rest, order, to_place, deltas, tiles, lat_tiles, lat_blocks
-):
+
+
+def collect(served, pos, received, order, to_place, tiles):
     n = len(order)
     per_dest = served.shape[0]
-    span, cols = rest[0].shape
-    rows = TILE + span
-    ins = 2 + len(late) + n + len(rest)
-    served, latent, expert, scales = pl.pallas_call(
-        functools.partial(
-            finish_kernel, order, tiles, lat_tiles, len(late), to_place, deltas, rows
-        ),
-        in_specs=[SMEM] * 2 + [VMEM] * len(late) + [ANY] * (n + len(rest) + 2),
-        out_specs=[ANY, ANY, VMEM, VMEM],
+    return pl.pallas_call(
+        functools.partial(collect_kernel, order, tiles, to_place),
+        in_specs=[SMEM] + [ANY] * (n + 1),
+        out_specs=[ANY, VMEM, VMEM],
         out_shape=[
             jax.ShapeDtypeStruct(served.shape, served.dtype),
-            jax.ShapeDtypeStruct(latent.shape, latent.dtype),
             jax.ShapeDtypeStruct((1, per_dest * n * tiles), F32),
-            jax.ShapeDtypeStruct((lat_blocks, n * lat_tiles), F32),
+            jax.ShapeDtypeStruct((8 * n, TILE), F32),
         ],
         scratch_shapes=[
             pltpu.VMEM((n, EXTRA, TILE), BF16),
-            pltpu.VMEM((TILE, TILE), F32),
-            pltpu.VMEM((len(rest), span, cols), BF16),
             pltpu.SemaphoreType.DMA((len(to_place), per_dest)),
             pltpu.SemaphoreType.DMA((n,)),
-            pltpu.SemaphoreType.DMA((len(rest),)),
-            pltpu.SemaphoreType.DMA((len(rest), span // CHUNK)),
-        ],
-        input_output_aliases={ins: 0, ins + 1: 1},
+        ],
+        input_output_aliases={1 + n: 0},
+        compiler_params=LIGHT,
+        cost_estimate=pl.CostEstimate(flops=1000000, bytes_accessed=1000000, transcendentals=0),
+        name="place_last",
+    )(pos, *received, served)
+
+
+def finish_kernel(deltas, chunks, lanes, rows, pos_ref, *refs):
+    n, peers = len(deltas), len(refs) - len(deltas) - 8
+    rest, maxima = refs[:n], refs[n : n + peers]
+    latent, scale_ref, buf, ext, tops_ref, in_sem, out_sem = refs[n + peers + 1 :]
+    per_tile = TILE // CHUNK
+    pos = pos_ref[0]
+    loads = [pltpu.make_async_copy(rest[i], buf.at[i], in_sem.at[i]) for i in range(n)]
+    copy_all(loads)
+    copies = []
+    for i, delta in enumerate(deltas):
+        loads[i].wait()
+        group = rest_stores(buf, i, pos ^ delta, rows, latent, out_sem)
+        copy_all(group)
+        copies += group
+    count = maxima[0].shape[0] // 8
+    for s in range(peers):
+        peer = lax.rem(pos + peers - s, peers)
+        for d in range(count):
+            ext[pl.ds((d * peers + peer) * chunks, chunks), :] = maxima[s][8 * d : 8 * d + chunks, :]
+    blocks, height = scale_ref.shape
+    tops = ext[pl.ds(0, height, stride=per_tile), :]
+    for r in range(1, per_tile):
+        tops = jnp.maximum(tops, ext[pl.ds(r, height, stride=per_tile), :])
+    tops_ref[...] = jnp.zeros_like(tops_ref)
+    tops_ref[0:height, :] = tops
+    scale_ref[...] = jnp.transpose(tops_ref[...])[0:blocks, 0:height]
+    wait_all(copies)
+
+
+def finish(latent, pos, rest, deltas, maxima, chunks, lat_blocks):
+    n, peers = len(rest), len(maxima)
+    span, cols = rest[0].shape
+    lat_rows = maxima[0].shape[0] // 8 * peers * chunks
+    latent, scales = pl.pallas_call(
+        functools.partial(finish_kernel, deltas, chunks, lat_blocks, TILE + span),
+        in_specs=[SMEM] + [ANY] * n + [VMEM] * peers + [ANY],
+        out_specs=[ANY, VMEM],
+        out_shape=[
+            jax.ShapeDtypeStruct(latent.shape, latent.dtype),
+            jax.ShapeDtypeStruct((lat_blocks, lat_rows * CHUNK // TILE), F32),
+        ],
+        scratch_shapes=[
+            pltpu.VMEM((n, span, cols), BF16),
+            pltpu.VMEM((lat_rows, TILE), F32),
+            pltpu.VMEM((TILE, TILE), F32),
+            pltpu.SemaphoreType.DMA((n,)),
+            pltpu.SemaphoreType.DMA((n, span // CHUNK)),
+        ],
+        input_output_aliases={1 + n + peers: 0},
         compiler_params=pltpu.CompilerParams(vmem_limit_bytes=4 * 1024 * 1024),
         cost_estimate=pl.CostEstimate(flops=1000000, bytes_accessed=1000000, transcendentals=0),
-        name="place_last",
-    )(pos, line, *late, *received, *rest, served, latent)
-    return served, latent, expert, scales.T
+        name="place_finish",
+    )(pos, *rest, *maxima, latent)
+    return latent, scales.T
 
 
 def whole_tile(pos, rows):
     return pl.multiple_of(lax.rem(pos * (TILE - rows % TILE), TILE), CHUNK)
 
 
-def full_kernel(pieces, rows, x_ref, *refs):
-    out_ref, buf, in_sem, out_sem = refs[-4:]
+def full_kernel(pieces, rows, pos_ref, x_ref, own_ref, *refs):
+    out_ref, buf, own, in_sem, out_sem, own_in, own_out = refs[1:]
     loads, stores = [], []
     for i in range(pieces):
         lead = i * (TILE - rows % TILE) % TILE
@@ -463,30 +497,37 @@
                 buf.at[at, :], out_ref.at[pl.ds(i * rows + lead, TILE), :], out_sem.at[i]
             )
         )
+    loads.append(pltpu.make_async_copy(own_ref, own.at[0], own_in.at[0]))
     copy_all(loads)
     for i in range(pieces):
         loads[i].wait()
         stores[i].start()
-    wait_all(stores)
-
-
-def place_full(out, x, rows):
+    loads[pieces].wait()
+    rest = rest_stores(own, 0, pos_ref[0], rows, out_ref, own_out)
+    copy_all(rest)
+    wait_all(stores + rest)
+
+
+def place_full(out, pos, x, own, rows):
     pieces = x.shape[0] // TILE
     return pl.pallas_call(
         functools.partial(full_kernel, pieces, rows),
-        in_specs=[ANY] * (1 + len(out)),
+        in_specs=[SMEM] + [ANY] * 3,
         out_specs=ANY,
         out_shape=jax.ShapeDtypeStruct((pieces * rows, x.shape[1]), BF16),
         scratch_shapes=[
             pltpu.VMEM(x.shape, BF16),
+            pltpu.VMEM((1,) + own.shape, BF16),
             pltpu.SemaphoreType.DMA((pieces,)),
             pltpu.SemaphoreType.DMA((pieces,)),
-        ],
-        input_output_aliases={1: 0} if out else {},
+            pltpu.SemaphoreType.DMA((1,)),
+            pltpu.SemaphoreType.DMA((1, own.shape[0] // CHUNK)),
+        ],
+        input_output_aliases={3: 0},
         compiler_params=PARAMS,
         cost_estimate=pl.CostEstimate(flops=0, bytes_accessed=4 * x.size, transcendentals=0),
         name="place_whole",
-    )(x, *out)
+    )(pos, x, own, out)
 
 
 def rest_stores(buf, i, peer, rows, out_ref, sem):
@@ -504,46 +545,36 @@
     return copies
 
 
-def rest_kernel(deltas, rows, pos_ref, *refs):
-    n = len(deltas)
-    x_refs = refs[:n]
-    out_ref, again_ref, side_ref, buf, in_sem, out_sem = refs[-6:]
-    side_ref[...] = refs[n][...]
-    loads = [pltpu.make_async_copy(x_refs[i], buf.at[i], in_sem.at[i]) for i in range(n)]
-    copy_all(loads)
-    stores = []
-    for i in reversed(range(n)):
-        loads[i].wait()
-        if i == n - 1:
-            stores.append(pltpu.make_async_copy(buf.at[i], again_ref, out_sem.at[n, 0]))
-            stores[-1].start()
-        group = rest_stores(buf, i, pos_ref[0] ^ deltas[i], rows, out_ref, out_sem)
-        copy_all(group)
-        stores += group
-    wait_all(stores)
-
-
-def place_rest(pos, xs, deltas, side, after, rows, peers):
-    span, cols = xs[0].shape
-    n = len(xs)
+def hop_kernel(delta, rows, n_after, pos_ref, x_ref, *refs):
+    out_ref, again_ref, buf, in_sem, out_sem = refs[n_after:]
+    load = pltpu.make_async_copy(x_ref, buf.at[0], in_sem.at[0])
+    load.start()
+    load.wait()
+    copies = [pltpu.make_async_copy(buf.at[0], again_ref, in_sem.at[1])]
+    copies += rest_stores(buf, 0, pos_ref[0] ^ delta, rows, out_ref, out_sem)
+    copy_all(copies)
+    wait_all(copies)
+
+
+def place_and_pass(pos, x, delta, after, rows, peers):
+    span, cols = x.shape
     return pl.pallas_call(
-        functools.partial(rest_kernel, deltas, rows),
-        in_specs=[SMEM] + [ANY] * n + [VMEM, ANY],
-        out_specs=[ANY, ANY, VMEM],
+        functools.partial(hop_kernel, delta, rows, len(after)),
+        in_specs=[SMEM, ANY] + [VMEM] * len(after),
+        out_specs=[ANY, ANY],
         out_shape=[
             jax.ShapeDtypeStruct((peers * rows, cols), BF16),
             jax.ShapeDtypeStruct((span, cols), BF16),
-            jax.ShapeDtypeStruct(side.shape, side.dtype),
         ],
         scratch_shapes=[
-            pltpu.VMEM((n, span, cols), BF16),
-            pltpu.SemaphoreType.DMA((n,)),
-            pltpu.SemaphoreType.DMA((n + 1, span // CHUNK)),
+            pltpu.VMEM((1, span, cols), BF16),
+            pltpu.SemaphoreType.DMA((2,)),
+            pltpu.SemaphoreType.DMA((1, span // CHUNK)),
         ],
         compiler_params=pltpu.CompilerParams(vmem_limit_bytes=4 * 1024 * 1024),
-        cost_estimate=pl.CostEstimate(flops=0, bytes_accessed=4 * n * span * cols, transcendentals=0),
-        name="place_rest",
-    )(pos, *xs, side, after)
+        cost_estimate=pl.CostEstimate(flops=0, bytes_accessed=6 * span * cols, transcendentals=0),
+        name="place_hop",
+    )(pos, x, *after)
 
 
 SLABS = 4
@@ -629,13 +660,13 @@
     )(step, pos, *arrays)
 
 
-def latent_rest_kernel(chunks, peers, pos_ref, w1_ref, *refs):
-    q_ref, again_ref, side_ref, w, q, ext, tops_ref, in_sem, out_sem = refs[-9:]
+def latent_rest_kernel(
+    chunks, pos_ref, w1_ref, own_ref, prev_ref, next_ref, after_ref, q_ref, w, q, ext, in_sem, out_sem
+):
     per_tile = TILE // CHUNK
     rows, cols = w1_ref.shape
     width = cols // SLABS
-    pos = pos_ref[0]
-    lead = whole_tile(pos, rows)
+    lead = whole_tile(pos_ref[0], rows)
     loads, stores = [], []
     for i in range(SLABS):
         at = pl.ds(i * width, width)
@@ -651,30 +682,15 @@
             )
         copy_all(group)
         loads.append(group)
-        stores.append(
-            [
-                pltpu.make_async_copy(q.at[:, at], out.at[:, at], out_sem.at[i, n])
-                for n, out in enumerate((q_ref, again_ref))
-            ]
-        )
-    for s in range(peers):
-        peer = lax.rem(pos + peers - s, peers)
-        ext[pl.ds(peer * chunks, chunks), :] = refs[s][0:chunks, :]
-    tops_ref[...] = jnp.zeros_like(tops_ref)
-    for t in range(peers * chunks // per_tile):
-        tops_ref[t : t + 1, :] = jnp.max(
-            ext[t * per_tile : (t + 1) * per_tile, :], axis=0, keepdims=True
-        )
+        stores.append(pltpu.make_async_copy(q.at[:, at], q_ref.at[:, at], out_sem.at[i]))
+    ext[0:chunks, :] = prev_ref[0:chunks, :]
+    ext[chunks : 2 * chunks, :] = own_ref[0:chunks, :]
+    ext[2 * chunks : 3 * chunks, :] = next_ref[0:chunks, :]
+    first = chunks + lead // CHUNK
+    above = jnp.max(ext[pl.ds(first - per_tile, per_tile), :], axis=0, keepdims=True)
+    below = jnp.max(ext[pl.ds(first + per_tile, per_tile), :], axis=0, keepdims=True)
+    both = jnp.concatenate([above] * 4 + [below] * 4, axis=0)
     lane = lax.broadcasted_iota(jnp.int32, (8, TILE), 1)
-    side = jnp.zeros((8, TILE), F32)
-    for p, value in enumerate(three_parts(tops_ref[...])):
-        at = SPARE + 16 * p
-        side = jnp.where((lane >= at) & (lane < at + 16), pltpu.roll(value, at, 1), side)
-    side_ref[...] = side
-    start = pos * chunks
-    above = tops_ref[pl.ds(start // per_tile, 1), :]
-    below = tops_ref[pl.ds((start + lead // CHUNK + per_tile) // per_tile, 1), :]
-    both = jnp.concatenate([above] * 4 + [below] * 4, axis=0)
     tops = [
         jnp.max(jnp.where(lane == b, both, 0.0), axis=1, keepdims=True) for b in range(cols // TILE)
     ]
@@ -687,38 +703,31 @@
                 span = pl.ds(c * CHUNK, CHUNK)
                 inv = jnp.where(c * CHUNK < lead, invs[b][0:1, :], invs[b][4:5, :])
                 q[span, at] = (w[span, at] * inv).astype(BF16)
-        copy_all(stores[i])
-    for group in stores:
-        wait_all(group)
-
-
-def latent_rest(w1, maxima, pos, after):
+        stores[i].start()
+    wait_all(stores)
+
+
+def latent_rest(w1, own, above, below, pos, after):
     rows, cols = w1.shape
     chunks = rows // CHUNK
-    peers = len(maxima)
     return pl.pallas_call(
-        functools.partial(latent_rest_kernel, chunks, peers),
-        in_specs=[SMEM, ANY] + [VMEM] * peers + [ANY],
-        out_specs=[ANY, ANY, VMEM],
-        out_shape=[
-            jax.ShapeDtypeStruct((rows - TILE, cols), BF16),
-            jax.ShapeDtypeStruct((rows - TILE, cols), BF16),
-            jax.ShapeDtypeStruct((8, TILE), F32),
-        ],
+        functools.partial(latent_rest_kernel, chunks),
+        in_specs=[SMEM, ANY] + [VMEM] * 3 + [ANY],
+        out_specs=ANY,
+        out_shape=jax.ShapeDtypeStruct((rows - TILE, cols), BF16),
         scratch_shapes=[
             pltpu.VMEM((rows - TILE, cols), F32),
             pltpu.VMEM((rows - TILE, cols), BF16),
-            pltpu.VMEM((8 * peers, TILE), F32),
-            pltpu.VMEM((8, TILE), F32),
+            pltpu.VMEM((24, TILE), F32),
             pltpu.SemaphoreType.DMA((SLABS, chunks)),
-            pltpu.SemaphoreType.DMA((SLABS, 2)),
+            pltpu.SemaphoreType.DMA((SLABS,)),
         ],
         compiler_params=PARAMS,
         cost_estimate=pl.CostEstimate(
             flops=rows * cols, bytes_accessed=3 * rows * cols, transcendentals=0
         ),
         name="latent_rest",
-    )(pos, w1, *maxima, after)
+    )(pos, w1, own, above, below, after)
 
 
 def fast_fits(expert_shape, latent_shape, dp_count, exp_axis):
@@ -735,7 +744,7 @@
         and latent_rows % CHUNK == 0
         and 2 * TILE - CHUNK <= latent_rows < 2 * TILE
         and latent_rows * exp_axis % TILE == 0
-        and latent_rows * exp_axis <= 8 * TILE
+        and latent_rows * exp_axis * dp_count <= TILE * TILE
         and exp_axis == 4
         and latent_cols % (SLABS * TILE) == 0
         and latent_cols <= 16 * TILE
@@ -776,10 +785,8 @@
     )
     latent_rows = latent_new.shape[0]
     whole = lax.all_gather(whole, "expert", axis=0, tiled=True)
-    maxima = [chunk_top] + [
-        lax.ppermute(chunk_top, "expert", [(i, (i + s) % exp_axis) for i in range(exp_axis)])
-        for s in range(1, exp_axis)
-    ]
+    above = lax.ppermute(chunk_top, "expert", [(i, i + 1) for i in range(exp_axis - 1)])
+    below = lax.ppermute(chunk_top, "expert", [(i + 1, i) for i in range(exp_axis - 1)])
 
     arrays = tuple(
         a.reshape(rows, cols) for a in (expert_master, expert_first, expert_second, expert_grad)
@@ -789,43 +796,43 @@
 
     groups = partner_groups(dp_count)
     order = [k for partners in groups for k in partners]
-    state, received, carry = (), [], ()
-    side = jnp.zeros((8, TILE), F32)
+    state, received, carry, tops = (), [], (), chunk_top
     for n, partners in enumerate(groups):
         state, sent, carried = expert_group(
-            arrays, state, column_owner, dp_at, step_count, side, carry, (), partners, per_dest
+            arrays, state, column_owner, dp_at, step_count, tops, carry, (), partners, per_dest
         )
         received += [swap(q, "dp", k) if k else q for k, q in zip(partners, sent)]
         if n == 1:
-            rest, again, side = latent_rest(latent_new, maxima, expert_at, sent[0])
-            far = swap(rest, "expert", 2)
-            served = place_blocks(
+            rest = latent_rest(latent_new, chunk_top, above, below, expert_at, sent[0])
+            far, near = swap(rest, "expert", 2), swap(rest, "expert", 1)
+            served, _ = place_blocks(
                 (), dp_at, received[: len(groups[0])], groups[0], (per_dest, dp_count, rows, TILE)
             )
-            carry = (served, again)
-    served, again, side = carried
-    near = swap(again, "expert", 1)
+            carry = (served,)
+    served, tops = carried
     first, count = len(groups[0]), len(groups[0]) + len(groups[1])
-    served = place_blocks((served,), dp_at, received[first:count], groups[1], served.shape)
-    latent_served, far_again, side = place_rest(
-        expert_at, [rest, far], [0, 2], side, sent[-1], latent_rows, exp_axis
+    served, token = place_blocks(
+        (served,), dp_at, received[first:count], groups[1], served.shape
+    )
+    latent_served, far_again = place_and_pass(
+        expert_at, far, 2, (tops, token), latent_rows, exp_axis
     )
     last = swap(far_again, "expert", 1)
-    late = [swap(side, "dp", k) for k in groups[0] + groups[1]]
-    latent_served = place_full((latent_served,), whole, latent_rows)
-    served, latent_served, expert_scales, latent_scales = finish(
-        served,
+    latent_served = place_full(latent_served, expert_at, whole, rest, latent_rows)
+    served, expert_scales, maxima = collect(
+        served, dp_at, received, order, range(count, dp_count - 1), tiles
+    )
+    maxima = [maxima] + [
+        lax.ppermute(maxima, "expert", [(i, (i + s) % exp_axis) for i in range(exp_axis)])
+        for s in range(1, exp_axis)
+    ]
+    latent_served, latent_scales = finish(
         latent_served,
-        dp_at,
         expert_at,
-        late,
-        received,
         [near, last],
-        order,
-        range(count, dp_count - 1),
         [1, 3],
-        tiles,
-        latent_rows * exp_axis // TILE,
+        maxima,
+        latent_rows // CHUNK,
         latent_new.shape[1] // TILE,
     )
     expert_served = served.reshape(1, block_count * rows, TILE)

time: 101 us -> 88.1 us (0.87)
  waiting for transfers between devices: 25.4 us -> 16.3 us
  starting transfers between devices: 22.2 us -> 20.1 us
  local copies, waits for them, and re-layouts: 2.57 us -> 0.61 us
    ppermute x14 -> x10, waiting for transfers between devices: 22.8 us -> 9.34 us  [swap(): lax.ppermute(x, axis, [(i, i ^ k) for i in range(lax.axis_size(axis))])]
    ppermute x3 -> x5, waiting for transfers between devices: 2.55 us -> 6.97 us  [the longest x1 5 us: fast_body(): lax.ppermute(chunk_top, 'expert', [(i + 1, i) for i in range(exp_axis - 1)])]
    ppermute x14 -> x10, starting transfers between devices: 15.7 us -> 11.5 us  [swap(): lax.ppermute(x, axis, [(i, i ^ k) for i in range(lax.axis_size(axis))])]
    ppermute x3 -> x5, starting transfers between devices: 6.47 us -> 8.59 us  [the longest x3 3.87 us: fast_body(): lax.ppermute(maxima, 'expert', [(i, (i + s) % exp_axis) for i in range(ex...]
    unnamed x16 -> x12, local copies, waits for them, and re-layouts: 1.98 us -> 0.61 us
    pallas_call x4 -> x5, Pallas kernels: 9.71 us -> 9.4 us  [the longest x1 2.76 us: latent_rest(): pl.pallas_call(functools.partial(latent_rest_kernel, chunks), in_specs=[S...]
  transfers between devices with their start and end apart: 18 -> 16, of which waited for: 9 -> 6; matrix products, arithmetic and copies ran while one was open for 1% -> 0% of each run, Pallas kernels for 28% -> 34%
where the time goes in v7:
time: 88.1 us; the launch traced here: 87.7 us
  Pallas kernels  35.8 us (41%)
  starting transfers between devices  20.1 us (23%)
  waiting for transfers between devices  16.3 us (19%)
  between operations  14.9 us (17%)
    pallas_call x3, Pallas kernels, expert_group(): pl.pallas_call(functools.partial(expert_kernel, partners, per_dest, n_ali...  19.5 us
    ppermute x10, starting transfers between devices, swap(): lax.ppermute(x, axis, [(i, i ^ k) for i in range(lax.axis_size(axis))])  11.5 us
    ppermute x10, waiting for transfers between devices, swap(): lax.ppermute(x, axis, [(i, i ^ k) for i in range(lax.axis_size(axis))])  9.34 us
    ppermute x1, waiting for transfers between devices, fast_body(): lax.ppermute(chunk_top, 'expert', [(i + 1, i) for i in range(exp_axis - 1)])  5 us
    pallas_call x1, Pallas kernels, latent_update(): pl.pallas_call(functools.partial(latent_kernel, rows // CHUNK), in_specs=...  4.32 us
    ppermute x3, starting transfers between devices, fast_body(): lax.ppermute(maxima, 'expert', [(i, (i + s) % exp_axis) for i in range(ex...  3.87 us
    ppermute x1, starting transfers between devices, fast_body(): lax.ppermute(chunk_top, 'expert', [(i, i + 1) for i in range(exp_axis - 1)])  3.44 us
    pallas_call x1, Pallas kernels, latent_rest(): pl.pallas_call(functools.partial(latent_rest_kernel, chunks), in_specs=[S...  2.76 us
  transfers between devices with their start and end apart: 16, of which 6 were waited for; matrix products, arithmetic and copies ran while one was open for 0% of the time, Pallas kernels for 34%

profile of v7, /device:TPU:0, one launch (start us, length us, event | category | flops | bytes accessed | tf_op | source)
XLA Modules:
  0.0 87.7 jit_solution(9170013859629504983)
XLA Ops:
  7.2 0.0 all-gather.2.cloned.1.call-start
  7.9 4.3 %latent_adamw.1 = (f32[224,1536]{1,0:T(8,128)}, bf16[224,1536]{1,0:T(8,128)(2,1)}, bf16[224,1536]{1,0:T(8,128)(2,1)}, bf16[128,1536]{1,0:T(8,128)(2,1)}, f32[8,128]{1,0:T(8,128)}) custom-call(s32[1]{0:T(128)S(6)} %copy.42.step_ref, s32[1]{0:T(128)} %bitcast.1.pos_ref, f32[224,1536]{1,0:T(8,128)} %refs_0_.1, bf16[224,1536]{1,0:T(8,128)(2,1)} %refs_1_.1, ...), custom_call_target="tpu_custom_call" | custom-call | flops 10321920 | bytes 6193152 | tf_op jit(solution)/shard_map/latent_adamw/pallas_call | solution.py:635
  12.2 0.0 all-gather.2.cloned.1.call-update
  12.2 5.0 %expert_adamw.3 = (f32[896,2048]{1,0:T(8,128)}, bf16[896,2048]{1,0:T(8,128)(2,1)}, bf16[896,2048]{1,0:T(8,128)(2,1)}, bf16[1808,128]{1,0:T(8,128)(2,1)}, bf16[1808,128]{1,0:T(8,128)(2,1)}) custom-call(s32[16]{0:T(128)} %owner_ref.5, s32[1]{0:T(128)} %bitcast.pos_ref, s32[1]{0:T(128)S(6)} %copy.42.step_ref, f32[8,128]{1,0:T(8,128)} %get-tuple-element.44.side_ref.own_ref, ...), custom_call_target="tpu_custom_call" | custom-call | flops 458752 | bytes 458752 | tf_op jit(solution)/shard_map/expert_adamw/pallas_call | solution.py:299
  17.2 3.0 %collective-permute-start = (bf16[1808,128]{1,0:T(8,128)(2,1)}, bf16[1808,128]{1,0:T(8,128)(2,1)S(1)}, u32[]{:S(2)}, u32[]{:S(2)}) collective-permute-start(bf16[1808,128]{1,0:T(8,128)(2,1)} %get-tuple-element.51), channel_id=1, source_target_pairs={{0,16},{4,20},{8,24},{12,28},{16,0},{20,4},{24,8},{28,12},{1,17},{... | collective-permute-start | bytes 1388552 | tf_op jit(solution)/shard_map/ppermute | solution.py:795
  20.3 1.5 %collective-permute-start.1 = (bf16[1808,128]{1,0:T(8,128)(2,1)}, bf16[1808,128]{1,0:T(8,128)(2,1)S(1)}, u32[]{:S(2)}, u32[]{:S(2)}) collective-permute-start(bf16[1808,128]{1,0:T(8,128)(2,1)} %get-tuple-element.52), channel_id=1, source_target_pairs={{0,8},{4,12},{8,0},{12,4},{16,24},{20,28},{24,16},{28,20},{1,9},{5... | collective-permute-start | bytes 1388552 | tf_op jit(solution)/shard_map/ppermute | solution.py:795
  21.8 5.2 %expert_adamw.4 = (f32[896,2048]{1,0:T(8,128)}, bf16[896,2048]{1,0:T(8,128)(2,1)}, bf16[896,2048]{1,0:T(8,128)(2,1)}, bf16[1808,128]{1,0:T(8,128)(2,1)}, bf16[1808,128]{1,0:T(8,128)(2,1)}) custom-call(s32[16]{0:T(128)} %owner_ref.5, s32[1]{0:T(128)} %bitcast.pos_ref, ...), custom_call_target="tpu_custom_call", output_to_operand_aliasing={{0}: (8, {}), {1}: (9, {}), {2}: (10, {})} | custom-call | flops 458752 | bytes 458752 | tf_op jit(solution)/shard_map/expert_adamw/pallas_call | solution.py:299
  27.0 0.1 collective-permute-start.2
  27.0 2.0 %collective-permute-start.3 = (bf16[1808,128]{1,0:T(8,128)(2,1)}, bf16[1808,128]{1,0:T(8,128)(2,1)S(1)}, u32[]{:S(2)}, u32[]{:S(2)}) collective-permute-start(bf16[1808,128]{1,0:T(8,128)(2,1)} %get-tuple-element.58), channel_id=1, source_target_pairs={{0,24},{4,28},{8,16},{12,20},{16,8},{20,12},{24,0},{28,4},{1,25},{... | collective-permute-start | bytes 1388552 | tf_op jit(solution)/shard_map/ppermute | solution.py:795
  29.0 3.4 %collective-permute-start.7 = (f32[8,128]{1,0:T(8,128)S(1)}, f32[8,128]{1,0:T(8,128)S(1)}, u32[]{:S(2)}, u32[]{:S(2)}) collective-permute-start(f32[8,128]{1,0:T(8,128)S(1)} %copy-done.3), channel_id=1, source_target_pairs={{0,1},{1,2},{2,3},{4,5},{5,6},{6,7},{8,9},{9,10},{10,11},{12,13},{... | collective-permute-start | bytes 12296 | tf_op jit(solution)/shard_map/ppermute | solution.py:788
  32.4 1.3 %collective-permute-done.7.prev_ref = f32[8,128]{1,0:T(8,128)S(1)} collective-permute-done((f32[8,128]{1,0:T(8,128)S(1)}, f32[8,128]{1,0:T(8,128)S(1)}, u32[]{:S(2)}, u32[]{:S(2)}) %collective-permute-start.7) | collective-permute-done | bytes 4128 | tf_op jit(solution)/shard_map/ppermute | solution.py:788
  33.8 1.3 %collective-permute-start.8 = (f32[8,128]{1,0:T(8,128)S(1)}, f32[8,128]{1,0:T(8,128)S(1)}, u32[]{:S(2)}, u32[]{:S(2)}) collective-permute-start(f32[8,128]{1,0:T(8,128)S(1)} %copy-done.3), channel_id=1, source_target_pairs={{1,0},{2,1},{3,2},{5,4},{6,5},{7,6},{9,8},{10,9},{11,10},{13,12},{... | collective-permute-start | bytes 12296 | tf_op jit(solution)/shard_map/ppermute | solution.py:789
  35.0 5.0 %collective-permute-done.8.next_ref = f32[8,128]{1,0:T(8,128)S(1)} collective-permute-done((f32[8,128]{1,0:T(8,128)S(1)}, f32[8,128]{1,0:T(8,128)S(1)}, u32[]{:S(2)}, u32[]{:S(2)}) %collective-permute-start.8) | collective-permute-done | bytes 4128 | tf_op jit(solution)/shard_map/ppermute | solution.py:789
  40.0 0.6 copy-done.5
  40.6 2.8 %latent_rest.1.own_ref = bf16[96,1536]{1,0:T(8,128)(2,1)} custom-call(s32[1]{0:T(128)} %bitcast.1.pos_ref, f32[224,1536]{1,0:T(8,128)} %get-tuple-element.39.w1_ref, f32[8,128]{1,0:T(8,128)} %get-tuple-element.44.side_ref.own_ref, f32[8,128]{1,0:T(8,128)} %copy-done.4, f32[8,128]{1,0:T(8,128)} %copy-done.5, bf16[1808,128]{1,0:T(8,128)(2,1)} %get-tuple-element.57.after_ref), custom_call_target="tpu_custom_call" | custom-call | flops 344064 | bytes 1032192 | tf_op jit(solution)/shard_map/latent_rest/pallas_call | solution.py:713
  43.4 2.7 %collective-permute-start.10 = (bf16[96,1536]{1,0:T(8,128)(2,1)}, bf16[96,1536]{1,0:T(8,128)(2,1)S(1)}, u32[]{:S(2)}, u32[]{:S(2)}) collective-permute-start(bf16[96,1536]{1,0:T(8,128)(2,1)} %latent_rest.1.own_ref), channel_id=1, source_target_pairs={{0,2},{1,3},{2,0},{3,1},{4,6},{5,7},{6,4},{7,5},{8,10},{9,11},{10,... | collective-permute-start | bytes 884744 | tf_op jit(solution)/shard_map/ppermute | solution.py:795
  46.1 0.0 collective-permute-done.refs_0_
  46.1 0.0 collective-permute-done.1.refs_1_
  46.1 1.5 %place_served.2 = (bf16[2,8,896,128]{3,2,1,0:T(8,128)(2,1)}, f32[8,128]{1,0:T(8,128)}) custom-call(s32[1]{0:T(128)} %bitcast.pos_ref, bf16[1808,128]{1,0:T(8,128)(2,1)S(1)} %collective-permute-done.refs_0_, bf16[1808,128]{1,0:T(8,128)(2,1)S(1)} %collective-permute-done.1.refs_1_), custom_call_target="tpu_custom_call" | custom-call | bytes 1851392 | tf_op jit(solution)/shard_map/place_served/pallas_call | solution.py:354
  47.7 9.4 %expert_adamw.5 = (f32[896,2048]{1,0:T(8,128)}, bf16[896,2048]{1,0:T(8,128)(2,1)}, bf16[896,2048]{1,0:T(8,128)(2,1)}, bf16[1808,128]{1,0:T(8,128)(2,1)}, bf16[18...) custom-call(s32[16]{0:T(128)} %owner_ref.5, ...), custom_call_target="tpu_custom_call", output_to_operand_aliasing={{0}: (8, {}), {1}: (9, {}), {2}: (10, {}), {7}: (11, {})} | custom-call | flops 917504 | bytes 917504 | tf_op jit(solution)/shard_map/expert_adamw/pallas_call | solution.py:299
  57.0 0.0 copy-start
  57.0 0.0 copy-start.1
  57.1 0.1 collective-permute-start.4
  57.1 2.0 %collective-permute-start.5 = (bf16[1808,128]{1,0:T(8,128)(2,1)}, bf16[1808,128]{1,0:T(8,128)(2,1)S(1)}, u32[]{:S(2)}, u32[]{:S(2)}) collective-permute-start(bf16[1808,128]{1,0:T(8,128)(2,1)} %get-tuple-element.60), channel_id=1, source_target_pairs={{0,12},{4,8},{8,4},{12,0},{16,28},{20,24},{24,20},{28,16},{1,13},{... | collective-permute-start | bytes 1388552 | tf_op jit(solution)/shard_map/ppermute | solution.py:795
  59.2 0.0 collective-permute-done.2.refs_0_.refs_2_
  59.2 0.0 collective-permute-start.6
  59.2 0.0 collective-permute-done.3.refs_1_.refs_3_
  59.2 0.1 collective-permute-start.9
  59.3 1.0 %place_served.3 = (bf16[2,8,896,128]{3,2,1,0:T(8,128)(2,1)}, f32[8,128]{1,0:T(8,128)S(1)}) custom-call(s32[1]{0:T(128)} %bitcast.pos_ref, bf16[1808,128]{1,0:T(8,128)(2,1)S(1)} %collective-permute-done.2.refs_0_.refs_2_, bf16[1808,128]{1,0:T(8,128)(2,1)S(1)} %collective-permute-done.3.refs_1_.refs_3_, ...), custom_call_target="tpu_custom_call", output_to_operand_aliasing={{0}: (3, {})} | custom-call | bytes 1851392 | tf_op jit(solution)/shard_map/place_served/pallas_call | solution.py:354
  60.2 4.4 %collective-permute-done.10.x_ref = bf16[96,1536]{1,0:T(8,128)(2,1)S(1)} collective-permute-done((bf16[96,1536]{1,0:T(8,128)(2,1)}, bf16[96,1536]{1,0:T(8,128)(2,1)S(1)}, u32[]{:S(2)}, u32[]{:S(2)}) %collective-permute-start.10) | collective-permute-done | bytes 294944 | tf_op jit(solution)/shard_map/ppermute | solution.py:795
  64.6 0.0 copy-done
  64.6 0.9 place_hop.1
  65.5 0.1 collective-permute-start.11
  65.6 4.1 %collective-permute-done.4.refs_4_ = bf16[1808,128]{1,0:T(8,128)(2,1)S(1)} collective-permute-done((bf16[1808,128]{1,0:T(8,128)(2,1)}, bf16[1808,128]{1,0:T(8,128)(2,1)S(1)}, u32[]{:S(2)}, u32[]{:S(2)}) %collective-permute-start.4) | collective-permute-done | bytes 462880 | tf_op jit(solution)/shard_map/ppermute | solution.py:795
  69.7 0.0 collective-permute-done.5.refs_5_
  69.7 0.0 collective-permute-done.6.refs_6_
  69.7 0.0 copy-done.1
  69.7 1.9 %place_last.1 = (bf16[2,8,896,128]{3,2,1,0:T(8,128)(2,1)}, f32[1,112]{1,0:T(1,128)}, f32[64,128]{1,0:T(8,128)S(1)}) custom-call(s32[1]{0:T(128)} %bitcast.pos_ref, bf16[1808,128]{1,0:T(8,128)(2,1)S(1)} %collective-permute-done.refs_0_, bf16[1808,128]{1,0:T(8,128)(2,1)S(1)} %collective-permute-done.1.refs_1_, ...), custom_call_target="tpu_custom_call", output_to_operand_aliasing={{0}: (9, {})} | custom-call | flops 1000000 | bytes 1000000 | tf_op jit(solution)/shard_map/place_last/pallas_call | solution.py:407
  71.6 0.1 collective-permute-start.12
  71.7 1.8 %collective-permute-start.13 = (f32[64,128]{1,0:T(8,128)S(1)}, f32[64,128]{1,0:T(8,128)S(1)}, u32[]{:S(2)}, u32[]{:S(2)}) collective-permute-start(f32[64,128]{1,0:T(8,128)S(1)} %get-tuple-element.73.refs_2_), channel_id=1, source_target_pairs={{0,2},{1,3},{2,0},{3,1},{4,6},{5,7},{6,4},{7,5},{8,10},{9,11},{10,... | collective-permute-start | bytes 98312 | tf_op jit(solution)/shard_map/ppermute | solution.py:826
  73.5 2.0 %collective-permute-start.14 = (f32[64,128]{1,0:T(8,128)S(1)}, f32[64,128]{1,0:T(8,128)S(1)}, u32[]{:S(2)}, u32[]{:S(2)}) collective-permute-start(f32[64,128]{1,0:T(8,128)S(1)} %get-tuple-element.73.refs_2_), channel_id=1, source_target_pairs={{0,3},{1,0},{2,1},{3,2},{4,7},{5,4},{6,5},{7,6},{8,11},{9,8},{10,9... | collective-permute-start | bytes 98312 | tf_op jit(solution)/shard_map/ppermute | solution.py:826
  75.5 2.3 %place_whole.1.refs_6_ = bf16[896,1536]{1,0:T(8,128)(2,1)} custom-call(s32[1]{0:T(128)} %bitcast.1.pos_ref, bf16[512,1536]{1,0:T(8,128)(2,1)} %all-gather.2.cloned.1.call-done.x_ref, bf16[96,1536]{1,0:T(8,128)(2,1)} %latent_rest.1.own_ref, bf16[896,1536]{1,0:T(8,128)(2,1)} %get-tuple-element.75.refs_0_), custom_call_target="tpu_custom_call", output_to_operand_aliasing={{}: (3, {})} | custom-call | bytes 3145728 | tf_op jit(solution)/shard_map/place_whole/pallas_call | solution.py:513
  77.8 0.0 collective-permute-done.9.refs_0_
  77.8 0.8 collective-permute-done.11.refs_1_
  78.6 0.0 collective-permute-done.12.refs_3_
  78.6 0.0 collective-permute-done.13.refs_4_
  78.6 0.7 collective-permute-done.14.refs_5_
  79.3 1.6 %place_finish.1 = (bf16[896,1536]{1,0:T(8,128)(2,1)}, f32[12,56]{1,0:T(8,128)}) custom-call(s32[1]{0:T(128)} %bitcast.1.pos_ref, bf16[96,1536]{1,0:T(8,128)(2,1)S(1)} %collective-permute-done.9.refs_0_, bf16[96,1536]{1,0:T(8,128)(2,1)S(1)} %collective-permute-done.11.refs_1_, ...), custom_call_target="tpu_custom_call", output_to_operand_aliasing={{0}: (7, {})} | custom-call | flops 1000000 | bytes 1000000 | tf_op jit(solution)/shard_map/place_finish/pallas_call | solution.py:461
  (8 shorter events, 0.0 us)
Async XLA Ops:
  7.2 68.3 %all-gather.2.cloned.1.call-start = ((), (), s32[]{:S(2)}) async-start(), calls=%async_computation | async-start | bytes 1966080 | tf_op jit(solution)/shard_map/all_gather | solution.py:787
  17.2 28.9 %collective-permute-start = (bf16[1808,128]{1,0:T(8,128)(2,1)}, bf16[1808,128]{1,0:T(8,128)(2,1)S(1)}, u32[]{:S(2)}, u32[]{:S(2)}) collective-permute-start(bf16[1808,128]{1,0:T(8,128)(2,1)} %get-tuple-element.51), channel_id=1, source_target_pairs={{0,16},{4,20},{8,24},{12,28},{16,0},{20,4},{24,8},{28,12},{1,17},{... | collective-permute-start | bytes 1388552 | tf_op jit(solution)/shard_map/ppermute | solution.py:795
  20.3 25.8 %collective-permute-start.1 = (bf16[1808,128]{1,0:T(8,128)(2,1)}, bf16[1808,128]{1,0:T(8,128)(2,1)S(1)}, u32[]{:S(2)}, u32[]{:S(2)}) collective-permute-start(bf16[1808,128]{1,0:T(8,128)(2,1)} %get-tuple-element.52), channel_id=1, source_target_pairs={{0,8},{4,12},{8,0},{12,4},{16,24},{20,28},{24,16},{28,20},{1,9},{5... | collective-permute-start | bytes 1388552 | tf_op jit(solution)/shard_map/ppermute | solution.py:795
  21.8 7.2 %copy-start.3 = (f32[8,128]{1,0:T(8,128)S(1)}, f32[8,128]{1,0:T(8,128)}, u32[]{:S(2)}) copy-start(f32[8,128]{1,0:T(8,128)} %get-tuple-element.44.side_ref.own_ref) | copy-start | bytes 12292
  27.0 32.2 %collective-permute-start.2 = (bf16[1808,128]{1,0:T(8,128)(2,1)}, bf16[1808,128]{1,0:T(8,128)(2,1)S(1)}, u32[]{:S(2)}, u32[]{:S(2)}) collective-permute-start(bf16[1808,128]{1,0:T(8,128)(2,1)} %get-tuple-element.57.after_ref), channel_id=1, source_target_pairs={{0,28},{4,24},{8,20},{12,16},{16,12},{20,8},{24,4},{28,0},{1,29},{... | collective-permute-start | bytes 1388552 | tf_op jit(solution)/shard_map/ppermute | solution.py:795
  27.0 32.1 %collective-permute-start.3 = (bf16[1808,128]{1,0:T(8,128)(2,1)}, bf16[1808,128]{1,0:T(8,128)(2,1)S(1)}, u32[]{:S(2)}, u32[]{:S(2)}) collective-permute-start(bf16[1808,128]{1,0:T(8,128)(2,1)} %get-tuple-element.58), channel_id=1, source_target_pairs={{0,24},{4,28},{8,16},{12,20},{16,8},{20,12},{24,0},{28,4},{1,25},{... | collective-permute-start | bytes 1388552 | tf_op jit(solution)/shard_map/ppermute | solution.py:795
  29.0 4.8 %collective-permute-start.7 = (f32[8,128]{1,0:T(8,128)S(1)}, f32[8,128]{1,0:T(8,128)S(1)}, u32[]{:S(2)}, u32[]{:S(2)}) collective-permute-start(f32[8,128]{1,0:T(8,128)S(1)} %copy-done.3), channel_id=1, source_target_pairs={{0,1},{1,2},{2,3},{4,5},{5,6},{6,7},{8,9},{9,10},{10,11},{12,13},{... | collective-permute-start | bytes 12296 | tf_op jit(solution)/shard_map/ppermute | solution.py:788
  33.8 6.3 %copy-start.4 = (f32[8,128]{1,0:T(8,128)}, f32[8,128]{1,0:T(8,128)S(1)}, u32[]{:S(2)}) copy-start(f32[8,128]{1,0:T(8,128)S(1)} %collective-permute-done.7.prev_ref) | copy-start | bytes 12292
  33.8 6.3 %collective-permute-start.8 = (f32[8,128]{1,0:T(8,128)S(1)}, f32[8,128]{1,0:T(8,128)S(1)}, u32[]{:S(2)}, u32[]{:S(2)}) collective-permute-start(f32[8,128]{1,0:T(8,128)S(1)} %copy-done.3), channel_id=1, source_target_pairs={{1,0},{2,1},{3,2},{5,4},{6,5},{7,6},{9,8},{10,9},{11,10},{13,12},{... | collective-permute-start | bytes 12296 | tf_op jit(solution)/shard_map/ppermute | solution.py:789
  40.0 0.6 copy-start.5
  43.4 21.2 %collective-permute-start.10 = (bf16[96,1536]{1,0:T(8,128)(2,1)}, bf16[96,1536]{1,0:T(8,128)(2,1)S(1)}, u32[]{:S(2)}, u32[]{:S(2)}) collective-permute-start(bf16[96,1536]{1,0:T(8,128)(2,1)} %latent_rest.1.own_ref), channel_id=1, source_target_pairs={{0,2},{1,3},{2,0},{3,1},{4,6},{5,7},{6,4},{7,5},{8,10},{9,11},{10,... | collective-permute-start | bytes 884744 | tf_op jit(solution)/shard_map/ppermute | solution.py:795
  47.6 11.5 %copy-start.2 = (bf16[96,1536]{1,0:T(8,128)(2,1)S(1)}, bf16[96,1536]{1,0:T(8,128)(2,1)}, u32[]{:S(2)}) copy-start(bf16[96,1536]{1,0:T(8,128)(2,1)} %latent_rest.1.own_ref) | copy-start | bytes 884740
  57.0 7.6 %copy-start = (f32[8,128]{1,0:T(8,128)S(1)}, f32[8,128]{1,0:T(8,128)}, u32[]{:S(2)}) copy-start(f32[8,128]{1,0:T(8,128)} %get-tuple-element.70.refs_0_) | copy-start | bytes 12292
  57.0 12.7 %copy-start.1 = (bf16[16,128]{1,0:T(8,128)(2,1)S(1)}, bf16[16,128]{1,0:T(8,128)(2,1)}, u32[]{:S(2)}) copy-start(bf16[16,128]{1,0:T(8,128)(2,1)} %get-tuple-element.62.refs_7_) | copy-start | bytes 12292
  57.1 12.7 %collective-permute-start.4 = (bf16[1808,128]{1,0:T(8,128)(2,1)}, bf16[1808,128]{1,0:T(8,128)(2,1)S(1)}, u32[]{:S(2)}, u32[]{:S(2)}) collective-permute-start(bf16[1808,128]{1,0:T(8,128)(2,1)} %get-tuple-element.59), channel_id=1, source_target_pairs={{0,20},{4,16},{8,28},{12,24},{16,4},{20,0},{24,12},{28,8},{1,21},{... | collective-permute-start | bytes 1388552 | tf_op jit(solution)/shard_map/ppermute | solution.py:795
  57.1 12.6 %collective-permute-start.5 = (bf16[1808,128]{1,0:T(8,128)(2,1)}, bf16[1808,128]{1,0:T(8,128)(2,1)S(1)}, u32[]{:S(2)}, u32[]{:S(2)}) collective-permute-start(bf16[1808,128]{1,0:T(8,128)(2,1)} %get-tuple-element.60), channel_id=1, source_target_pairs={{0,12},{4,8},{8,4},{12,0},{16,28},{20,24},{24,20},{28,16},{1,13},{... | collective-permute-start | bytes 1388552 | tf_op jit(solution)/shard_map/ppermute | solution.py:795
  59.2 10.6 %collective-permute-start.6 = (bf16[1808,128]{1,0:T(8,128)(2,1)}, bf16[1808,128]{1,0:T(8,128)(2,1)S(1)}, u32[]{:S(2)}, u32[]{:S(2)}) collective-permute-start(bf16[1808,128]{1,0:T(8,128)(2,1)} %get-tuple-element.61), channel_id=1, source_target_pairs={{0,4},{4,0},{8,12},{12,8},{16,20},{20,16},{24,28},{28,24},{1,5},{5... | collective-permute-start | bytes 1388552 | tf_op jit(solution)/shard_map/ppermute | solution.py:795
  59.2 18.6 %collective-permute-start.9 = (bf16[96,1536]{1,0:T(8,128)(2,1)S(1)}, bf16[96,1536]{1,0:T(8,128)(2,1)S(1)}, u32[]{:S(2)}, u32[]{:S(2)}) collective-permute-start(bf16[96,1536]{1,0:T(8,128)(2,1)S(1)} %copy-done.2), channel_id=1, source_target_pairs={{0,1},{1,0},{2,3},{3,2},{4,5},{5,4},{6,7},{7,6},{8,9},{9,8},{10,11... | collective-permute-start | bytes 884744 | tf_op jit(solution)/shard_map/ppermute | solution.py:795
  65.5 13.1 %collective-permute-start.11 = (bf16[96,1536]{1,0:T(8,128)(2,1)S(1)}, bf16[96,1536]{1,0:T(8,128)(2,1)S(1)}, u32[]{:S(2)}, u32[]{:S(2)}) collective-permute-start(bf16[96,1536]{1,0:T(8,128)(2,1)S(1)} %get-tuple-element.72), channel_id=1, source_target_pairs={{0,1},{1,0},{2,3},{3,2},{4,5},{5,4},{6,7},{7,6},{8,9},{9,8},{10,11... | collective-permute-start | bytes 884744 | tf_op jit(solution)/shard_map/ppermute | solution.py:795
  71.6 7.0 %collective-permute-start.12 = (f32[64,128]{1,0:T(8,128)S(1)}, f32[64,128]{1,0:T(8,128)S(1)}, u32[]{:S(2)}, u32[]{:S(2)}) collective-permute-start(f32[64,128]{1,0:T(8,128)S(1)} %get-tuple-element.73.refs_2_), channel_id=1, source_target_pairs={{0,1},{1,2},{2,3},{3,0},{4,5},{5,6},{6,7},{7,4},{8,9},{9,10},{10,1... | collective-permute-start | bytes 98312 | tf_op jit(solution)/shard_map/ppermute | solution.py:826
  71.7 6.9 %collective-permute-start.13 = (f32[64,128]{1,0:T(8,128)S(1)}, f32[64,128]{1,0:T(8,128)S(1)}, u32[]{:S(2)}, u32[]{:S(2)}) collective-permute-start(f32[64,128]{1,0:T(8,128)S(1)} %get-tuple-element.73.refs_2_), channel_id=1, source_target_pairs={{0,2},{1,3},{2,0},{3,1},{4,6},{5,7},{6,4},{7,5},{8,10},{9,11},{10,... | collective-permute-start | bytes 98312 | tf_op jit(solution)/shard_map/ppermute | solution.py:826
  73.5 5.7 %collective-permute-start.14 = (f32[64,128]{1,0:T(8,128)S(1)}, f32[64,128]{1,0:T(8,128)S(1)}, u32[]{:S(2)}, u32[]{:S(2)}) collective-permute-start(f32[64,128]{1,0:T(8,128)S(1)} %get-tuple-element.73.refs_2_), channel_id=1, source_target_pairs={{0,3},{1,0},{2,1},{3,2},{4,7},{5,4},{6,5},{7,6},{8,11},{9,8},{10,9... | collective-permute-start | bytes 98312 | tf_op jit(solution)/shard_map/ppermute | solution.py:826
Sparse Core Ops, SparseCore 0:
  12.3 48.7 all-gather.1

commit v8 on v7

--- a/solution.py
+++ b/solution.py
@@ -545,39 +545,43 @@
     return copies
 
 
-def hop_kernel(delta, rows, n_after, pos_ref, x_ref, *refs):
-    out_ref, again_ref, buf, in_sem, out_sem = refs[n_after:]
-    load = pltpu.make_async_copy(x_ref, buf.at[0], in_sem.at[0])
-    load.start()
-    load.wait()
-    copies = [pltpu.make_async_copy(buf.at[0], again_ref, in_sem.at[1])]
-    copies += rest_stores(buf, 0, pos_ref[0] ^ delta, rows, out_ref, out_sem)
-    copy_all(copies)
+def hop_kernel(deltas, rows, pos_ref, *refs):
+    n = len(deltas)
+    out_ref, again_ref, buf, in_sem, out_sem = refs[-5:]
+    loads = [pltpu.make_async_copy(refs[i], buf.at[i], in_sem.at[i]) for i in range(n)]
+    copy_all(loads)
+    copies = [pltpu.make_async_copy(buf.at[n - 1], again_ref, in_sem.at[n])]
+    for i in reversed(range(n)):
+        loads[i].wait()
+        group = rest_stores(buf, i, pos_ref[0] ^ deltas[i], rows, out_ref, out_sem)
+        copy_all(copies + group if i == n - 1 else group)
+        copies += group
     wait_all(copies)
 
 
-def place_and_pass(pos, x, delta, after, rows, peers):
-    span, cols = x.shape
+def place_and_pass(pos, xs, deltas, after, rows, peers):
+    span, cols = xs[0].shape
+    n = len(xs)
     return pl.pallas_call(
-        functools.partial(hop_kernel, delta, rows, len(after)),
-        in_specs=[SMEM, ANY] + [VMEM] * len(after),
+        functools.partial(hop_kernel, deltas, rows),
+        in_specs=[SMEM] + [ANY] * n + [VMEM] * len(after),
         out_specs=[ANY, ANY],
         out_shape=[
             jax.ShapeDtypeStruct((peers * rows, cols), BF16),
             jax.ShapeDtypeStruct((span, cols), BF16),
         ],
         scratch_shapes=[
-            pltpu.VMEM((1, span, cols), BF16),
-            pltpu.SemaphoreType.DMA((2,)),
-            pltpu.SemaphoreType.DMA((1, span // CHUNK)),
+            pltpu.VMEM((n, span, cols), BF16),
+            pltpu.SemaphoreType.DMA((n + 1,)),
+            pltpu.SemaphoreType.DMA((n, span // CHUNK)),
         ],
         compiler_params=pltpu.CompilerParams(vmem_limit_bytes=4 * 1024 * 1024),
         cost_estimate=pl.CostEstimate(flops=0, bytes_accessed=6 * span * cols, transcendentals=0),
         name="place_hop",
-    )(pos, x, *after)
-
-
-SLABS = 4
+    )(pos, *xs, *after)
+
+
+SLABS = 6
 
 
 def latent_kernel(chunks, step_ref, pos_ref, *refs):
@@ -796,12 +800,13 @@
 
     groups = partner_groups(dp_count)
     order = [k for partners in groups for k in partners]
-    state, received, carry, tops = (), [], (), chunk_top
+    state, received, carry, after, tops = (), [], (), (), chunk_top
     for n, partners in enumerate(groups):
         state, sent, carried = expert_group(
-            arrays, state, column_owner, dp_at, step_count, tops, carry, (), partners, per_dest
+            arrays, state, column_owner, dp_at, step_count, tops, carry, after, partners, per_dest
         )
         received += [swap(q, "dp", k) if k else q for k, q in zip(partners, sent)]
+        after = (above, below) if n == 0 else ()
         if n == 1:
             rest = latent_rest(latent_new, chunk_top, above, below, expert_at, sent[0])
             far, near = swap(rest, "expert", 2), swap(rest, "expert", 1)
@@ -815,7 +820,7 @@
         (served,), dp_at, received[first:count], groups[1], served.shape
     )
     latent_served, far_again = place_and_pass(
-        expert_at, far, 2, (tops, token), latent_rows, exp_axis
+        expert_at, [near, far], [1, 2], (tops, token), latent_rows, exp_axis
     )
     last = swap(far_again, "expert", 1)
     latent_served = place_full(latent_served, expert_at, whole, rest, latent_rows)
@@ -829,8 +834,8 @@
     latent_served, latent_scales = finish(
         latent_served,
         expert_at,
-        [near, last],
-        [1, 3],
+        [last],
+        [3],
         maxima,
         latent_rows // CHUNK,
         latent_new.shape[1] // TILE,

time: 88.1 us -> 86.8 us (0.985)
  waiting for transfers between devices: 16.3 us -> 12.5 us
  starting transfers between devices: 20.1 us -> 22.4 us
    ppermute x1, waiting for transfers between devices: 5 us -> 2.79 us  [fast_body(): lax.ppermute(chunk_top, 'expert', [(i + 1, i) for i in range(exp_axis - 1)])]
    ppermute x3, starting transfers between devices: 3.87 us -> 5.5 us  [fast_body(): lax.ppermute(maxima, 'expert', [(i, (i + s) % exp_axis) for i in range(ex...]
    ppermute x1, waiting for transfers between devices: 1.31 us -> 0.01 us  [fast_body(): lax.ppermute(chunk_top, 'expert', [(i, i + 1) for i in range(exp_axis - 1)])]
  transfers between devices with their start and end apart: 16 -> 16, of which waited for: 6 -> 4; matrix products, arithmetic and copies ran while one was open for 0% -> 0% of each run, Pallas kernels for 34% -> 35%
where the time goes in v8:
time: 86.8 us; the launch traced here: 86.3 us
  Pallas kernels  36 us (41%)
  starting transfers between devices  22.4 us (26%)
  between operations  14.9 us (17%)
  waiting for transfers between devices  12.5 us (14%)
    pallas_call x3, Pallas kernels, expert_group(): pl.pallas_call(functools.partial(expert_kernel, partners, per_dest, n_ali...  19.4 us
    ppermute x10, starting transfers between devices, swap(): lax.ppermute(x, axis, [(i, i ^ k) for i in range(lax.axis_size(axis))])  12.1 us
    ppermute x10, waiting for transfers between devices, swap(): lax.ppermute(x, axis, [(i, i ^ k) for i in range(lax.axis_size(axis))])  9.65 us
    ppermute x3, starting transfers between devices, fast_body(): lax.ppermute(maxima, 'expert', [(i, (i + s) % exp_axis) for i in range(ex...  5.5 us
    pallas_call x1, Pallas kernels, latent_update(): pl.pallas_call(functools.partial(latent_kernel, rows // CHUNK), in_specs=...  4.55 us
    ppermute x1, starting transfers between devices, fast_body(): lax.ppermute(chunk_top, 'expert', [(i, i + 1) for i in range(exp_axis - 1)])  3.47 us
    pallas_call x1, Pallas kernels, latent_rest(): pl.pallas_call(functools.partial(latent_rest_kernel, chunks), in_specs=[S...  2.83 us
    ppermute x1, waiting for transfers between devices, fast_body(): lax.ppermute(chunk_top, 'expert', [(i + 1, i) for i in range(exp_axis - 1)])  2.79 us
  transfers between devices with their start and end apart: 16, of which 4 were waited for; matrix products, arithmetic and copies ran while one was open for 0% of the time, Pallas kernels for 35%

profile of v8, /device:TPU:0, one launch (start us, length us, event | category | flops | bytes accessed | tf_op | source)
XLA Modules:
  0.0 86.3 jit_solution(16846250156192089758)
XLA Ops:
  7.2 0.0 all-gather.2.cloned.1.call-start
  7.9 4.5 %latent_adamw.1 = (f32[224,1536]{1,0:T(8,128)}, bf16[224,1536]{1,0:T(8,128)(2,1)}, bf16[224,1536]{1,0:T(8,128)(2,1)}, bf16[128,1536]{1,0:T(8,128)(2,1)}, f32[8,128]{1,0:T(8,128)}) custom-call(s32[1]{0:T(128)S(6)} %copy.42.step_ref, s32[1]{0:T(128)} %bitcast.1.pos_ref, f32[224,1536]{1,0:T(8,128)} %refs_0_.1, bf16[224,1536]{1,0:T(8,128)(2,1)} %refs_1_.1, ...), custom_call_target="tpu_custom_call" | custom-call | flops 10321920 | bytes 6193152 | tf_op jit(solution)/shard_map/latent_adamw/pallas_call | solution.py:639
  12.4 0.0 all-gather.2.cloned.1.call-update
  12.5 0.0 copy-start.2
  12.5 5.1 %expert_adamw.3 = (f32[896,2048]{1,0:T(8,128)}, bf16[896,2048]{1,0:T(8,128)(2,1)}, bf16[896,2048]{1,0:T(8,128)(2,1)}, bf16[1808,128]{1,0:T(8,128)(2,1)}, bf16[1808,128]{1,0:T(8,128)(2,1)}) custom-call(s32[16]{0:T(128)} %owner_ref.5, s32[1]{0:T(128)} %bitcast.pos_ref, s32[1]{0:T(128)S(6)} %copy.42.step_ref, f32[8,128]{1,0:T(8,128)} %get-tuple-element.44.side_ref.own_ref, ...), custom_call_target="tpu_custom_call" | custom-call | flops 458752 | bytes 458752 | tf_op jit(solution)/shard_map/expert_adamw/pallas_call | solution.py:299
  17.5 3.0 %collective-permute-start.2 = (bf16[1808,128]{1,0:T(8,128)(2,1)}, bf16[1808,128]{1,0:T(8,128)(2,1)S(1)}, u32[]{:S(2)}, u32[]{:S(2)}) collective-permute-start(bf16[1808,128]{1,0:T(8,128)(2,1)} %get-tuple-element.51), channel_id=1, source_target_pairs={{0,16},{4,20},{8,24},{12,28},{16,0},{20,4},{24,8},{28,12},{1,17},{... | collective-permute-start | bytes 1388552 | tf_op jit(solution)/shard_map/ppermute | solution.py:799
  20.6 0.0 copy-done.2
  20.6 3.5 %collective-permute-start = (f32[8,128]{1,0:T(8,128)S(1)}, f32[8,128]{1,0:T(8,128)S(1)}, u32[]{:S(2)}, u32[]{:S(2)}) collective-permute-start(f32[8,128]{1,0:T(8,128)S(1)} %copy-done.2), channel_id=1, source_target_pairs={{0,1},{1,2},{2,3},{4,5},{5,6},{6,7},{8,9},{9,10},{10,11},{12,13},{... | collective-permute-start | bytes 12296 | tf_op jit(solution)/shard_map/ppermute | solution.py:792
  24.0 1.3 %collective-permute-start.1 = (f32[8,128]{1,0:T(8,128)S(1)}, f32[8,128]{1,0:T(8,128)S(1)}, u32[]{:S(2)}, u32[]{:S(2)}) collective-permute-start(f32[8,128]{1,0:T(8,128)S(1)} %copy-done.2), channel_id=1, source_target_pairs={{1,0},{2,1},{3,2},{5,4},{6,5},{7,6},{9,8},{10,9},{11,10},{13,12},{... | collective-permute-start | bytes 12296 | tf_op jit(solution)/shard_map/ppermute | solution.py:793
  25.3 1.6 %collective-permute-start.3 = (bf16[1808,128]{1,0:T(8,128)(2,1)}, bf16[1808,128]{1,0:T(8,128)(2,1)S(1)}, u32[]{:S(2)}, u32[]{:S(2)}) collective-permute-start(bf16[1808,128]{1,0:T(8,128)(2,1)} %get-tuple-element.52), channel_id=1, source_target_pairs={{0,8},{4,12},{8,0},{12,4},{16,24},{20,28},{24,16},{28,20},{1,9},{5... | collective-permute-start | bytes 1388552 | tf_op jit(solution)/shard_map/ppermute | solution.py:799
  26.9 0.0 collective-permute-done.refs_7_.prev_ref
  26.9 2.8 %collective-permute-done.1.refs_8_.next_ref = f32[8,128]{1,0:T(8,128)S(1)} collective-permute-done((f32[8,128]{1,0:T(8,128)S(1)}, f32[8,128]{1,0:T(8,128)S(1)}, u32[]{:S(2)}, u32[]{:S(2)}) %collective-permute-start.1) | collective-permute-done | bytes 4128 | tf_op jit(solution)/shard_map/ppermute | solution.py:793
  29.7 0.0 copy-done.3
  29.7 0.6 copy-done.4
  30.3 5.1 %expert_adamw.4 = (f32[896,2048]{1,0:T(8,128)}, bf16[896,2048]{1,0:T(8,128)(2,1)}, bf16[896,2048]{1,0:T(8,128)(2,1)}, bf16[1808,128]{1,0:T(8,128)(2,1)}, bf16[1808,128]{1,0:T(8,128)(2,1)}) custom-call(s32[16]{0:T(128)} %owner_ref.5, s32[1]{0:T(128)} %bitcast.pos_ref, ...), custom_call_target="tpu_custom_call", output_to_operand_aliasing={{0}: (8, {}), {1}: (9, {}), {2}: (10, {})} | custom-call | flops 458752 | bytes 458752 | tf_op jit(solution)/shard_map/expert_adamw/pallas_call | solution.py:299
  35.4 0.3 collective-permute-start.4
  35.7 1.3 %collective-permute-start.5 = (bf16[1808,128]{1,0:T(8,128)(2,1)}, bf16[1808,128]{1,0:T(8,128)(2,1)S(1)}, u32[]{:S(2)}, u32[]{:S(2)}) collective-permute-start(bf16[1808,128]{1,0:T(8,128)(2,1)} %get-tuple-element.58), channel_id=1, source_target_pairs={{0,24},{4,28},{8,16},{12,20},{16,8},{20,12},{24,0},{28,4},{1,25},{... | collective-permute-start | bytes 1388552 | tf_op jit(solution)/shard_map/ppermute | solution.py:799
  37.0 2.8 %latent_rest.1.own_ref = bf16[96,1536]{1,0:T(8,128)(2,1)} custom-call(s32[1]{0:T(128)} %bitcast.1.pos_ref, f32[224,1536]{1,0:T(8,128)} %get-tuple-element.39.w1_ref, f32[8,128]{1,0:T(8,128)} %get-tuple-element.44.side_ref.own_ref, f32[8,128]{1,0:T(8,128)} %copy-done.3, f32[8,128]{1,0:T(8,128)} %copy-done.4, bf16[1808,128]{1,0:T(8,128)(2,1)} %get-tuple-element.57.after_ref), custom_call_target="tpu_custom_call" | custom-call | flops 344064 | bytes 1032192 | tf_op jit(solution)/shard_map/latent_rest/pallas_call | solution.py:717
  39.8 2.6 %collective-permute-start.10 = (bf16[96,1536]{1,0:T(8,128)(2,1)}, bf16[96,1536]{1,0:T(8,128)(2,1)S(1)}, u32[]{:S(2)}, u32[]{:S(2)}) collective-permute-start(bf16[96,1536]{1,0:T(8,128)(2,1)} %latent_rest.1.own_ref), channel_id=1, source_target_pairs={{0,2},{1,3},{2,0},{3,1},{4,6},{5,7},{6,4},{7,5},{8,10},{9,11},{10,... | collective-permute-start | bytes 884744 | tf_op jit(solution)/shard_map/ppermute | solution.py:799
  42.4 0.0 collective-permute-done.2.refs_0_
  42.4 0.0 collective-permute-start.9
  42.4 0.0 collective-permute-done.3.refs_1_
  42.4 1.5 %place_served.2 = (bf16[2,8,896,128]{3,2,1,0:T(8,128)(2,1)}, f32[8,128]{1,0:T(8,128)}) custom-call(s32[1]{0:T(128)} %bitcast.pos_ref, bf16[1808,128]{1,0:T(8,128)(2,1)S(1)} %collective-permute-done.2.refs_0_, bf16[1808,128]{1,0:T(8,128)(2,1)S(1)} %collective-permute-done.3.refs_1_), custom_call_target="tpu_custom_call" | custom-call | bytes 1851392 | tf_op jit(solution)/shard_map/place_served/pallas_call | solution.py:354
  43.9 9.3 %expert_adamw.5 = (f32[896,2048]{1,0:T(8,128)}, bf16[896,2048]{1,0:T(8,128)(2,1)}, bf16[896,2048]{1,0:T(8,128)(2,1)}, bf16[1808,128]{1,0:T(8,128)(2,1)}, bf16[18...) custom-call(s32[16]{0:T(128)} %owner_ref.5, ...), custom_call_target="tpu_custom_call", output_to_operand_aliasing={{0}: (8, {}), {1}: (9, {}), {2}: (10, {}), {7}: (11, {})} | custom-call | flops 917504 | bytes 917504 | tf_op jit(solution)/shard_map/expert_adamw/pallas_call | solution.py:299
  53.2 0.0 copy-start
  53.2 1.1 %collective-permute-start.6 = (bf16[1808,128]{1,0:T(8,128)(2,1)}, bf16[1808,128]{1,0:T(8,128)(2,1)S(1)}, u32[]{:S(2)}, u32[]{:S(2)}) collective-permute-start(bf16[1808,128]{1,0:T(8,128)(2,1)} %get-tuple-element.59), channel_id=1, source_target_pairs={{0,20},{4,16},{8,28},{12,24},{16,4},{20,0},{24,12},{28,8},{1,21},{... | collective-permute-start | bytes 1388552 | tf_op jit(solution)/shard_map/ppermute | solution.py:799
  54.4 0.0 collective-permute-done.4.refs_0_.refs_2_
  54.4 1.1 %collective-permute-start.7 = (bf16[1808,128]{1,0:T(8,128)(2,1)}, bf16[1808,128]{1,0:T(8,128)(2,1)S(1)}, u32[]{:S(2)}, u32[]{:S(2)}) collective-permute-start(bf16[1808,128]{1,0:T(8,128)(2,1)} %get-tuple-element.60), channel_id=1, source_target_pairs={{0,12},{4,8},{8,4},{12,0},{16,28},{20,24},{24,20},{28,16},{1,13},{... | collective-permute-start | bytes 1388552 | tf_op jit(solution)/shard_map/ppermute | solution.py:799
  55.5 2.2 %collective-permute-done.5.refs_1_.refs_3_ = bf16[1808,128]{1,0:T(8,128)(2,1)S(1)} collective-permute-done((bf16[1808,128]{1,0:T(8,128)(2,1)}, bf16[1808,128]{1,0:T(8,128)(2,1)S(1)}, u32[]{:S(2)}, u32[]{:S(2)}) %collective-permute-start.5) | collective-permute-done | bytes 462880 | tf_op jit(solution)/shard_map/ppermute | solution.py:799
  57.7 1.1 %collective-permute-start.8 = (bf16[1808,128]{1,0:T(8,128)(2,1)}, bf16[1808,128]{1,0:T(8,128)(2,1)S(1)}, u32[]{:S(2)}, u32[]{:S(2)}) collective-permute-start(bf16[1808,128]{1,0:T(8,128)(2,1)} %get-tuple-element.61), channel_id=1, source_target_pairs={{0,4},{4,0},{8,12},{12,8},{16,20},{20,16},{24,28},{28,24},{1,5},{5... | collective-permute-start | bytes 1388552 | tf_op jit(solution)/shard_map/ppermute | solution.py:799
  58.7 0.9 %place_served.3 = (bf16[2,8,896,128]{3,2,1,0:T(8,128)(2,1)}, f32[8,128]{1,0:T(8,128)S(1)}) custom-call(s32[1]{0:T(128)} %bitcast.pos_ref, bf16[1808,128]{1,0:T(8,128)(2,1)S(1)} %collective-permute-done.4.refs_0_.refs_2_, bf16[1808,128]{1,0:T(8,128)(2,1)S(1)} %collective-permute-done.5.refs_1_.refs_3_, ...), custom_call_target="tpu_custom_call", output_to_operand_aliasing={{0}: (3, {})} | custom-call | bytes 1851392 | tf_op jit(solution)/shard_map/place_served/pallas_call | solution.py:354
  59.7 5.0 %collective-permute-done.10.refs_1_ = bf16[96,1536]{1,0:T(8,128)(2,1)S(1)} collective-permute-done((bf16[96,1536]{1,0:T(8,128)(2,1)}, bf16[96,1536]{1,0:T(8,128)(2,1)S(1)}, u32[]{:S(2)}, u32[]{:S(2)}) %collective-permute-start.10) | collective-permute-done | bytes 294944 | tf_op jit(solution)/shard_map/ppermute | solution.py:799
  64.7 0.0 collective-permute-done.9.refs_0_
  64.7 1.1 %place_hop.1 = (bf16[896,1536]{1,0:T(8,128)(2,1)}, bf16[96,1536]{1,0:T(8,128)(2,1)S(1)}) custom-call(s32[1]{0:T(128)} %bitcast.1.pos_ref, bf16[96,1536]{1,0:T(8,128)(2,1)S(1)} %collective-permute-done.9.refs_0_, bf16[96,1536]{1,0:T(8,128)(2,1)S(1)} %collective-permute-done.10.refs_1_, f32[8,128]{1,0:T(8,128)S(1)} %copy-done, ...), custom_call_target="tpu_custom_call" | custom-call | bytes 884736 | tf_op jit(solution)/shard_map/place_hop/pallas_call | solution.py:565
  65.8 0.1 collective-permute-start.11
  65.9 2.4 %collective-permute-done.6.refs_4_ = bf16[1808,128]{1,0:T(8,128)(2,1)S(1)} collective-permute-done((bf16[1808,128]{1,0:T(8,128)(2,1)}, bf16[1808,128]{1,0:T(8,128)(2,1)S(1)}, u32[]{:S(2)}, u32[]{:S(2)}) %collective-permute-start.6) | collective-permute-done | bytes 462880 | tf_op jit(solution)/shard_map/ppermute | solution.py:799
  68.3 0.0 collective-permute-done.7.refs_5_
  68.3 0.0 collective-permute-done.8.refs_6_
  68.3 1.9 %place_last.1 = (bf16[2,8,896,128]{3,2,1,0:T(8,128)(2,1)}, f32[1,112]{1,0:T(1,128)}, f32[64,128]{1,0:T(8,128)S(1)}) custom-call(s32[1]{0:T(128)} %bitcast.pos_ref, bf16[1808,128]{1,0:T(8,128)(2,1)S(1)} %collective-permute-done.2.refs_0_, bf16[1808,128]{1,0:T(8,128)(2,1)S(1)} %collective-permute-done.3.refs_1_, ...), custom_call_target="tpu_custom_call", output_to_operand_aliasing={{0}: (9, {})} | custom-call | flops 1000000 | bytes 1000000 | tf_op jit(solution)/shard_map/place_last/pallas_call | solution.py:407
  70.2 1.7 %collective-permute-start.12 = (f32[64,128]{1,0:T(8,128)S(1)}, f32[64,128]{1,0:T(8,128)S(1)}, u32[]{:S(2)}, u32[]{:S(2)}) collective-permute-start(f32[64,128]{1,0:T(8,128)S(1)} %get-tuple-element.73.refs_1_), channel_id=1, source_target_pairs={{0,1},{1,2},{2,3},{3,0},{4,5},{5,6},{6,7},{7,4},{8,9},{9,10},{10,1... | collective-permute-start | bytes 98312 | tf_op jit(solution)/shard_map/ppermute | solution.py:831
  71.8 2.1 %collective-permute-start.13 = (f32[64,128]{1,0:T(8,128)S(1)}, f32[64,128]{1,0:T(8,128)S(1)}, u32[]{:S(2)}, u32[]{:S(2)}) collective-permute-start(f32[64,128]{1,0:T(8,128)S(1)} %get-tuple-element.73.refs_1_), channel_id=1, source_target_pairs={{0,2},{1,3},{2,0},{3,1},{4,6},{5,7},{6,4},{7,5},{8,10},{9,11},{10,... | collective-permute-start | bytes 98312 | tf_op jit(solution)/shard_map/ppermute | solution.py:831
  73.9 1.8 %collective-permute-start.14 = (f32[64,128]{1,0:T(8,128)S(1)}, f32[64,128]{1,0:T(8,128)S(1)}, u32[]{:S(2)}, u32[]{:S(2)}) collective-permute-start(f32[64,128]{1,0:T(8,128)S(1)} %get-tuple-element.73.refs_1_), channel_id=1, source_target_pairs={{0,3},{1,0},{2,1},{3,2},{4,7},{5,4},{6,5},{7,6},{8,11},{9,8},{10,9... | collective-permute-start | bytes 98312 | tf_op jit(solution)/shard_map/ppermute | solution.py:831
  75.7 2.3 %place_whole.1.refs_5_ = bf16[896,1536]{1,0:T(8,128)(2,1)} custom-call(s32[1]{0:T(128)} %bitcast.1.pos_ref, bf16[512,1536]{1,0:T(8,128)(2,1)} %all-gather.2.cloned.1.call-done.x_ref, bf16[96,1536]{1,0:T(8,128)(2,1)} %latent_rest.1.own_ref, bf16[896,1536]{1,0:T(8,128)(2,1)} %get-tuple-element.75.refs_0_), custom_call_target="tpu_custom_call", output_to_operand_aliasing={{}: (3, {})} | custom-call | bytes 3145728 | tf_op jit(solution)/shard_map/place_whole/pallas_call | solution.py:513
  78.0 0.0 collective-permute-done.11.refs_0_
  78.0 0.0 collective-permute-done.12.refs_2_
  78.0 0.0 collective-permute-done.13.refs_3_
  78.0 0.0 collective-permute-done.14.refs_4_
  78.0 1.4 %place_finish.1 = (bf16[896,1536]{1,0:T(8,128)(2,1)}, f32[12,56]{1,0:T(8,128)}) custom-call(s32[1]{0:T(128)} %bitcast.1.pos_ref, bf16[96,1536]{1,0:T(8,128)(2,1)S(1)} %collective-permute-done.11.refs_0_, f32[64,128]{1,0:T(8,128)S(1)} %get-tuple-element.73.refs_1_, f32[64,128]{1,0:T(8,128)S(1)} %collective-permute-done.12.refs_2_, ...), custom_call_target="tpu_custom_call", output_to_operand_aliasing={{0}: (6, {})} | custom-call | flops 1000000 | bytes 1000000 | tf_op jit(solution)/shard_map/place_finish/pallas_call | solution.py:461
  (6 shorter events, 0.0 us)
Async XLA Ops:
  7.2 68.5 %all-gather.2.cloned.1.call-start = ((), (), s32[]{:S(2)}) async-start(), calls=%async_computation | async-start | bytes 1966080 | tf_op jit(solution)/shard_map/all_gather | solution.py:791
  12.5 8.1 %copy-start.2 = (f32[8,128]{1,0:T(8,128)S(1)}, f32[8,128]{1,0:T(8,128)}, u32[]{:S(2)}) copy-start(f32[8,128]{1,0:T(8,128)} %get-tuple-element.44.side_ref.own_ref) | copy-start | bytes 12292
  17.5 24.8 %collective-permute-start.2 = (bf16[1808,128]{1,0:T(8,128)(2,1)}, bf16[1808,128]{1,0:T(8,128)(2,1)S(1)}, u32[]{:S(2)}, u32[]{:S(2)}) collective-permute-start(bf16[1808,128]{1,0:T(8,128)(2,1)} %get-tuple-element.51), channel_id=1, source_target_pairs={{0,16},{4,20},{8,24},{12,28},{16,0},{20,4},{24,8},{28,12},{1,17},{... | collective-permute-start | bytes 1388552 | tf_op jit(solution)/shard_map/ppermute | solution.py:799
  20.6 6.3 %collective-permute-start = (f32[8,128]{1,0:T(8,128)S(1)}, f32[8,128]{1,0:T(8,128)S(1)}, u32[]{:S(2)}, u32[]{:S(2)}) collective-permute-start(f32[8,128]{1,0:T(8,128)S(1)} %copy-done.2), channel_id=1, source_target_pairs={{0,1},{1,2},{2,3},{4,5},{5,6},{6,7},{8,9},{9,10},{10,11},{12,13},{... | collective-permute-start | bytes 12296 | tf_op jit(solution)/shard_map/ppermute | solution.py:792
  24.0 5.7 %collective-permute-start.1 = (f32[8,128]{1,0:T(8,128)S(1)}, f32[8,128]{1,0:T(8,128)S(1)}, u32[]{:S(2)}, u32[]{:S(2)}) collective-permute-start(f32[8,128]{1,0:T(8,128)S(1)} %copy-done.2), channel_id=1, source_target_pairs={{1,0},{2,1},{3,2},{5,4},{6,5},{7,6},{9,8},{10,9},{11,10},{13,12},{... | collective-permute-start | bytes 12296 | tf_op jit(solution)/shard_map/ppermute | solution.py:793
  25.3 17.0 %collective-permute-start.3 = (bf16[1808,128]{1,0:T(8,128)(2,1)}, bf16[1808,128]{1,0:T(8,128)(2,1)S(1)}, u32[]{:S(2)}, u32[]{:S(2)}) collective-permute-start(bf16[1808,128]{1,0:T(8,128)(2,1)} %get-tuple-element.52), channel_id=1, source_target_pairs={{0,8},{4,12},{8,0},{12,4},{16,24},{20,28},{24,16},{28,20},{1,9},{5... | collective-permute-start | bytes 1388552 | tf_op jit(solution)/shard_map/ppermute | solution.py:799
  26.9 2.8 %copy-start.3 = (f32[8,128]{1,0:T(8,128)}, f32[8,128]{1,0:T(8,128)S(1)}, u32[]{:S(2)}) copy-start(f32[8,128]{1,0:T(8,128)S(1)} %collective-permute-done.refs_7_.prev_ref) | copy-start | bytes 12292
  29.7 0.6 copy-start.4
  35.4 19.0 %collective-permute-start.4 = (bf16[1808,128]{1,0:T(8,128)(2,1)}, bf16[1808,128]{1,0:T(8,128)(2,1)S(1)}, u32[]{:S(2)}, u32[]{:S(2)}) collective-permute-start(bf16[1808,128]{1,0:T(8,128)(2,1)} %get-tuple-element.57.after_ref), channel_id=1, source_target_pairs={{0,28},{4,24},{8,20},{12,16},{16,12},{20,8},{24,4},{28,0},{1,29},{... | collective-permute-start | bytes 1388552 | tf_op jit(solution)/shard_map/ppermute | solution.py:799
  35.7 22.0 %collective-permute-start.5 = (bf16[1808,128]{1,0:T(8,128)(2,1)}, bf16[1808,128]{1,0:T(8,128)(2,1)S(1)}, u32[]{:S(2)}, u32[]{:S(2)}) collective-permute-start(bf16[1808,128]{1,0:T(8,128)(2,1)} %get-tuple-element.58), channel_id=1, source_target_pairs={{0,24},{4,28},{8,16},{12,20},{16,8},{20,12},{24,0},{28,4},{1,25},{... | collective-permute-start | bytes 1388552 | tf_op jit(solution)/shard_map/ppermute | solution.py:799
  39.8 24.9 %collective-permute-start.10 = (bf16[96,1536]{1,0:T(8,128)(2,1)}, bf16[96,1536]{1,0:T(8,128)(2,1)S(1)}, u32[]{:S(2)}, u32[]{:S(2)}) collective-permute-start(bf16[96,1536]{1,0:T(8,128)(2,1)} %latent_rest.1.own_ref), channel_id=1, source_target_pairs={{0,2},{1,3},{2,0},{3,1},{4,6},{5,7},{6,4},{7,5},{8,10},{9,11},{10,... | collective-permute-start | bytes 884744 | tf_op jit(solution)/shard_map/ppermute | solution.py:799
  42.4 22.3 %collective-permute-start.9 = (bf16[96,1536]{1,0:T(8,128)(2,1)}, bf16[96,1536]{1,0:T(8,128)(2,1)S(1)}, u32[]{:S(2)}, u32[]{:S(2)}) collective-permute-start(bf16[96,1536]{1,0:T(8,128)(2,1)} %latent_rest.1.own_ref), channel_id=1, source_target_pairs={{0,1},{1,0},{2,3},{3,2},{4,5},{5,4},{6,7},{7,6},{8,9},{9,8},{10,11... | collective-permute-start | bytes 884744 | tf_op jit(solution)/shard_map/ppermute | solution.py:799
  53.2 11.5 %copy-start = (f32[8,128]{1,0:T(8,128)S(1)}, f32[8,128]{1,0:T(8,128)}, u32[]{:S(2)}) copy-start(f32[8,128]{1,0:T(8,128)} %get-tuple-element.70.refs_2_) | copy-start | bytes 12292
  53.2 15.1 %copy-start.1 = (bf16[16,128]{1,0:T(8,128)(2,1)S(1)}, bf16[16,128]{1,0:T(8,128)(2,1)}, u32[]{:S(2)}) copy-start(bf16[16,128]{1,0:T(8,128)(2,1)} %get-tuple-element.62.refs_7_) | copy-start | bytes 12292
  53.2 15.0 %collective-permute-start.6 = (bf16[1808,128]{1,0:T(8,128)(2,1)}, bf16[1808,128]{1,0:T(8,128)(2,1)S(1)}, u32[]{:S(2)}, u32[]{:S(2)}) collective-permute-start(bf16[1808,128]{1,0:T(8,128)(2,1)} %get-tuple-element.59), channel_id=1, source_target_pairs={{0,20},{4,16},{8,28},{12,24},{16,4},{20,0},{24,12},{28,8},{1,21},{... | collective-permute-start | bytes 1388552 | tf_op jit(solution)/shard_map/ppermute | solution.py:799
  54.4 13.9 %collective-permute-start.7 = (bf16[1808,128]{1,0:T(8,128)(2,1)}, bf16[1808,128]{1,0:T(8,128)(2,1)S(1)}, u32[]{:S(2)}, u32[]{:S(2)}) collective-permute-start(bf16[1808,128]{1,0:T(8,128)(2,1)} %get-tuple-element.60), channel_id=1, source_target_pairs={{0,12},{4,8},{8,4},{12,0},{16,28},{20,24},{24,20},{28,16},{1,13},{... | collective-permute-start | bytes 1388552 | tf_op jit(solution)/shard_map/ppermute | solution.py:799
  57.7 10.6 %collective-permute-start.8 = (bf16[1808,128]{1,0:T(8,128)(2,1)}, bf16[1808,128]{1,0:T(8,128)(2,1)S(1)}, u32[]{:S(2)}, u32[]{:S(2)}) collective-permute-start(bf16[1808,128]{1,0:T(8,128)(2,1)} %get-tuple-element.61), channel_id=1, source_target_pairs={{0,4},{4,0},{8,12},{12,8},{16,20},{20,16},{24,28},{28,24},{1,5},{5... | collective-permute-start | bytes 1388552 | tf_op jit(solution)/shard_map/ppermute | solution.py:799
  65.8 12.2 %collective-permute-start.11 = (bf16[96,1536]{1,0:T(8,128)(2,1)S(1)}, bf16[96,1536]{1,0:T(8,128)(2,1)S(1)}, u32[]{:S(2)}, u32[]{:S(2)}) collective-permute-start(bf16[96,1536]{1,0:T(8,128)(2,1)S(1)} %get-tuple-element.72), channel_id=1, source_target_pairs={{0,1},{1,0},{2,3},{3,2},{4,5},{5,4},{6,7},{7,6},{8,9},{9,8},{10,11... | collective-permute-start | bytes 884744 | tf_op jit(solution)/shard_map/ppermute | solution.py:799
  70.2 7.8 %collective-permute-start.12 = (f32[64,128]{1,0:T(8,128)S(1)}, f32[64,128]{1,0:T(8,128)S(1)}, u32[]{:S(2)}, u32[]{:S(2)}) collective-permute-start(f32[64,128]{1,0:T(8,128)S(1)} %get-tuple-element.73.refs_1_), channel_id=1, source_target_pairs={{0,1},{1,2},{2,3},{3,0},{4,5},{5,6},{6,7},{7,4},{8,9},{9,10},{10,1... | collective-permute-start | bytes 98312 | tf_op jit(solution)/shard_map/ppermute | solution.py:831
  71.8 6.2 %collective-permute-start.13 = (f32[64,128]{1,0:T(8,128)S(1)}, f32[64,128]{1,0:T(8,128)S(1)}, u32[]{:S(2)}, u32[]{:S(2)}) collective-permute-start(f32[64,128]{1,0:T(8,128)S(1)} %get-tuple-element.73.refs_1_), channel_id=1, source_target_pairs={{0,2},{1,3},{2,0},{3,1},{4,6},{5,7},{6,4},{7,5},{8,10},{9,11},{10,... | collective-permute-start | bytes 98312 | tf_op jit(solution)/shard_map/ppermute | solution.py:831
  73.9 4.1 %collective-permute-start.14 = (f32[64,128]{1,0:T(8,128)S(1)}, f32[64,128]{1,0:T(8,128)S(1)}, u32[]{:S(2)}, u32[]{:S(2)}) collective-permute-start(f32[64,128]{1,0:T(8,128)S(1)} %get-tuple-element.73.refs_1_), channel_id=1, source_target_pairs={{0,3},{1,0},{2,1},{3,2},{4,7},{5,4},{6,5},{7,6},{8,11},{9,8},{10,9... | collective-permute-start | bytes 98312 | tf_op jit(solution)/shard_map/ppermute | solution.py:831
Sparse Core Ops, SparseCore 0:
  12.6 49.9 all-gather.1

commit v9 on v8

--- a/solution.py
+++ b/solution.py
@@ -150,7 +150,7 @@
 
 CHUNK = 32
 EXTRA = 16
-SPARE = 64
+MAXIMA_AT = (64, 16)
 F32 = jnp.float32
 BF16 = jnp.bfloat16
 VMEM_LIMIT = 56 * 1024 * 1024
@@ -207,8 +207,11 @@
         c.wait()
 
 
-def expert_kernel(partners, per_dest, n_alias, n_skip, has_side, owner_ref, pos_ref, step_ref, side_ref, *refs):
-    hbm, refs = refs[:4], refs[4 + n_alias + n_skip :]
+def expert_kernel(
+    partners, per_dest, n_alias, n_carry, chunks, n_maxima, owner_ref, pos_ref, step_ref, *refs
+):
+    maxima, refs = refs[:n_maxima], refs[n_maxima:]
+    hbm, refs = refs[:4], refs[4 + n_alias + n_carry :]
     n_dest = len(partners)
     outs, q_refs, served_ref = refs[:3], refs[3 : 3 + n_dest], refs[3 + n_dest]
     w, m, v, g, extra, in_sem, out_sem, extra_sem = refs[-8:]
@@ -217,8 +220,6 @@
     rows = w.shape[1]
     tiles = rows // TILE
     pos = pos_ref[0]
-    if has_side:
-        refs[-9][...] = side_ref[...]
 
     loads, stores = [], []
     for d, k in enumerate(partners):
@@ -246,15 +247,26 @@
             copy_all(loads[-1])
     rate, corr = corrections(step_ref)
     lane = lax.broadcasted_iota(jnp.int32, (8, TILE), 1)
-    parts_of_maxima = jnp.zeros((8, TILE), F32)
-    for p, value in enumerate(three_parts(side_ref[...])):
-        at = SPARE + 16 * p
-        parts_of_maxima = jnp.where(
-            (lane >= at) & (lane < at + 16), pltpu.roll(value, at, 1), parts_of_maxima
-        )
+    if chunks:
+        tops_ref, ext = refs[3 + n_dest + n_carry], refs[-9]
+        per_tile = TILE // CHUNK
+        for s in range(n_maxima):
+            peer = lax.rem(pos_ref[1] + n_maxima - s, n_maxima)
+            ext[pl.ds(peer * chunks, chunks), :] = maxima[s][0:chunks, :]
+        tops_ref[...] = jnp.zeros_like(tops_ref)
+        for t in range(n_maxima * chunks // per_tile):
+            tops_ref[t : t + 1, :] = jnp.max(
+                ext[t * per_tile : (t + 1) * per_tile, :], axis=0, keepdims=True
+            )
+        maxima = (tops_ref,)
+    carried = jnp.zeros((8, TILE), F32)
+    for first, x_ref in zip(MAXIMA_AT, maxima):
+        for p, value in enumerate(three_parts(x_ref[...])):
+            at = first + 16 * p
+            carried = jnp.where((lane >= at) & (lane < at + 16), pltpu.roll(value, at, 1), carried)
     extras = []
     for d, k in enumerate(partners):
-        side = parts_of_maxima
+        side = carried
         for j in range(per_dest):
             i = d * per_dest + j
             wait_all(loads[i])
@@ -288,20 +300,21 @@
     wait_all(extras)
 
 
-def expert_group(arrays, state, owner, pos, step, side, carry, after, partners, per_dest):
+def expert_group(arrays, state, owner, pos, step, maxima, chunks, carry, partners, per_dest):
     rows, cols = arrays[0].shape
-    n_alias = len(state)
+    n_alias, n_maxima = len(state), len(maxima)
     n = len(partners) * per_dest
     elems = rows * TILE * n
-    sides = [jax.ShapeDtypeStruct(side.shape, side.dtype)] * (len(carry) > 0)
-    aliases = {8 + i: i for i in range(n_alias)}
-    aliases.update({8 + n_alias + i: 3 + len(partners) + i for i in range(len(carry))})
+    flat = [jax.ShapeDtypeStruct((8, TILE), F32)] * (chunks > 0)
+    first = 7 + n_maxima
+    aliases = {first + i: i for i in range(n_alias)}
+    aliases.update({first + n_alias + i: 3 + len(partners) + i for i in range(len(carry))})
     out = pl.pallas_call(
         functools.partial(
-            expert_kernel, partners, per_dest, n_alias, len(carry) + len(after), len(sides)
+            expert_kernel, partners, per_dest, n_alias, len(carry), chunks, n_maxima
         ),
-        in_specs=[SMEM] * 3 + [VMEM] + [ANY] * (4 + n_alias + len(carry) + len(after)),
-        out_specs=[ANY] * (3 + len(partners) + len(carry)) + [VMEM] * len(sides),
+        in_specs=[SMEM] * 3 + [VMEM] * n_maxima + [ANY] * (4 + n_alias + len(carry)),
+        out_specs=[ANY] * (3 + len(partners) + len(carry)) + [VMEM] * len(flat),
         out_shape=[
             jax.ShapeDtypeStruct((rows, cols), F32),
             jax.ShapeDtypeStruct((rows, cols), BF16),
@@ -312,8 +325,9 @@
             for k in partners
         ]
         + [jax.ShapeDtypeStruct(x.shape, x.dtype) for x in carry]
-        + sides,
+        + flat,
         scratch_shapes=[
+            pltpu.VMEM((32, TILE), F32),
             pltpu.VMEM((n, rows, TILE), F32),
             pltpu.VMEM((n, rows, TILE), BF16),
             pltpu.VMEM((n, rows, TILE), BF16),
@@ -327,7 +341,7 @@
         compiler_params=PARAMS,
         cost_estimate=pl.CostEstimate(flops=elems, bytes_accessed=elems, transcendentals=0),
         name="expert_adamw",
-    )(owner, pos, step, side, *arrays, *state, *carry, *after)
+    )(owner, pos, step, *maxima, *arrays, *state, *carry)
     return out[:3], out[3 : 3 + len(partners)], out[3 + len(partners) :]
 
 
@@ -366,10 +380,10 @@
     )(pos, *payloads, *served)
 
 
-def collect_kernel(order, tiles, to_place, pos_ref, *refs):
+def collect_kernel(order, tiles, lat_tiles, to_place, groups, pos_ref, after_ref, *refs):
     n = len(order)
     q_refs = refs[:n]
-    served, exp_ref, maxima_ref, extra, place_sem, sem = refs[n + 1 :]
+    served, exp_ref, lat_ref, extra, rows_ref, place_sem, sem = refs[n + 1 :]
     pos = pos_ref[0]
     per_dest = served.shape[0]
     blocks_copies = block_copies(
@@ -383,6 +397,7 @@
     ]
     copy_all(copies)
     copy_all(blocks_copies)
+    rows_ref[...] = jnp.zeros_like(rows_ref)
     flat = jnp.zeros((8, exp_ref.shape[1]), F32)
     wide = lax.broadcasted_iota(jnp.int32, flat.shape, 1)
     deep = lax.broadcasted_iota(jnp.int32, flat.shape, 0)
@@ -390,95 +405,81 @@
         copies[i].wait()
         src = pos ^ k
         x = extra[i].astype(F32)[0:8, :]
-        lat = sum(pltpu.roll(x, TILE - SPARE - 16 * p, 1) for p in range(3))
-        maxima_ref[pl.ds(pl.multiple_of(8 * src, 8), 8), :] = lat
+        known = (src, src ^ 1) if k in groups[2] else (src,) if k in groups[1] else ()
+        for first, peer in zip(MAXIMA_AT, known):
+            lat = sum(pltpu.roll(x, TILE - first - 16 * p, 1) for p in range(3))
+            rows_ref[pl.ds(peer * lat_tiles, lat_tiles), :] = lat[0:lat_tiles, :]
         for j in range(per_dest):
             first = 3 * j
             top = x[:, first : first + 1] + x[:, first + 1 : first + 2] + x[:, first + 2 : first + 3]
             hit = (wide == (j * n + src) * tiles + deep) & (deep < tiles)
             flat = jnp.where(hit, top, flat)
     exp_ref[...] = jnp.max(flat, axis=0, keepdims=True)
+    blocks, height = lat_ref.shape
+    lat_ref[...] = jnp.transpose(rows_ref[...])[0:blocks, 0:height]
     wait_all(blocks_copies)
 
 
-def collect(served, pos, received, order, to_place, tiles):
+def collect(served, pos, after, received, groups, tiles, lat_tiles, lat_blocks):
+    order = [k for partners in groups for k in partners]
     n = len(order)
     per_dest = served.shape[0]
-    return pl.pallas_call(
-        functools.partial(collect_kernel, order, tiles, to_place),
-        in_specs=[SMEM] + [ANY] * (n + 1),
+    to_place = [i for i, k in enumerate(order) if k in groups[2] and k]
+    served, expert, latent = pl.pallas_call(
+        functools.partial(collect_kernel, order, tiles, lat_tiles, to_place, groups),
+        in_specs=[SMEM, VMEM] + [ANY] * (n + 1),
         out_specs=[ANY, VMEM, VMEM],
         out_shape=[
             jax.ShapeDtypeStruct(served.shape, served.dtype),
             jax.ShapeDtypeStruct((1, per_dest * n * tiles), F32),
-            jax.ShapeDtypeStruct((8 * n, TILE), F32),
+            jax.ShapeDtypeStruct((lat_blocks, n * lat_tiles), F32),
         ],
         scratch_shapes=[
             pltpu.VMEM((n, EXTRA, TILE), BF16),
+            pltpu.VMEM((TILE, TILE), F32),
             pltpu.SemaphoreType.DMA((len(to_place), per_dest)),
             pltpu.SemaphoreType.DMA((n,)),
         ],
-        input_output_aliases={1 + n: 0},
+        input_output_aliases={2 + n: 0},
         compiler_params=LIGHT,
         cost_estimate=pl.CostEstimate(flops=1000000, bytes_accessed=1000000, transcendentals=0),
         name="place_last",
-    )(pos, *received, served)
-
-
-def finish_kernel(deltas, chunks, lanes, rows, pos_ref, *refs):
-    n, peers = len(deltas), len(refs) - len(deltas) - 8
-    rest, maxima = refs[:n], refs[n : n + peers]
-    latent, scale_ref, buf, ext, tops_ref, in_sem, out_sem = refs[n + peers + 1 :]
-    per_tile = TILE // CHUNK
-    pos = pos_ref[0]
-    loads = [pltpu.make_async_copy(rest[i], buf.at[i], in_sem.at[i]) for i in range(n)]
+    )(pos, after, *received, served)
+    return served, expert, latent.T
+
+
+def finish_kernel(deltas, rows, pos_ref, *refs):
+    n = len(deltas)
+    latent, buf, in_sem, out_sem = refs[n + 2 :]
+    loads = [pltpu.make_async_copy(refs[i], buf.at[i], in_sem.at[i]) for i in range(n)]
     copy_all(loads)
     copies = []
     for i, delta in enumerate(deltas):
         loads[i].wait()
-        group = rest_stores(buf, i, pos ^ delta, rows, latent, out_sem)
+        group = rest_stores(buf, i, pos_ref[0] ^ delta, rows, latent, out_sem)
         copy_all(group)
         copies += group
-    count = maxima[0].shape[0] // 8
-    for s in range(peers):
-        peer = lax.rem(pos + peers - s, peers)
-        for d in range(count):
-            ext[pl.ds((d * peers + peer) * chunks, chunks), :] = maxima[s][8 * d : 8 * d + chunks, :]
-    blocks, height = scale_ref.shape
-    tops = ext[pl.ds(0, height, stride=per_tile), :]
-    for r in range(1, per_tile):
-        tops = jnp.maximum(tops, ext[pl.ds(r, height, stride=per_tile), :])
-    tops_ref[...] = jnp.zeros_like(tops_ref)
-    tops_ref[0:height, :] = tops
-    scale_ref[...] = jnp.transpose(tops_ref[...])[0:blocks, 0:height]
     wait_all(copies)
 
 
-def finish(latent, pos, rest, deltas, maxima, chunks, lat_blocks):
-    n, peers = len(rest), len(maxima)
+def finish(latent, pos, rest, deltas, after):
+    n = len(rest)
     span, cols = rest[0].shape
-    lat_rows = maxima[0].shape[0] // 8 * peers * chunks
-    latent, scales = pl.pallas_call(
-        functools.partial(finish_kernel, deltas, chunks, lat_blocks, TILE + span),
-        in_specs=[SMEM] + [ANY] * n + [VMEM] * peers + [ANY],
-        out_specs=[ANY, VMEM],
-        out_shape=[
-            jax.ShapeDtypeStruct(latent.shape, latent.dtype),
-            jax.ShapeDtypeStruct((lat_blocks, lat_rows * CHUNK // TILE), F32),
-        ],
+    return pl.pallas_call(
+        functools.partial(finish_kernel, deltas, TILE + span),
+        in_specs=[SMEM] + [ANY] * (n + 2),
+        out_specs=ANY,
+        out_shape=jax.ShapeDtypeStruct(latent.shape, latent.dtype),
         scratch_shapes=[
             pltpu.VMEM((n, span, cols), BF16),
-            pltpu.VMEM((lat_rows, TILE), F32),
-            pltpu.VMEM((TILE, TILE), F32),
             pltpu.SemaphoreType.DMA((n,)),
             pltpu.SemaphoreType.DMA((n, span // CHUNK)),
         ],
-        input_output_aliases={1 + n + peers: 0},
+        input_output_aliases={1 + n: 0},
         compiler_params=pltpu.CompilerParams(vmem_limit_bytes=4 * 1024 * 1024),
-        cost_estimate=pl.CostEstimate(flops=1000000, bytes_accessed=1000000, transcendentals=0),
+        cost_estimate=pl.CostEstimate(flops=0, bytes_accessed=1000000, transcendentals=0),
         name="place_finish",
-    )(pos, *rest, *maxima, latent)
-    return latent, scales.T
+    )(pos, *rest, latent, after)
 
 
 def whole_tile(pos, rows):
@@ -486,7 +487,8 @@
 
 
 def full_kernel(pieces, rows, pos_ref, x_ref, own_ref, *refs):
-    out_ref, buf, own, in_sem, out_sem, own_in, own_out = refs[1:]
+    out_ref, token, buf, own, in_sem, out_sem, own_in, own_out = refs[1:]
+    token[...] = jnp.zeros_like(token)
     loads, stores = [], []
     for i in range(pieces):
         lead = i * (TILE - rows % TILE) % TILE
@@ -513,8 +515,11 @@
     return pl.pallas_call(
         functools.partial(full_kernel, pieces, rows),
         in_specs=[SMEM] + [ANY] * 3,
-        out_specs=ANY,
-        out_shape=jax.ShapeDtypeStruct((pieces * rows, x.shape[1]), BF16),
+        out_specs=[ANY, VMEM],
+        out_shape=[
+            jax.ShapeDtypeStruct((pieces * rows, x.shape[1]), BF16),
+            jax.ShapeDtypeStruct((8, TILE), F32),
+        ],
         scratch_shapes=[
             pltpu.VMEM(x.shape, BF16),
             pltpu.VMEM((1,) + own.shape, BF16),
@@ -742,13 +747,13 @@
         and rows % TILE == 0
         and rows <= 8 * TILE
         and cols % (TILE * dp_count) == 0
-        and cols // TILE // dp_count <= 16
+        and cols // TILE // dp_count <= 5
         and dp_count == 8
         and dp_count * latent_rows * exp_axis <= TILE * TILE
         and latent_rows % CHUNK == 0
         and 2 * TILE - CHUNK <= latent_rows < 2 * TILE
         and latent_rows * exp_axis % TILE == 0
-        and latent_rows * exp_axis * dp_count <= TILE * TILE
+        and latent_rows * exp_axis <= 8 * TILE
         and exp_axis == 4
         and latent_cols % (SLABS * TILE) == 0
         and latent_cols <= 16 * TILE
@@ -789,8 +794,10 @@
     )
     latent_rows = latent_new.shape[0]
     whole = lax.all_gather(whole, "expert", axis=0, tiled=True)
-    above = lax.ppermute(chunk_top, "expert", [(i, i + 1) for i in range(exp_axis - 1)])
-    below = lax.ppermute(chunk_top, "expert", [(i + 1, i) for i in range(exp_axis - 1)])
+    maxima = [chunk_top] + [
+        lax.ppermute(chunk_top, "expert", [(i, (i + s) % exp_axis) for i in range(exp_axis)])
+        for s in range(1, exp_axis)
+    ]
 
     arrays = tuple(
         a.reshape(rows, cols) for a in (expert_master, expert_first, expert_second, expert_grad)
@@ -800,21 +807,32 @@
 
     groups = partner_groups(dp_count)
     order = [k for partners in groups for k in partners]
-    state, received, carry, after, tops = (), [], (), (), chunk_top
-    for n, partners in enumerate(groups):
-        state, sent, carried = expert_group(
-            arrays, state, column_owner, dp_at, step_count, tops, carry, after, partners, per_dest
-        )
-        received += [swap(q, "dp", k) if k else q for k, q in zip(partners, sent)]
-        after = (above, below) if n == 0 else ()
-        if n == 1:
-            rest = latent_rest(latent_new, chunk_top, above, below, expert_at, sent[0])
-            far, near = swap(rest, "expert", 2), swap(rest, "expert", 1)
-            served, _ = place_blocks(
-                (), dp_at, received[: len(groups[0])], groups[0], (per_dest, dp_count, rows, TILE)
-            )
-            carry = (served,)
-    served, tops = carried
+    both_at = jnp.concatenate([dp_at, expert_at])
+    send = lambda sent, partners: [swap(q, "dp", k) if k else q for k, q in zip(partners, sent)]
+    group = functools.partial(expert_group, arrays, owner=column_owner, pos=both_at, step=step_count)
+    chunks = latent_rows // CHUNK
+    state, sent, _ = group(
+        state=(), maxima=(), chunks=0, carry=(), partners=groups[0], per_dest=per_dest
+    )
+    received = send(sent, groups[0])
+    state, sent, (tops,) = group(
+        state=state, maxima=maxima, chunks=chunks, carry=(), partners=groups[1], per_dest=per_dest
+    )
+    received += send(sent, groups[1])
+    rest = latent_rest(latent_new, chunk_top, maxima[1], maxima[-1], expert_at, sent[0])
+    far, near = swap(rest, "expert", 2), swap(rest, "expert", 1)
+    served, _ = place_blocks(
+        (), dp_at, received[: len(groups[0])], groups[0], (per_dest, dp_count, rows, TILE)
+    )
+    state, sent, (served,) = group(
+        state=state,
+        maxima=[tops, swap(tops, "dp", 1)],
+        chunks=0,
+        carry=(served,),
+        partners=groups[2],
+        per_dest=per_dest,
+    )
+    received += send(sent, groups[2])
     first, count = len(groups[0]), len(groups[0]) + len(groups[1])
     served, token = place_blocks(
         (served,), dp_at, received[first:count], groups[1], served.shape
@@ -823,23 +841,18 @@
         expert_at, [near, far], [1, 2], (tops, token), latent_rows, exp_axis
     )
     last = swap(far_again, "expert", 1)
-    latent_served = place_full(latent_served, expert_at, whole, rest, latent_rows)
-    served, expert_scales, maxima = collect(
-        served, dp_at, received, order, range(count, dp_count - 1), tiles
-    )
-    maxima = [maxima] + [
-        lax.ppermute(maxima, "expert", [(i, (i + s) % exp_axis) for i in range(exp_axis)])
-        for s in range(1, exp_axis)
-    ]
-    latent_served, latent_scales = finish(
-        latent_served,
-        expert_at,
-        [last],
-        [3],
-        maxima,
-        latent_rows // CHUNK,
+    latent_served, token = place_full(latent_served, expert_at, whole, rest, latent_rows)
+    served, expert_scales, latent_scales = collect(
+        served,
+        dp_at,
+        token,
+        received,
+        groups,
+        tiles,
+        latent_rows * exp_axis // TILE,
         latent_new.shape[1] // TILE,
     )
+    latent_served = finish(latent_served, expert_at, [last], [3], expert_scales)
     expert_served = served.reshape(1, block_count * rows, TILE)
 
     return (

time: 86.8 us -> 83.3 us (0.960)
  starting transfers between devices: 22.4 us -> 18.7 us
  waiting for transfers between devices: 12.5 us -> 10.1 us
  local copies, waits for them, and re-layouts: 0.61 us -> 2.53 us
    ppermute x5 -> x3, starting transfers between devices: 10.3 us -> 4.61 us  [fast_body(): lax.ppermute(chunk_top, 'expert', [(i, (i + s) % exp_axis) for i in range...]
    ppermute x10 -> x11, waiting for transfers between devices: 9.65 us -> 6.15 us  [swap(): lax.ppermute(x, axis, [(i, i ^ k) for i in range(lax.axis_size(axis))])]
    ppermute x10 -> x11, starting transfers between devices: 12.1 us -> 14 us  [swap(): lax.ppermute(x, axis, [(i, i ^ k) for i in range(lax.axis_size(axis))])]
    unnamed x10 -> x18, local copies, waits for them, and re-layouts: 0.61 us -> 2.53 us
    ppermute x5 -> x3, waiting for transfers between devices: 2.8 us -> 3.92 us  [fast_body(): lax.ppermute(chunk_top, 'expert', [(i, (i + s) % exp_axis) for i in range...]
  transfers between devices with their start and end apart: 16 -> 15, of which waited for: 4 -> 6; matrix products, arithmetic and copies ran while one was open for 0% -> 1% of each run, Pallas kernels for 35% -> 37%
where the time goes in v9:
time: 83.3 us; the launch traced here: 82.9 us
  Pallas kernels  36.1 us (43%)
  starting transfers between devices  18.7 us (22%)
  between operations  14.9 us (18%)
  waiting for transfers between devices  10.1 us (12%)
  local copies, waits for them, and re-layouts  2.53 us (3%)
    pallas_call x3, Pallas kernels, expert_group(): pl.pallas_call(functools.partial(expert_kernel, partners, per_dest, n_ali...  19.5 us
    ppermute x11, starting transfers between devices, swap(): lax.ppermute(x, axis, [(i, i ^ k) for i in range(lax.axis_size(axis))])  14 us
    ppermute x11, waiting for transfers between devices, swap(): lax.ppermute(x, axis, [(i, i ^ k) for i in range(lax.axis_size(axis))])  6.15 us
    ppermute x3, starting transfers between devices, fast_body(): lax.ppermute(chunk_top, 'expert', [(i, (i + s) % exp_axis) for i in range...  4.61 us
    pallas_call x1, Pallas kernels, latent_update(): pl.pallas_call(functools.partial(latent_kernel, rows // CHUNK), in_specs=...  4.54 us
    ppermute x3, waiting for transfers between devices, fast_body(): lax.ppermute(chunk_top, 'expert', [(i, (i + s) % exp_axis) for i in range...  3.92 us
    pallas_call x1, Pallas kernels, place_full(): pl.pallas_call(functools.partial(full_kernel, pieces, rows), in_specs=[SM...  2.91 us
    pallas_call x1, Pallas kernels, latent_rest(): pl.pallas_call(functools.partial(latent_rest_kernel, chunks), in_specs=[S...  2.83 us
  transfers between devices with their start and end apart: 15, of which 6 were waited for; matrix products, arithmetic and copies ran while one was open for 1% of the time, Pallas kernels for 37%

profile of v9, /device:TPU:0, one launch (start us, length us, event | category | flops | bytes accessed | tf_op | source)
XLA Modules:
  0.0 82.9 jit_solution(17512209195036806560)
XLA Ops:
  7.2 0.0 all-gather.2.cloned.1.call-start
  7.9 4.5 %latent_adamw.1 = (f32[224,1536]{1,0:T(8,128)}, bf16[224,1536]{1,0:T(8,128)(2,1)}, bf16[224,1536]{1,0:T(8,128)(2,1)}, bf16[128,1536]{1,0:T(8,128)(2,1)}, f32[8,128]{1,0:T(8,128)}) custom-call(s32[1]{0:T(128)S(6)} %copy.42.step_ref, s32[1]{0:T(128)} %bitcast.1.pos_ref, f32[224,1536]{1,0:T(8,128)} %refs_0_.1, bf16[224,1536]{1,0:T(8,128)(2,1)} %refs_1_.1, ...), custom_call_target="tpu_custom_call" | custom-call | flops 10321920 | bytes 6193152 | tf_op jit(solution)/shard_map/latent_adamw/pallas_call | solution.py:644
  12.4 0.0 all-gather.2.cloned.1.call-update
  12.5 0.6 pad_add_fusion.pos_ref
  13.0 5.1 %expert_adamw.3 = (f32[896,2048]{1,0:T(8,128)}, bf16[896,2048]{1,0:T(8,128)(2,1)}, bf16[896,2048]{1,0:T(8,128)(2,1)}, bf16[1808,128]{1,0:T(8,128)(2,1)}, bf16[1808,128]{1,0:T(8,128)(2,1)}) custom-call(s32[16]{0:T(128)} %owner_ref.5, s32[2]{0:T(128)} %pad_add_fusion.pos_ref, s32[1]{0:T(128)S(6)} %copy.42.step_ref, f32[896,2048]{1,0:T(8,128)} %bitcast.11, ...), custom_call_target="tpu_custom_call" | custom-call | flops 458752 | bytes 458752 | tf_op jit(solution)/shard_map/expert_adamw/pallas_call | solution.py:312
  18.1 3.0 %collective-permute-start.4 = (bf16[1808,128]{1,0:T(8,128)(2,1)}, bf16[1808,128]{1,0:T(8,128)(2,1)S(1)}, u32[]{:S(2)}, u32[]{:S(2)}) collective-permute-start(bf16[1808,128]{1,0:T(8,128)(2,1)} %get-tuple-element.52), channel_id=1, source_target_pairs={{0,16},{4,20},{8,24},{12,28},{16,0},{20,4},{24,8},{28,12},{1,17},{... | collective-permute-start | bytes 1388552 | tf_op jit(solution)/shard_map/ppermute | solution.py:806
  21.2 1.5 %collective-permute-start.5 = (bf16[1808,128]{1,0:T(8,128)(2,1)}, bf16[1808,128]{1,0:T(8,128)(2,1)S(1)}, u32[]{:S(2)}, u32[]{:S(2)}) collective-permute-start(bf16[1808,128]{1,0:T(8,128)(2,1)} %get-tuple-element.53), channel_id=1, source_target_pairs={{0,8},{4,12},{8,0},{12,4},{16,24},{20,28},{24,16},{28,20},{1,9},{5... | collective-permute-start | bytes 1388552 | tf_op jit(solution)/shard_map/ppermute | solution.py:806
  22.7 1.6 %collective-permute-start = (f32[8,128]{1,0:T(8,128)S(1)}, f32[8,128]{1,0:T(8,128)S(1)}, u32[]{:S(2)}, u32[]{:S(2)}) collective-permute-start(f32[8,128]{1,0:T(8,128)S(1)} %copy-done.4), channel_id=1, source_target_pairs={{0,1},{1,2},{2,3},{3,0},{4,5},{5,6},{6,7},{7,4},{8,9},{9,10},{10,1... | collective-permute-start | bytes 12296 | tf_op jit(solution)/shard_map/ppermute | solution.py:798
  24.3 2.2 %collective-permute-start.2 = (f32[8,128]{1,0:T(8,128)S(1)}, f32[8,128]{1,0:T(8,128)S(1)}, u32[]{:S(2)}, u32[]{:S(2)}) collective-permute-start(f32[8,128]{1,0:T(8,128)S(1)} %copy-done.4), channel_id=1, source_target_pairs={{0,3},{1,0},{2,1},{3,2},{4,7},{5,4},{6,5},{7,6},{8,11},{9,8},{10,9... | collective-permute-start | bytes 12296 | tf_op jit(solution)/shard_map/ppermute | solution.py:798
  26.5 0.8 collective-permute-start.1
  27.3 0.9 %collective-permute-done.refs_1_.prev_ref = f32[8,128]{1,0:T(8,128)S(1)} collective-permute-done((f32[8,128]{1,0:T(8,128)S(1)}, f32[8,128]{1,0:T(8,128)S(1)}, u32[]{:S(2)}, u32[]{:S(2)}) %collective-permute-start) | collective-permute-done | bytes 4128 | tf_op jit(solution)/shard_map/ppermute | solution.py:798
  28.2 0.0 collective-permute-done.2.refs_3_.next_ref
  28.2 3.0 %collective-permute-done.1.refs_2_ = f32[8,128]{1,0:T(8,128)S(1)} collective-permute-done((f32[8,128]{1,0:T(8,128)S(1)}, f32[8,128]{1,0:T(8,128)S(1)}, u32[]{:S(2)}, u32[]{:S(2)}) %collective-permute-start.1) | collective-permute-done | bytes 4128 | tf_op jit(solution)/shard_map/ppermute | solution.py:798
  31.2 0.6 copy-done.8
  31.8 5.7 %expert_adamw.4 = (f32[896,2048]{1,0:T(8,128)}, bf16[896,2048]{1,0:T(8,128)(2,1)}, bf16[896,2048]{1,0:T(8,128)(2,1)}, bf16[1808,128]{1,0:T(8,128)(2,1)}, bf16[1808,128]{1,0:T(8,128)(2,1)}, /*index=5*/f32[8,128]{1,0:T(8,128)}) custom-call(s32[16]{0:T(128)} %owner_ref.5, ...), custom_call_target="tpu_custom_call", output_to_operand_aliasing={{0}: (11, {}), {1}: (12, {}), {2}: (13, {})} | custom-call | flops 458752 | bytes 458752 | tf_op jit(solution)/shard_map/expert_adamw/pallas_call | solution.py:312
  37.5 0.1 collective-permute-start.8
  37.6 0.5 collective-permute-start.9
  38.1 2.8 %latent_rest.1.own_ref = bf16[96,1536]{1,0:T(8,128)(2,1)} custom-call(s32[1]{0:T(128)} %bitcast.1.pos_ref, f32[224,1536]{1,0:T(8,128)} %get-tuple-element.39.w1_ref, f32[8,128]{1,0:T(8,128)} %get-tuple-element.44.refs_0_.own_ref, f32[8,128]{1,0:T(8,128)} %copy-done.5, f32[8,128]{1,0:T(8,128)} %copy-done.6, bf16[1808,128]{1,0:T(8,128)(2,1)} %get-tuple-element.60.after_ref), custom_call_target="tpu_custom_call" | custom-call | flops 344064 | bytes 1032192 | tf_op jit(solution)/shard_map/latent_rest/pallas_call | solution.py:722
  40.9 0.1 collective-permute-start.6
  41.0 0.0 collective-permute-done.4.refs_0_
  41.0 2.8 %collective-permute-start.7 = (bf16[96,1536]{1,0:T(8,128)(2,1)}, bf16[96,1536]{1,0:T(8,128)(2,1)S(1)}, u32[]{:S(2)}, u32[]{:S(2)}) collective-permute-start(bf16[96,1536]{1,0:T(8,128)(2,1)} %latent_rest.1.own_ref), channel_id=1, source_target_pairs={{0,2},{1,3},{2,0},{3,1},{4,6},{5,7},{6,4},{7,5},{8,10},{9,11},{10,... | collective-permute-start | bytes 884744 | tf_op jit(solution)/shard_map/ppermute | solution.py:806
  43.8 0.0 collective-permute-done.5.refs_1_
  43.8 1.7 %collective-permute-start.3 = (f32[8,128]{1,0:T(8,128)}, f32[8,128]{1,0:T(8,128)S(1)}, u32[]{:S(2)}, u32[]{:S(2)}) collective-permute-start(f32[8,128]{1,0:T(8,128)} %get-tuple-element.48.refs_0_.refs_2_), channel_id=1, source_target_pairs={{0,4},{4,0},{8,12},{12,8},{16,20},{20,16},{24,28},{28,24},{1,5},{5... | collective-permute-start | bytes 12296 | tf_op jit(solution)/shard_map/ppermute | solution.py:806
  45.5 1.5 %place_served.2 = (bf16[2,8,896,128]{3,2,1,0:T(8,128)(2,1)}, f32[8,128]{1,0:T(8,128)}) custom-call(s32[1]{0:T(128)} %bitcast.pos_ref, bf16[1808,128]{1,0:T(8,128)(2,1)S(1)} %collective-permute-done.4.refs_0_, bf16[1808,128]{1,0:T(8,128)(2,1)S(1)} %collective-permute-done.5.refs_1_), custom_call_target="tpu_custom_call" | custom-call | bytes 1851392 | tf_op jit(solution)/shard_map/place_served/pallas_call | solution.py:368
  47.1 0.0 collective-permute-done.3.refs_1_
  47.1 0.0 copy-start.7
  47.1 0.6 copy-done.7
  47.7 8.7 %expert_adamw.5 = (f32[896,2048]{1,0:T(8,128)}, bf16[896,2048]{1,0:T(8,128)(2,1)}, bf16[896,2048]{1,0:T(8,128)(2,1)}, bf16[1808,128]{1,0:T(8,128)(2,1)}, bf16[18...) custom-call(s32[16]{0:T(128)} %owner_ref.5, ...), custom_call_target="tpu_custom_call", output_to_operand_aliasing={{0}: (9, {}), {1}: (10, {}), {2}: (11, {}), {7}: (12, {})} | custom-call | flops 917504 | bytes 917504 | tf_op jit(solution)/shard_map/expert_adamw/pallas_call | solution.py:312
  56.3 0.0 copy-start
  56.4 0.1 collective-permute-start.10
  56.4 0.0 collective-permute-done.8.refs_0_.refs_2_
  56.4 1.1 %collective-permute-start.11 = (bf16[1808,128]{1,0:T(8,128)(2,1)}, bf16[1808,128]{1,0:T(8,128)(2,1)S(1)}, u32[]{:S(2)}, u32[]{:S(2)}) collective-permute-start(bf16[1808,128]{1,0:T(8,128)(2,1)} %get-tuple-element.67), channel_id=1, source_target_pairs={{0,12},{4,8},{8,4},{12,0},{16,28},{20,24},{24,20},{28,16},{1,13},{... | collective-permute-start | bytes 1388552 | tf_op jit(solution)/shard_map/ppermute | solution.py:806
  57.5 0.9 %collective-permute-done.9.refs_1_.refs_3_ = bf16[1808,128]{1,0:T(8,128)(2,1)S(1)} collective-permute-done((bf16[1808,128]{1,0:T(8,128)(2,1)}, bf16[1808,128]{1,0:T(8,128)(2,1)S(1)}, u32[]{:S(2)}, u32[]{:S(2)}) %collective-permute-start.9) | collective-permute-done | bytes 462880 | tf_op jit(solution)/shard_map/ppermute | solution.py:806
  58.4 1.1 %collective-permute-start.12 = (bf16[1808,128]{1,0:T(8,128)(2,1)}, bf16[1808,128]{1,0:T(8,128)(2,1)S(1)}, u32[]{:S(2)}, u32[]{:S(2)}) collective-permute-start(bf16[1808,128]{1,0:T(8,128)(2,1)} %get-tuple-element.68), channel_id=1, source_target_pairs={{0,4},{4,0},{8,12},{12,8},{16,20},{20,16},{24,28},{28,24},{1,5},{5... | collective-permute-start | bytes 1388552 | tf_op jit(solution)/shard_map/ppermute | solution.py:806
  59.5 0.9 %place_served.3 = (bf16[2,8,896,128]{3,2,1,0:T(8,128)(2,1)}, f32[8,128]{1,0:T(8,128)S(1)}) custom-call(s32[1]{0:T(128)} %bitcast.pos_ref, bf16[1808,128]{1,0:T(8,128)(2,1)S(1)} %collective-permute-done.8.refs_0_.refs_2_, bf16[1808,128]{1,0:T(8,128)(2,1)S(1)} %collective-permute-done.9.refs_1_.refs_3_, ...), custom_call_target="tpu_custom_call", output_to_operand_aliasing={{0}: (3, {})} | custom-call | bytes 1851392 | tf_op jit(solution)/shard_map/place_served/pallas_call | solution.py:368
  60.5 3.1 %collective-permute-done.6.refs_0_ = bf16[96,1536]{1,0:T(8,128)(2,1)S(1)} collective-permute-done((bf16[96,1536]{1,0:T(8,128)(2,1)}, bf16[96,1536]{1,0:T(8,128)(2,1)S(1)}, u32[]{:S(2)}, u32[]{:S(2)}) %collective-permute-start.6) | collective-permute-done | bytes 294944 | tf_op jit(solution)/shard_map/ppermute | solution.py:806
  63.5 0.0 collective-permute-done.7.refs_1_
  63.5 1.1 %place_hop.1 = (bf16[896,1536]{1,0:T(8,128)(2,1)}, bf16[96,1536]{1,0:T(8,128)(2,1)}) custom-call(s32[1]{0:T(128)} %bitcast.1.pos_ref, bf16[96,1536]{1,0:T(8,128)(2,1)S(1)} %collective-permute-done.6.refs_0_, bf16[96,1536]{1,0:T(8,128)(2,1)S(1)} %collective-permute-done.7.refs_1_, f32[8,128]{1,0:T(8,128)S(1)} %copy-done, f32[8,128]{1,0:T(8,128)S(1)} %get-tuple-element.63.refs_3_), custom_call_target="tpu_custom_call" | custom-call | bytes 884736 | tf_op jit(solution)/shard_map/place_hop/pallas_call | solution.py:570
  64.6 2.2 %collective-permute-start.13 = (bf16[96,1536]{1,0:T(8,128)(2,1)}, bf16[96,1536]{1,0:T(8,128)(2,1)S(1)}, u32[]{:S(2)}, u32[]{:S(2)}) collective-permute-start(bf16[96,1536]{1,0:T(8,128)(2,1)} %get-tuple-element.75), channel_id=1, source_target_pairs={{0,1},{1,0},{2,3},{3,2},{4,5},{5,4},{6,7},{7,6},{8,9},{9,8},{10,11... | collective-permute-start | bytes 884744 | tf_op jit(solution)/shard_map/ppermute | solution.py:806
  66.8 2.9 %place_whole.1 = (bf16[896,1536]{1,0:T(8,128)(2,1)}, f32[8,128]{1,0:T(8,128)}) custom-call(s32[1]{0:T(128)} %bitcast.1.pos_ref, bf16[512,1536]{1,0:T(8,128)(2,1)} %all-gather.2.cloned.1.call-done.x_ref, bf16[96,1536]{1,0:T(8,128)(2,1)} %latent_rest.1.own_ref, bf16[896,1536]{1,0:T(8,128)(2,1)} %get-tuple-element.64.refs_0_), custom_call_target="tpu_custom_call", output_to_operand_aliasing={{0}: (3, {})} | custom-call | bytes 3145728 | tf_op jit(solution)/shard_map/place_whole/pallas_call | solution.py:515
  69.7 0.0 collective-permute-done.10.refs_4_
  69.7 0.3 collective-permute-done.11.refs_5_
  70.1 0.0 collective-permute-done.12.refs_6_
  70.1 0.7 copy-done.2
  70.8 1.9 %place_last.1 = (bf16[2,8,896,128]{3,2,1,0:T(8,128)(2,1)}, f32[1,112]{1,0:T(1,128)}, f32[12,56]{1,0:T(8,128)}) custom-call(s32[1]{0:T(128)} %bitcast.pos_ref, f32[8,128]{1,0:T(8,128)S(1)} %copy-done.2, bf16[1808,128]{1,0:T(8,128)(2,1)S(1)} %collective-permute-done.4.refs_0_, ...), custom_call_target="tpu_custom_call", output_to_operand_aliasing={{0}: (10, {})} | custom-call | flops 1000000 | bytes 1000000 | tf_op jit(solution)/shard_map/place_last/pallas_call | solution.py:428
  72.7 1.8 %collective-permute-done.13.refs_0_ = bf16[96,1536]{1,0:T(8,128)(2,1)S(1)} collective-permute-done((bf16[96,1536]{1,0:T(8,128)(2,1)}, bf16[96,1536]{1,0:T(8,128)(2,1)S(1)}, u32[]{:S(2)}, u32[]{:S(2)}) %collective-permute-start.13) | collective-permute-done | bytes 294944 | tf_op jit(solution)/shard_map/ppermute | solution.py:806
  74.5 0.7 copy-done.3
  75.2 0.8 place_finish.1
  (13 shorter events, 0.0 us)
Async XLA Ops:
  7.2 59.6 %all-gather.2.cloned.1.call-start = ((), (), s32[]{:S(2)}) async-start(), calls=%async_computation | async-start | bytes 1966080 | tf_op jit(solution)/shard_map/all_gather | solution.py:796
  13.0 9.6 %copy-start.4 = (f32[8,128]{1,0:T(8,128)S(1)}, f32[8,128]{1,0:T(8,128)}, u32[]{:S(2)}) copy-start(f32[8,128]{1,0:T(8,128)} %get-tuple-element.44.refs_0_.own_ref) | copy-start | bytes 12292
  18.1 22.8 %collective-permute-start.4 = (bf16[1808,128]{1,0:T(8,128)(2,1)}, bf16[1808,128]{1,0:T(8,128)(2,1)S(1)}, u32[]{:S(2)}, u32[]{:S(2)}) collective-permute-start(bf16[1808,128]{1,0:T(8,128)(2,1)} %get-tuple-element.52), channel_id=1, source_target_pairs={{0,16},{4,20},{8,24},{12,28},{16,0},{20,4},{24,8},{28,12},{1,17},{... | collective-permute-start | bytes 1388552 | tf_op jit(solution)/shard_map/ppermute | solution.py:806
  21.2 22.6 %collective-permute-start.5 = (bf16[1808,128]{1,0:T(8,128)(2,1)}, bf16[1808,128]{1,0:T(8,128)(2,1)S(1)}, u32[]{:S(2)}, u32[]{:S(2)}) collective-permute-start(bf16[1808,128]{1,0:T(8,128)(2,1)} %get-tuple-element.53), channel_id=1, source_target_pairs={{0,8},{4,12},{8,0},{12,4},{16,24},{20,28},{24,16},{28,20},{1,9},{5... | collective-permute-start | bytes 1388552 | tf_op jit(solution)/shard_map/ppermute | solution.py:806
  22.7 5.6 %collective-permute-start = (f32[8,128]{1,0:T(8,128)S(1)}, f32[8,128]{1,0:T(8,128)S(1)}, u32[]{:S(2)}, u32[]{:S(2)}) collective-permute-start(f32[8,128]{1,0:T(8,128)S(1)} %copy-done.4), channel_id=1, source_target_pairs={{0,1},{1,2},{2,3},{3,0},{4,5},{5,6},{6,7},{7,4},{8,9},{9,10},{10,1... | collective-permute-start | bytes 12296 | tf_op jit(solution)/shard_map/ppermute | solution.py:798
  24.3 4.0 %collective-permute-start.2 = (f32[8,128]{1,0:T(8,128)S(1)}, f32[8,128]{1,0:T(8,128)S(1)}, u32[]{:S(2)}, u32[]{:S(2)}) collective-permute-start(f32[8,128]{1,0:T(8,128)S(1)} %copy-done.4), channel_id=1, source_target_pairs={{0,3},{1,0},{2,1},{3,2},{4,7},{5,4},{6,5},{7,6},{8,11},{9,8},{10,9... | collective-permute-start | bytes 12296 | tf_op jit(solution)/shard_map/ppermute | solution.py:798
  26.5 4.7 %collective-permute-start.1 = (f32[8,128]{1,0:T(8,128)S(1)}, f32[8,128]{1,0:T(8,128)S(1)}, u32[]{:S(2)}, u32[]{:S(2)}) collective-permute-start(f32[8,128]{1,0:T(8,128)S(1)} %copy-done.4), channel_id=1, source_target_pairs={{0,2},{1,3},{2,0},{3,1},{4,6},{5,7},{6,4},{7,5},{8,10},{9,11},{10,... | collective-permute-start | bytes 12296 | tf_op jit(solution)/shard_map/ppermute | solution.py:798
  28.2 3.0 %copy-start.5 = (f32[8,128]{1,0:T(8,128)}, f32[8,128]{1,0:T(8,128)S(1)}, u32[]{:S(2)}) copy-start(f32[8,128]{1,0:T(8,128)S(1)} %collective-permute-done.refs_1_.prev_ref) | copy-start | bytes 12292
  28.2 3.0 %copy-start.6 = (f32[8,128]{1,0:T(8,128)}, f32[8,128]{1,0:T(8,128)S(1)}, u32[]{:S(2)}) copy-start(f32[8,128]{1,0:T(8,128)S(1)} %collective-permute-done.2.refs_3_.next_ref) | copy-start | bytes 12292
  31.2 0.6 copy-start.8
  37.5 18.9 %collective-permute-start.8 = (bf16[1808,128]{1,0:T(8,128)(2,1)}, bf16[1808,128]{1,0:T(8,128)(2,1)S(1)}, u32[]{:S(2)}, u32[]{:S(2)}) collective-permute-start(bf16[1808,128]{1,0:T(8,128)(2,1)} %get-tuple-element.60.after_ref), channel_id=1, source_target_pairs={{0,28},{4,24},{8,20},{12,16},{16,12},{20,8},{24,4},{28,0},{1,29},{... | collective-permute-start | bytes 1388552 | tf_op jit(solution)/shard_map/ppermute | solution.py:806
  37.6 20.9 %collective-permute-start.9 = (bf16[1808,128]{1,0:T(8,128)(2,1)}, bf16[1808,128]{1,0:T(8,128)(2,1)S(1)}, u32[]{:S(2)}, u32[]{:S(2)}) collective-permute-start(bf16[1808,128]{1,0:T(8,128)(2,1)} %get-tuple-element.61), channel_id=1, source_target_pairs={{0,24},{4,28},{8,16},{12,20},{16,8},{20,12},{24,0},{28,4},{1,25},{... | collective-permute-start | bytes 1388552 | tf_op jit(solution)/shard_map/ppermute | solution.py:806
  40.9 22.6 %collective-permute-start.6 = (bf16[96,1536]{1,0:T(8,128)(2,1)}, bf16[96,1536]{1,0:T(8,128)(2,1)S(1)}, u32[]{:S(2)}, u32[]{:S(2)}) collective-permute-start(bf16[96,1536]{1,0:T(8,128)(2,1)} %latent_rest.1.own_ref), channel_id=1, source_target_pairs={{0,1},{1,0},{2,3},{3,2},{4,5},{5,4},{6,7},{7,6},{8,9},{9,8},{10,11... | collective-permute-start | bytes 884744 | tf_op jit(solution)/shard_map/ppermute | solution.py:806
  41.0 22.6 %collective-permute-start.7 = (bf16[96,1536]{1,0:T(8,128)(2,1)}, bf16[96,1536]{1,0:T(8,128)(2,1)S(1)}, u32[]{:S(2)}, u32[]{:S(2)}) collective-permute-start(bf16[96,1536]{1,0:T(8,128)(2,1)} %latent_rest.1.own_ref), channel_id=1, source_target_pairs={{0,2},{1,3},{2,0},{3,1},{4,6},{5,7},{6,4},{7,5},{8,10},{9,11},{10,... | collective-permute-start | bytes 884744 | tf_op jit(solution)/shard_map/ppermute | solution.py:806
  43.8 3.3 %collective-permute-start.3 = (f32[8,128]{1,0:T(8,128)}, f32[8,128]{1,0:T(8,128)S(1)}, u32[]{:S(2)}, u32[]{:S(2)}) collective-permute-start(f32[8,128]{1,0:T(8,128)} %get-tuple-element.48.refs_0_.refs_2_), channel_id=1, source_target_pairs={{0,4},{4,0},{8,12},{12,8},{16,20},{20,16},{24,28},{28,24},{1,5},{5... | collective-permute-start | bytes 12296 | tf_op jit(solution)/shard_map/ppermute | solution.py:806
  47.1 0.6 copy-start.7
  56.3 7.2 %copy-start = (f32[8,128]{1,0:T(8,128)S(1)}, f32[8,128]{1,0:T(8,128)}, u32[]{:S(2)}) copy-start(f32[8,128]{1,0:T(8,128)} %get-tuple-element.48.refs_0_.refs_2_) | copy-start | bytes 12292
  56.4 13.4 %collective-permute-start.10 = (bf16[1808,128]{1,0:T(8,128)(2,1)}, bf16[1808,128]{1,0:T(8,128)(2,1)S(1)}, u32[]{:S(2)}, u32[]{:S(2)}) collective-permute-start(bf16[1808,128]{1,0:T(8,128)(2,1)} %get-tuple-element.66), channel_id=1, source_target_pairs={{0,20},{4,16},{8,28},{12,24},{16,4},{20,0},{24,12},{28,8},{1,21},{... | collective-permute-start | bytes 1388552 | tf_op jit(solution)/shard_map/ppermute | solution.py:806
  56.4 13.6 %collective-permute-start.11 = (bf16[1808,128]{1,0:T(8,128)(2,1)}, bf16[1808,128]{1,0:T(8,128)(2,1)S(1)}, u32[]{:S(2)}, u32[]{:S(2)}) collective-permute-start(bf16[1808,128]{1,0:T(8,128)(2,1)} %get-tuple-element.67), channel_id=1, source_target_pairs={{0,12},{4,8},{8,4},{12,0},{16,28},{20,24},{24,20},{28,16},{1,13},{... | collective-permute-start | bytes 1388552 | tf_op jit(solution)/shard_map/ppermute | solution.py:806
  58.4 11.6 %collective-permute-start.12 = (bf16[1808,128]{1,0:T(8,128)(2,1)}, bf16[1808,128]{1,0:T(8,128)(2,1)S(1)}, u32[]{:S(2)}, u32[]{:S(2)}) collective-permute-start(bf16[1808,128]{1,0:T(8,128)(2,1)} %get-tuple-element.68), channel_id=1, source_target_pairs={{0,4},{4,0},{8,12},{12,8},{16,20},{20,16},{24,28},{28,24},{1,5},{5... | collective-permute-start | bytes 1388552 | tf_op jit(solution)/shard_map/ppermute | solution.py:806
  60.5 9.6 %copy-start.1 = (bf16[16,128]{1,0:T(8,128)(2,1)S(1)}, bf16[16,128]{1,0:T(8,128)(2,1)}, u32[]{:S(2)}) copy-start(bf16[16,128]{1,0:T(8,128)(2,1)} %get-tuple-element.69.refs_7_) | copy-start | bytes 12292
  64.6 9.9 %collective-permute-start.13 = (bf16[96,1536]{1,0:T(8,128)(2,1)}, bf16[96,1536]{1,0:T(8,128)(2,1)S(1)}, u32[]{:S(2)}, u32[]{:S(2)}) collective-permute-start(bf16[96,1536]{1,0:T(8,128)(2,1)} %get-tuple-element.75), channel_id=1, source_target_pairs={{0,1},{1,0},{2,3},{3,2},{4,5},{5,4},{6,7},{7,6},{8,9},{9,8},{10,11... | collective-permute-start | bytes 884744 | tf_op jit(solution)/shard_map/ppermute | solution.py:806
  70.1 0.7 copy-start.2
  74.5 0.7 copy-start.3
Sparse Core Ops, SparseCore 0:
  12.6 48.0 all-gather.1

commit v10 on v9

--- a/solution.py
+++ b/solution.py
@@ -150,7 +150,7 @@
 
 CHUNK = 32
 EXTRA = 16
-MAXIMA_AT = (64, 16)
+MAXIMA_AT = 64
 F32 = jnp.float32
 BF16 = jnp.bfloat16
 VMEM_LIMIT = 56 * 1024 * 1024
@@ -208,10 +208,11 @@
 
 
 def expert_kernel(
-    partners, per_dest, n_alias, n_carry, chunks, n_maxima, owner_ref, pos_ref, step_ref, *refs
+    partners, per_dest, n_alias, n_carry, n_after, chunks, n_maxima,
+    owner_ref, pos_ref, line_ref, step_ref, *refs
 ):
     maxima, refs = refs[:n_maxima], refs[n_maxima:]
-    hbm, refs = refs[:4], refs[4 + n_alias + n_carry :]
+    hbm, refs = refs[:4], refs[4 + n_alias + n_carry + n_after :]
     n_dest = len(partners)
     outs, q_refs, served_ref = refs[:3], refs[3 : 3 + n_dest], refs[3 + n_dest]
     w, m, v, g, extra, in_sem, out_sem, extra_sem = refs[-8:]
@@ -251,7 +252,7 @@
         tops_ref, ext = refs[3 + n_dest + n_carry], refs[-9]
         per_tile = TILE // CHUNK
         for s in range(n_maxima):
-            peer = lax.rem(pos_ref[1] + n_maxima - s, n_maxima)
+            peer = lax.rem(line_ref[0] + n_maxima - s, n_maxima)
             ext[pl.ds(peer * chunks, chunks), :] = maxima[s][0:chunks, :]
         tops_ref[...] = jnp.zeros_like(tops_ref)
         for t in range(n_maxima * chunks // per_tile):
@@ -260,10 +261,9 @@
             )
         maxima = (tops_ref,)
     carried = jnp.zeros((8, TILE), F32)
-    for first, x_ref in zip(MAXIMA_AT, maxima):
-        for p, value in enumerate(three_parts(x_ref[...])):
-            at = first + 16 * p
-            carried = jnp.where((lane >= at) & (lane < at + 16), pltpu.roll(value, at, 1), carried)
+    for p, value in enumerate(three_parts(maxima[0][...])):
+        at = MAXIMA_AT + 16 * p
+        carried = jnp.where((lane >= at) & (lane < at + 16), pltpu.roll(value, at, 1), carried)
     extras = []
     for d, k in enumerate(partners):
         side = carried
@@ -300,20 +300,24 @@
     wait_all(extras)
 
 
-def expert_group(arrays, state, owner, pos, step, maxima, chunks, carry, partners, per_dest):
+def expert_group(
+    arrays, state, owner, pos, line, step, maxima, chunks, carry, after, partners, per_dest
+):
     rows, cols = arrays[0].shape
     n_alias, n_maxima = len(state), len(maxima)
     n = len(partners) * per_dest
     elems = rows * TILE * n
     flat = [jax.ShapeDtypeStruct((8, TILE), F32)] * (chunks > 0)
-    first = 7 + n_maxima
+    first = 8 + n_maxima
     aliases = {first + i: i for i in range(n_alias)}
     aliases.update({first + n_alias + i: 3 + len(partners) + i for i in range(len(carry))})
     out = pl.pallas_call(
         functools.partial(
-            expert_kernel, partners, per_dest, n_alias, len(carry), chunks, n_maxima
+            expert_kernel, partners, per_dest, n_alias, len(carry), len(after), chunks, n_maxima
         ),
-        in_specs=[SMEM] * 3 + [VMEM] * n_maxima + [ANY] * (4 + n_alias + len(carry)),
+        in_specs=[SMEM] * 4
+        + [VMEM] * n_maxima
+        + [ANY] * (4 + n_alias + len(carry) + len(after)),
         out_specs=[ANY] * (3 + len(partners) + len(carry)) + [VMEM] * len(flat),
         out_shape=[
             jax.ShapeDtypeStruct((rows, cols), F32),
@@ -341,7 +345,7 @@
         compiler_params=PARAMS,
         cost_estimate=pl.CostEstimate(flops=elems, bytes_accessed=elems, transcendentals=0),
         name="expert_adamw",
-    )(owner, pos, step, *maxima, *arrays, *state, *carry)
+    )(owner, pos, line, step, *maxima, *arrays, *state, *carry, *after)
     return out[:3], out[3 : 3 + len(partners)], out[3 + len(partners) :]
 
 
@@ -356,8 +360,7 @@
 
 def place_kernel(partners, pos_ref, *refs):
     n = len(partners)
-    served, token, sem = refs[-3:]
-    token[...] = jnp.zeros_like(token)
+    served, sem = refs[-2:]
     copies = block_copies(served, refs[:n], [pos_ref[0] ^ k for k in partners], sem)
     copy_all(copies)
     wait_all(copies)
@@ -368,8 +371,8 @@
     return pl.pallas_call(
         functools.partial(place_kernel, partners),
         in_specs=[SMEM] + [ANY] * (n + len(served)),
-        out_specs=[ANY, VMEM],
-        out_shape=[jax.ShapeDtypeStruct(shape, BF16), jax.ShapeDtypeStruct((8, TILE), F32)],
+        out_specs=ANY,
+        out_shape=jax.ShapeDtypeStruct(shape, BF16),
         scratch_shapes=[pltpu.SemaphoreType.DMA((n, shape[0]))],
         input_output_aliases={1 + n: 0} if served else {},
         compiler_params=LIGHT,
@@ -380,10 +383,10 @@
     )(pos, *payloads, *served)
 
 
-def collect_kernel(order, tiles, lat_tiles, to_place, groups, pos_ref, after_ref, *refs):
+def collect_kernel(order, tiles, lat_tiles, to_place, pos_ref, *refs):
     n = len(order)
     q_refs = refs[:n]
-    served, exp_ref, lat_ref, extra, rows_ref, place_sem, sem = refs[n + 1 :]
+    served, _, exp_ref, lat_ref, extra, rows_ref, place_sem, sem = refs[n + 2 :]
     pos = pos_ref[0]
     per_dest = served.shape[0]
     blocks_copies = block_copies(
@@ -405,10 +408,8 @@
         copies[i].wait()
         src = pos ^ k
         x = extra[i].astype(F32)[0:8, :]
-        known = (src, src ^ 1) if k in groups[2] else (src,) if k in groups[1] else ()
-        for first, peer in zip(MAXIMA_AT, known):
-            lat = sum(pltpu.roll(x, TILE - first - 16 * p, 1) for p in range(3))
-            rows_ref[pl.ds(peer * lat_tiles, lat_tiles), :] = lat[0:lat_tiles, :]
+        lat = sum(pltpu.roll(x, TILE - MAXIMA_AT - 16 * p, 1) for p in range(3))
+        rows_ref[pl.ds(src * lat_tiles, lat_tiles), :] = lat[0:lat_tiles, :]
         for j in range(per_dest):
             first = 3 * j
             top = x[:, first : first + 1] + x[:, first + 1 : first + 2] + x[:, first + 2 : first + 3]
@@ -420,17 +421,18 @@
     wait_all(blocks_copies)
 
 
-def collect(served, pos, after, received, groups, tiles, lat_tiles, lat_blocks):
+def collect(served, through, pos, received, groups, tiles, lat_tiles, lat_blocks):
     order = [k for partners in groups for k in partners]
     n = len(order)
     per_dest = served.shape[0]
     to_place = [i for i, k in enumerate(order) if k in groups[2] and k]
-    served, expert, latent = pl.pallas_call(
-        functools.partial(collect_kernel, order, tiles, lat_tiles, to_place, groups),
-        in_specs=[SMEM, VMEM] + [ANY] * (n + 1),
-        out_specs=[ANY, VMEM, VMEM],
+    served, through, expert, latent = pl.pallas_call(
+        functools.partial(collect_kernel, order, tiles, lat_tiles, to_place),
+        in_specs=[SMEM] + [ANY] * (n + 2),
+        out_specs=[ANY, ANY, VMEM, VMEM],
         out_shape=[
             jax.ShapeDtypeStruct(served.shape, served.dtype),
+            jax.ShapeDtypeStruct(through.shape, through.dtype),
             jax.ShapeDtypeStruct((1, per_dest * n * tiles), F32),
             jax.ShapeDtypeStruct((lat_blocks, n * lat_tiles), F32),
         ],
@@ -440,17 +442,17 @@
             pltpu.SemaphoreType.DMA((len(to_place), per_dest)),
             pltpu.SemaphoreType.DMA((n,)),
         ],
-        input_output_aliases={2 + n: 0},
+        input_output_aliases={1 + n: 0, 2 + n: 1},
         compiler_params=LIGHT,
         cost_estimate=pl.CostEstimate(flops=1000000, bytes_accessed=1000000, transcendentals=0),
         name="place_last",
-    )(pos, after, *received, served)
-    return served, expert, latent.T
+    )(pos, *received, served, through)
+    return served, through, expert, latent.T
 
 
 def finish_kernel(deltas, rows, pos_ref, *refs):
     n = len(deltas)
-    latent, buf, in_sem, out_sem = refs[n + 2 :]
+    latent, buf, in_sem, out_sem = refs[n + 1 :]
     loads = [pltpu.make_async_copy(refs[i], buf.at[i], in_sem.at[i]) for i in range(n)]
     copy_all(loads)
     copies = []
@@ -462,12 +464,12 @@
     wait_all(copies)
 
 
-def finish(latent, pos, rest, deltas, after):
+def finish(latent, pos, rest, deltas):
     n = len(rest)
     span, cols = rest[0].shape
     return pl.pallas_call(
         functools.partial(finish_kernel, deltas, TILE + span),
-        in_specs=[SMEM] + [ANY] * (n + 2),
+        in_specs=[SMEM] + [ANY] * (n + 1),
         out_specs=ANY,
         out_shape=jax.ShapeDtypeStruct(latent.shape, latent.dtype),
         scratch_shapes=[
@@ -479,7 +481,7 @@
         compiler_params=pltpu.CompilerParams(vmem_limit_bytes=4 * 1024 * 1024),
         cost_estimate=pl.CostEstimate(flops=0, bytes_accessed=1000000, transcendentals=0),
         name="place_finish",
-    )(pos, *rest, latent, after)
+    )(pos, *rest, latent)
 
 
 def whole_tile(pos, rows):
@@ -487,8 +489,7 @@
 
 
 def full_kernel(pieces, rows, pos_ref, x_ref, own_ref, *refs):
-    out_ref, token, buf, own, in_sem, out_sem, own_in, own_out = refs[1:]
-    token[...] = jnp.zeros_like(token)
+    out_ref, buf, own, in_sem, out_sem, own_in, own_out = refs[1:]
     loads, stores = [], []
     for i in range(pieces):
         lead = i * (TILE - rows % TILE) % TILE
@@ -515,11 +516,8 @@
     return pl.pallas_call(
         functools.partial(full_kernel, pieces, rows),
         in_specs=[SMEM] + [ANY] * 3,
-        out_specs=[ANY, VMEM],
-        out_shape=[
-            jax.ShapeDtypeStruct((pieces * rows, x.shape[1]), BF16),
-            jax.ShapeDtypeStruct((8, TILE), F32),
-        ],
+        out_specs=ANY,
+        out_shape=jax.ShapeDtypeStruct((pieces * rows, x.shape[1]), BF16),
         scratch_shapes=[
             pltpu.VMEM(x.shape, BF16),
             pltpu.VMEM((1,) + own.shape, BF16),
@@ -552,7 +550,7 @@
 
 def hop_kernel(deltas, rows, pos_ref, *refs):
     n = len(deltas)
-    out_ref, again_ref, buf, in_sem, out_sem = refs[-5:]
+    out_ref, again_ref, _, buf, in_sem, out_sem = refs[-6:]
     loads = [pltpu.make_async_copy(refs[i], buf.at[i], in_sem.at[i]) for i in range(n)]
     copy_all(loads)
     copies = [pltpu.make_async_copy(buf.at[n - 1], again_ref, in_sem.at[n])]
@@ -564,17 +562,19 @@
     wait_all(copies)
 
 
-def place_and_pass(pos, xs, deltas, after, rows, peers):
+def place_and_pass(pos, xs, deltas, through, rows, peers):
     span, cols = xs[0].shape
     n = len(xs)
     return pl.pallas_call(
         functools.partial(hop_kernel, deltas, rows),
-        in_specs=[SMEM] + [ANY] * n + [VMEM] * len(after),
-        out_specs=[ANY, ANY],
+        in_specs=[SMEM] + [ANY] * (n + 1),
+        out_specs=[ANY] * 3,
         out_shape=[
             jax.ShapeDtypeStruct((peers * rows, cols), BF16),
             jax.ShapeDtypeStruct((span, cols), BF16),
+            jax.ShapeDtypeStruct(through.shape, through.dtype),
         ],
+        input_output_aliases={1 + n: 2},
         scratch_shapes=[
             pltpu.VMEM((n, span, cols), BF16),
             pltpu.SemaphoreType.DMA((n + 1,)),
@@ -583,10 +583,10 @@
         compiler_params=pltpu.CompilerParams(vmem_limit_bytes=4 * 1024 * 1024),
         cost_estimate=pl.CostEstimate(flops=0, bytes_accessed=6 * span * cols, transcendentals=0),
         name="place_hop",
-    )(pos, *xs, *after)
-
-
-SLABS = 6
+    )(pos, *xs, through)
+
+
+SLABS = 4
 
 
 def latent_kernel(chunks, step_ref, pos_ref, *refs):
@@ -762,7 +762,7 @@
 
 def partner_groups(dp_count):
     hops = lambda k: bin(k >> 1).count("1")
-    stage = lambda k: 3 if k < 2 else (1 if hops(k) > 1 else (2 if k & 1 else 0))
+    stage = lambda k: 2 if k & 1 and hops(k) < 2 else (3 if k == 0 else hops(k) - 1)
     order = sorted(range(dp_count), key=lambda k: (stage(k), -k))
     return [[k for k in order if stage(k) in n] for n in ((0,), (1,), (2, 3))]
 
@@ -807,52 +807,59 @@
 
     groups = partner_groups(dp_count)
     order = [k for partners in groups for k in partners]
-    both_at = jnp.concatenate([dp_at, expert_at])
     send = lambda sent, partners: [swap(q, "dp", k) if k else q for k, q in zip(partners, sent)]
-    group = functools.partial(expert_group, arrays, owner=column_owner, pos=both_at, step=step_count)
+    group = functools.partial(
+        expert_group,
+        arrays,
+        owner=column_owner,
+        pos=dp_at,
+        line=expert_at,
+        step=step_count,
+        per_dest=per_dest,
+    )
     chunks = latent_rows // CHUNK
+    state, sent, (tops,) = group(
+        state=(), maxima=maxima, chunks=chunks, carry=(), after=(), partners=groups[0]
+    )
+    received = send(sent, groups[0])
     state, sent, _ = group(
-        state=(), maxima=(), chunks=0, carry=(), partners=groups[0], per_dest=per_dest
-    )
-    received = send(sent, groups[0])
-    state, sent, (tops,) = group(
-        state=state, maxima=maxima, chunks=chunks, carry=(), partners=groups[1], per_dest=per_dest
+        state=state, maxima=(tops,), chunks=0, carry=(), after=(), partners=groups[1]
     )
     received += send(sent, groups[1])
     rest = latent_rest(latent_new, chunk_top, maxima[1], maxima[-1], expert_at, sent[0])
     far, near = swap(rest, "expert", 2), swap(rest, "expert", 1)
-    served, _ = place_blocks(
-        (), dp_at, received[: len(groups[0])], groups[0], (per_dest, dp_count, rows, TILE)
+    first, count = len(groups[0]), len(received)
+    served = place_blocks(
+        (), dp_at, received[:first], groups[0], (per_dest, dp_count, rows, TILE)
     )
     state, sent, (served,) = group(
         state=state,
-        maxima=[tops, swap(tops, "dp", 1)],
+        maxima=(tops,),
         chunks=0,
         carry=(served,),
+        after=(),
         partners=groups[2],
-        per_dest=per_dest,
     )
     received += send(sent, groups[2])
-    first, count = len(groups[0]), len(groups[0]) + len(groups[1])
-    served, token = place_blocks(
+    served = place_blocks(
         (served,), dp_at, received[first:count], groups[1], served.shape
     )
-    latent_served, far_again = place_and_pass(
-        expert_at, [near, far], [1, 2], (tops, token), latent_rows, exp_axis
+    latent_served, far_again, served = place_and_pass(
+        expert_at, [near, far], [1, 2], served, latent_rows, exp_axis
     )
     last = swap(far_again, "expert", 1)
-    latent_served, token = place_full(latent_served, expert_at, whole, rest, latent_rows)
-    served, expert_scales, latent_scales = collect(
+    latent_served = place_full(latent_served, expert_at, whole, rest, latent_rows)
+    served, latent_served, expert_scales, latent_scales = collect(
         served,
+        latent_served,
         dp_at,
-        token,
         received,
         groups,
         tiles,
         latent_rows * exp_axis // TILE,
         latent_new.shape[1] // TILE,
     )
-    latent_served = finish(latent_served, expert_at, [last], [3], expert_scales)
+    latent_served = finish(latent_served, expert_at, [last], [3])
     expert_served = served.reshape(1, block_count * rows, TILE)
 
     return (

time: 83.3 us -> 82.1 us (0.986)
  waiting for transfers between devices: 10.1 us -> 14.3 us
  local copies, waits for them, and re-layouts: 2.53 us -> 0.6 us
  Pallas kernels: 36.1 us -> 34.6 us
  starting transfers between devices: 18.7 us -> 17.4 us
    ppermute x11 -> x10, waiting for transfers between devices: 6.15 us -> 10.5 us  [swap(): lax.ppermute(x, axis, [(i, i ^ k) for i in range(lax.axis_size(axis))])]
    ppermute x11 -> x10, starting transfers between devices: 14 us -> 11.3 us  [swap(): lax.ppermute(x, axis, [(i, i ^ k) for i in range(lax.axis_size(axis))])]
    unnamed x18 -> x8, local copies, waits for them, and re-layouts: 2.53 us -> 0.6 us
    ppermute x3, starting transfers between devices: 4.61 us -> 6.11 us  [fast_body(): lax.ppermute(chunk_top, 'expert', [(i, (i + s) % exp_axis) for i in range...]
  transfers between devices with their start and end apart: 15 -> 14, of which waited for: 6 -> 5; matrix products, arithmetic and copies ran while one was open for 1% -> 0% of each run, Pallas kernels for 37% -> 36%
where the time goes in v10:
time: 82.1 us; the launch traced here: 81.8 us
  Pallas kernels  34.6 us (42%)
  starting transfers between devices  17.4 us (21%)
  between operations  14.8 us (18%)
  waiting for transfers between devices  14.3 us (17%)
    pallas_call x3, Pallas kernels, expert_group(): pl.pallas_call(functools.partial(expert_kernel, partners, per_dest, n_ali...  19.4 us
    ppermute x10, starting transfers between devices, swap(): lax.ppermute(x, axis, [(i, i ^ k) for i in range(lax.axis_size(axis))])  11.3 us
    ppermute x10, waiting for transfers between devices, swap(): lax.ppermute(x, axis, [(i, i ^ k) for i in range(lax.axis_size(axis))])  10.5 us
    ppermute x3, starting transfers between devices, fast_body(): lax.ppermute(chunk_top, 'expert', [(i, (i + s) % exp_axis) for i in range...  6.11 us
    pallas_call x1, Pallas kernels, latent_update(): pl.pallas_call(functools.partial(latent_kernel, rows // CHUNK), in_specs=...  4.32 us
    ppermute x3, waiting for transfers between devices, fast_body(): lax.ppermute(chunk_top, 'expert', [(i, (i + s) % exp_axis) for i in range...  3.76 us
    pallas_call x1, Pallas kernels, latent_rest(): pl.pallas_call(functools.partial(latent_rest_kernel, chunks), in_specs=[S...  2.76 us
    pallas_call x1, Pallas kernels, place_full(): pl.pallas_call(functools.partial(full_kernel, pieces, rows), in_specs=[SM...  2.33 us
  transfers between devices with their start and end apart: 14, of which 5 were waited for; matrix products, arithmetic and copies ran while one was open for 0% of the time, Pallas kernels for 36%

profile of v10, /device:TPU:0, one launch (start us, length us, event | category | flops | bytes accessed | tf_op | source)
XLA Modules:
  0.0 81.8 jit_solution(7931866203065112579)
XLA Ops:
  7.2 0.0 all-gather.2.cloned.1.call-start
  7.9 4.3 %latent_adamw.1 = (f32[224,1536]{1,0:T(8,128)}, bf16[224,1536]{1,0:T(8,128)(2,1)}, bf16[224,1536]{1,0:T(8,128)(2,1)}, bf16[128,1536]{1,0:T(8,128)(2,1)}, f32[8,128]{1,0:T(8,128)}) custom-call(s32[1]{0:T(128)S(6)} %copy.46.step_ref, s32[1]{0:T(128)} %bitcast.1.pos_ref.line_ref, f32[224,1536]{1,0:T(8,128)} %refs_0_.1, bf16[224,1536]{1,0:T(8,128)(2,1)} %refs_1_.1, ...), custom_call_target="tpu_custom_call" | custom-call | flops 10321920 | bytes 6193152 | tf_op jit(solution)/shard_map/latent_adamw/pallas_call | solution.py:644
  12.2 0.0 all-gather.2.cloned.1.call-update
  12.2 3.1 %collective-permute-start = (f32[8,128]{1,0:T(8,128)}, f32[8,128]{1,0:T(8,128)S(1)}, u32[]{:S(2)}, u32[]{:S(2)}) collective-permute-start(f32[8,128]{1,0:T(8,128)} %get-tuple-element.41.refs_0_.own_ref), channel_id=1, source_target_pairs={{0,1},{1,2},{2,3},{3,0},{4,5},{5,6},{6,7},{7,4},{8,9},{9,10},{10,1... | collective-permute-start | bytes 12296 | tf_op jit(solution)/shard_map/ppermute | solution.py:798
  15.3 2.1 %collective-permute-start.2 = (f32[8,128]{1,0:T(8,128)}, f32[8,128]{1,0:T(8,128)S(1)}, u32[]{:S(2)}, u32[]{:S(2)}) collective-permute-start(f32[8,128]{1,0:T(8,128)} %get-tuple-element.41.refs_0_.own_ref), channel_id=1, source_target_pairs={{0,3},{1,0},{2,1},{3,2},{4,7},{5,4},{6,5},{7,6},{8,11},{9,8},{10,9... | collective-permute-start | bytes 12296 | tf_op jit(solution)/shard_map/ppermute | solution.py:798
  17.4 0.9 %collective-permute-start.1 = (f32[8,128]{1,0:T(8,128)}, f32[8,128]{1,0:T(8,128)S(1)}, u32[]{:S(2)}, u32[]{:S(2)}) collective-permute-start(f32[8,128]{1,0:T(8,128)} %get-tuple-element.41.refs_0_.own_ref), channel_id=1, source_target_pairs={{0,2},{1,3},{2,0},{3,1},{4,6},{5,7},{6,4},{7,5},{8,10},{9,11},{10,... | collective-permute-start | bytes 12296 | tf_op jit(solution)/shard_map/ppermute | solution.py:798
  18.3 0.8 %collective-permute-done.refs_1_.prev_ref = f32[8,128]{1,0:T(8,128)S(1)} collective-permute-done((f32[8,128]{1,0:T(8,128)}, f32[8,128]{1,0:T(8,128)S(1)}, u32[]{:S(2)}, u32[]{:S(2)}) %collective-permute-start) | collective-permute-done | bytes 4128 | tf_op jit(solution)/shard_map/ppermute | solution.py:798
  19.2 0.0 copy-start.1
  19.2 0.0 collective-permute-done.2.refs_3_.next_ref
  19.2 0.0 copy-start.2
  19.2 2.9 %collective-permute-done.1.refs_2_ = f32[8,128]{1,0:T(8,128)S(1)} collective-permute-done((f32[8,128]{1,0:T(8,128)}, f32[8,128]{1,0:T(8,128)S(1)}, u32[]{:S(2)}, u32[]{:S(2)}) %collective-permute-start.1) | collective-permute-done | bytes 4128 | tf_op jit(solution)/shard_map/ppermute | solution.py:798
  22.1 0.0 copy-start.3
  22.1 0.0 copy-done.1
  22.1 0.0 copy-done.2
  22.1 0.6 copy-done.3
  22.7 5.7 %expert_adamw.3 = (f32[896,2048]{1,0:T(8,128)}, bf16[896,2048]{1,0:T(8,128)(2,1)}, bf16[896,2048]{1,0:T(8,128)(2,1)}, bf16[1808,128]{1,0:T(8,128)(2,1)}, bf16[1808,128]{1,0:T(8,128)(2,1)}, /*index=5*/f32[8,128]{1,0:T(8,128)}) custom-call(s32[16]{0:T(128)} %owner_ref.5, s32[1]{0:T(128)} %bitcast.pos_ref, s32[1]{0:T(128)} %bitcast.1.pos_ref.line_ref, ...), custom_call_target="tpu_custom_call" | custom-call | flops 458752 | bytes 458752 | tf_op jit(solution)/shard_map/expert_adamw/pallas_call | solution.py:314
  28.4 1.7 %collective-permute-start.3 = (bf16[1808,128]{1,0:T(8,128)(2,1)}, bf16[1808,128]{1,0:T(8,128)(2,1)S(1)}, u32[]{:S(2)}, u32[]{:S(2)}) collective-permute-start(bf16[1808,128]{1,0:T(8,128)(2,1)} %get-tuple-element.49), channel_id=1, source_target_pairs={{0,16},{4,20},{8,24},{12,28},{16,0},{20,4},{24,8},{28,12},{1,17},{... | collective-permute-start | bytes 1388552 | tf_op jit(solution)/shard_map/ppermute | solution.py:806
  30.1 1.5 %collective-permute-start.4 = (bf16[1808,128]{1,0:T(8,128)(2,1)}, bf16[1808,128]{1,0:T(8,128)(2,1)S(1)}, u32[]{:S(2)}, u32[]{:S(2)}) collective-permute-start(bf16[1808,128]{1,0:T(8,128)(2,1)} %get-tuple-element.50), channel_id=1, source_target_pairs={{0,8},{4,12},{8,0},{12,4},{16,24},{20,28},{24,16},{28,20},{1,9},{5... | collective-permute-start | bytes 1388552 | tf_op jit(solution)/shard_map/ppermute | solution.py:806
  31.6 5.1 %expert_adamw.4 = (f32[896,2048]{1,0:T(8,128)}, bf16[896,2048]{1,0:T(8,128)(2,1)}, bf16[896,2048]{1,0:T(8,128)(2,1)}, bf16[1808,128]{1,0:T(8,128)(2,1)}, bf16[1808,128]{1,0:T(8,128)(2,1)}) custom-call(s32[16]{0:T(128)} %owner_ref.5, s32[1]{0:T(128)} %bitcast.pos_ref, ...), custom_call_target="tpu_custom_call", output_to_operand_aliasing={{0}: (9, {}), {1}: (10, {}), {2}: (11, {})} | custom-call | flops 458752 | bytes 458752 | tf_op jit(solution)/shard_map/expert_adamw/pallas_call | solution.py:314
  36.7 0.1 collective-permute-start.5
  36.8 0.5 collective-permute-start.6
  37.2 2.8 %latent_rest.1.own_ref = bf16[96,1536]{1,0:T(8,128)(2,1)} custom-call(s32[1]{0:T(128)} %bitcast.1.pos_ref.line_ref, f32[224,1536]{1,0:T(8,128)} %get-tuple-element.36.w1_ref, f32[8,128]{1,0:T(8,128)} %get-tuple-element.41.refs_0_.own_ref, f32[8,128]{1,0:T(8,128)} %copy-done.1, f32[8,128]{1,0:T(8,128)} %copy-done.2, bf16[1808,128]{1,0:T(8,128)(2,1)} %get-tuple-element.54.after_ref), custom_call_target="tpu_custom_call" | custom-call | flops 344064 | bytes 1032192 | tf_op jit(solution)/shard_map/latent_rest/pallas_call | solution.py:722
  40.0 0.2 collective-permute-start.10
  40.2 0.0 collective-permute-done.3.refs_0_
  40.2 2.5 %collective-permute-start.11 = (bf16[96,1536]{1,0:T(8,128)(2,1)}, bf16[96,1536]{1,0:T(8,128)(2,1)S(1)}, u32[]{:S(2)}, u32[]{:S(2)}) collective-permute-start(bf16[96,1536]{1,0:T(8,128)(2,1)} %latent_rest.1.own_ref), channel_id=1, source_target_pairs={{0,2},{1,3},{2,0},{3,1},{4,6},{5,7},{6,4},{7,5},{8,10},{9,11},{10,... | collective-permute-start | bytes 884744 | tf_op jit(solution)/shard_map/ppermute | solution.py:806
  42.7 0.0 collective-permute-done.4.refs_1_
  42.7 0.9 %place_served.2.refs_8_ = bf16[2,8,896,128]{3,2,1,0:T(8,128)(2,1)} custom-call(s32[1]{0:T(128)} %bitcast.pos_ref, bf16[1808,128]{1,0:T(8,128)(2,1)S(1)} %collective-permute-done.3.refs_0_, bf16[1808,128]{1,0:T(8,128)(2,1)S(1)} %collective-permute-done.4.refs_1_), custom_call_target="tpu_custom_call" | custom-call | bytes 1851392 | tf_op jit(solution)/shard_map/place_served/pallas_call | solution.py:371
  43.6 8.7 %expert_adamw.5 = (f32[896,2048]{1,0:T(8,128)}, bf16[896,2048]{1,0:T(8,128)(2,1)}, bf16[896,2048]{1,0:T(8,128)(2,1)}, bf16[1808,128]{1,0:T(8,128)(2,1)}, bf16[18...) custom-call(s32[16]{0:T(128)} %owner_ref.5, ...), custom_call_target="tpu_custom_call", output_to_operand_aliasing={{0}: (9, {}), {1}: (10, {}), {2}: (11, {}), {7}: (12, {})} | custom-call | flops 917504 | bytes 917504 | tf_op jit(solution)/shard_map/expert_adamw/pallas_call | solution.py:314
  52.3 1.8 %collective-permute-start.7 = (bf16[1808,128]{1,0:T(8,128)(2,1)}, bf16[1808,128]{1,0:T(8,128)(2,1)S(1)}, u32[]{:S(2)}, u32[]{:S(2)}) collective-permute-start(bf16[1808,128]{1,0:T(8,128)(2,1)} %get-tuple-element.56), channel_id=1, source_target_pairs={{0,20},{4,16},{8,28},{12,24},{16,4},{20,0},{24,12},{28,8},{1,21},{... | collective-permute-start | bytes 1388552 | tf_op jit(solution)/shard_map/ppermute | solution.py:806
  54.1 0.0 collective-permute-done.5.refs_0_.refs_2_
  54.1 1.0 %collective-permute-start.8 = (bf16[1808,128]{1,0:T(8,128)(2,1)}, bf16[1808,128]{1,0:T(8,128)(2,1)S(1)}, u32[]{:S(2)}, u32[]{:S(2)}) collective-permute-start(bf16[1808,128]{1,0:T(8,128)(2,1)} %get-tuple-element.57), channel_id=1, source_target_pairs={{0,12},{4,8},{8,4},{12,0},{16,28},{20,24},{24,20},{28,16},{1,13},{... | collective-permute-start | bytes 1388552 | tf_op jit(solution)/shard_map/ppermute | solution.py:806
  55.1 7.2 %collective-permute-done.6.refs_1_.refs_3_ = bf16[1808,128]{1,0:T(8,128)(2,1)S(1)} collective-permute-done((bf16[1808,128]{1,0:T(8,128)(2,1)}, bf16[1808,128]{1,0:T(8,128)(2,1)S(1)}, u32[]{:S(2)}, u32[]{:S(2)}) %collective-permute-start.6) | collective-permute-done | bytes 462880 | tf_op jit(solution)/shard_map/ppermute | solution.py:806
  62.3 0.0 collective-permute-start.9
  62.3 0.9 %place_served.3.refs_2_ = bf16[2,8,896,128]{3,2,1,0:T(8,128)(2,1)} custom-call(s32[1]{0:T(128)} %bitcast.pos_ref, bf16[1808,128]{1,0:T(8,128)(2,1)S(1)} %collective-permute-done.5.refs_0_.refs_2_, bf16[1808,128]{1,0:T(8,128)(2,1)S(1)} %collective-permute-done.6.refs_1_.refs_3_, ...), custom_call_target="tpu_custom_call", output_to_operand_aliasing={{}: (3, {})} | custom-call | bytes 1851392 | tf_op jit(solution)/shard_map/place_served/pallas_call | solution.py:371
  63.2 0.0 collective-permute-done.10.refs_0_
  63.3 0.0 collective-permute-done.11.refs_1_
  63.3 1.1 %place_hop.1 = (bf16[896,1536]{1,0:T(8,128)(2,1)}, bf16[96,1536]{1,0:T(8,128)(2,1)}, bf16[2,8,896,128]{3,2,1,0:T(8,128)(2,1)}) custom-call(s32[1]{0:T(128)} %bitcast.1.pos_ref.line_ref, bf16[96,1536]{1,0:T(8,128)(2,1)S(1)} %collective-permute-done.10.refs_0_, bf16[96,1536]{1,0:T(8,128)(2,1)S(1)} %collective-permute-done.11.refs_1_, ...), custom_call_target="tpu_custom_call", output_to_operand_aliasing={{2}: (3, {})} | custom-call | bytes 884736 | tf_op jit(solution)/shard_map/place_hop/pallas_call | solution.py:568
  64.4 2.1 %collective-permute-start.12 = (bf16[96,1536]{1,0:T(8,128)(2,1)}, bf16[96,1536]{1,0:T(8,128)(2,1)S(1)}, u32[]{:S(2)}, u32[]{:S(2)}) collective-permute-start(bf16[96,1536]{1,0:T(8,128)(2,1)} %get-tuple-element.69), channel_id=1, source_target_pairs={{0,1},{1,0},{2,3},{3,2},{4,5},{5,4},{6,7},{7,6},{8,9},{9,8},{10,11... | collective-permute-start | bytes 884744 | tf_op jit(solution)/shard_map/ppermute | solution.py:806
  66.5 0.0 all-gather.2.cloned.1.call-done.x_ref
  66.5 0.0 copy-start
  66.5 2.3 %place_whole.1.refs_9_ = bf16[896,1536]{1,0:T(8,128)(2,1)} custom-call(s32[1]{0:T(128)} %bitcast.1.pos_ref.line_ref, bf16[512,1536]{1,0:T(8,128)(2,1)} %all-gather.2.cloned.1.call-done.x_ref, bf16[96,1536]{1,0:T(8,128)(2,1)} %latent_rest.1.own_ref, bf16[896,1536]{1,0:T(8,128)(2,1)} %get-tuple-element.64.refs_0_), custom_call_target="tpu_custom_call", output_to_operand_aliasing={{}: (3, {})} | custom-call | bytes 3145728 | tf_op jit(solution)/shard_map/place_whole/pallas_call | solution.py:516
  68.8 1.8 %collective-permute-done.7.refs_4_ = bf16[1808,128]{1,0:T(8,128)(2,1)S(1)} collective-permute-done((bf16[1808,128]{1,0:T(8,128)(2,1)}, bf16[1808,128]{1,0:T(8,128)(2,1)S(1)}, u32[]{:S(2)}, u32[]{:S(2)}) %collective-permute-start.7) | collective-permute-done | bytes 462880 | tf_op jit(solution)/shard_map/ppermute | solution.py:806
  70.7 0.0 collective-permute-done.8.refs_5_
  70.7 0.0 collective-permute-done.9.refs_6_
  70.7 0.0 copy-done
  70.7 2.0 %place_last.1 = (bf16[2,8,896,128]{3,2,1,0:T(8,128)(2,1)}, bf16[896,1536]{1,0:T(8,128)(2,1)}, f32[1,112]{1,0:T(1,128)}, f32[12,56]{1,0:T(8,128)}) custom-call(s32[1]{0:T(128)} %bitcast.pos_ref, bf16[1808,128]{1,0:T(8,128)(2,1)S(1)} %collective-permute-done.3.refs_0_, ...), custom_call_target="tpu_custom_call", output_to_operand_aliasing={{0}: (9, {}), {1}: (10, {})} | custom-call | flops 1000000 | bytes 1000000 | tf_op jit(solution)/shard_map/place_last/pallas_call | solution.py:429
  72.6 1.5 %collective-permute-done.12.refs_0_ = bf16[96,1536]{1,0:T(8,128)(2,1)S(1)} collective-permute-done((bf16[96,1536]{1,0:T(8,128)(2,1)}, bf16[96,1536]{1,0:T(8,128)(2,1)S(1)}, u32[]{:S(2)}, u32[]{:S(2)}) %collective-permute-start.12) | collective-permute-done | bytes 294944 | tf_op jit(solution)/shard_map/ppermute | solution.py:806
  74.1 0.8 place_finish.1
Async XLA Ops:
  7.2 59.3 %all-gather.2.cloned.1.call-start = ((), (), s32[]{:S(2)}) async-start(), calls=%async_computation | async-start | bytes 1966080 | tf_op jit(solution)/shard_map/all_gather | solution.py:796
  12.2 6.9 %collective-permute-start = (f32[8,128]{1,0:T(8,128)}, f32[8,128]{1,0:T(8,128)S(1)}, u32[]{:S(2)}, u32[]{:S(2)}) collective-permute-start(f32[8,128]{1,0:T(8,128)} %get-tuple-element.41.refs_0_.own_ref), channel_id=1, source_target_pairs={{0,1},{1,2},{2,3},{3,0},{4,5},{5,6},{6,7},{7,4},{8,9},{9,10},{10,1... | collective-permute-start | bytes 12296 | tf_op jit(solution)/shard_map/ppermute | solution.py:798
  15.3 3.9 %collective-permute-start.2 = (f32[8,128]{1,0:T(8,128)}, f32[8,128]{1,0:T(8,128)S(1)}, u32[]{:S(2)}, u32[]{:S(2)}) collective-permute-start(f32[8,128]{1,0:T(8,128)} %get-tuple-element.41.refs_0_.own_ref), channel_id=1, source_target_pairs={{0,3},{1,0},{2,1},{3,2},{4,7},{5,4},{6,5},{7,6},{8,11},{9,8},{10,9... | collective-permute-start | bytes 12296 | tf_op jit(solution)/shard_map/ppermute | solution.py:798
  17.4 4.7 %collective-permute-start.1 = (f32[8,128]{1,0:T(8,128)}, f32[8,128]{1,0:T(8,128)S(1)}, u32[]{:S(2)}, u32[]{:S(2)}) collective-permute-start(f32[8,128]{1,0:T(8,128)} %get-tuple-element.41.refs_0_.own_ref), channel_id=1, source_target_pairs={{0,2},{1,3},{2,0},{3,1},{4,6},{5,7},{6,4},{7,5},{8,10},{9,11},{10,... | collective-permute-start | bytes 12296 | tf_op jit(solution)/shard_map/ppermute | solution.py:798
  19.2 3.0 %copy-start.1 = (f32[8,128]{1,0:T(8,128)}, f32[8,128]{1,0:T(8,128)S(1)}, u32[]{:S(2)}) copy-start(f32[8,128]{1,0:T(8,128)S(1)} %collective-permute-done.refs_1_.prev_ref) | copy-start | bytes 12292
  19.2 2.9 %copy-start.2 = (f32[8,128]{1,0:T(8,128)}, f32[8,128]{1,0:T(8,128)S(1)}, u32[]{:S(2)}) copy-start(f32[8,128]{1,0:T(8,128)S(1)} %collective-permute-done.2.refs_3_.next_ref) | copy-start | bytes 12292
  22.1 0.6 copy-start.3
  28.4 11.8 %collective-permute-start.3 = (bf16[1808,128]{1,0:T(8,128)(2,1)}, bf16[1808,128]{1,0:T(8,128)(2,1)S(1)}, u32[]{:S(2)}, u32[]{:S(2)}) collective-permute-start(bf16[1808,128]{1,0:T(8,128)(2,1)} %get-tuple-element.49), channel_id=1, source_target_pairs={{0,16},{4,20},{8,24},{12,28},{16,0},{20,4},{24,8},{28,12},{1,17},{... | collective-permute-start | bytes 1388552 | tf_op jit(solution)/shard_map/ppermute | solution.py:806
  30.1 12.6 %collective-permute-start.4 = (bf16[1808,128]{1,0:T(8,128)(2,1)}, bf16[1808,128]{1,0:T(8,128)(2,1)S(1)}, u32[]{:S(2)}, u32[]{:S(2)}) collective-permute-start(bf16[1808,128]{1,0:T(8,128)(2,1)} %get-tuple-element.50), channel_id=1, source_target_pairs={{0,8},{4,12},{8,0},{12,4},{16,24},{20,28},{24,16},{28,20},{1,9},{5... | collective-permute-start | bytes 1388552 | tf_op jit(solution)/shard_map/ppermute | solution.py:806
  36.7 17.4 %collective-permute-start.5 = (bf16[1808,128]{1,0:T(8,128)(2,1)}, bf16[1808,128]{1,0:T(8,128)(2,1)S(1)}, u32[]{:S(2)}, u32[]{:S(2)}) collective-permute-start(bf16[1808,128]{1,0:T(8,128)(2,1)} %get-tuple-element.54.after_ref), channel_id=1, source_target_pairs={{0,28},{4,24},{8,20},{12,16},{16,12},{20,8},{24,4},{28,0},{1,29},{... | collective-permute-start | bytes 1388552 | tf_op jit(solution)/shard_map/ppermute | solution.py:806
  36.8 25.5 %collective-permute-start.6 = (bf16[1808,128]{1,0:T(8,128)(2,1)}, bf16[1808,128]{1,0:T(8,128)(2,1)S(1)}, u32[]{:S(2)}, u32[]{:S(2)}) collective-permute-start(bf16[1808,128]{1,0:T(8,128)(2,1)} %get-tuple-element.55), channel_id=1, source_target_pairs={{0,24},{4,28},{8,16},{12,20},{16,8},{20,12},{24,0},{28,4},{1,25},{... | collective-permute-start | bytes 1388552 | tf_op jit(solution)/shard_map/ppermute | solution.py:806
  40.0 23.2 %collective-permute-start.10 = (bf16[96,1536]{1,0:T(8,128)(2,1)}, bf16[96,1536]{1,0:T(8,128)(2,1)S(1)}, u32[]{:S(2)}, u32[]{:S(2)}) collective-permute-start(bf16[96,1536]{1,0:T(8,128)(2,1)} %latent_rest.1.own_ref), channel_id=1, source_target_pairs={{0,1},{1,0},{2,3},{3,2},{4,5},{5,4},{6,7},{7,6},{8,9},{9,8},{10,11... | collective-permute-start | bytes 884744 | tf_op jit(solution)/shard_map/ppermute | solution.py:806
  40.2 23.1 %collective-permute-start.11 = (bf16[96,1536]{1,0:T(8,128)(2,1)}, bf16[96,1536]{1,0:T(8,128)(2,1)S(1)}, u32[]{:S(2)}, u32[]{:S(2)}) collective-permute-start(bf16[96,1536]{1,0:T(8,128)(2,1)} %latent_rest.1.own_ref), channel_id=1, source_target_pairs={{0,2},{1,3},{2,0},{3,1},{4,6},{5,7},{6,4},{7,5},{8,10},{9,11},{10,... | collective-permute-start | bytes 884744 | tf_op jit(solution)/shard_map/ppermute | solution.py:806
  52.3 18.3 %collective-permute-start.7 = (bf16[1808,128]{1,0:T(8,128)(2,1)}, bf16[1808,128]{1,0:T(8,128)(2,1)S(1)}, u32[]{:S(2)}, u32[]{:S(2)}) collective-permute-start(bf16[1808,128]{1,0:T(8,128)(2,1)} %get-tuple-element.56), channel_id=1, source_target_pairs={{0,20},{4,16},{8,28},{12,24},{16,4},{20,0},{24,12},{28,8},{1,21},{... | collective-permute-start | bytes 1388552 | tf_op jit(solution)/shard_map/ppermute | solution.py:806
  54.1 16.6 %collective-permute-start.8 = (bf16[1808,128]{1,0:T(8,128)(2,1)}, bf16[1808,128]{1,0:T(8,128)(2,1)S(1)}, u32[]{:S(2)}, u32[]{:S(2)}) collective-permute-start(bf16[1808,128]{1,0:T(8,128)(2,1)} %get-tuple-element.57), channel_id=1, source_target_pairs={{0,12},{4,8},{8,4},{12,0},{16,28},{20,24},{24,20},{28,16},{1,13},{... | collective-permute-start | bytes 1388552 | tf_op jit(solution)/shard_map/ppermute | solution.py:806
  62.3 8.4 %collective-permute-start.9 = (bf16[1808,128]{1,0:T(8,128)(2,1)}, bf16[1808,128]{1,0:T(8,128)(2,1)S(1)}, u32[]{:S(2)}, u32[]{:S(2)}) collective-permute-start(bf16[1808,128]{1,0:T(8,128)(2,1)} %get-tuple-element.58), channel_id=1, source_target_pairs={{0,4},{4,0},{8,12},{12,8},{16,20},{20,16},{24,28},{28,24},{1,5},{5... | collective-permute-start | bytes 1388552 | tf_op jit(solution)/shard_map/ppermute | solution.py:806
  64.4 9.7 %collective-permute-start.12 = (bf16[96,1536]{1,0:T(8,128)(2,1)}, bf16[96,1536]{1,0:T(8,128)(2,1)S(1)}, u32[]{:S(2)}, u32[]{:S(2)}) collective-permute-start(bf16[96,1536]{1,0:T(8,128)(2,1)} %get-tuple-element.69), channel_id=1, source_target_pairs={{0,1},{1,0},{2,3},{3,2},{4,5},{5,4},{6,7},{7,6},{8,9},{9,8},{10,11... | collective-permute-start | bytes 884744 | tf_op jit(solution)/shard_map/ppermute | solution.py:806
  66.5 4.2 %copy-start = (bf16[16,128]{1,0:T(8,128)(2,1)S(1)}, bf16[16,128]{1,0:T(8,128)(2,1)}, u32[]{:S(2)}) copy-start(bf16[16,128]{1,0:T(8,128)(2,1)} %get-tuple-element.59.refs_7_) | copy-start | bytes 12292
Sparse Core Ops, SparseCore 0:
  12.3 47.9 all-gather.1

commit v11 on v10

--- a/solution.py
+++ b/solution.py
@@ -248,25 +248,9 @@
             copy_all(loads[-1])
     rate, corr = corrections(step_ref)
     lane = lax.broadcasted_iota(jnp.int32, (8, TILE), 1)
-    if chunks:
-        tops_ref, ext = refs[3 + n_dest + n_carry], refs[-9]
-        per_tile = TILE // CHUNK
-        for s in range(n_maxima):
-            peer = lax.rem(line_ref[0] + n_maxima - s, n_maxima)
-            ext[pl.ds(peer * chunks, chunks), :] = maxima[s][0:chunks, :]
-        tops_ref[...] = jnp.zeros_like(tops_ref)
-        for t in range(n_maxima * chunks // per_tile):
-            tops_ref[t : t + 1, :] = jnp.max(
-                ext[t * per_tile : (t + 1) * per_tile, :], axis=0, keepdims=True
-            )
-        maxima = (tops_ref,)
-    carried = jnp.zeros((8, TILE), F32)
-    for p, value in enumerate(three_parts(maxima[0][...])):
-        at = MAXIMA_AT + 16 * p
-        carried = jnp.where((lane >= at) & (lane < at + 16), pltpu.roll(value, at, 1), carried)
     extras = []
     for d, k in enumerate(partners):
-        side = carried
+        side = jnp.zeros((8, TILE), F32)
         for j in range(per_dest):
             i = d * per_dest + j
             wait_all(loads[i])
@@ -287,6 +271,24 @@
             stores[i][3].start()
             for p, value in enumerate(three_parts(top)):
                 side = jnp.where(lane == 3 * j + p, value, side)
+        if d == 0:
+            if chunks:
+                tops_ref, ext = refs[3 + n_dest + n_carry], refs[-9]
+                per_tile = TILE // CHUNK
+                for s in range(n_maxima):
+                    peer = lax.rem(line_ref[0] + n_maxima - s, n_maxima)
+                    ext[pl.ds(peer * chunks, chunks), :] = maxima[s][0:chunks, :]
+                tops_ref[...] = jnp.zeros_like(tops_ref)
+                for t in range(n_maxima * chunks // per_tile):
+                    tops_ref[t : t + 1, :] = jnp.max(
+                        ext[t * per_tile : (t + 1) * per_tile, :], axis=0, keepdims=True
+                    )
+                maxima = (tops_ref,)
+            carried = jnp.zeros((8, TILE), F32)
+            for p, value in enumerate(three_parts(maxima[0][...])):
+                at = MAXIMA_AT + 16 * p
+                carried = jnp.where((lane >= at) & (lane < at + 16), pltpu.roll(value, at, 1), carried)
+        side += carried
         extra[d] = jnp.concatenate([side, jnp.zeros_like(side)], axis=0).astype(BF16)
         first = per_dest * rows if k else 0
         extras.append(
@@ -450,7 +452,7 @@
     return served, through, expert, latent.T
 
 
-def finish_kernel(deltas, rows, pos_ref, *refs):
+def rest_kernel(deltas, rows, pos_ref, *refs):
     n = len(deltas)
     latent, buf, in_sem, out_sem = refs[n + 1 :]
     loads = [pltpu.make_async_copy(refs[i], buf.at[i], in_sem.at[i]) for i in range(n)]
@@ -464,11 +466,11 @@
     wait_all(copies)
 
 
-def finish(latent, pos, rest, deltas):
+def place_rest(latent, pos, rest, deltas):
     n = len(rest)
     span, cols = rest[0].shape
     return pl.pallas_call(
-        functools.partial(finish_kernel, deltas, TILE + span),
+        functools.partial(rest_kernel, deltas, TILE + span),
         in_specs=[SMEM] + [ANY] * (n + 1),
         out_specs=ANY,
         out_shape=jax.ShapeDtypeStruct(latent.shape, latent.dtype),
@@ -480,7 +482,7 @@
         input_output_aliases={1 + n: 0},
         compiler_params=pltpu.CompilerParams(vmem_limit_bytes=4 * 1024 * 1024),
         cost_estimate=pl.CostEstimate(flops=0, bytes_accessed=1000000, transcendentals=0),
-        name="place_finish",
+        name="place_rest",
     )(pos, *rest, latent)
 
 
@@ -488,8 +490,9 @@
     return pl.multiple_of(lax.rem(pos * (TILE - rows % TILE), TILE), CHUNK)
 
 
-def full_kernel(pieces, rows, pos_ref, x_ref, own_ref, *refs):
-    out_ref, buf, own, in_sem, out_sem, own_in, own_out = refs[1:]
+def full_kernel(pieces, rows, deltas, pos_ref, x_ref, *refs):
+    n = len(deltas)
+    out_ref, buf, rest, in_sem, out_sem, rest_in, rest_out = refs[n:]
     loads, stores = [], []
     for i in range(pieces):
         lead = i * (TILE - rows % TILE) % TILE
@@ -500,37 +503,39 @@
                 buf.at[at, :], out_ref.at[pl.ds(i * rows + lead, TILE), :], out_sem.at[i]
             )
         )
-    loads.append(pltpu.make_async_copy(own_ref, own.at[0], own_in.at[0]))
-    copy_all(loads)
+    rest_loads = [pltpu.make_async_copy(refs[i], rest.at[i], rest_in.at[i]) for i in range(n)]
+    copy_all(loads + rest_loads)
     for i in range(pieces):
         loads[i].wait()
         stores[i].start()
-    loads[pieces].wait()
-    rest = rest_stores(own, 0, pos_ref[0], rows, out_ref, own_out)
-    copy_all(rest)
-    wait_all(stores + rest)
-
-
-def place_full(out, pos, x, own, rows):
-    pieces = x.shape[0] // TILE
+    for i, delta in enumerate(deltas):
+        rest_loads[i].wait()
+        group = rest_stores(rest, i, pos_ref[0] ^ delta, rows, out_ref, rest_out)
+        copy_all(group)
+        stores += group
+    wait_all(stores)
+
+
+def place_full(pos, x, xs, deltas, rows):
+    pieces, n = x.shape[0] // TILE, len(xs)
+    span, cols = xs[0].shape
     return pl.pallas_call(
-        functools.partial(full_kernel, pieces, rows),
-        in_specs=[SMEM] + [ANY] * 3,
+        functools.partial(full_kernel, pieces, rows, deltas),
+        in_specs=[SMEM] + [ANY] * (1 + n),
         out_specs=ANY,
-        out_shape=jax.ShapeDtypeStruct((pieces * rows, x.shape[1]), BF16),
+        out_shape=jax.ShapeDtypeStruct((pieces * rows, cols), BF16),
         scratch_shapes=[
             pltpu.VMEM(x.shape, BF16),
-            pltpu.VMEM((1,) + own.shape, BF16),
+            pltpu.VMEM((n, span, cols), BF16),
             pltpu.SemaphoreType.DMA((pieces,)),
             pltpu.SemaphoreType.DMA((pieces,)),
-            pltpu.SemaphoreType.DMA((1,)),
-            pltpu.SemaphoreType.DMA((1, own.shape[0] // CHUNK)),
+            pltpu.SemaphoreType.DMA((n,)),
+            pltpu.SemaphoreType.DMA((n, span // CHUNK)),
         ],
-        input_output_aliases={3: 0},
         compiler_params=PARAMS,
         cost_estimate=pl.CostEstimate(flops=0, bytes_accessed=4 * x.size, transcendentals=0),
         name="place_whole",
-    )(pos, x, own, out)
+    )(pos, x, *xs)
 
 
 def rest_stores(buf, i, peer, rows, out_ref, sem):
@@ -548,42 +553,17 @@
     return copies
 
 
-def hop_kernel(deltas, rows, pos_ref, *refs):
-    n = len(deltas)
-    out_ref, again_ref, _, buf, in_sem, out_sem = refs[-6:]
-    loads = [pltpu.make_async_copy(refs[i], buf.at[i], in_sem.at[i]) for i in range(n)]
-    copy_all(loads)
-    copies = [pltpu.make_async_copy(buf.at[n - 1], again_ref, in_sem.at[n])]
-    for i in reversed(range(n)):
-        loads[i].wait()
-        group = rest_stores(buf, i, pos_ref[0] ^ deltas[i], rows, out_ref, out_sem)
-        copy_all(copies + group if i == n - 1 else group)
-        copies += group
-    wait_all(copies)
-
-
-def place_and_pass(pos, xs, deltas, through, rows, peers):
-    span, cols = xs[0].shape
-    n = len(xs)
+def in_order(*arrays):
     return pl.pallas_call(
-        functools.partial(hop_kernel, deltas, rows),
-        in_specs=[SMEM] + [ANY] * (n + 1),
-        out_specs=[ANY] * 3,
-        out_shape=[
-            jax.ShapeDtypeStruct((peers * rows, cols), BF16),
-            jax.ShapeDtypeStruct((span, cols), BF16),
-            jax.ShapeDtypeStruct(through.shape, through.dtype),
-        ],
-        input_output_aliases={1 + n: 2},
-        scratch_shapes=[
-            pltpu.VMEM((n, span, cols), BF16),
-            pltpu.SemaphoreType.DMA((n + 1,)),
-            pltpu.SemaphoreType.DMA((n, span // CHUNK)),
-        ],
-        compiler_params=pltpu.CompilerParams(vmem_limit_bytes=4 * 1024 * 1024),
-        cost_estimate=pl.CostEstimate(flops=0, bytes_accessed=6 * span * cols, transcendentals=0),
-        name="place_hop",
-    )(pos, *xs, through)
+        lambda *refs: None,
+        in_specs=[ANY] * len(arrays),
+        out_specs=[ANY] * len(arrays),
+        out_shape=[jax.ShapeDtypeStruct(x.shape, x.dtype) for x in arrays],
+        input_output_aliases={i: i for i in range(len(arrays))},
+        compiler_params=pltpu.CompilerParams(vmem_limit_bytes=1024 * 1024),
+        cost_estimate=pl.CostEstimate(flops=1, bytes_accessed=1, transcendentals=0),
+        name="in_order",
+    )(*arrays)
 
 
 SLABS = 4
@@ -844,11 +824,10 @@
     served = place_blocks(
         (served,), dp_at, received[first:count], groups[1], served.shape
     )
-    latent_served, far_again, served = place_and_pass(
-        expert_at, [near, far], [1, 2], served, latent_rows, exp_axis
-    )
-    last = swap(far_again, "expert", 1)
-    latent_served = place_full(latent_served, expert_at, whole, rest, latent_rows)
+    near, far, served = in_order(near, far, served)
+    last = swap(far, "expert", 1)
+    latent_served = place_full(expert_at, whole, [rest], [0], latent_rows)
+    latent_served = place_rest(latent_served, expert_at, [near, far], [1, 2])
     served, latent_served, expert_scales, latent_scales = collect(
         served,
         latent_served,
@@ -859,7 +838,7 @@
         latent_rows * exp_axis // TILE,
         latent_new.shape[1] // TILE,
     )
-    latent_served = finish(latent_served, expert_at, [last], [3])
+    latent_served = place_rest(latent_served, expert_at, [last], [3])
     expert_served = served.reshape(1, block_count * rows, TILE)
 
     return (

time: 82.1 us -> 95.4 us (1.16)
  Pallas kernels: 34.6 us -> 49.2 us
  waiting for transfers between devices: 14.3 us -> 13 us
    pallas_call x1, Pallas kernels: 1.96 us -> 15.8 us  [collect(): pl.pallas_call(functools.partial(collect_kernel, order, tiles, lat_tiles,...]
    ppermute x10, waiting for transfers between devices: 10.5 us -> 9.21 us  [swap(): lax.ppermute(x, axis, [(i, i ^ k) for i in range(lax.axis_size(axis))])]
    pallas_call x3 -> x4, Pallas kernels: 4.24 us -> 5.04 us  [the longest x2 2.71 us: place_rest(): pl.pallas_call(functools.partial(rest_kernel, deltas, TILE + span), in_sp...]
  transfers between devices with their start and end apart: 14 -> 14, of which waited for: 5 -> 4; matrix products, arithmetic and copies ran while one was open for 0% -> 0% of each run, Pallas kernels for 36% -> 45%
where the time goes in v11:
time: 95.4 us; the launch traced here: 95 us
  Pallas kernels  49.2 us (52%)
  starting transfers between devices  17.4 us (18%)
  between operations  14.9 us (16%)
  waiting for transfers between devices  13 us (14%)
    pallas_call x3, Pallas kernels, expert_group(): pl.pallas_call(functools.partial(expert_kernel, partners, per_dest, n_ali...  19.4 us
    pallas_call x1, Pallas kernels, collect(): pl.pallas_call(functools.partial(collect_kernel, order, tiles, lat_tiles,...  15.8 us
    ppermute x10, starting transfers between devices, swap(): lax.ppermute(x, axis, [(i, i ^ k) for i in range(lax.axis_size(axis))])  11.2 us
    ppermute x10, waiting for transfers between devices, swap(): lax.ppermute(x, axis, [(i, i ^ k) for i in range(lax.axis_size(axis))])  9.21 us
    ppermute x3, starting transfers between devices, fast_body(): lax.ppermute(chunk_top, 'expert', [(i, (i + s) % exp_axis) for i in range...  6.11 us
    pallas_call x1, Pallas kernels, latent_update(): pl.pallas_call(functools.partial(latent_kernel, rows // CHUNK), in_specs=...  4.32 us
    ppermute x3, waiting for transfers between devices, fast_body(): lax.ppermute(chunk_top, 'expert', [(i, (i + s) % exp_axis) for i in range...  3.76 us
    pallas_call x1, Pallas kernels, latent_rest(): pl.pallas_call(functools.partial(latent_rest_kernel, chunks), in_specs=[S...  2.76 us
  transfers between devices with their start and end apart: 14, of which 4 were waited for; matrix products, arithmetic and copies ran while one was open for 0% of the time, Pallas kernels for 45%

profile of v11, /device:TPU:0, one launch (start us, length us, event | category | flops | bytes accessed | tf_op | source)
XLA Modules:
  0.0 95.0 jit_solution(15461845376444576754)
XLA Ops:
  7.2 0.0 all-gather.2.cloned.1.call-start
  7.9 4.3 %latent_adamw.1 = (f32[224,1536]{1,0:T(8,128)}, bf16[224,1536]{1,0:T(8,128)(2,1)}, bf16[224,1536]{1,0:T(8,128)(2,1)}, bf16[128,1536]{1,0:T(8,128)(2,1)}, f32[8,128]{1,0:T(8,128)}) custom-call(s32[1]{0:T(128)S(6)} %copy.50.step_ref, s32[1]{0:T(128)} %bitcast.1.pos_ref.line_ref, f32[224,1536]{1,0:T(8,128)} %refs_0_.1, bf16[224,1536]{1,0:T(8,128)(2,1)} %refs_1_.1, ...), custom_call_target="tpu_custom_call" | custom-call | flops 10321920 | bytes 6193152 | tf_op jit(solution)/shard_map/latent_adamw/pallas_call | solution.py:624
  12.2 0.0 all-gather.2.cloned.1.call-update
  12.2 3.1 %collective-permute-start = (f32[8,128]{1,0:T(8,128)}, f32[8,128]{1,0:T(8,128)S(1)}, u32[]{:S(2)}, u32[]{:S(2)}) collective-permute-start(f32[8,128]{1,0:T(8,128)} %get-tuple-element.41.refs_0_.own_ref), channel_id=1, source_target_pairs={{0,1},{1,2},{2,3},{3,0},{4,5},{5,6},{6,7},{7,4},{8,9},{9,10},{10,1... | collective-permute-start | bytes 12296 | tf_op jit(solution)/shard_map/ppermute | solution.py:778
  15.3 2.1 %collective-permute-start.2 = (f32[8,128]{1,0:T(8,128)}, f32[8,128]{1,0:T(8,128)S(1)}, u32[]{:S(2)}, u32[]{:S(2)}) collective-permute-start(f32[8,128]{1,0:T(8,128)} %get-tuple-element.41.refs_0_.own_ref), channel_id=1, source_target_pairs={{0,3},{1,0},{2,1},{3,2},{4,7},{5,4},{6,5},{7,6},{8,11},{9,8},{10,9... | collective-permute-start | bytes 12296 | tf_op jit(solution)/shard_map/ppermute | solution.py:778
  17.4 0.9 collective-permute-start.1
  18.3 0.8 collective-permute-done.refs_1_.prev_ref
  19.2 0.0 copy-start.1
  19.2 0.0 collective-permute-done.2.refs_3_.next_ref
  19.2 0.0 copy-start.2
  19.2 2.9 %collective-permute-done.1.refs_2_ = f32[8,128]{1,0:T(8,128)S(1)} collective-permute-done((f32[8,128]{1,0:T(8,128)}, f32[8,128]{1,0:T(8,128)S(1)}, u32[]{:S(2)}, u32[]{:S(2)}) %collective-permute-start.1) | collective-permute-done | bytes 4128 | tf_op jit(solution)/shard_map/ppermute | solution.py:778
  22.1 0.0 copy-start.3
  22.1 0.0 copy-done.1
  22.1 0.0 copy-done.2
  22.1 0.6 copy-done.3
  22.7 5.7 %expert_adamw.3 = (f32[896,2048]{1,0:T(8,128)}, bf16[896,2048]{1,0:T(8,128)(2,1)}, bf16[896,2048]{1,0:T(8,128)(2,1)}, bf16[1808,128]{1,0:T(8,128)(2,1)}, bf16[1808,128]{1,0:T(8,128)(2,1)}, /*index=5*/f32[8,128]{1,0:T(8,128)}) custom-call(s32[16]{0:T(128)} %owner_ref.5, s32[1]{0:T(128)} %bitcast.pos_ref, s32[1]{0:T(128)} %bitcast.1.pos_ref.line_ref, ...), custom_call_target="tpu_custom_call" | custom-call | flops 458752 | bytes 458752 | tf_op jit(solution)/shard_map/expert_adamw/pallas_call | solution.py:316
  28.4 1.7 %collective-permute-start.3 = (bf16[1808,128]{1,0:T(8,128)(2,1)}, bf16[1808,128]{1,0:T(8,128)(2,1)S(1)}, u32[]{:S(2)}, u32[]{:S(2)}) collective-permute-start(bf16[1808,128]{1,0:T(8,128)(2,1)} %get-tuple-element.49), channel_id=1, source_target_pairs={{0,16},{4,20},{8,24},{12,28},{16,0},{20,4},{24,8},{28,12},{1,17},{... | collective-permute-start | bytes 1388552 | tf_op jit(solution)/shard_map/ppermute | solution.py:786
  30.1 1.5 %collective-permute-start.4 = (bf16[1808,128]{1,0:T(8,128)(2,1)}, bf16[1808,128]{1,0:T(8,128)(2,1)S(1)}, u32[]{:S(2)}, u32[]{:S(2)}) collective-permute-start(bf16[1808,128]{1,0:T(8,128)(2,1)} %get-tuple-element.50), channel_id=1, source_target_pairs={{0,8},{4,12},{8,0},{12,4},{16,24},{20,28},{24,16},{28,20},{1,9},{5... | collective-permute-start | bytes 1388552 | tf_op jit(solution)/shard_map/ppermute | solution.py:786
  31.6 5.1 %expert_adamw.4 = (f32[896,2048]{1,0:T(8,128)}, bf16[896,2048]{1,0:T(8,128)(2,1)}, bf16[896,2048]{1,0:T(8,128)(2,1)}, bf16[1808,128]{1,0:T(8,128)(2,1)}, bf16[1808,128]{1,0:T(8,128)(2,1)}) custom-call(s32[16]{0:T(128)} %owner_ref.5, s32[1]{0:T(128)} %bitcast.pos_ref, ...), custom_call_target="tpu_custom_call", output_to_operand_aliasing={{0}: (9, {}), {1}: (10, {}), {2}: (11, {})} | custom-call | flops 458752 | bytes 458752 | tf_op jit(solution)/shard_map/expert_adamw/pallas_call | solution.py:316
  36.7 0.1 collective-permute-start.5
  36.8 0.5 collective-permute-start.6
  37.2 2.8 %latent_rest.1.refs_0_ = bf16[96,1536]{1,0:T(8,128)(2,1)} custom-call(s32[1]{0:T(128)} %bitcast.1.pos_ref.line_ref, f32[224,1536]{1,0:T(8,128)} %get-tuple-element.36.w1_ref, f32[8,128]{1,0:T(8,128)} %get-tuple-element.41.refs_0_.own_ref, f32[8,128]{1,0:T(8,128)} %copy-done.1, f32[8,128]{1,0:T(8,128)} %copy-done.2, bf16[1808,128]{1,0:T(8,128)(2,1)} %get-tuple-element.54.after_ref), custom_call_target="tpu_custom_call" | custom-call | flops 344064 | bytes 1032192 | tf_op jit(solution)/shard_map/latent_rest/pallas_call | solution.py:702
  40.0 0.2 collective-permute-start.10
  40.2 0.0 collective-permute-done.3.refs_0_
  40.2 2.5 %collective-permute-start.11 = (bf16[96,1536]{1,0:T(8,128)(2,1)}, bf16[96,1536]{1,0:T(8,128)(2,1)S(1)}, u32[]{:S(2)}, u32[]{:S(2)}) collective-permute-start(bf16[96,1536]{1,0:T(8,128)(2,1)} %latent_rest.1.refs_0_), channel_id=1, source_target_pairs={{0,2},{1,3},{2,0},{3,1},{4,6},{5,7},{6,4},{7,5},{8,10},{9,11},{10,... | collective-permute-start | bytes 884744 | tf_op jit(solution)/shard_map/ppermute | solution.py:786
  42.7 0.0 collective-permute-done.4.refs_1_
  42.7 0.9 place_served.2.refs_8_
  43.6 8.7 %expert_adamw.5 = (f32[896,2048]{1,0:T(8,128)}, bf16[896,2048]{1,0:T(8,128)(2,1)}, bf16[896,2048]{1,0:T(8,128)(2,1)}, bf16[1808,128]{1,0:T(8,128)(2,1)}, bf16[18...) custom-call(s32[16]{0:T(128)} %owner_ref.5, ...), custom_call_target="tpu_custom_call", output_to_operand_aliasing={{0}: (9, {}), {1}: (10, {}), {2}: (11, {}), {7}: (12, {})} | custom-call | flops 917504 | bytes 917504 | tf_op jit(solution)/shard_map/expert_adamw/pallas_call | solution.py:316
  52.3 1.8 %collective-permute-start.7 = (bf16[1808,128]{1,0:T(8,128)(2,1)}, bf16[1808,128]{1,0:T(8,128)(2,1)S(1)}, u32[]{:S(2)}, u32[]{:S(2)}) collective-permute-start(bf16[1808,128]{1,0:T(8,128)(2,1)} %get-tuple-element.56), channel_id=1, source_target_pairs={{0,20},{4,16},{8,28},{12,24},{16,4},{20,0},{24,12},{28,8},{1,21},{... | collective-permute-start | bytes 1388552 | tf_op jit(solution)/shard_map/ppermute | solution.py:786
  54.1 0.0 collective-permute-done.5.refs_0_.refs_2_
  54.1 1.0 %collective-permute-start.8 = (bf16[1808,128]{1,0:T(8,128)(2,1)}, bf16[1808,128]{1,0:T(8,128)(2,1)S(1)}, u32[]{:S(2)}, u32[]{:S(2)}) collective-permute-start(bf16[1808,128]{1,0:T(8,128)(2,1)} %get-tuple-element.57), channel_id=1, source_target_pairs={{0,12},{4,8},{8,4},{12,0},{16,28},{20,24},{24,20},{28,16},{1,13},{... | collective-permute-start | bytes 1388552 | tf_op jit(solution)/shard_map/ppermute | solution.py:786
  55.1 7.2 %collective-permute-done.6.refs_1_.refs_3_ = bf16[1808,128]{1,0:T(8,128)(2,1)S(1)} collective-permute-done((bf16[1808,128]{1,0:T(8,128)(2,1)}, bf16[1808,128]{1,0:T(8,128)(2,1)S(1)}, u32[]{:S(2)}, u32[]{:S(2)}) %collective-permute-start.6) | collective-permute-done | bytes 462880 | tf_op jit(solution)/shard_map/ppermute | solution.py:786
  62.3 0.0 collective-permute-start.9
  62.3 0.9 place_served.3.refs_2_
  63.2 0.0 collective-permute-done.10.refs_0_
  63.3 0.0 collective-permute-done.11.refs_1_
  63.3 2.0 %collective-permute-start.12 = (bf16[96,1536]{1,0:T(8,128)(2,1)S(1)}, bf16[96,1536]{1,0:T(8,128)(2,1)}, u32[]{:S(2)}, u32[]{:S(2)}) collective-permute-start(bf16[96,1536]{1,0:T(8,128)(2,1)S(1)} %get-tuple-element.64.refs_1_), channel_id=1, source_target_pairs={{0,1},{1,0},{2,3},{3,2},{4,5},{5,4},{6,7},{7,6},{8,9},{9,8},{10,11... | collective-permute-start | bytes 884744 | tf_op jit(solution)/shard_map/ppermute | solution.py:786
  65.3 0.0 all-gather.2.cloned.1.call-done.x_ref
  65.3 2.3 %place_whole.1.refs_2_ = bf16[896,1536]{1,0:T(8,128)(2,1)} custom-call(s32[1]{0:T(128)} %bitcast.1.pos_ref.line_ref, bf16[512,1536]{1,0:T(8,128)(2,1)} %all-gather.2.cloned.1.call-done.x_ref, bf16[96,1536]{1,0:T(8,128)(2,1)} %latent_rest.1.refs_0_), custom_call_target="tpu_custom_call" | custom-call | bytes 3145728 | tf_op jit(solution)/shard_map/place_whole/pallas_call | solution.py:522
  67.7 0.0 copy-start
  67.7 1.0 %place_rest.2.refs_9_ = bf16[896,1536]{1,0:T(8,128)(2,1)} custom-call(s32[1]{0:T(128)} %bitcast.1.pos_ref.line_ref, bf16[96,1536]{1,0:T(8,128)(2,1)S(1)} %get-tuple-element.63.refs_0_, bf16[96,1536]{1,0:T(8,128)(2,1)S(1)} %get-tuple-element.64.refs_1_, bf16[896,1536]{1,0:T(8,128)(2,1)} %place_whole.1.refs_2_), custom_call_target="tpu_custom_call", output_to_operand_aliasing={{}: (3, {})} | custom-call | bytes 1000000 | tf_op jit(solution)/shard_map/place_rest/pallas_call | solution.py:472
  68.7 2.0 %collective-permute-done.7.refs_4_ = bf16[1808,128]{1,0:T(8,128)(2,1)S(1)} collective-permute-done((bf16[1808,128]{1,0:T(8,128)(2,1)}, bf16[1808,128]{1,0:T(8,128)(2,1)S(1)}, u32[]{:S(2)}, u32[]{:S(2)}) %collective-permute-start.7) | collective-permute-done | bytes 462880 | tf_op jit(solution)/shard_map/ppermute | solution.py:786
  70.7 0.0 collective-permute-done.8.refs_5_
  70.7 0.0 collective-permute-done.9.refs_6_
  70.7 0.0 copy-done
  70.7 15.8 %place_last.1 = (bf16[2,8,896,128]{3,2,1,0:T(8,128)(2,1)}, bf16[896,1536]{1,0:T(8,128)(2,1)}, f32[1,112]{1,0:T(1,128)}, f32[12,56]{1,0:T(8,128)}) custom-call(s32[1]{0:T(128)} %bitcast.pos_ref, bf16[1808,128]{1,0:T(8,128)(2,1)S(1)} %collective-permute-done.3.refs_0_, ...), custom_call_target="tpu_custom_call", output_to_operand_aliasing={{0}: (9, {}), {1}: (10, {})} | custom-call | flops 1000000 | bytes 1000000 | tf_op jit(solution)/shard_map/place_last/pallas_call | solution.py:431
  86.5 0.0 collective-permute-done.12.refs_0_
  86.5 1.7 %place_rest.3 = bf16[896,1536]{1,0:T(8,128)(2,1)} custom-call(s32[1]{0:T(128)} %bitcast.1.pos_ref.line_ref, bf16[96,1536]{1,0:T(8,128)(2,1)} %collective-permute-done.12.refs_0_, bf16[896,1536]{1,0:T(8,128)(2,1)} %get-tuple-element.70.refs_1_), custom_call_target="tpu_custom_call", output_to_operand_aliasing={{}: (2, {})} | custom-call | bytes 1000000 | tf_op jit(solution)/shard_map/place_rest/pallas_call | solution.py:472
  (1 shorter events, 0.0 us)
Async XLA Ops:
  7.2 58.1 %all-gather.2.cloned.1.call-start = ((), (), s32[]{:S(2)}) async-start(), calls=%async_computation | async-start | bytes 1966080 | tf_op jit(solution)/shard_map/all_gather | solution.py:776
  12.2 6.9 %collective-permute-start = (f32[8,128]{1,0:T(8,128)}, f32[8,128]{1,0:T(8,128)S(1)}, u32[]{:S(2)}, u32[]{:S(2)}) collective-permute-start(f32[8,128]{1,0:T(8,128)} %get-tuple-element.41.refs_0_.own_ref), channel_id=1, source_target_pairs={{0,1},{1,2},{2,3},{3,0},{4,5},{5,6},{6,7},{7,4},{8,9},{9,10},{10,1... | collective-permute-start | bytes 12296 | tf_op jit(solution)/shard_map/ppermute | solution.py:778
  15.3 3.9 %collective-permute-start.2 = (f32[8,128]{1,0:T(8,128)}, f32[8,128]{1,0:T(8,128)S(1)}, u32[]{:S(2)}, u32[]{:S(2)}) collective-permute-start(f32[8,128]{1,0:T(8,128)} %get-tuple-element.41.refs_0_.own_ref), channel_id=1, source_target_pairs={{0,3},{1,0},{2,1},{3,2},{4,7},{5,4},{6,5},{7,6},{8,11},{9,8},{10,9... | collective-permute-start | bytes 12296 | tf_op jit(solution)/shard_map/ppermute | solution.py:778
  17.4 4.7 %collective-permute-start.1 = (f32[8,128]{1,0:T(8,128)}, f32[8,128]{1,0:T(8,128)S(1)}, u32[]{:S(2)}, u32[]{:S(2)}) collective-permute-start(f32[8,128]{1,0:T(8,128)} %get-tuple-element.41.refs_0_.own_ref), channel_id=1, source_target_pairs={{0,2},{1,3},{2,0},{3,1},{4,6},{5,7},{6,4},{7,5},{8,10},{9,11},{10,... | collective-permute-start | bytes 12296 | tf_op jit(solution)/shard_map/ppermute | solution.py:778
  19.2 3.0 %copy-start.1 = (f32[8,128]{1,0:T(8,128)}, f32[8,128]{1,0:T(8,128)S(1)}, u32[]{:S(2)}) copy-start(f32[8,128]{1,0:T(8,128)S(1)} %collective-permute-done.refs_1_.prev_ref) | copy-start | bytes 12292
  19.2 2.9 %copy-start.2 = (f32[8,128]{1,0:T(8,128)}, f32[8,128]{1,0:T(8,128)S(1)}, u32[]{:S(2)}) copy-start(f32[8,128]{1,0:T(8,128)S(1)} %collective-permute-done.2.refs_3_.next_ref) | copy-start | bytes 12292
  22.1 0.6 copy-start.3
  28.4 11.8 %collective-permute-start.3 = (bf16[1808,128]{1,0:T(8,128)(2,1)}, bf16[1808,128]{1,0:T(8,128)(2,1)S(1)}, u32[]{:S(2)}, u32[]{:S(2)}) collective-permute-start(bf16[1808,128]{1,0:T(8,128)(2,1)} %get-tuple-element.49), channel_id=1, source_target_pairs={{0,16},{4,20},{8,24},{12,28},{16,0},{20,4},{24,8},{28,12},{1,17},{... | collective-permute-start | bytes 1388552 | tf_op jit(solution)/shard_map/ppermute | solution.py:786
  30.1 12.6 %collective-permute-start.4 = (bf16[1808,128]{1,0:T(8,128)(2,1)}, bf16[1808,128]{1,0:T(8,128)(2,1)S(1)}, u32[]{:S(2)}, u32[]{:S(2)}) collective-permute-start(bf16[1808,128]{1,0:T(8,128)(2,1)} %get-tuple-element.50), channel_id=1, source_target_pairs={{0,8},{4,12},{8,0},{12,4},{16,24},{20,28},{24,16},{28,20},{1,9},{5... | collective-permute-start | bytes 1388552 | tf_op jit(solution)/shard_map/ppermute | solution.py:786
  36.7 17.4 %collective-permute-start.5 = (bf16[1808,128]{1,0:T(8,128)(2,1)}, bf16[1808,128]{1,0:T(8,128)(2,1)S(1)}, u32[]{:S(2)}, u32[]{:S(2)}) collective-permute-start(bf16[1808,128]{1,0:T(8,128)(2,1)} %get-tuple-element.54.after_ref), channel_id=1, source_target_pairs={{0,28},{4,24},{8,20},{12,16},{16,12},{20,8},{24,4},{28,0},{1,29},{... | collective-permute-start | bytes 1388552 | tf_op jit(solution)/shard_map/ppermute | solution.py:786
  36.8 25.5 %collective-permute-start.6 = (bf16[1808,128]{1,0:T(8,128)(2,1)}, bf16[1808,128]{1,0:T(8,128)(2,1)S(1)}, u32[]{:S(2)}, u32[]{:S(2)}) collective-permute-start(bf16[1808,128]{1,0:T(8,128)(2,1)} %get-tuple-element.55), channel_id=1, source_target_pairs={{0,24},{4,28},{8,16},{12,20},{16,8},{20,12},{24,0},{28,4},{1,25},{... | collective-permute-start | bytes 1388552 | tf_op jit(solution)/shard_map/ppermute | solution.py:786
  40.0 23.2 %collective-permute-start.10 = (bf16[96,1536]{1,0:T(8,128)(2,1)}, bf16[96,1536]{1,0:T(8,128)(2,1)S(1)}, u32[]{:S(2)}, u32[]{:S(2)}) collective-permute-start(bf16[96,1536]{1,0:T(8,128)(2,1)} %latent_rest.1.refs_0_), channel_id=1, source_target_pairs={{0,1},{1,0},{2,3},{3,2},{4,5},{5,4},{6,7},{7,6},{8,9},{9,8},{10,11... | collective-permute-start | bytes 884744 | tf_op jit(solution)/shard_map/ppermute | solution.py:786
  40.2 23.1 %collective-permute-start.11 = (bf16[96,1536]{1,0:T(8,128)(2,1)}, bf16[96,1536]{1,0:T(8,128)(2,1)S(1)}, u32[]{:S(2)}, u32[]{:S(2)}) collective-permute-start(bf16[96,1536]{1,0:T(8,128)(2,1)} %latent_rest.1.refs_0_), channel_id=1, source_target_pairs={{0,2},{1,3},{2,0},{3,1},{4,6},{5,7},{6,4},{7,5},{8,10},{9,11},{10,... | collective-permute-start | bytes 884744 | tf_op jit(solution)/shard_map/ppermute | solution.py:786
  52.3 18.3 %collective-permute-start.7 = (bf16[1808,128]{1,0:T(8,128)(2,1)}, bf16[1808,128]{1,0:T(8,128)(2,1)S(1)}, u32[]{:S(2)}, u32[]{:S(2)}) collective-permute-start(bf16[1808,128]{1,0:T(8,128)(2,1)} %get-tuple-element.56), channel_id=1, source_target_pairs={{0,20},{4,16},{8,28},{12,24},{16,4},{20,0},{24,12},{28,8},{1,21},{... | collective-permute-start | bytes 1388552 | tf_op jit(solution)/shard_map/ppermute | solution.py:786
  54.1 16.6 %collective-permute-start.8 = (bf16[1808,128]{1,0:T(8,128)(2,1)}, bf16[1808,128]{1,0:T(8,128)(2,1)S(1)}, u32[]{:S(2)}, u32[]{:S(2)}) collective-permute-start(bf16[1808,128]{1,0:T(8,128)(2,1)} %get-tuple-element.57), channel_id=1, source_target_pairs={{0,12},{4,8},{8,4},{12,0},{16,28},{20,24},{24,20},{28,16},{1,13},{... | collective-permute-start | bytes 1388552 | tf_op jit(solution)/shard_map/ppermute | solution.py:786
  62.3 8.4 %collective-permute-start.9 = (bf16[1808,128]{1,0:T(8,128)(2,1)}, bf16[1808,128]{1,0:T(8,128)(2,1)}, u32[]{:S(2)}, u32[]{:S(2)}) collective-permute-start(bf16[1808,128]{1,0:T(8,128)(2,1)} %get-tuple-element.58), channel_id=1, source_target_pairs={{0,4},{4,0},{8,12},{12,8},{16,20},{20,16},{24,28},{28,24},{1,5},{5... | collective-permute-start | bytes 1388552 | tf_op jit(solution)/shard_map/ppermute | solution.py:786
  63.3 23.2 %collective-permute-start.12 = (bf16[96,1536]{1,0:T(8,128)(2,1)S(1)}, bf16[96,1536]{1,0:T(8,128)(2,1)}, u32[]{:S(2)}, u32[]{:S(2)}) collective-permute-start(bf16[96,1536]{1,0:T(8,128)(2,1)S(1)} %get-tuple-element.64.refs_1_), channel_id=1, source_target_pairs={{0,1},{1,0},{2,3},{3,2},{4,5},{5,4},{6,7},{7,6},{8,9},{9,8},{10,11... | collective-permute-start | bytes 884744 | tf_op jit(solution)/shard_map/ppermute | solution.py:786
  67.7 3.0 %copy-start = (bf16[16,128]{1,0:T(8,128)(2,1)S(1)}, bf16[16,128]{1,0:T(8,128)(2,1)}, u32[]{:S(2)}) copy-start(bf16[16,128]{1,0:T(8,128)(2,1)} %get-tuple-element.59.refs_7_) | copy-start | bytes 12292
Sparse Core Ops, SparseCore 0:
  12.3 47.9 all-gather.1

commit v12 on v11

--- a/solution.py
+++ b/solution.py
@@ -158,7 +158,7 @@
 SMEM = pl.BlockSpec(memory_space=pltpu.SMEM)
 VMEM = pl.BlockSpec(memory_space=pltpu.VMEM)
 PARAMS = pltpu.CompilerParams(vmem_limit_bytes=VMEM_LIMIT)
-LIGHT = pltpu.CompilerParams(vmem_limit_bytes=1024 * 1024)
+LIGHT = pltpu.CompilerParams(vmem_limit_bytes=4 * 1024 * 1024)
 
 
 def corrections(step_ref):
@@ -351,31 +351,47 @@
     return out[:3], out[3 : 3 + len(partners)], out[3 + len(partners) :]
 
 
-def block_copies(served, payloads, srcs, sem):
+def load_blocks(payloads, buf, sem):
+    return [
+        pltpu.make_async_copy(q.at[pl.ds(0, buf.shape[1]), :], buf.at[i], sem.at[i])
+        for i, q in enumerate(payloads)
+    ]
+
+
+def store_blocks(served, buf, i, src, sem):
     per_dest, _, rows, _ = served.shape
     return [
-        pltpu.make_async_copy(q.at[pl.ds(j * rows, rows), :], served.at[j, src], sem.at[i, j])
-        for i, (q, src) in enumerate(zip(payloads, srcs))
+        pltpu.make_async_copy(buf.at[i, pl.ds(j * rows, rows), :], served.at[j, src], sem.at[i, j])
         for j in range(per_dest)
     ]
 
 
 def place_kernel(partners, pos_ref, *refs):
     n = len(partners)
-    served, sem = refs[-2:]
-    copies = block_copies(served, refs[:n], [pos_ref[0] ^ k for k in partners], sem)
-    copy_all(copies)
-    wait_all(copies)
+    served, buf, in_sem, out_sem = refs[-4:]
+    loads = load_blocks(refs[:n], buf, in_sem)
+    copy_all(loads)
+    stores = []
+    for i, k in enumerate(partners):
+        loads[i].wait()
+        group = store_blocks(served, buf, i, pos_ref[0] ^ k, out_sem)
+        copy_all(group)
+        stores += group
+    wait_all(stores)
 
 
 def place_blocks(served, pos, payloads, partners, shape):
-    n = len(partners)
+    n, per_dest = len(partners), shape[0]
     return pl.pallas_call(
         functools.partial(place_kernel, partners),
         in_specs=[SMEM] + [ANY] * (n + len(served)),
         out_specs=ANY,
         out_shape=jax.ShapeDtypeStruct(shape, BF16),
-        scratch_shapes=[pltpu.SemaphoreType.DMA((n, shape[0]))],
+        scratch_shapes=[
+            pltpu.VMEM((n, per_dest * shape[2], TILE), BF16),
+            pltpu.SemaphoreType.DMA((n,)),
+            pltpu.SemaphoreType.DMA((n, per_dest)),
+        ],
         input_output_aliases={1 + n: 0} if served else {},
         compiler_params=LIGHT,
         cost_estimate=pl.CostEstimate(
@@ -388,12 +404,11 @@
 def collect_kernel(order, tiles, lat_tiles, to_place, pos_ref, *refs):
     n = len(order)
     q_refs = refs[:n]
-    served, _, exp_ref, lat_ref, extra, rows_ref, place_sem, sem = refs[n + 2 :]
+    served, _, exp_ref, lat_ref, extra, rows_ref, buf, in_sem, out_sem, sem = refs[n + 2 :]
     pos = pos_ref[0]
     per_dest = served.shape[0]
-    blocks_copies = block_copies(
-        served, [q_refs[i] for i in to_place], [pos ^ order[i] for i in to_place], place_sem
-    )
+    loads = load_blocks([q_refs[i] for i in to_place], buf, in_sem)
+    copy_all(loads)
     copies = [
         pltpu.make_async_copy(
             q.at[pl.ds(q.shape[0] - EXTRA, EXTRA), :], extra.at[i], sem.at[i]
@@ -401,7 +416,12 @@
         for i, q in enumerate(q_refs)
     ]
     copy_all(copies)
-    copy_all(blocks_copies)
+    stores = []
+    for i, at in enumerate(to_place):
+        loads[i].wait()
+        group = store_blocks(served, buf, i, pos ^ order[at], out_sem)
+        copy_all(group)
+        stores += group
     rows_ref[...] = jnp.zeros_like(rows_ref)
     flat = jnp.zeros((8, exp_ref.shape[1]), F32)
     wide = lax.broadcasted_iota(jnp.int32, flat.shape, 1)
@@ -420,7 +440,7 @@
     exp_ref[...] = jnp.max(flat, axis=0, keepdims=True)
     blocks, height = lat_ref.shape
     lat_ref[...] = jnp.transpose(rows_ref[...])[0:blocks, 0:height]
-    wait_all(blocks_copies)
+    wait_all(stores)
 
 
 def collect(served, through, pos, received, groups, tiles, lat_tiles, lat_blocks):
@@ -441,6 +461,8 @@
         scratch_shapes=[
             pltpu.VMEM((n, EXTRA, TILE), BF16),
             pltpu.VMEM((TILE, TILE), F32),
+            pltpu.VMEM((len(to_place), per_dest * served.shape[2], TILE), BF16),
+            pltpu.SemaphoreType.DMA((len(to_place),)),
             pltpu.SemaphoreType.DMA((len(to_place), per_dest)),
             pltpu.SemaphoreType.DMA((n,)),
         ],

time: 95.4 us -> 83.4 us (0.87)
  Pallas kernels: 49.2 us -> 38.2 us
    pallas_call x1, Pallas kernels: 15.8 us -> 3.69 us  [collect(): pl.pallas_call(functools.partial(collect_kernel, order, tiles, lat_tiles,...]
    pallas_call x2, Pallas kernels: 1.9 us -> 3.02 us  [place_blocks(): pl.pallas_call(functools.partial(place_kernel, partners), in_specs=[SMEM]...]
  transfers between devices with their start and end apart: 14 -> 14, of which waited for: 4 -> 4; matrix products, arithmetic and copies ran while one was open for 0% -> 0% of each run, Pallas kernels for 45% -> 39%
where the time goes in v12:
time: 83.4 us; the launch traced here: 82.9 us
  Pallas kernels  38.2 us (46%)
  starting transfers between devices  16.8 us (20%)
  between operations  14.9 us (18%)
  waiting for transfers between devices  12.4 us (15%)
    pallas_call x3, Pallas kernels, expert_group(): pl.pallas_call(functools.partial(expert_kernel, partners, per_dest, n_ali...  19.4 us
    ppermute x10, starting transfers between devices, swap(): lax.ppermute(x, axis, [(i, i ^ k) for i in range(lax.axis_size(axis))])  10.7 us
    ppermute x10, waiting for transfers between devices, swap(): lax.ppermute(x, axis, [(i, i ^ k) for i in range(lax.axis_size(axis))])  8.65 us
    ppermute x3, starting transfers between devices, fast_body(): lax.ppermute(chunk_top, 'expert', [(i, (i + s) % exp_axis) for i in range...  6.11 us
    pallas_call x1, Pallas kernels, latent_update(): pl.pallas_call(functools.partial(latent_kernel, rows // CHUNK), in_specs=...  4.32 us
    ppermute x3, waiting for transfers between devices, fast_body(): lax.ppermute(chunk_top, 'expert', [(i, (i + s) % exp_axis) for i in range...  3.76 us
    pallas_call x1, Pallas kernels, collect(): pl.pallas_call(functools.partial(collect_kernel, order, tiles, lat_tiles,...  3.69 us
    pallas_call x2, Pallas kernels, place_blocks(): pl.pallas_call(functools.partial(place_kernel, partners), in_specs=[SMEM]...  3.02 us
  transfers between devices with their start and end apart: 14, of which 4 were waited for; matrix products, arithmetic and copies ran while one was open for 0% of the time, Pallas kernels for 39%

profile of v12, /device:TPU:0, one launch (start us, length us, event | category | flops | bytes accessed | tf_op | source)
XLA Modules:
  0.0 82.9 jit_solution(5190915966697880317)
XLA Ops:
  7.2 0.0 all-gather.2.cloned.1.call-start
  7.9 4.3 %latent_adamw.1 = (f32[224,1536]{1,0:T(8,128)}, bf16[224,1536]{1,0:T(8,128)(2,1)}, bf16[224,1536]{1,0:T(8,128)(2,1)}, bf16[128,1536]{1,0:T(8,128)(2,1)}, f32[8,128]{1,0:T(8,128)}) custom-call(s32[1]{0:T(128)S(6)} %copy.50.step_ref, s32[1]{0:T(128)} %bitcast.1.pos_ref.line_ref, f32[224,1536]{1,0:T(8,128)} %refs_0_.1, bf16[224,1536]{1,0:T(8,128)(2,1)} %refs_1_.1, ...), custom_call_target="tpu_custom_call" | custom-call | flops 10321920 | bytes 6193152 | tf_op jit(solution)/shard_map/latent_adamw/pallas_call | solution.py:646
  12.2 0.0 all-gather.2.cloned.1.call-update
  12.2 3.1 %collective-permute-start = (f32[8,128]{1,0:T(8,128)}, f32[8,128]{1,0:T(8,128)S(1)}, u32[]{:S(2)}, u32[]{:S(2)}) collective-permute-start(f32[8,128]{1,0:T(8,128)} %get-tuple-element.41.refs_0_.own_ref), channel_id=1, source_target_pairs={{0,1},{1,2},{2,3},{3,0},{4,5},{5,6},{6,7},{7,4},{8,9},{9,10},{10,1... | collective-permute-start | bytes 12296 | tf_op jit(solution)/shard_map/ppermute | solution.py:800
  15.3 2.1 %collective-permute-start.2 = (f32[8,128]{1,0:T(8,128)}, f32[8,128]{1,0:T(8,128)S(1)}, u32[]{:S(2)}, u32[]{:S(2)}) collective-permute-start(f32[8,128]{1,0:T(8,128)} %get-tuple-element.41.refs_0_.own_ref), channel_id=1, source_target_pairs={{0,3},{1,0},{2,1},{3,2},{4,7},{5,4},{6,5},{7,6},{8,11},{9,8},{10,9... | collective-permute-start | bytes 12296 | tf_op jit(solution)/shard_map/ppermute | solution.py:800
  17.4 0.9 %collective-permute-start.1 = (f32[8,128]{1,0:T(8,128)}, f32[8,128]{1,0:T(8,128)S(1)}, u32[]{:S(2)}, u32[]{:S(2)}) collective-permute-start(f32[8,128]{1,0:T(8,128)} %get-tuple-element.41.refs_0_.own_ref), channel_id=1, source_target_pairs={{0,2},{1,3},{2,0},{3,1},{4,6},{5,7},{6,4},{7,5},{8,10},{9,11},{10,... | collective-permute-start | bytes 12296 | tf_op jit(solution)/shard_map/ppermute | solution.py:800
  18.3 0.8 collective-permute-done.refs_1_.prev_ref
  19.2 0.0 copy-start.1
  19.2 0.0 collective-permute-done.2.refs_3_.next_ref
  19.2 0.0 copy-start.2
  19.2 2.9 %collective-permute-done.1.refs_2_ = f32[8,128]{1,0:T(8,128)S(1)} collective-permute-done((f32[8,128]{1,0:T(8,128)}, f32[8,128]{1,0:T(8,128)S(1)}, u32[]{:S(2)}, u32[]{:S(2)}) %collective-permute-start.1) | collective-permute-done | bytes 4128 | tf_op jit(solution)/shard_map/ppermute | solution.py:800
  22.1 0.0 copy-start.3
  22.1 0.0 copy-done.1
  22.1 0.0 copy-done.2
  22.1 0.6 copy-done.3
  22.7 5.7 %expert_adamw.3 = (f32[896,2048]{1,0:T(8,128)}, bf16[896,2048]{1,0:T(8,128)(2,1)}, bf16[896,2048]{1,0:T(8,128)(2,1)}, bf16[1808,128]{1,0:T(8,128)(2,1)}, bf16[1808,128]{1,0:T(8,128)(2,1)}, /*index=5*/f32[8,128]{1,0:T(8,128)}) custom-call(s32[16]{0:T(128)} %owner_ref.5, s32[1]{0:T(128)} %bitcast.pos_ref, s32[1]{0:T(128)} %bitcast.1.pos_ref.line_ref, ...), custom_call_target="tpu_custom_call" | custom-call | flops 458752 | bytes 458752 | tf_op jit(solution)/shard_map/expert_adamw/pallas_call | solution.py:316
  28.4 1.7 %collective-permute-start.3 = (bf16[1808,128]{1,0:T(8,128)(2,1)}, bf16[1808,128]{1,0:T(8,128)(2,1)S(1)}, u32[]{:S(2)}, u32[]{:S(2)}) collective-permute-start(bf16[1808,128]{1,0:T(8,128)(2,1)} %get-tuple-element.49), channel_id=1, source_target_pairs={{0,16},{4,20},{8,24},{12,28},{16,0},{20,4},{24,8},{28,12},{1,17},{... | collective-permute-start | bytes 1388552 | tf_op jit(solution)/shard_map/ppermute | solution.py:808
  30.1 1.5 %collective-permute-start.4 = (bf16[1808,128]{1,0:T(8,128)(2,1)}, bf16[1808,128]{1,0:T(8,128)(2,1)S(1)}, u32[]{:S(2)}, u32[]{:S(2)}) collective-permute-start(bf16[1808,128]{1,0:T(8,128)(2,1)} %get-tuple-element.50), channel_id=1, source_target_pairs={{0,8},{4,12},{8,0},{12,4},{16,24},{20,28},{24,16},{28,20},{1,9},{5... | collective-permute-start | bytes 1388552 | tf_op jit(solution)/shard_map/ppermute | solution.py:808
  31.6 5.1 %expert_adamw.4 = (f32[896,2048]{1,0:T(8,128)}, bf16[896,2048]{1,0:T(8,128)(2,1)}, bf16[896,2048]{1,0:T(8,128)(2,1)}, bf16[1808,128]{1,0:T(8,128)(2,1)}, bf16[1808,128]{1,0:T(8,128)(2,1)}) custom-call(s32[16]{0:T(128)} %owner_ref.5, s32[1]{0:T(128)} %bitcast.pos_ref, ...), custom_call_target="tpu_custom_call", output_to_operand_aliasing={{0}: (9, {}), {1}: (10, {}), {2}: (11, {})} | custom-call | flops 458752 | bytes 458752 | tf_op jit(solution)/shard_map/expert_adamw/pallas_call | solution.py:316
  36.7 0.1 collective-permute-start.5
  36.8 0.5 collective-permute-start.6
  37.2 2.8 %latent_rest.1.refs_0_ = bf16[96,1536]{1,0:T(8,128)(2,1)} custom-call(s32[1]{0:T(128)} %bitcast.1.pos_ref.line_ref, f32[224,1536]{1,0:T(8,128)} %get-tuple-element.36.w1_ref, f32[8,128]{1,0:T(8,128)} %get-tuple-element.41.refs_0_.own_ref, f32[8,128]{1,0:T(8,128)} %copy-done.1, f32[8,128]{1,0:T(8,128)} %copy-done.2, bf16[1808,128]{1,0:T(8,128)(2,1)} %get-tuple-element.54.after_ref), custom_call_target="tpu_custom_call" | custom-call | flops 344064 | bytes 1032192 | tf_op jit(solution)/shard_map/latent_rest/pallas_call | solution.py:724
  40.0 0.2 collective-permute-start.10
  40.2 0.0 collective-permute-done.3.refs_0_
  40.2 2.5 %collective-permute-start.11 = (bf16[96,1536]{1,0:T(8,128)(2,1)}, bf16[96,1536]{1,0:T(8,128)(2,1)S(1)}, u32[]{:S(2)}, u32[]{:S(2)}) collective-permute-start(bf16[96,1536]{1,0:T(8,128)(2,1)} %latent_rest.1.refs_0_), channel_id=1, source_target_pairs={{0,2},{1,3},{2,0},{3,1},{4,6},{5,7},{6,4},{7,5},{8,10},{9,11},{10,... | collective-permute-start | bytes 884744 | tf_op jit(solution)/shard_map/ppermute | solution.py:808
  42.7 0.0 collective-permute-done.4.refs_1_
  42.7 1.5 %place_served.2.refs_8_ = bf16[2,8,896,128]{3,2,1,0:T(8,128)(2,1)} custom-call(s32[1]{0:T(128)} %bitcast.pos_ref, bf16[1808,128]{1,0:T(8,128)(2,1)S(1)} %collective-permute-done.3.refs_0_, bf16[1808,128]{1,0:T(8,128)(2,1)S(1)} %collective-permute-done.4.refs_1_), custom_call_target="tpu_custom_call" | custom-call | bytes 1851392 | tf_op jit(solution)/shard_map/place_served/pallas_call | solution.py:385
  44.2 8.7 %expert_adamw.5 = (f32[896,2048]{1,0:T(8,128)}, bf16[896,2048]{1,0:T(8,128)(2,1)}, bf16[896,2048]{1,0:T(8,128)(2,1)}, bf16[1808,128]{1,0:T(8,128)(2,1)}, bf16[18...) custom-call(s32[16]{0:T(128)} %owner_ref.5, ...), custom_call_target="tpu_custom_call", output_to_operand_aliasing={{0}: (9, {}), {1}: (10, {}), {2}: (11, {}), {7}: (12, {})} | custom-call | flops 917504 | bytes 917504 | tf_op jit(solution)/shard_map/expert_adamw/pallas_call | solution.py:316
  52.9 1.8 %collective-permute-start.7 = (bf16[1808,128]{1,0:T(8,128)(2,1)}, bf16[1808,128]{1,0:T(8,128)(2,1)S(1)}, u32[]{:S(2)}, u32[]{:S(2)}) collective-permute-start(bf16[1808,128]{1,0:T(8,128)(2,1)} %get-tuple-element.56), channel_id=1, source_target_pairs={{0,20},{4,16},{8,28},{12,24},{16,4},{20,0},{24,12},{28,8},{1,21},{... | collective-permute-start | bytes 1388552 | tf_op jit(solution)/shard_map/ppermute | solution.py:808
  54.7 0.0 collective-permute-done.5.refs_0_.refs_2_
  54.7 1.0 %collective-permute-start.8 = (bf16[1808,128]{1,0:T(8,128)(2,1)}, bf16[1808,128]{1,0:T(8,128)(2,1)S(1)}, u32[]{:S(2)}, u32[]{:S(2)}) collective-permute-start(bf16[1808,128]{1,0:T(8,128)(2,1)} %get-tuple-element.57), channel_id=1, source_target_pairs={{0,12},{4,8},{8,4},{12,0},{16,28},{20,24},{24,20},{28,16},{1,13},{... | collective-permute-start | bytes 1388552 | tf_op jit(solution)/shard_map/ppermute | solution.py:808
  55.6 6.7 %collective-permute-done.6.refs_1_.refs_3_ = bf16[1808,128]{1,0:T(8,128)(2,1)S(1)} collective-permute-done((bf16[1808,128]{1,0:T(8,128)(2,1)}, bf16[1808,128]{1,0:T(8,128)(2,1)S(1)}, u32[]{:S(2)}, u32[]{:S(2)}) %collective-permute-start.6) | collective-permute-done | bytes 462880 | tf_op jit(solution)/shard_map/ppermute | solution.py:808
  62.3 0.0 collective-permute-start.9
  62.3 1.5 %place_served.3.refs_2_ = bf16[2,8,896,128]{3,2,1,0:T(8,128)(2,1)} custom-call(s32[1]{0:T(128)} %bitcast.pos_ref, bf16[1808,128]{1,0:T(8,128)(2,1)S(1)} %collective-permute-done.5.refs_0_.refs_2_, bf16[1808,128]{1,0:T(8,128)(2,1)S(1)} %collective-permute-done.6.refs_1_.refs_3_, ...), custom_call_target="tpu_custom_call", output_to_operand_aliasing={{}: (3, {})} | custom-call | bytes 1851392 | tf_op jit(solution)/shard_map/place_served/pallas_call | solution.py:385
  63.8 0.0 collective-permute-done.10.refs_0_
  63.8 0.0 collective-permute-done.11.refs_1_
  63.8 1.5 %collective-permute-start.12 = (bf16[96,1536]{1,0:T(8,128)(2,1)S(1)}, bf16[96,1536]{1,0:T(8,128)(2,1)}, u32[]{:S(2)}, u32[]{:S(2)}) collective-permute-start(bf16[96,1536]{1,0:T(8,128)(2,1)S(1)} %get-tuple-element.64.refs_1_), channel_id=1, source_target_pairs={{0,1},{1,0},{2,3},{3,2},{4,5},{5,4},{6,7},{7,6},{8,9},{9,8},{10,11... | collective-permute-start | bytes 884744 | tf_op jit(solution)/shard_map/ppermute | solution.py:808
  65.3 0.0 all-gather.2.cloned.1.call-done.x_ref
  65.3 2.3 %place_whole.1.refs_2_ = bf16[896,1536]{1,0:T(8,128)(2,1)} custom-call(s32[1]{0:T(128)} %bitcast.1.pos_ref.line_ref, bf16[512,1536]{1,0:T(8,128)(2,1)} %all-gather.2.cloned.1.call-done.x_ref, bf16[96,1536]{1,0:T(8,128)(2,1)} %latent_rest.1.refs_0_), custom_call_target="tpu_custom_call" | custom-call | bytes 3145728 | tf_op jit(solution)/shard_map/place_whole/pallas_call | solution.py:544
  67.7 0.0 copy-start
  67.7 1.0 %place_rest.2.refs_9_ = bf16[896,1536]{1,0:T(8,128)(2,1)} custom-call(s32[1]{0:T(128)} %bitcast.1.pos_ref.line_ref, bf16[96,1536]{1,0:T(8,128)(2,1)S(1)} %get-tuple-element.63.refs_0_, bf16[96,1536]{1,0:T(8,128)(2,1)S(1)} %get-tuple-element.64.refs_1_, bf16[896,1536]{1,0:T(8,128)(2,1)} %place_whole.1.refs_2_), custom_call_target="tpu_custom_call", output_to_operand_aliasing={{}: (3, {})} | custom-call | bytes 1000000 | tf_op jit(solution)/shard_map/place_rest/pallas_call | solution.py:494
  68.7 2.0 %collective-permute-done.7.refs_4_ = bf16[1808,128]{1,0:T(8,128)(2,1)S(1)} collective-permute-done((bf16[1808,128]{1,0:T(8,128)(2,1)}, bf16[1808,128]{1,0:T(8,128)(2,1)S(1)}, u32[]{:S(2)}, u32[]{:S(2)}) %collective-permute-start.7) | collective-permute-done | bytes 462880 | tf_op jit(solution)/shard_map/ppermute | solution.py:808
  70.7 0.0 collective-permute-done.8.refs_5_
  70.7 0.0 collective-permute-done.9.refs_6_
  70.7 0.0 copy-done
  70.7 3.7 %place_last.1 = (bf16[2,8,896,128]{3,2,1,0:T(8,128)(2,1)}, bf16[896,1536]{1,0:T(8,128)(2,1)}, f32[1,112]{1,0:T(1,128)}, f32[12,56]{1,0:T(8,128)}) custom-call(s32[1]{0:T(128)} %bitcast.pos_ref, bf16[1808,128]{1,0:T(8,128)(2,1)S(1)} %collective-permute-done.3.refs_0_, ...), custom_call_target="tpu_custom_call", output_to_operand_aliasing={{0}: (9, {}), {1}: (10, {})} | custom-call | flops 1000000 | bytes 1000000 | tf_op jit(solution)/shard_map/place_last/pallas_call | solution.py:451
  74.4 0.0 collective-permute-done.12.refs_0_
  74.4 1.7 %place_rest.3 = bf16[896,1536]{1,0:T(8,128)(2,1)} custom-call(s32[1]{0:T(128)} %bitcast.1.pos_ref.line_ref, bf16[96,1536]{1,0:T(8,128)(2,1)} %collective-permute-done.12.refs_0_, bf16[896,1536]{1,0:T(8,128)(2,1)} %get-tuple-element.70.refs_1_), custom_call_target="tpu_custom_call", output_to_operand_aliasing={{}: (2, {})} | custom-call | bytes 1000000 | tf_op jit(solution)/shard_map/place_rest/pallas_call | solution.py:494
  (1 shorter events, 0.0 us)
Async XLA Ops:
  7.2 58.1 %all-gather.2.cloned.1.call-start = ((), (), s32[]{:S(2)}) async-start(), calls=%async_computation | async-start | bytes 1966080 | tf_op jit(solution)/shard_map/all_gather | solution.py:798
  12.2 6.9 %collective-permute-start = (f32[8,128]{1,0:T(8,128)}, f32[8,128]{1,0:T(8,128)S(1)}, u32[]{:S(2)}, u32[]{:S(2)}) collective-permute-start(f32[8,128]{1,0:T(8,128)} %get-tuple-element.41.refs_0_.own_ref), channel_id=1, source_target_pairs={{0,1},{1,2},{2,3},{3,0},{4,5},{5,6},{6,7},{7,4},{8,9},{9,10},{10,1... | collective-permute-start | bytes 12296 | tf_op jit(solution)/shard_map/ppermute | solution.py:800
  15.3 3.9 %collective-permute-start.2 = (f32[8,128]{1,0:T(8,128)}, f32[8,128]{1,0:T(8,128)S(1)}, u32[]{:S(2)}, u32[]{:S(2)}) collective-permute-start(f32[8,128]{1,0:T(8,128)} %get-tuple-element.41.refs_0_.own_ref), channel_id=1, source_target_pairs={{0,3},{1,0},{2,1},{3,2},{4,7},{5,4},{6,5},{7,6},{8,11},{9,8},{10,9... | collective-permute-start | bytes 12296 | tf_op jit(solution)/shard_map/ppermute | solution.py:800
  17.4 4.7 %collective-permute-start.1 = (f32[8,128]{1,0:T(8,128)}, f32[8,128]{1,0:T(8,128)S(1)}, u32[]{:S(2)}, u32[]{:S(2)}) collective-permute-start(f32[8,128]{1,0:T(8,128)} %get-tuple-element.41.refs_0_.own_ref), channel_id=1, source_target_pairs={{0,2},{1,3},{2,0},{3,1},{4,6},{5,7},{6,4},{7,5},{8,10},{9,11},{10,... | collective-permute-start | bytes 12296 | tf_op jit(solution)/shard_map/ppermute | solution.py:800
  19.2 3.0 %copy-start.1 = (f32[8,128]{1,0:T(8,128)}, f32[8,128]{1,0:T(8,128)S(1)}, u32[]{:S(2)}) copy-start(f32[8,128]{1,0:T(8,128)S(1)} %collective-permute-done.refs_1_.prev_ref) | copy-start | bytes 12292
  19.2 2.9 %copy-start.2 = (f32[8,128]{1,0:T(8,128)}, f32[8,128]{1,0:T(8,128)S(1)}, u32[]{:S(2)}) copy-start(f32[8,128]{1,0:T(8,128)S(1)} %collective-permute-done.2.refs_3_.next_ref) | copy-start | bytes 12292
  22.1 0.6 copy-start.3
  28.4 11.8 %collective-permute-start.3 = (bf16[1808,128]{1,0:T(8,128)(2,1)}, bf16[1808,128]{1,0:T(8,128)(2,1)S(1)}, u32[]{:S(2)}, u32[]{:S(2)}) collective-permute-start(bf16[1808,128]{1,0:T(8,128)(2,1)} %get-tuple-element.49), channel_id=1, source_target_pairs={{0,16},{4,20},{8,24},{12,28},{16,0},{20,4},{24,8},{28,12},{1,17},{... | collective-permute-start | bytes 1388552 | tf_op jit(solution)/shard_map/ppermute | solution.py:808
  30.1 12.6 %collective-permute-start.4 = (bf16[1808,128]{1,0:T(8,128)(2,1)}, bf16[1808,128]{1,0:T(8,128)(2,1)S(1)}, u32[]{:S(2)}, u32[]{:S(2)}) collective-permute-start(bf16[1808,128]{1,0:T(8,128)(2,1)} %get-tuple-element.50), channel_id=1, source_target_pairs={{0,8},{4,12},{8,0},{12,4},{16,24},{20,28},{24,16},{28,20},{1,9},{5... | collective-permute-start | bytes 1388552 | tf_op jit(solution)/shard_map/ppermute | solution.py:808
  36.7 18.0 %collective-permute-start.5 = (bf16[1808,128]{1,0:T(8,128)(2,1)}, bf16[1808,128]{1,0:T(8,128)(2,1)S(1)}, u32[]{:S(2)}, u32[]{:S(2)}) collective-permute-start(bf16[1808,128]{1,0:T(8,128)(2,1)} %get-tuple-element.54.after_ref), channel_id=1, source_target_pairs={{0,28},{4,24},{8,20},{12,16},{16,12},{20,8},{24,4},{28,0},{1,29},{... | collective-permute-start | bytes 1388552 | tf_op jit(solution)/shard_map/ppermute | solution.py:808
  36.8 25.5 %collective-permute-start.6 = (bf16[1808,128]{1,0:T(8,128)(2,1)}, bf16[1808,128]{1,0:T(8,128)(2,1)S(1)}, u32[]{:S(2)}, u32[]{:S(2)}) collective-permute-start(bf16[1808,128]{1,0:T(8,128)(2,1)} %get-tuple-element.55), channel_id=1, source_target_pairs={{0,24},{4,28},{8,16},{12,20},{16,8},{20,12},{24,0},{28,4},{1,25},{... | collective-permute-start | bytes 1388552 | tf_op jit(solution)/shard_map/ppermute | solution.py:808
  40.0 23.8 %collective-permute-start.10 = (bf16[96,1536]{1,0:T(8,128)(2,1)}, bf16[96,1536]{1,0:T(8,128)(2,1)S(1)}, u32[]{:S(2)}, u32[]{:S(2)}) collective-permute-start(bf16[96,1536]{1,0:T(8,128)(2,1)} %latent_rest.1.refs_0_), channel_id=1, source_target_pairs={{0,1},{1,0},{2,3},{3,2},{4,5},{5,4},{6,7},{7,6},{8,9},{9,8},{10,11... | collective-permute-start | bytes 884744 | tf_op jit(solution)/shard_map/ppermute | solution.py:808
  40.2 23.6 %collective-permute-start.11 = (bf16[96,1536]{1,0:T(8,128)(2,1)}, bf16[96,1536]{1,0:T(8,128)(2,1)S(1)}, u32[]{:S(2)}, u32[]{:S(2)}) collective-permute-start(bf16[96,1536]{1,0:T(8,128)(2,1)} %latent_rest.1.refs_0_), channel_id=1, source_target_pairs={{0,2},{1,3},{2,0},{3,1},{4,6},{5,7},{6,4},{7,5},{8,10},{9,11},{10,... | collective-permute-start | bytes 884744 | tf_op jit(solution)/shard_map/ppermute | solution.py:808
  52.9 17.8 %collective-permute-start.7 = (bf16[1808,128]{1,0:T(8,128)(2,1)}, bf16[1808,128]{1,0:T(8,128)(2,1)S(1)}, u32[]{:S(2)}, u32[]{:S(2)}) collective-permute-start(bf16[1808,128]{1,0:T(8,128)(2,1)} %get-tuple-element.56), channel_id=1, source_target_pairs={{0,20},{4,16},{8,28},{12,24},{16,4},{20,0},{24,12},{28,8},{1,21},{... | collective-permute-start | bytes 1388552 | tf_op jit(solution)/shard_map/ppermute | solution.py:808
  54.7 16.0 %collective-permute-start.8 = (bf16[1808,128]{1,0:T(8,128)(2,1)}, bf16[1808,128]{1,0:T(8,128)(2,1)S(1)}, u32[]{:S(2)}, u32[]{:S(2)}) collective-permute-start(bf16[1808,128]{1,0:T(8,128)(2,1)} %get-tuple-element.57), channel_id=1, source_target_pairs={{0,12},{4,8},{8,4},{12,0},{16,28},{20,24},{24,20},{28,16},{1,13},{... | collective-permute-start | bytes 1388552 | tf_op jit(solution)/shard_map/ppermute | solution.py:808
  62.3 8.4 %collective-permute-start.9 = (bf16[1808,128]{1,0:T(8,128)(2,1)}, bf16[1808,128]{1,0:T(8,128)(2,1)}, u32[]{:S(2)}, u32[]{:S(2)}) collective-permute-start(bf16[1808,128]{1,0:T(8,128)(2,1)} %get-tuple-element.58), channel_id=1, source_target_pairs={{0,4},{4,0},{8,12},{12,8},{16,20},{20,16},{24,28},{28,24},{1,5},{5... | collective-permute-start | bytes 1388552 | tf_op jit(solution)/shard_map/ppermute | solution.py:808
  63.8 10.5 %collective-permute-start.12 = (bf16[96,1536]{1,0:T(8,128)(2,1)S(1)}, bf16[96,1536]{1,0:T(8,128)(2,1)}, u32[]{:S(2)}, u32[]{:S(2)}) collective-permute-start(bf16[96,1536]{1,0:T(8,128)(2,1)S(1)} %get-tuple-element.64.refs_1_), channel_id=1, source_target_pairs={{0,1},{1,0},{2,3},{3,2},{4,5},{5,4},{6,7},{7,6},{8,9},{9,8},{10,11... | collective-permute-start | bytes 884744 | tf_op jit(solution)/shard_map/ppermute | solution.py:808
  67.7 3.0 %copy-start = (bf16[16,128]{1,0:T(8,128)(2,1)S(1)}, bf16[16,128]{1,0:T(8,128)(2,1)}, u32[]{:S(2)}) copy-start(bf16[16,128]{1,0:T(8,128)(2,1)} %get-tuple-element.59.refs_7_) | copy-start | bytes 12292
Sparse Core Ops, SparseCore 0:
  12.3 47.9 all-gather.1

commit v13 on v11

--- a/solution.py
+++ b/solution.py
@@ -454,7 +454,7 @@
 
 def rest_kernel(deltas, rows, pos_ref, *refs):
     n = len(deltas)
-    latent, buf, in_sem, out_sem = refs[n + 1 :]
+    latent, buf, in_sem, out_sem = refs[-4:]
     loads = [pltpu.make_async_copy(refs[i], buf.at[i], in_sem.at[i]) for i in range(n)]
     copy_all(loads)
     copies = []
@@ -466,24 +466,24 @@
     wait_all(copies)
 
 
-def place_rest(latent, pos, rest, deltas):
+def place_rest(out, pos, rest, deltas, rows, peers):
     n = len(rest)
     span, cols = rest[0].shape
     return pl.pallas_call(
-        functools.partial(rest_kernel, deltas, TILE + span),
-        in_specs=[SMEM] + [ANY] * (n + 1),
+        functools.partial(rest_kernel, deltas, rows),
+        in_specs=[SMEM] + [ANY] * (n + len(out)),
         out_specs=ANY,
-        out_shape=jax.ShapeDtypeStruct(latent.shape, latent.dtype),
+        out_shape=jax.ShapeDtypeStruct((peers * rows, cols), BF16),
         scratch_shapes=[
             pltpu.VMEM((n, span, cols), BF16),
             pltpu.SemaphoreType.DMA((n,)),
             pltpu.SemaphoreType.DMA((n, span // CHUNK)),
         ],
-        input_output_aliases={1 + n: 0},
+        input_output_aliases={1 + n: 0} if out else {},
         compiler_params=pltpu.CompilerParams(vmem_limit_bytes=4 * 1024 * 1024),
         cost_estimate=pl.CostEstimate(flops=0, bytes_accessed=1000000, transcendentals=0),
         name="place_rest",
-    )(pos, *rest, latent)
+    )(pos, *rest, *out)
 
 
 def whole_tile(pos, rows):
@@ -492,7 +492,7 @@
 
 def full_kernel(pieces, rows, deltas, pos_ref, x_ref, *refs):
     n = len(deltas)
-    out_ref, buf, rest, in_sem, out_sem, rest_in, rest_out = refs[n:]
+    out_ref, buf, rest, in_sem, out_sem, rest_in, rest_out = refs[n + 1 :]
     loads, stores = [], []
     for i in range(pieces):
         lead = i * (TILE - rows % TILE) % TILE
@@ -516,12 +516,12 @@
     wait_all(stores)
 
 
-def place_full(pos, x, xs, deltas, rows):
+def place_full(out, pos, x, xs, deltas, rows):
     pieces, n = x.shape[0] // TILE, len(xs)
     span, cols = xs[0].shape
     return pl.pallas_call(
         functools.partial(full_kernel, pieces, rows, deltas),
-        in_specs=[SMEM] + [ANY] * (1 + n),
+        in_specs=[SMEM] + [ANY] * (2 + n),
         out_specs=ANY,
         out_shape=jax.ShapeDtypeStruct((pieces * rows, cols), BF16),
         scratch_shapes=[
@@ -532,10 +532,11 @@
             pltpu.SemaphoreType.DMA((n,)),
             pltpu.SemaphoreType.DMA((n, span // CHUNK)),
         ],
+        input_output_aliases={2 + n: 0},
         compiler_params=PARAMS,
         cost_estimate=pl.CostEstimate(flops=0, bytes_accessed=4 * x.size, transcendentals=0),
         name="place_whole",
-    )(pos, x, *xs)
+    )(pos, x, *xs, out)
 
 
 def rest_stores(buf, i, peer, rows, out_ref, sem):
@@ -826,8 +827,8 @@
     )
     near, far, served = in_order(near, far, served)
     last = swap(far, "expert", 1)
-    latent_served = place_full(expert_at, whole, [rest], [0], latent_rows)
-    latent_served = place_rest(latent_served, expert_at, [near, far], [1, 2])
+    latent_served = place_rest((), expert_at, [near, far], [1, 2], latent_rows, exp_axis)
+    latent_served = place_full(latent_served, expert_at, whole, [rest], [0], latent_rows)
     served, latent_served, expert_scales, latent_scales = collect(
         served,
         latent_served,
@@ -838,7 +839,9 @@
         latent_rows * exp_axis // TILE,
         latent_new.shape[1] // TILE,
     )
-    latent_served = place_rest(latent_served, expert_at, [last], [3])
+    latent_served = place_rest(
+        (latent_served,), expert_at, [last], [3], latent_rows, exp_axis
+    )
     expert_served = served.reshape(1, block_count * rows, TILE)
 
     return (

time: 95.4 us -> 81.8 us (0.86)
  Pallas kernels: 49.2 us -> 35.4 us
    pallas_call x1, Pallas kernels: 15.8 us -> 1.96 us  [collect(): pl.pallas_call(functools.partial(collect_kernel, order, tiles, lat_tiles,...]
  transfers between devices with their start and end apart: 14 -> 14, of which waited for: 4 -> 5; matrix products, arithmetic and copies ran while one was open for 0% -> 0% of each run, Pallas kernels for 45% -> 36%
where the time goes in v13:
time: 81.8 us; the launch traced here: 81.4 us
  Pallas kernels  35.4 us (43%)
  starting transfers between devices  17.4 us (21%)
  between operations  14.9 us (18%)
  waiting for transfers between devices  13.2 us (16%)
    pallas_call x3, Pallas kernels, expert_group(): pl.pallas_call(functools.partial(expert_kernel, partners, per_dest, n_ali...  19.4 us
    ppermute x10, starting transfers between devices, swap(): lax.ppermute(x, axis, [(i, i ^ k) for i in range(lax.axis_size(axis))])  11.2 us
    ppermute x10, waiting for transfers between devices, swap(): lax.ppermute(x, axis, [(i, i ^ k) for i in range(lax.axis_size(axis))])  9.41 us
    ppermute x3, starting transfers between devices, fast_body(): lax.ppermute(chunk_top, 'expert', [(i, (i + s) % exp_axis) for i in range...  6.11 us
    pallas_call x1, Pallas kernels, latent_update(): pl.pallas_call(functools.partial(latent_kernel, rows // CHUNK), in_specs=...  4.32 us
    ppermute x3, waiting for transfers between devices, fast_body(): lax.ppermute(chunk_top, 'expert', [(i, (i + s) % exp_axis) for i in range...  3.76 us
    pallas_call x1, Pallas kernels, latent_rest(): pl.pallas_call(functools.partial(latent_rest_kernel, chunks), in_specs=[S...  2.76 us
    pallas_call x2, Pallas kernels, place_rest(): pl.pallas_call(functools.partial(rest_kernel, deltas, rows), in_specs=[SM...  2.7 us
  transfers between devices with their start and end apart: 14, of which 5 were waited for; matrix products, arithmetic and copies ran while one was open for 0% of the time, Pallas kernels for 36%

profile of v13, /device:TPU:0, one launch (start us, length us, event | category | flops | bytes accessed | tf_op | source)
XLA Modules:
  0.0 81.4 jit_solution(15924006872658319039)
XLA Ops:
  7.2 0.0 all-gather.2.cloned.1.call-start
  7.9 4.3 %latent_adamw.1 = (f32[224,1536]{1,0:T(8,128)}, bf16[224,1536]{1,0:T(8,128)(2,1)}, bf16[224,1536]{1,0:T(8,128)(2,1)}, bf16[128,1536]{1,0:T(8,128)(2,1)}, f32[8,128]{1,0:T(8,128)}) custom-call(s32[1]{0:T(128)S(6)} %copy.50.step_ref, s32[1]{0:T(128)} %bitcast.1.pos_ref.line_ref, f32[224,1536]{1,0:T(8,128)} %refs_0_.1, bf16[224,1536]{1,0:T(8,128)(2,1)} %refs_1_.1, ...), custom_call_target="tpu_custom_call" | custom-call | flops 10321920 | bytes 6193152 | tf_op jit(solution)/shard_map/latent_adamw/pallas_call | solution.py:625
  12.2 0.0 all-gather.2.cloned.1.call-update
  12.2 3.1 %collective-permute-start = (f32[8,128]{1,0:T(8,128)}, f32[8,128]{1,0:T(8,128)S(1)}, u32[]{:S(2)}, u32[]{:S(2)}) collective-permute-start(f32[8,128]{1,0:T(8,128)} %get-tuple-element.41.refs_0_.own_ref), channel_id=1, source_target_pairs={{0,1},{1,2},{2,3},{3,0},{4,5},{5,6},{6,7},{7,4},{8,9},{9,10},{10,1... | collective-permute-start | bytes 12296 | tf_op jit(solution)/shard_map/ppermute | solution.py:779
  15.3 2.1 %collective-permute-start.2 = (f32[8,128]{1,0:T(8,128)}, f32[8,128]{1,0:T(8,128)S(1)}, u32[]{:S(2)}, u32[]{:S(2)}) collective-permute-start(f32[8,128]{1,0:T(8,128)} %get-tuple-element.41.refs_0_.own_ref), channel_id=1, source_target_pairs={{0,3},{1,0},{2,1},{3,2},{4,7},{5,4},{6,5},{7,6},{8,11},{9,8},{10,9... | collective-permute-start | bytes 12296 | tf_op jit(solution)/shard_map/ppermute | solution.py:779
  17.4 0.9 %collective-permute-start.1 = (f32[8,128]{1,0:T(8,128)}, f32[8,128]{1,0:T(8,128)S(1)}, u32[]{:S(2)}, u32[]{:S(2)}) collective-permute-start(f32[8,128]{1,0:T(8,128)} %get-tuple-element.41.refs_0_.own_ref), channel_id=1, source_target_pairs={{0,2},{1,3},{2,0},{3,1},{4,6},{5,7},{6,4},{7,5},{8,10},{9,11},{10,... | collective-permute-start | bytes 12296 | tf_op jit(solution)/shard_map/ppermute | solution.py:779
  18.3 0.8 %collective-permute-done.refs_1_.prev_ref = f32[8,128]{1,0:T(8,128)S(1)} collective-permute-done((f32[8,128]{1,0:T(8,128)}, f32[8,128]{1,0:T(8,128)S(1)}, u32[]{:S(2)}, u32[]{:S(2)}) %collective-permute-start) | collective-permute-done | bytes 4128 | tf_op jit(solution)/shard_map/ppermute | solution.py:779
  19.2 0.0 copy-start.1
  19.2 0.0 collective-permute-done.2.refs_3_.next_ref
  19.2 0.0 copy-start.2
  19.2 2.9 %collective-permute-done.1.refs_2_ = f32[8,128]{1,0:T(8,128)S(1)} collective-permute-done((f32[8,128]{1,0:T(8,128)}, f32[8,128]{1,0:T(8,128)S(1)}, u32[]{:S(2)}, u32[]{:S(2)}) %collective-permute-start.1) | collective-permute-done | bytes 4128 | tf_op jit(solution)/shard_map/ppermute | solution.py:779
  22.1 0.0 copy-start.3
  22.1 0.0 copy-done.1
  22.1 0.0 copy-done.2
  22.1 0.6 copy-done.3
  22.7 5.7 %expert_adamw.3 = (f32[896,2048]{1,0:T(8,128)}, bf16[896,2048]{1,0:T(8,128)(2,1)}, bf16[896,2048]{1,0:T(8,128)(2,1)}, bf16[1808,128]{1,0:T(8,128)(2,1)}, bf16[1808,128]{1,0:T(8,128)(2,1)}, /*index=5*/f32[8,128]{1,0:T(8,128)}) custom-call(s32[16]{0:T(128)} %owner_ref.5, s32[1]{0:T(128)} %bitcast.pos_ref, s32[1]{0:T(128)} %bitcast.1.pos_ref.line_ref, ...), custom_call_target="tpu_custom_call" | custom-call | flops 458752 | bytes 458752 | tf_op jit(solution)/shard_map/expert_adamw/pallas_call | solution.py:316
  28.4 1.7 %collective-permute-start.3 = (bf16[1808,128]{1,0:T(8,128)(2,1)}, bf16[1808,128]{1,0:T(8,128)(2,1)S(1)}, u32[]{:S(2)}, u32[]{:S(2)}) collective-permute-start(bf16[1808,128]{1,0:T(8,128)(2,1)} %get-tuple-element.49), channel_id=1, source_target_pairs={{0,16},{4,20},{8,24},{12,28},{16,0},{20,4},{24,8},{28,12},{1,17},{... | collective-permute-start | bytes 1388552 | tf_op jit(solution)/shard_map/ppermute | solution.py:787
  30.1 1.5 %collective-permute-start.4 = (bf16[1808,128]{1,0:T(8,128)(2,1)}, bf16[1808,128]{1,0:T(8,128)(2,1)S(1)}, u32[]{:S(2)}, u32[]{:S(2)}) collective-permute-start(bf16[1808,128]{1,0:T(8,128)(2,1)} %get-tuple-element.50), channel_id=1, source_target_pairs={{0,8},{4,12},{8,0},{12,4},{16,24},{20,28},{24,16},{28,20},{1,9},{5... | collective-permute-start | bytes 1388552 | tf_op jit(solution)/shard_map/ppermute | solution.py:787
  31.6 5.1 %expert_adamw.4 = (f32[896,2048]{1,0:T(8,128)}, bf16[896,2048]{1,0:T(8,128)(2,1)}, bf16[896,2048]{1,0:T(8,128)(2,1)}, bf16[1808,128]{1,0:T(8,128)(2,1)}, bf16[1808,128]{1,0:T(8,128)(2,1)}) custom-call(s32[16]{0:T(128)} %owner_ref.5, s32[1]{0:T(128)} %bitcast.pos_ref, ...), custom_call_target="tpu_custom_call", output_to_operand_aliasing={{0}: (9, {}), {1}: (10, {}), {2}: (11, {})} | custom-call | flops 458752 | bytes 458752 | tf_op jit(solution)/shard_map/expert_adamw/pallas_call | solution.py:316
  36.7 0.1 collective-permute-start.5
  36.8 0.5 collective-permute-start.6
  37.2 2.8 %latent_rest.1.refs_0_ = bf16[96,1536]{1,0:T(8,128)(2,1)} custom-call(s32[1]{0:T(128)} %bitcast.1.pos_ref.line_ref, f32[224,1536]{1,0:T(8,128)} %get-tuple-element.36.w1_ref, f32[8,128]{1,0:T(8,128)} %get-tuple-element.41.refs_0_.own_ref, f32[8,128]{1,0:T(8,128)} %copy-done.1, f32[8,128]{1,0:T(8,128)} %copy-done.2, bf16[1808,128]{1,0:T(8,128)(2,1)} %get-tuple-element.54.after_ref), custom_call_target="tpu_custom_call" | custom-call | flops 344064 | bytes 1032192 | tf_op jit(solution)/shard_map/latent_rest/pallas_call | solution.py:703
  40.0 0.2 collective-permute-start.10
  40.2 0.0 collective-permute-done.3.refs_0_
  40.2 2.5 %collective-permute-start.11 = (bf16[96,1536]{1,0:T(8,128)(2,1)}, bf16[96,1536]{1,0:T(8,128)(2,1)S(1)}, u32[]{:S(2)}, u32[]{:S(2)}) collective-permute-start(bf16[96,1536]{1,0:T(8,128)(2,1)} %latent_rest.1.refs_0_), channel_id=1, source_target_pairs={{0,2},{1,3},{2,0},{3,1},{4,6},{5,7},{6,4},{7,5},{8,10},{9,11},{10,... | collective-permute-start | bytes 884744 | tf_op jit(solution)/shard_map/ppermute | solution.py:787
  42.7 0.0 collective-permute-done.4.refs_1_
  42.7 0.9 %place_served.2.refs_8_ = bf16[2,8,896,128]{3,2,1,0:T(8,128)(2,1)} custom-call(s32[1]{0:T(128)} %bitcast.pos_ref, bf16[1808,128]{1,0:T(8,128)(2,1)S(1)} %collective-permute-done.3.refs_0_, bf16[1808,128]{1,0:T(8,128)(2,1)S(1)} %collective-permute-done.4.refs_1_), custom_call_target="tpu_custom_call" | custom-call | bytes 1851392 | tf_op jit(solution)/shard_map/place_served/pallas_call | solution.py:373
  43.6 8.7 %expert_adamw.5 = (f32[896,2048]{1,0:T(8,128)}, bf16[896,2048]{1,0:T(8,128)(2,1)}, bf16[896,2048]{1,0:T(8,128)(2,1)}, bf16[1808,128]{1,0:T(8,128)(2,1)}, bf16[18...) custom-call(s32[16]{0:T(128)} %owner_ref.5, ...), custom_call_target="tpu_custom_call", output_to_operand_aliasing={{0}: (9, {}), {1}: (10, {}), {2}: (11, {}), {7}: (12, {})} | custom-call | flops 917504 | bytes 917504 | tf_op jit(solution)/shard_map/expert_adamw/pallas_call | solution.py:316
  52.3 1.8 %collective-permute-start.7 = (bf16[1808,128]{1,0:T(8,128)(2,1)}, bf16[1808,128]{1,0:T(8,128)(2,1)S(1)}, u32[]{:S(2)}, u32[]{:S(2)}) collective-permute-start(bf16[1808,128]{1,0:T(8,128)(2,1)} %get-tuple-element.56), channel_id=1, source_target_pairs={{0,20},{4,16},{8,28},{12,24},{16,4},{20,0},{24,12},{28,8},{1,21},{... | collective-permute-start | bytes 1388552 | tf_op jit(solution)/shard_map/ppermute | solution.py:787
  54.1 0.0 collective-permute-done.5.refs_0_.refs_2_
  54.1 1.0 %collective-permute-start.8 = (bf16[1808,128]{1,0:T(8,128)(2,1)}, bf16[1808,128]{1,0:T(8,128)(2,1)S(1)}, u32[]{:S(2)}, u32[]{:S(2)}) collective-permute-start(bf16[1808,128]{1,0:T(8,128)(2,1)} %get-tuple-element.57), channel_id=1, source_target_pairs={{0,12},{4,8},{8,4},{12,0},{16,28},{20,24},{24,20},{28,16},{1,13},{... | collective-permute-start | bytes 1388552 | tf_op jit(solution)/shard_map/ppermute | solution.py:787
  55.1 7.2 %collective-permute-done.6.refs_1_.refs_3_ = bf16[1808,128]{1,0:T(8,128)(2,1)S(1)} collective-permute-done((bf16[1808,128]{1,0:T(8,128)(2,1)}, bf16[1808,128]{1,0:T(8,128)(2,1)S(1)}, u32[]{:S(2)}, u32[]{:S(2)}) %collective-permute-start.6) | collective-permute-done | bytes 462880 | tf_op jit(solution)/shard_map/ppermute | solution.py:787
  62.3 0.0 collective-permute-start.9
  62.3 0.9 %place_served.3.refs_2_ = bf16[2,8,896,128]{3,2,1,0:T(8,128)(2,1)} custom-call(s32[1]{0:T(128)} %bitcast.pos_ref, bf16[1808,128]{1,0:T(8,128)(2,1)S(1)} %collective-permute-done.5.refs_0_.refs_2_, bf16[1808,128]{1,0:T(8,128)(2,1)S(1)} %collective-permute-done.6.refs_1_.refs_3_, ...), custom_call_target="tpu_custom_call", output_to_operand_aliasing={{}: (3, {})} | custom-call | bytes 1851392 | tf_op jit(solution)/shard_map/place_served/pallas_call | solution.py:373
  63.2 0.0 collective-permute-done.10.refs_0_
  63.3 0.0 collective-permute-done.11.refs_1_
  63.3 2.0 %collective-permute-start.12 = (bf16[96,1536]{1,0:T(8,128)(2,1)S(1)}, bf16[96,1536]{1,0:T(8,128)(2,1)}, u32[]{:S(2)}, u32[]{:S(2)}) collective-permute-start(bf16[96,1536]{1,0:T(8,128)(2,1)S(1)} %get-tuple-element.65.refs_1_), channel_id=1, source_target_pairs={{0,1},{1,0},{2,3},{3,2},{4,5},{5,4},{6,7},{7,6},{8,9},{9,8},{10,11... | collective-permute-start | bytes 884744 | tf_op jit(solution)/shard_map/ppermute | solution.py:787
  65.3 1.0 %place_rest.2.refs_1_ = bf16[896,1536]{1,0:T(8,128)(2,1)} custom-call(s32[1]{0:T(128)} %bitcast.1.pos_ref.line_ref, bf16[96,1536]{1,0:T(8,128)(2,1)S(1)} %get-tuple-element.64.refs_0_, bf16[96,1536]{1,0:T(8,128)(2,1)S(1)} %get-tuple-element.65.refs_1_), custom_call_target="tpu_custom_call" | custom-call | bytes 1000000 | tf_op jit(solution)/shard_map/place_rest/pallas_call | solution.py:472
  66.3 0.0 copy-start
  66.3 0.0 all-gather.2.cloned.1.call-done.x_ref
  66.4 2.3 %place_whole.1.refs_9_ = bf16[896,1536]{1,0:T(8,128)(2,1)} custom-call(s32[1]{0:T(128)} %bitcast.1.pos_ref.line_ref, bf16[512,1536]{1,0:T(8,128)(2,1)} %all-gather.2.cloned.1.call-done.x_ref, bf16[96,1536]{1,0:T(8,128)(2,1)} %latent_rest.1.refs_0_, bf16[896,1536]{1,0:T(8,128)(2,1)} %place_rest.2.refs_1_), custom_call_target="tpu_custom_call", output_to_operand_aliasing={{}: (3, {})} | custom-call | bytes 3145728 | tf_op jit(solution)/shard_map/place_whole/pallas_call | solution.py:522
  68.7 2.0 %collective-permute-done.7.refs_4_ = bf16[1808,128]{1,0:T(8,128)(2,1)S(1)} collective-permute-done((bf16[1808,128]{1,0:T(8,128)(2,1)}, bf16[1808,128]{1,0:T(8,128)(2,1)S(1)}, u32[]{:S(2)}, u32[]{:S(2)}) %collective-permute-start.7) | collective-permute-done | bytes 462880 | tf_op jit(solution)/shard_map/ppermute | solution.py:787
  70.7 0.0 collective-permute-done.8.refs_5_
  70.7 0.0 collective-permute-done.9.refs_6_
  70.7 0.0 copy-done
  70.7 2.0 %place_last.1 = (bf16[2,8,896,128]{3,2,1,0:T(8,128)(2,1)}, bf16[896,1536]{1,0:T(8,128)(2,1)}, f32[1,112]{1,0:T(1,128)}, f32[12,56]{1,0:T(8,128)}) custom-call(s32[1]{0:T(128)} %bitcast.pos_ref, bf16[1808,128]{1,0:T(8,128)(2,1)S(1)} %collective-permute-done.3.refs_0_, ...), custom_call_target="tpu_custom_call", output_to_operand_aliasing={{0}: (9, {}), {1}: (10, {})} | custom-call | flops 1000000 | bytes 1000000 | tf_op jit(solution)/shard_map/place_last/pallas_call | solution.py:431
  72.6 0.2 collective-permute-done.12.refs_0_
  72.9 1.7 %place_rest.3 = bf16[896,1536]{1,0:T(8,128)(2,1)} custom-call(s32[1]{0:T(128)} %bitcast.1.pos_ref.line_ref, bf16[96,1536]{1,0:T(8,128)(2,1)} %collective-permute-done.12.refs_0_, bf16[896,1536]{1,0:T(8,128)(2,1)} %get-tuple-element.70.refs_1_), custom_call_target="tpu_custom_call", output_to_operand_aliasing={{}: (2, {})} | custom-call | bytes 1000000 | tf_op jit(solution)/shard_map/place_rest/pallas_call | solution.py:472
  (1 shorter events, 0.0 us)
Async XLA Ops:
  7.2 59.2 %all-gather.2.cloned.1.call-start = ((), (), s32[]{:S(2)}) async-start(), calls=%async_computation | async-start | bytes 1966080 | tf_op jit(solution)/shard_map/all_gather | solution.py:777
  12.2 6.9 %collective-permute-start = (f32[8,128]{1,0:T(8,128)}, f32[8,128]{1,0:T(8,128)S(1)}, u32[]{:S(2)}, u32[]{:S(2)}) collective-permute-start(f32[8,128]{1,0:T(8,128)} %get-tuple-element.41.refs_0_.own_ref), channel_id=1, source_target_pairs={{0,1},{1,2},{2,3},{3,0},{4,5},{5,6},{6,7},{7,4},{8,9},{9,10},{10,1... | collective-permute-start | bytes 12296 | tf_op jit(solution)/shard_map/ppermute | solution.py:779
  15.3 3.9 %collective-permute-start.2 = (f32[8,128]{1,0:T(8,128)}, f32[8,128]{1,0:T(8,128)S(1)}, u32[]{:S(2)}, u32[]{:S(2)}) collective-permute-start(f32[8,128]{1,0:T(8,128)} %get-tuple-element.41.refs_0_.own_ref), channel_id=1, source_target_pairs={{0,3},{1,0},{2,1},{3,2},{4,7},{5,4},{6,5},{7,6},{8,11},{9,8},{10,9... | collective-permute-start | bytes 12296 | tf_op jit(solution)/shard_map/ppermute | solution.py:779
  17.4 4.7 %collective-permute-start.1 = (f32[8,128]{1,0:T(8,128)}, f32[8,128]{1,0:T(8,128)S(1)}, u32[]{:S(2)}, u32[]{:S(2)}) collective-permute-start(f32[8,128]{1,0:T(8,128)} %get-tuple-element.41.refs_0_.own_ref), channel_id=1, source_target_pairs={{0,2},{1,3},{2,0},{3,1},{4,6},{5,7},{6,4},{7,5},{8,10},{9,11},{10,... | collective-permute-start | bytes 12296 | tf_op jit(solution)/shard_map/ppermute | solution.py:779
  19.2 3.0 %copy-start.1 = (f32[8,128]{1,0:T(8,128)}, f32[8,128]{1,0:T(8,128)S(1)}, u32[]{:S(2)}) copy-start(f32[8,128]{1,0:T(8,128)S(1)} %collective-permute-done.refs_1_.prev_ref) | copy-start | bytes 12292
  19.2 2.9 %copy-start.2 = (f32[8,128]{1,0:T(8,128)}, f32[8,128]{1,0:T(8,128)S(1)}, u32[]{:S(2)}) copy-start(f32[8,128]{1,0:T(8,128)S(1)} %collective-permute-done.2.refs_3_.next_ref) | copy-start | bytes 12292
  22.1 0.6 copy-start.3
  28.4 11.8 %collective-permute-start.3 = (bf16[1808,128]{1,0:T(8,128)(2,1)}, bf16[1808,128]{1,0:T(8,128)(2,1)S(1)}, u32[]{:S(2)}, u32[]{:S(2)}) collective-permute-start(bf16[1808,128]{1,0:T(8,128)(2,1)} %get-tuple-element.49), channel_id=1, source_target_pairs={{0,16},{4,20},{8,24},{12,28},{16,0},{20,4},{24,8},{28,12},{1,17},{... | collective-permute-start | bytes 1388552 | tf_op jit(solution)/shard_map/ppermute | solution.py:787
  30.1 12.6 %collective-permute-start.4 = (bf16[1808,128]{1,0:T(8,128)(2,1)}, bf16[1808,128]{1,0:T(8,128)(2,1)S(1)}, u32[]{:S(2)}, u32[]{:S(2)}) collective-permute-start(bf16[1808,128]{1,0:T(8,128)(2,1)} %get-tuple-element.50), channel_id=1, source_target_pairs={{0,8},{4,12},{8,0},{12,4},{16,24},{20,28},{24,16},{28,20},{1,9},{5... | collective-permute-start | bytes 1388552 | tf_op jit(solution)/shard_map/ppermute | solution.py:787
  36.7 17.4 %collective-permute-start.5 = (bf16[1808,128]{1,0:T(8,128)(2,1)}, bf16[1808,128]{1,0:T(8,128)(2,1)S(1)}, u32[]{:S(2)}, u32[]{:S(2)}) collective-permute-start(bf16[1808,128]{1,0:T(8,128)(2,1)} %get-tuple-element.54.after_ref), channel_id=1, source_target_pairs={{0,28},{4,24},{8,20},{12,16},{16,12},{20,8},{24,4},{28,0},{1,29},{... | collective-permute-start | bytes 1388552 | tf_op jit(solution)/shard_map/ppermute | solution.py:787
  36.8 25.5 %collective-permute-start.6 = (bf16[1808,128]{1,0:T(8,128)(2,1)}, bf16[1808,128]{1,0:T(8,128)(2,1)S(1)}, u32[]{:S(2)}, u32[]{:S(2)}) collective-permute-start(bf16[1808,128]{1,0:T(8,128)(2,1)} %get-tuple-element.55), channel_id=1, source_target_pairs={{0,24},{4,28},{8,16},{12,20},{16,8},{20,12},{24,0},{28,4},{1,25},{... | collective-permute-start | bytes 1388552 | tf_op jit(solution)/shard_map/ppermute | solution.py:787
  40.0 23.2 %collective-permute-start.10 = (bf16[96,1536]{1,0:T(8,128)(2,1)}, bf16[96,1536]{1,0:T(8,128)(2,1)S(1)}, u32[]{:S(2)}, u32[]{:S(2)}) collective-permute-start(bf16[96,1536]{1,0:T(8,128)(2,1)} %latent_rest.1.refs_0_), channel_id=1, source_target_pairs={{0,1},{1,0},{2,3},{3,2},{4,5},{5,4},{6,7},{7,6},{8,9},{9,8},{10,11... | collective-permute-start | bytes 884744 | tf_op jit(solution)/shard_map/ppermute | solution.py:787
  40.2 23.1 %collective-permute-start.11 = (bf16[96,1536]{1,0:T(8,128)(2,1)}, bf16[96,1536]{1,0:T(8,128)(2,1)S(1)}, u32[]{:S(2)}, u32[]{:S(2)}) collective-permute-start(bf16[96,1536]{1,0:T(8,128)(2,1)} %latent_rest.1.refs_0_), channel_id=1, source_target_pairs={{0,2},{1,3},{2,0},{3,1},{4,6},{5,7},{6,4},{7,5},{8,10},{9,11},{10,... | collective-permute-start | bytes 884744 | tf_op jit(solution)/shard_map/ppermute | solution.py:787
  52.3 18.3 %collective-permute-start.7 = (bf16[1808,128]{1,0:T(8,128)(2,1)}, bf16[1808,128]{1,0:T(8,128)(2,1)S(1)}, u32[]{:S(2)}, u32[]{:S(2)}) collective-permute-start(bf16[1808,128]{1,0:T(8,128)(2,1)} %get-tuple-element.56), channel_id=1, source_target_pairs={{0,20},{4,16},{8,28},{12,24},{16,4},{20,0},{24,12},{28,8},{1,21},{... | collective-permute-start | bytes 1388552 | tf_op jit(solution)/shard_map/ppermute | solution.py:787
  54.1 16.6 %collective-permute-start.8 = (bf16[1808,128]{1,0:T(8,128)(2,1)}, bf16[1808,128]{1,0:T(8,128)(2,1)S(1)}, u32[]{:S(2)}, u32[]{:S(2)}) collective-permute-start(bf16[1808,128]{1,0:T(8,128)(2,1)} %get-tuple-element.57), channel_id=1, source_target_pairs={{0,12},{4,8},{8,4},{12,0},{16,28},{20,24},{24,20},{28,16},{1,13},{... | collective-permute-start | bytes 1388552 | tf_op jit(solution)/shard_map/ppermute | solution.py:787
  62.3 8.4 %collective-permute-start.9 = (bf16[1808,128]{1,0:T(8,128)(2,1)}, bf16[1808,128]{1,0:T(8,128)(2,1)S(1)}, u32[]{:S(2)}, u32[]{:S(2)}) collective-permute-start(bf16[1808,128]{1,0:T(8,128)(2,1)} %get-tuple-element.58), channel_id=1, source_target_pairs={{0,4},{4,0},{8,12},{12,8},{16,20},{20,16},{24,28},{28,24},{1,5},{5... | collective-permute-start | bytes 1388552 | tf_op jit(solution)/shard_map/ppermute | solution.py:787
  63.3 9.6 %collective-permute-start.12 = (bf16[96,1536]{1,0:T(8,128)(2,1)S(1)}, bf16[96,1536]{1,0:T(8,128)(2,1)}, u32[]{:S(2)}, u32[]{:S(2)}) collective-permute-start(bf16[96,1536]{1,0:T(8,128)(2,1)S(1)} %get-tuple-element.65.refs_1_), channel_id=1, source_target_pairs={{0,1},{1,0},{2,3},{3,2},{4,5},{5,4},{6,7},{7,6},{8,9},{9,8},{10,11... | collective-permute-start | bytes 884744 | tf_op jit(solution)/shard_map/ppermute | solution.py:787
  66.3 4.3 %copy-start = (bf16[16,128]{1,0:T(8,128)(2,1)S(1)}, bf16[16,128]{1,0:T(8,128)(2,1)}, u32[]{:S(2)}) copy-start(bf16[16,128]{1,0:T(8,128)(2,1)} %get-tuple-element.59.refs_7_) | copy-start | bytes 12292
Sparse Core Ops, SparseCore 0:
  12.3 47.9 all-gather.1

commit v14 on v13

--- a/solution.py
+++ b/solution.py
@@ -455,14 +455,19 @@
 def rest_kernel(deltas, rows, pos_ref, *refs):
     n = len(deltas)
     latent, buf, in_sem, out_sem = refs[-4:]
-    loads = [pltpu.make_async_copy(refs[i], buf.at[i], in_sem.at[i]) for i in range(n)]
+    spans = [pl.ds(c * CHUNK, CHUNK) for c in range(buf.shape[1] // CHUNK)]
+    loads = [
+        pltpu.make_async_copy(refs[i].at[at, :], buf.at[i, at, :], in_sem.at[i, c])
+        for i in range(n)
+        for c, at in enumerate(spans)
+    ]
     copy_all(loads)
     copies = []
     for i, delta in enumerate(deltas):
-        loads[i].wait()
-        group = rest_stores(buf, i, pos_ref[0] ^ delta, rows, latent, out_sem)
-        copy_all(group)
-        copies += group
+        copies += rest_stores(buf, i, pos_ref[0] ^ delta, rows, latent, out_sem)
+    for load, copy in zip(loads, copies):
+        load.wait()
+        copy.start()
     wait_all(copies)
 
 
@@ -476,7 +481,7 @@
         out_shape=jax.ShapeDtypeStruct((peers * rows, cols), BF16),
         scratch_shapes=[
             pltpu.VMEM((n, span, cols), BF16),
-            pltpu.SemaphoreType.DMA((n,)),
+            pltpu.SemaphoreType.DMA((n, span // CHUNK)),
             pltpu.SemaphoreType.DMA((n, span // CHUNK)),
         ],
         input_output_aliases={1 + n: 0} if out else {},
@@ -533,7 +538,7 @@
             pltpu.SemaphoreType.DMA((n, span // CHUNK)),
         ],
         input_output_aliases={2 + n: 0},
-        compiler_params=PARAMS,
+        compiler_params=pltpu.CompilerParams(vmem_limit_bytes=VMEM_LIMIT - 4 * 1024 * 1024),
         cost_estimate=pl.CostEstimate(flops=0, bytes_accessed=4 * x.size, transcendentals=0),
         name="place_whole",
     )(pos, x, *xs, out)

time: 81.8 us -> 95.4 us (1.17)
  Pallas kernels: 35.4 us -> 49.7 us
  waiting for transfers between devices: 13.2 us -> 11.1 us
  local copies, waits for them, and re-layouts: 0.6 us -> 2 us
    pallas_call x1, Pallas kernels: 1.96 us -> 15.8 us  [collect(): pl.pallas_call(functools.partial(collect_kernel, order, tiles, lat_tiles,...]
    ppermute x10, waiting for transfers between devices: 9.41 us -> 7.31 us  [swap(): lax.ppermute(x, axis, [(i, i ^ k) for i in range(lax.axis_size(axis))])]
    unnamed x8 -> x12, local copies, waits for them, and re-layouts: 0.6 us -> 2 us
  transfers between devices with their start and end apart: 14 -> 14, of which waited for: 5 -> 4; matrix products, arithmetic and copies ran while one was open for 0% -> 0% of each run, Pallas kernels for 36% -> 46%
where the time goes in v14:
time: 95.4 us; the launch traced here: 95 us
  Pallas kernels  49.7 us (52%)
  starting transfers between devices  17.4 us (18%)
  between operations  14.9 us (16%)
  waiting for transfers between devices  11.1 us (12%)
  local copies, waits for them, and re-layouts  2 us (2%)
    pallas_call x3, Pallas kernels, expert_group(): pl.pallas_call(functools.partial(expert_kernel, partners, per_dest, n_ali...  19.4 us
    pallas_call x1, Pallas kernels, collect(): pl.pallas_call(functools.partial(collect_kernel, order, tiles, lat_tiles,...  15.8 us
    ppermute x10, starting transfers between devices, swap(): lax.ppermute(x, axis, [(i, i ^ k) for i in range(lax.axis_size(axis))])  11.2 us
    ppermute x10, waiting for transfers between devices, swap(): lax.ppermute(x, axis, [(i, i ^ k) for i in range(lax.axis_size(axis))])  7.31 us
    ppermute x3, starting transfers between devices, fast_body(): lax.ppermute(chunk_top, 'expert', [(i, (i + s) % exp_axis) for i in range...  6.11 us
    pallas_call x1, Pallas kernels, latent_update(): pl.pallas_call(functools.partial(latent_kernel, rows // CHUNK), in_specs=...  4.33 us
    ppermute x3, waiting for transfers between devices, fast_body(): lax.ppermute(chunk_top, 'expert', [(i, (i + s) % exp_axis) for i in range...  3.76 us
    pallas_call x2, Pallas kernels, place_rest(): pl.pallas_call(functools.partial(rest_kernel, deltas, rows), in_specs=[SM...  3.33 us
  transfers between devices with their start and end apart: 14, of which 4 were waited for; matrix products, arithmetic and copies ran while one was open for 0% of the time, Pallas kernels for 46%

profile of v14, /device:TPU:0, one launch (start us, length us, event | category | flops | bytes accessed | tf_op | source)
XLA Modules:
  0.0 95.0 jit_solution(9164061076303795536)
XLA Ops:
  7.2 0.0 all-gather.2.cloned.1.call-start
  7.9 4.3 %latent_adamw.1 = (f32[224,1536]{1,0:T(8,128)}, bf16[224,1536]{1,0:T(8,128)(2,1)}, bf16[224,1536]{1,0:T(8,128)(2,1)}, bf16[128,1536]{1,0:T(8,128)(2,1)}, f32[8,128]{1,0:T(8,128)}) custom-call(s32[1]{0:T(128)S(6)} %copy.50.step_ref, s32[1]{0:T(128)} %bitcast.1.pos_ref.line_ref, f32[224,1536]{1,0:T(8,128)} %refs_0_.1, bf16[224,1536]{1,0:T(8,128)(2,1)} %refs_1_.1, ...), custom_call_target="tpu_custom_call" | custom-call | flops 10321920 | bytes 6193152 | tf_op jit(solution)/shard_map/latent_adamw/pallas_call | solution.py:630
  12.2 0.0 all-gather.2.cloned.1.call-update
  12.2 3.1 %collective-permute-start = (f32[8,128]{1,0:T(8,128)}, f32[8,128]{1,0:T(8,128)S(1)}, u32[]{:S(2)}, u32[]{:S(2)}) collective-permute-start(f32[8,128]{1,0:T(8,128)} %get-tuple-element.41.refs_0_.own_ref), channel_id=1, source_target_pairs={{0,1},{1,2},{2,3},{3,0},{4,5},{5,6},{6,7},{7,4},{8,9},{9,10},{10,1... | collective-permute-start | bytes 12296 | tf_op jit(solution)/shard_map/ppermute | solution.py:784
  15.3 2.1 %collective-permute-start.2 = (f32[8,128]{1,0:T(8,128)}, f32[8,128]{1,0:T(8,128)S(1)}, u32[]{:S(2)}, u32[]{:S(2)}) collective-permute-start(f32[8,128]{1,0:T(8,128)} %get-tuple-element.41.refs_0_.own_ref), channel_id=1, source_target_pairs={{0,3},{1,0},{2,1},{3,2},{4,7},{5,4},{6,5},{7,6},{8,11},{9,8},{10,9... | collective-permute-start | bytes 12296 | tf_op jit(solution)/shard_map/ppermute | solution.py:784
  17.4 0.9 collective-permute-start.1
  18.3 0.8 collective-permute-done.refs_1_.prev_ref
  19.2 0.0 collective-permute-done.2.refs_3_.next_ref
  19.2 2.9 %collective-permute-done.1.refs_2_ = f32[8,128]{1,0:T(8,128)S(1)} collective-permute-done((f32[8,128]{1,0:T(8,128)}, f32[8,128]{1,0:T(8,128)S(1)}, u32[]{:S(2)}, u32[]{:S(2)}) %collective-permute-start.1) | collective-permute-done | bytes 4128 | tf_op jit(solution)/shard_map/ppermute | solution.py:784
  22.1 0.0 copy-done.3
  22.1 0.0 copy-done.4
  22.1 0.6 copy-done.5
  22.7 5.7 %expert_adamw.3 = (f32[896,2048]{1,0:T(8,128)}, bf16[896,2048]{1,0:T(8,128)(2,1)}, bf16[896,2048]{1,0:T(8,128)(2,1)}, bf16[1808,128]{1,0:T(8,128)(2,1)}, bf16[1808,128]{1,0:T(8,128)(2,1)}, /*index=5*/f32[8,128]{1,0:T(8,128)}) custom-call(s32[16]{0:T(128)} %owner_ref.5, s32[1]{0:T(128)} %bitcast.pos_ref, s32[1]{0:T(128)} %bitcast.1.pos_ref.line_ref, ...), custom_call_target="tpu_custom_call" | custom-call | flops 458752 | bytes 458752 | tf_op jit(solution)/shard_map/expert_adamw/pallas_call | solution.py:316
  28.4 1.7 %collective-permute-start.3 = (bf16[1808,128]{1,0:T(8,128)(2,1)}, bf16[1808,128]{1,0:T(8,128)(2,1)S(1)}, u32[]{:S(2)}, u32[]{:S(2)}) collective-permute-start(bf16[1808,128]{1,0:T(8,128)(2,1)} %get-tuple-element.49), channel_id=1, source_target_pairs={{0,16},{4,20},{8,24},{12,28},{16,0},{20,4},{24,8},{28,12},{1,17},{... | collective-permute-start | bytes 1388552 | tf_op jit(solution)/shard_map/ppermute | solution.py:792
  30.1 1.5 %collective-permute-start.4 = (bf16[1808,128]{1,0:T(8,128)(2,1)}, bf16[1808,128]{1,0:T(8,128)(2,1)S(1)}, u32[]{:S(2)}, u32[]{:S(2)}) collective-permute-start(bf16[1808,128]{1,0:T(8,128)(2,1)} %get-tuple-element.50), channel_id=1, source_target_pairs={{0,8},{4,12},{8,0},{12,4},{16,24},{20,28},{24,16},{28,20},{1,9},{5... | collective-permute-start | bytes 1388552 | tf_op jit(solution)/shard_map/ppermute | solution.py:792
  31.6 5.1 %expert_adamw.4 = (f32[896,2048]{1,0:T(8,128)}, bf16[896,2048]{1,0:T(8,128)(2,1)}, bf16[896,2048]{1,0:T(8,128)(2,1)}, bf16[1808,128]{1,0:T(8,128)(2,1)}, bf16[1808,128]{1,0:T(8,128)(2,1)}) custom-call(s32[16]{0:T(128)} %owner_ref.5, s32[1]{0:T(128)} %bitcast.pos_ref, ...), custom_call_target="tpu_custom_call", output_to_operand_aliasing={{0}: (9, {}), {1}: (10, {}), {2}: (11, {})} | custom-call | flops 458752 | bytes 458752 | tf_op jit(solution)/shard_map/expert_adamw/pallas_call | solution.py:316
  36.7 0.1 collective-permute-start.5
  36.8 0.5 collective-permute-start.6
  37.3 2.8 %latent_rest.1.refs_0_ = bf16[96,1536]{1,0:T(8,128)(2,1)} custom-call(s32[1]{0:T(128)} %bitcast.1.pos_ref.line_ref, f32[224,1536]{1,0:T(8,128)} %get-tuple-element.36.w1_ref, f32[8,128]{1,0:T(8,128)} %get-tuple-element.41.refs_0_.own_ref, f32[8,128]{1,0:T(8,128)} %copy-done.3, f32[8,128]{1,0:T(8,128)} %copy-done.4, bf16[1808,128]{1,0:T(8,128)(2,1)} %get-tuple-element.54.after_ref), custom_call_target="tpu_custom_call" | custom-call | flops 344064 | bytes 1032192 | tf_op jit(solution)/shard_map/latent_rest/pallas_call | solution.py:708
  40.0 0.2 collective-permute-start.10
  40.2 0.0 collective-permute-done.3.refs_0_
  40.2 2.5 %collective-permute-start.11 = (bf16[96,1536]{1,0:T(8,128)(2,1)}, bf16[96,1536]{1,0:T(8,128)(2,1)S(1)}, u32[]{:S(2)}, u32[]{:S(2)}) collective-permute-start(bf16[96,1536]{1,0:T(8,128)(2,1)} %latent_rest.1.refs_0_), channel_id=1, source_target_pairs={{0,2},{1,3},{2,0},{3,1},{4,6},{5,7},{6,4},{7,5},{8,10},{9,11},{10,... | collective-permute-start | bytes 884744 | tf_op jit(solution)/shard_map/ppermute | solution.py:792
  42.7 0.0 collective-permute-done.4.refs_1_
  42.7 0.9 place_served.2.refs_8_
  43.7 8.7 %expert_adamw.5 = (f32[896,2048]{1,0:T(8,128)}, bf16[896,2048]{1,0:T(8,128)(2,1)}, bf16[896,2048]{1,0:T(8,128)(2,1)}, bf16[1808,128]{1,0:T(8,128)(2,1)}, bf16[18...) custom-call(s32[16]{0:T(128)} %owner_ref.5, ...), custom_call_target="tpu_custom_call", output_to_operand_aliasing={{0}: (9, {}), {1}: (10, {}), {2}: (11, {}), {7}: (12, {})} | custom-call | flops 917504 | bytes 917504 | tf_op jit(solution)/shard_map/expert_adamw/pallas_call | solution.py:316
  52.3 1.8 %collective-permute-start.7 = (bf16[1808,128]{1,0:T(8,128)(2,1)}, bf16[1808,128]{1,0:T(8,128)(2,1)S(1)}, u32[]{:S(2)}, u32[]{:S(2)}) collective-permute-start(bf16[1808,128]{1,0:T(8,128)(2,1)} %get-tuple-element.56), channel_id=1, source_target_pairs={{0,20},{4,16},{8,28},{12,24},{16,4},{20,0},{24,12},{28,8},{1,21},{... | collective-permute-start | bytes 1388552 | tf_op jit(solution)/shard_map/ppermute | solution.py:792
  54.1 0.0 collective-permute-done.5.refs_0_.refs_2_
  54.1 1.0 %collective-permute-start.8 = (bf16[1808,128]{1,0:T(8,128)(2,1)}, bf16[1808,128]{1,0:T(8,128)(2,1)S(1)}, u32[]{:S(2)}, u32[]{:S(2)}) collective-permute-start(bf16[1808,128]{1,0:T(8,128)(2,1)} %get-tuple-element.57), channel_id=1, source_target_pairs={{0,12},{4,8},{8,4},{12,0},{16,28},{20,24},{24,20},{28,16},{1,13},{... | collective-permute-start | bytes 1388552 | tf_op jit(solution)/shard_map/ppermute | solution.py:792
  55.1 7.2 %collective-permute-done.6.refs_1_.refs_3_ = bf16[1808,128]{1,0:T(8,128)(2,1)S(1)} collective-permute-done((bf16[1808,128]{1,0:T(8,128)(2,1)}, bf16[1808,128]{1,0:T(8,128)(2,1)S(1)}, u32[]{:S(2)}, u32[]{:S(2)}) %collective-permute-start.6) | collective-permute-done | bytes 462880 | tf_op jit(solution)/shard_map/ppermute | solution.py:792
  62.3 0.0 collective-permute-start.9
  62.3 0.9 place_served.3.refs_2_
  63.2 0.0 copy-start.1
  63.3 0.0 collective-permute-done.10.refs_0_
  63.3 0.0 collective-permute-done.11.refs_1_
  63.3 2.0 %collective-permute-start.12 = (bf16[96,1536]{1,0:T(8,128)(2,1)S(1)}, bf16[96,1536]{1,0:T(8,128)(2,1)}, u32[]{:S(2)}, u32[]{:S(2)}) collective-permute-start(bf16[96,1536]{1,0:T(8,128)(2,1)S(1)} %get-tuple-element.65.refs_1_), channel_id=1, source_target_pairs={{0,1},{1,0},{2,3},{3,2},{4,5},{5,4},{6,7},{7,6},{8,9},{9,8},{10,11... | collective-permute-start | bytes 884744 | tf_op jit(solution)/shard_map/ppermute | solution.py:792
  65.3 1.6 %place_rest.2.refs_1_ = bf16[896,1536]{1,0:T(8,128)(2,1)} custom-call(s32[1]{0:T(128)} %bitcast.1.pos_ref.line_ref, bf16[96,1536]{1,0:T(8,128)(2,1)S(1)} %get-tuple-element.64.refs_0_, bf16[96,1536]{1,0:T(8,128)(2,1)S(1)} %get-tuple-element.65.refs_1_), custom_call_target="tpu_custom_call" | custom-call | bytes 1000000 | tf_op jit(solution)/shard_map/place_rest/pallas_call | solution.py:477
  67.0 0.0 all-gather.2.cloned.1.call-done.x_ref
  67.0 0.0 copy-done.1
  67.0 0.0 copy-start
  67.0 1.4 %copy-done = bf16[512,1536]{1,0:T(8,128)(2,1)S(1)} copy-done((bf16[512,1536]{1,0:T(8,128)(2,1)S(1)}, bf16[512,1536]{1,0:T(8,128)(2,1)}, u32[]{:S(2)}) %copy-start) | copy-done | bytes 1572888
  68.4 2.1 %place_whole.1.refs_9_ = bf16[896,1536]{1,0:T(8,128)(2,1)} custom-call(s32[1]{0:T(128)} %bitcast.1.pos_ref.line_ref, bf16[512,1536]{1,0:T(8,128)(2,1)S(1)} %copy-done, bf16[96,1536]{1,0:T(8,128)(2,1)S(1)} %copy-done.1, bf16[896,1536]{1,0:T(8,128)(2,1)} %place_rest.2.refs_1_), custom_call_target="tpu_custom_call", output_to_operand_aliasing={{}: (3, {})} | custom-call | bytes 3145728 | tf_op jit(solution)/shard_map/place_whole/pallas_call | solution.py:527
  70.6 0.1 collective-permute-done.7.refs_4_
  70.7 0.0 collective-permute-done.8.refs_5_
  70.7 0.0 collective-permute-done.9.refs_6_
  70.7 0.0 copy-done.2
  70.7 15.8 %place_last.1 = (bf16[2,8,896,128]{3,2,1,0:T(8,128)(2,1)}, bf16[896,1536]{1,0:T(8,128)(2,1)}, f32[1,112]{1,0:T(1,128)}, f32[12,56]{1,0:T(8,128)}) custom-call(s32[1]{0:T(128)} %bitcast.pos_ref, bf16[1808,128]{1,0:T(8,128)(2,1)S(1)} %collective-permute-done.3.refs_0_, ...), custom_call_target="tpu_custom_call", output_to_operand_aliasing={{0}: (9, {}), {1}: (10, {})} | custom-call | flops 1000000 | bytes 1000000 | tf_op jit(solution)/shard_map/place_last/pallas_call | solution.py:431
  86.5 0.0 collective-permute-done.12.refs_0_
  86.5 1.7 %place_rest.3 = bf16[896,1536]{1,0:T(8,128)(2,1)} custom-call(s32[1]{0:T(128)} %bitcast.1.pos_ref.line_ref, bf16[96,1536]{1,0:T(8,128)(2,1)} %collective-permute-done.12.refs_0_, bf16[896,1536]{1,0:T(8,128)(2,1)} %get-tuple-element.70.refs_1_), custom_call_target="tpu_custom_call", output_to_operand_aliasing={{}: (2, {})} | custom-call | bytes 1000000 | tf_op jit(solution)/shard_map/place_rest/pallas_call | solution.py:477
  (5 shorter events, 0.0 us)
Async XLA Ops:
  7.2 59.8 %all-gather.2.cloned.1.call-start = ((), (), s32[]{:S(2)}) async-start(), calls=%async_computation | async-start | bytes 1966080 | tf_op jit(solution)/shard_map/all_gather | solution.py:782
  12.2 6.9 %collective-permute-start = (f32[8,128]{1,0:T(8,128)}, f32[8,128]{1,0:T(8,128)S(1)}, u32[]{:S(2)}, u32[]{:S(2)}) collective-permute-start(f32[8,128]{1,0:T(8,128)} %get-tuple-element.41.refs_0_.own_ref), channel_id=1, source_target_pairs={{0,1},{1,2},{2,3},{3,0},{4,5},{5,6},{6,7},{7,4},{8,9},{9,10},{10,1... | collective-permute-start | bytes 12296 | tf_op jit(solution)/shard_map/ppermute | solution.py:784
  15.3 3.9 %collective-permute-start.2 = (f32[8,128]{1,0:T(8,128)}, f32[8,128]{1,0:T(8,128)S(1)}, u32[]{:S(2)}, u32[]{:S(2)}) collective-permute-start(f32[8,128]{1,0:T(8,128)} %get-tuple-element.41.refs_0_.own_ref), channel_id=1, source_target_pairs={{0,3},{1,0},{2,1},{3,2},{4,7},{5,4},{6,5},{7,6},{8,11},{9,8},{10,9... | collective-permute-start | bytes 12296 | tf_op jit(solution)/shard_map/ppermute | solution.py:784
  17.4 4.7 %collective-permute-start.1 = (f32[8,128]{1,0:T(8,128)}, f32[8,128]{1,0:T(8,128)S(1)}, u32[]{:S(2)}, u32[]{:S(2)}) collective-permute-start(f32[8,128]{1,0:T(8,128)} %get-tuple-element.41.refs_0_.own_ref), channel_id=1, source_target_pairs={{0,2},{1,3},{2,0},{3,1},{4,6},{5,7},{6,4},{7,5},{8,10},{9,11},{10,... | collective-permute-start | bytes 12296 | tf_op jit(solution)/shard_map/ppermute | solution.py:784
  19.2 3.0 %copy-start.3 = (f32[8,128]{1,0:T(8,128)}, f32[8,128]{1,0:T(8,128)S(1)}, u32[]{:S(2)}) copy-start(f32[8,128]{1,0:T(8,128)S(1)} %collective-permute-done.refs_1_.prev_ref) | copy-start | bytes 12292
  19.2 2.9 %copy-start.4 = (f32[8,128]{1,0:T(8,128)}, f32[8,128]{1,0:T(8,128)S(1)}, u32[]{:S(2)}) copy-start(f32[8,128]{1,0:T(8,128)S(1)} %collective-permute-done.2.refs_3_.next_ref) | copy-start | bytes 12292
  22.1 0.6 copy-start.5
  28.4 11.8 %collective-permute-start.3 = (bf16[1808,128]{1,0:T(8,128)(2,1)}, bf16[1808,128]{1,0:T(8,128)(2,1)S(1)}, u32[]{:S(2)}, u32[]{:S(2)}) collective-permute-start(bf16[1808,128]{1,0:T(8,128)(2,1)} %get-tuple-element.49), channel_id=1, source_target_pairs={{0,16},{4,20},{8,24},{12,28},{16,0},{20,4},{24,8},{28,12},{1,17},{... | collective-permute-start | bytes 1388552 | tf_op jit(solution)/shard_map/ppermute | solution.py:792
  30.1 12.6 %collective-permute-start.4 = (bf16[1808,128]{1,0:T(8,128)(2,1)}, bf16[1808,128]{1,0:T(8,128)(2,1)S(1)}, u32[]{:S(2)}, u32[]{:S(2)}) collective-permute-start(bf16[1808,128]{1,0:T(8,128)(2,1)} %get-tuple-element.50), channel_id=1, source_target_pairs={{0,8},{4,12},{8,0},{12,4},{16,24},{20,28},{24,16},{28,20},{1,9},{5... | collective-permute-start | bytes 1388552 | tf_op jit(solution)/shard_map/ppermute | solution.py:792
  36.7 17.4 %collective-permute-start.5 = (bf16[1808,128]{1,0:T(8,128)(2,1)}, bf16[1808,128]{1,0:T(8,128)(2,1)S(1)}, u32[]{:S(2)}, u32[]{:S(2)}) collective-permute-start(bf16[1808,128]{1,0:T(8,128)(2,1)} %get-tuple-element.54.after_ref), channel_id=1, source_target_pairs={{0,28},{4,24},{8,20},{12,16},{16,12},{20,8},{24,4},{28,0},{1,29},{... | collective-permute-start | bytes 1388552 | tf_op jit(solution)/shard_map/ppermute | solution.py:792
  36.8 25.5 %collective-permute-start.6 = (bf16[1808,128]{1,0:T(8,128)(2,1)}, bf16[1808,128]{1,0:T(8,128)(2,1)S(1)}, u32[]{:S(2)}, u32[]{:S(2)}) collective-permute-start(bf16[1808,128]{1,0:T(8,128)(2,1)} %get-tuple-element.55), channel_id=1, source_target_pairs={{0,24},{4,28},{8,16},{12,20},{16,8},{20,12},{24,0},{28,4},{1,25},{... | collective-permute-start | bytes 1388552 | tf_op jit(solution)/shard_map/ppermute | solution.py:792
  40.0 23.2 %collective-permute-start.10 = (bf16[96,1536]{1,0:T(8,128)(2,1)}, bf16[96,1536]{1,0:T(8,128)(2,1)S(1)}, u32[]{:S(2)}, u32[]{:S(2)}) collective-permute-start(bf16[96,1536]{1,0:T(8,128)(2,1)} %latent_rest.1.refs_0_), channel_id=1, source_target_pairs={{0,1},{1,0},{2,3},{3,2},{4,5},{5,4},{6,7},{7,6},{8,9},{9,8},{10,11... | collective-permute-start | bytes 884744 | tf_op jit(solution)/shard_map/ppermute | solution.py:792
  40.2 23.1 %collective-permute-start.11 = (bf16[96,1536]{1,0:T(8,128)(2,1)}, bf16[96,1536]{1,0:T(8,128)(2,1)S(1)}, u32[]{:S(2)}, u32[]{:S(2)}) collective-permute-start(bf16[96,1536]{1,0:T(8,128)(2,1)} %latent_rest.1.refs_0_), channel_id=1, source_target_pairs={{0,2},{1,3},{2,0},{3,1},{4,6},{5,7},{6,4},{7,5},{8,10},{9,11},{10,... | collective-permute-start | bytes 884744 | tf_op jit(solution)/shard_map/ppermute | solution.py:792
  52.3 18.3 %collective-permute-start.7 = (bf16[1808,128]{1,0:T(8,128)(2,1)}, bf16[1808,128]{1,0:T(8,128)(2,1)S(1)}, u32[]{:S(2)}, u32[]{:S(2)}) collective-permute-start(bf16[1808,128]{1,0:T(8,128)(2,1)} %get-tuple-element.56), channel_id=1, source_target_pairs={{0,20},{4,16},{8,28},{12,24},{16,4},{20,0},{24,12},{28,8},{1,21},{... | collective-permute-start | bytes 1388552 | tf_op jit(solution)/shard_map/ppermute | solution.py:792
  54.1 16.5 %collective-permute-start.8 = (bf16[1808,128]{1,0:T(8,128)(2,1)}, bf16[1808,128]{1,0:T(8,128)(2,1)S(1)}, u32[]{:S(2)}, u32[]{:S(2)}) collective-permute-start(bf16[1808,128]{1,0:T(8,128)(2,1)} %get-tuple-element.57), channel_id=1, source_target_pairs={{0,12},{4,8},{8,4},{12,0},{16,28},{20,24},{24,20},{28,16},{1,13},{... | collective-permute-start | bytes 1388552 | tf_op jit(solution)/shard_map/ppermute | solution.py:792
  62.3 8.4 %collective-permute-start.9 = (bf16[1808,128]{1,0:T(8,128)(2,1)}, bf16[1808,128]{1,0:T(8,128)(2,1)}, u32[]{:S(2)}, u32[]{:S(2)}) collective-permute-start(bf16[1808,128]{1,0:T(8,128)(2,1)} %get-tuple-element.58), channel_id=1, source_target_pairs={{0,4},{4,0},{8,12},{12,8},{16,20},{20,16},{24,28},{28,24},{1,5},{5... | collective-permute-start | bytes 1388552 | tf_op jit(solution)/shard_map/ppermute | solution.py:792
  63.2 3.8 %copy-start.1 = (bf16[96,1536]{1,0:T(8,128)(2,1)S(1)}, bf16[96,1536]{1,0:T(8,128)(2,1)}, u32[]{:S(2)}) copy-start(bf16[96,1536]{1,0:T(8,128)(2,1)} %latent_rest.1.refs_0_) | copy-start | bytes 884740
  63.3 23.2 %collective-permute-start.12 = (bf16[96,1536]{1,0:T(8,128)(2,1)S(1)}, bf16[96,1536]{1,0:T(8,128)(2,1)}, u32[]{:S(2)}, u32[]{:S(2)}) collective-permute-start(bf16[96,1536]{1,0:T(8,128)(2,1)S(1)} %get-tuple-element.65.refs_1_), channel_id=1, source_target_pairs={{0,1},{1,0},{2,3},{3,2},{4,5},{5,4},{6,7},{7,6},{8,9},{9,8},{10,11... | collective-permute-start | bytes 884744 | tf_op jit(solution)/shard_map/ppermute | solution.py:792
  67.0 1.4 %copy-start = (bf16[512,1536]{1,0:T(8,128)(2,1)S(1)}, bf16[512,1536]{1,0:T(8,128)(2,1)}, u32[]{:S(2)}) copy-start(bf16[512,1536]{1,0:T(8,128)(2,1)} %all-gather.2.cloned.1.call-done.x_ref) | copy-start | bytes 4718596
  68.4 2.2 %copy-start.2 = (bf16[16,128]{1,0:T(8,128)(2,1)S(1)}, bf16[16,128]{1,0:T(8,128)(2,1)}, u32[]{:S(2)}) copy-start(bf16[16,128]{1,0:T(8,128)(2,1)} %get-tuple-element.59.refs_7_) | copy-start | bytes 12292
Sparse Core Ops, SparseCore 0:
  12.4 47.9 all-gather.1
